TPU v7x, 32 devices: a whole 2x2x4 slice. The times are simulated.
32 devices in a mesh: shard: 4 (over z), context: 2 (over y), tensor: 4 (over x, core).
Axes of the slice: x: 2, y: 2, z: 4, core: 2. Of those that a mesh axis runs over, the one named last changes fastest.
Arguments:
- residual_in: bfloat16 [8192, 1536], P(('shard', 'context')), may hold values from -6 to 6
- gain_attn: bfloat16 [1536], P(('shard', 'context')), may hold values from 0.5 to 1.5
- query_weight: bfloat16 [1536, 1536], P(('shard', 'context'), 'tensor'), may hold values from -0.15625 to 0.15625
- key_projection_weight: bfloat16 [1536, 512], P(('shard', 'context'), 'tensor'), may hold values from -0.15625 to 0.15625
- value_projection_weight: bfloat16 [1536, 512], P(('shard', 'context'), 'tensor'), may hold values from -0.15625 to 0.15625
- out_weight: bfloat16 [1536, 1536], P('tensor', ('shard', 'context')), may hold values from -1.25 to 1.25
- gain_ffn: bfloat16 [1536], P(('shard', 'context')), may hold values from 0.5 to 1.5
- gate_weight: bfloat16 [40, 1536, 512], P(None, ('shard', 'context'), 'tensor'), may hold values from -0.15625 to 0.15625
- up_weight: bfloat16 [40, 1536, 512], P(None, ('shard', 'context'), 'tensor'), may hold values from -0.15625 to 0.15625
- down_weight: bfloat16 [40, 512, 1536], P(None, 'tensor', ('shard', 'context')), may hold values from -1 to 1
- segments: int32 [8192], P('shard'), may hold values from 0 to 4, as said below
- routes: int32 [8192, 8], P(('shard', 'context')), may hold values from 0 to 39, all different within a row; in each aligned block of 1024 rows (0 to 1023, 1024 to 2047, ...) at most 256 rows name the same one
- shares: float32 [8192, 8], P(('shard', 'context')), may hold values from 0.05 to 0.25
- cotangent: bfloat16 [8192, 1536], P(('shard', 'context')), may hold values from -6 to 6
Outputs:
- output: bfloat16 [8192, 1536], P(('shard', 'context'))
- grad_input: bfloat16 [8192, 1536], P(('shard', 'context'))
- grad_gain_attn: float32 [1536], P(('shard', 'context'))
- grad_query: float32 [1536, 1536], P(('shard', 'context'), 'tensor')
- grad_key: float32 [1536, 512], P(('shard', 'context'), 'tensor')
- grad_value: float32 [1536, 512], P(('shard', 'context'), 'tensor')
- grad_out: float32 [1536, 1536], P('tensor', ('shard', 'context'))
- grad_gain_ffn: float32 [1536], P(('shard', 'context'))
- grad_gate: float32 [40, 1536, 512], P(None, ('shard', 'context'), 'tensor')
- grad_up: float32 [40, 1536, 512], P(None, ('shard', 'context'), 'tensor')
- grad_down: float32 [40, 512, 1536], P(None, 'tensor', ('shard', 'context'))
Inputs may be any that keep to these rules, and one draw needn't show every extreme that they name: `segments`: within each group of 2048 tokens the numbers start at 0, never fall and rise by one at each new document, 5 documents a group; every document has at most 1024 tokens, and one document in each group has exactly 1024 and reaches from the first half of the group into the second. `routes`: each row names 8 different experts; in each aligned block of 1024 rows (the tokens of one index of shard and context) no expert is named by more than 256 rows.
All inputs are finite; a program needn't handle non-finite values.
Results may differ from a plain program's by a relative error of at most 0.025.
Values may be sent and summed in bfloat16 or wider, within the bound.
A program may use at most 256 MiB of HBM per device.

v0:
```python
from functools import partial

import jax
import jax.numpy as jnp
from jax import lax
from jax.sharding import PartitionSpec as P

HEAD_DIM = 64
NDOCS = 5


epsilon = 1e-06


def rms_scale(values, gain):
    return values * lax.rsqrt(jnp.mean(values * values, axis=-1, keepdims=True) + epsilon) * gain


def doc_positions(segment_ids):
    sequence_length = segment_ids.shape[-1]
    index_row = jnp.arange(sequence_length, dtype=jnp.int32)
    documents = jnp.arange(NDOCS, dtype=jnp.int32)
    doc_starts = jnp.sum((segment_ids[..., :, None] < documents).astype(jnp.int32), axis=-2)
    own_start = jnp.sum(
        jnp.where(segment_ids[..., :, None] == documents, doc_starts[..., None, :], 0), axis=-1
    )
    return index_row - own_start


def rotary(values, positions):
    half_dim = values.shape[-1] // 2
    frequencies = 10000.0 ** (-2.0 * jnp.arange(half_dim, dtype=jnp.float32) / values.shape[-1])
    angles = positions.astype(jnp.float32)[:, None] * frequencies[None, :]
    cosine = jnp.cos(angles)[:, None, :]
    sines = jnp.sin(angles)[:, None, :]
    first_half = values[..., :half_dim]
    second_half = values[..., half_dim:]
    return jnp.concatenate(
        [first_half * cosine - second_half * sines, second_half * cosine + first_half * sines],
        axis=-1,
    )


def swiglu(gate_value, up_value):
    return jax.nn.silu(gate_value) * up_value


def dispatch(routes, shares, block_rows, capacity, expert_count):
    block_count = routes.shape[0] // block_rows
    picks = routes.shape[1]
    chosen = routes.reshape(block_count, block_rows * picks)
    onehot = (chosen[:, :, None] == jnp.arange(expert_count, dtype=jnp.int32)).astype(jnp.int32)
    ranked = jnp.sum((jnp.cumsum(onehot, axis=1) - onehot) * onehot, axis=2)
    slot_index = (
        chosen * (block_count * capacity)
        + jnp.arange(block_count, dtype=jnp.int32)[:, None] * capacity
        + ranked
    )
    tokens = jnp.arange(block_count * block_rows * picks, dtype=jnp.int32) // picks
    total_slots = expert_count * block_count * capacity
    slot_rows = jnp.zeros((total_slots,), jnp.int32).at[slot_index.reshape(-1)].set(tokens)
    slot_share = (
        jnp.zeros((total_slots,), jnp.float32).at[slot_index.reshape(-1)].set(shares.reshape(-1))
    )
    return (slot_rows, slot_share)


def on_device(
    residual_in,
    gain_attn,
    query_weight,
    key_projection_weight,
    value_projection_weight,
    out_weight,
    gain_ffn,
    gate_weight,
    up_weight,
    down_weight,
    segments,
    routes,
    shares,
    cotangent,
):
    row_count, model_width = residual_in.shape
    head_size = HEAD_DIM
    query_cols = query_weight.shape[1]
    kv_heads = key_projection_weight.shape[1] // head_size
    group_size = query_cols // head_size // kv_heads
    expert_count = gate_weight.shape[0]
    capacity = row_count * routes.shape[1] * 5 // (4 * expert_count)
    score_scale = head_size ** (-0.5)
    context_rank = lax.axis_index("context")
    own_first = context_rank * row_count
    gain_attn_full, gain_ffn_full, query_full, key_full, value_full, out_full = (
        lax.all_gather(gain_attn, ("shard", "context"), axis=0, tiled=True),
        lax.all_gather(gain_ffn, ("shard", "context"), axis=0, tiled=True),
        lax.all_gather(query_weight, ("shard", "context"), axis=0, tiled=True),
        lax.all_gather(key_projection_weight, ("shard", "context"), axis=0, tiled=True),
        lax.all_gather(value_projection_weight, ("shard", "context"), axis=0, tiled=True),
        lax.all_gather(out_weight, ("shard", "context"), axis=1, tiled=True),
    )
    gain_attn_float = gain_attn_full.astype(jnp.float32)
    gain_ffn_float = gain_ffn_full.astype(jnp.float32)
    positions = doc_positions(segments)
    own_positions = lax.dynamic_slice_in_dim(positions, own_first, row_count)
    own_ids = lax.dynamic_slice_in_dim(segments, own_first, row_count)
    own_index = own_first + jnp.arange(row_count, dtype=jnp.int32)
    input_float = residual_in.astype(jnp.float32)
    normed_attn, attn_norm_back = jax.vjp(rms_scale, input_float, gain_attn_float)
    first_normalized = normed_attn.astype(jnp.bfloat16)
    query_lin = jnp.dot(first_normalized, query_full, preferred_element_type=jnp.float32).reshape(
        row_count, -1, head_size
    )
    key_linear = jnp.dot(first_normalized, key_full, preferred_element_type=jnp.float32).reshape(
        row_count, -1, head_size
    )
    value_tokens = jnp.dot(first_normalized, value_full, preferred_element_type=jnp.float32).astype(
        jnp.bfloat16
    )
    rope_local = partial(rotary, positions=own_positions)
    query_rot, rope_query_back = jax.vjp(rope_local, query_lin)
    key_rot, rope_key_back = jax.vjp(rope_local, key_linear)
    query_low = query_rot.astype(jnp.bfloat16)
    key_low = key_rot.astype(jnp.bfloat16).reshape(row_count, -1)
    key_all, value_all = (
        lax.all_gather(key_low, "context", axis=0, tiled=True),
        lax.all_gather(value_tokens, "context", axis=0, tiled=True),
    )
    key_index = jnp.arange(key_all.shape[0], dtype=jnp.int32)
    key_ids = jnp.take(segments, jnp.clip(key_index, 0, segments.shape[0] - 1))
    key_valid = key_index >= 0
    key_heads = key_all.reshape(-1, kv_heads, head_size)
    value_heads = value_all.reshape(-1, kv_heads, head_size)
    query_heads = query_low.reshape(row_count, kv_heads, group_size, head_size)
    block_rows = min(512, row_count)
    block_starts = list(range(0, row_count, block_rows))

    def block_scores(block_first):
        query_block = query_heads[block_first : block_first + block_rows]
        raw_scores = jnp.einsum(
            "qgrd,kgd->grqk", query_block, key_heads, preferred_element_type=jnp.float32
        )
        block_ids = own_ids[block_first : block_first + block_rows]
        block_index = own_index[block_first : block_first + block_rows]
        allowed = (
            key_valid[None, :]
            & (key_ids[None, :] == block_ids[:, None])
            & (key_index[None, :] <= block_index[:, None])
        )
        return (query_block, jnp.where(allowed, raw_scores * score_scale, -1e30))

    mixed_parts = []
    lse_parts = []
    for block_first in block_starts:
        query_block, scores = block_scores(block_first)
        row_max = jnp.max(scores, axis=-1, keepdims=True)
        exponent = jnp.exp(scores - row_max)
        row_total = jnp.sum(exponent, axis=-1, keepdims=True)
        probs = (exponent / row_total).astype(jnp.bfloat16)
        mixed_parts.append(
            jnp.einsum("grqk,kgd->qgrd", probs, value_heads, preferred_element_type=jnp.float32)
        )
        lse_parts.append(row_max + jnp.log(row_total))
    attended = (
        jnp.concatenate(mixed_parts, axis=0).reshape(row_count, query_cols).astype(jnp.bfloat16)
    )
    attn_part = jnp.dot(attended, out_full, preferred_element_type=jnp.float32)
    hidden = input_float + lax.psum(attn_part.astype(jnp.bfloat16), "tensor").astype(jnp.float32)
    normed_ffn, ffn_norm_back = jax.vjp(rms_scale, hidden, gain_ffn_float)
    normed_second = normed_ffn.astype(jnp.bfloat16)
    slot_rows, slot_share = dispatch(routes, shares, row_count, capacity, expert_count)
    per_turn = expert_count // 5
    turn_count = expert_count // per_turn
    turn_slots = per_turn * capacity

    def local_experts(turn_index):
        gate_part = lax.dynamic_slice_in_dim(gate_weight, turn_index * per_turn, per_turn, 0)
        up_part = lax.dynamic_slice_in_dim(up_weight, turn_index * per_turn, per_turn, 0)
        down_part = lax.dynamic_slice_in_dim(down_weight, turn_index * per_turn, per_turn, 0)
        return (gate_part, up_part, down_part)

    def turn_inputs(turn_index):
        token_rows = lax.dynamic_slice_in_dim(slot_rows, turn_index * turn_slots, turn_slots)
        share_rows = lax.dynamic_slice_in_dim(slot_share, turn_index * turn_slots, turn_slots)
        picked = normed_second[token_rows].reshape(per_turn, capacity, model_width)
        return (token_rows, share_rows, picked)

    def forward_turn(running, turn_index):
        gate_part, up_part, down_part = local_experts(turn_index)
        gate_full, up_full, down_full = (
            lax.all_gather(gate_part, ("shard", "context"), axis=1, tiled=True),
            lax.all_gather(up_part, ("shard", "context"), axis=1, tiled=True),
            lax.all_gather(down_part, ("shard", "context"), axis=2, tiled=True),
        )
        token_rows, share_rows, picked = turn_inputs(turn_index)
        gate_value = jnp.einsum(
            "ecd,edf->ecf", picked, gate_full, preferred_element_type=jnp.float32
        )
        up_value = jnp.einsum("ecd,edf->ecf", picked, up_full, preferred_element_type=jnp.float32)
        inner = swiglu(gate_value, up_value).astype(jnp.bfloat16)
        expert_result = jnp.einsum(
            "ecf,efd->ecd", inner, down_full, preferred_element_type=jnp.float32
        ).reshape(turn_slots, model_width)
        return (running.at[token_rows].add(expert_result * share_rows[:, None]), None)

    turn_ids = jnp.arange(turn_count, dtype=jnp.int32)
    expert_part, _ = lax.scan(
        forward_turn, jnp.zeros((row_count, model_width), jnp.float32), turn_ids
    )
    expert_total = lax.psum(expert_part.astype(jnp.bfloat16), "tensor").astype(jnp.float32)
    output = (hidden + expert_total).astype(jnp.bfloat16)
    upstream = cotangent.astype(jnp.float32)

    def backward_turn(running, turn_index):
        gate_part, up_part, down_part = local_experts(turn_index)
        gate_full, up_full, down_full = (
            lax.all_gather(gate_part, ("shard", "context"), axis=1, tiled=True),
            lax.all_gather(up_part, ("shard", "context"), axis=1, tiled=True),
            lax.all_gather(down_part, ("shard", "context"), axis=2, tiled=True),
        )
        token_rows, share_rows, picked = turn_inputs(turn_index)
        gate_value = jnp.einsum(
            "ecd,edf->ecf", picked, gate_full, preferred_element_type=jnp.float32
        )
        up_value = jnp.einsum("ecd,edf->ecf", picked, up_full, preferred_element_type=jnp.float32)
        inner_float, swiglu_back = jax.vjp(swiglu, gate_value, up_value)
        inner = inner_float.astype(jnp.bfloat16)
        grad_slot = (
            (upstream[token_rows] * share_rows[:, None])
            .astype(jnp.bfloat16)
            .reshape(per_turn, capacity, model_width)
        )
        grad_inner = jnp.einsum(
            "ecd,efd->ecf", grad_slot, down_full, preferred_element_type=jnp.float32
        )
        grad_gate_value, grad_up_value = swiglu_back(grad_inner)
        grad_gate_low = grad_gate_value.astype(jnp.bfloat16)
        grad_up_low = grad_up_value.astype(jnp.bfloat16)
        grad_picked = jnp.einsum(
            "ecf,edf->ecd", grad_gate_low, gate_full, preferred_element_type=jnp.float32
        )
        grad_picked = grad_picked + jnp.einsum(
            "ecf,edf->ecd", grad_up_low, up_full, preferred_element_type=jnp.float32
        )
        running = running.at[token_rows].add(grad_picked.reshape(turn_slots, model_width))
        shard_grads = (
            lax.psum_scatter(
                jnp.einsum(
                    "ecd,ecf->edf", picked, grad_gate_low, preferred_element_type=jnp.float32
                ).astype(jnp.bfloat16),
                ("shard", "context"),
                scatter_dimension=1,
                tiled=True,
            ).astype(jnp.float32),
            lax.psum_scatter(
                jnp.einsum(
                    "ecd,ecf->edf", picked, grad_up_low, preferred_element_type=jnp.float32
                ).astype(jnp.bfloat16),
                ("shard", "context"),
                scatter_dimension=1,
                tiled=True,
            ).astype(jnp.float32),
            lax.psum_scatter(
                jnp.einsum(
                    "ecf,ecd->efd", inner, grad_slot, preferred_element_type=jnp.float32
                ).astype(jnp.bfloat16),
                ("shard", "context"),
                scatter_dimension=2,
                tiled=True,
            ).astype(jnp.float32),
        )
        return (running, shard_grads)

    grad_second_part, stacked_grads = lax.scan(
        backward_turn, jnp.zeros((row_count, model_width), jnp.float32), turn_ids
    )
    grad_gate_out = stacked_grads[0].reshape(gate_weight.shape)
    grad_up_out = stacked_grads[1].reshape(up_weight.shape)
    grad_down_out = stacked_grads[2].reshape(down_weight.shape)
    grad_second = lax.psum(grad_second_part.astype(jnp.bfloat16), "tensor").astype(jnp.float32)
    grad_hidden_norm, grad_gain_ffn_local = ffn_norm_back(grad_second)
    grad_hidden = upstream + grad_hidden_norm
    grad_hidden_low = grad_hidden.astype(jnp.bfloat16)
    grad_out_local = jnp.einsum(
        "tc,td->cd", attended, grad_hidden_low, preferred_element_type=jnp.float32
    )
    grad_attended = jnp.einsum(
        "td,cd->tc", grad_hidden_low, out_full, preferred_element_type=jnp.float32
    )
    grad_attended = grad_attended.astype(jnp.bfloat16).reshape(
        row_count, kv_heads, group_size, head_size
    )
    grad_query_parts = []
    grad_keys = jnp.zeros(key_heads.shape, jnp.float32)
    grad_values = jnp.zeros(value_heads.shape, jnp.float32)
    for block_number in range(len(block_starts)):
        block_first = block_starts[block_number]
        query_block, scores = block_scores(block_first)
        probs_float = jnp.exp(scores - lse_parts[block_number])
        probs = probs_float.astype(jnp.bfloat16)
        grad_block = grad_attended[block_first : block_first + block_rows]
        grad_probs = jnp.einsum(
            "qgrd,kgd->grqk", grad_block, value_heads, preferred_element_type=jnp.float32
        )
        inner_sum = jnp.sum(grad_probs * probs_float, axis=-1, keepdims=True)
        grad_scores = (score_scale * (probs_float * (grad_probs - inner_sum))).astype(jnp.bfloat16)
        grad_query_parts.append(
            jnp.einsum("grqk,kgd->qgrd", grad_scores, key_heads, preferred_element_type=jnp.float32)
        )
        grad_keys = grad_keys + jnp.einsum(
            "grqk,qgrd->kgd", grad_scores, query_block, preferred_element_type=jnp.float32
        )
        grad_values = grad_values + jnp.einsum(
            "grqk,qgrd->kgd", probs, grad_block, preferred_element_type=jnp.float32
        )
    grad_key_own, grad_value_own = (
        lax.psum_scatter(
            grad_keys.astype(jnp.bfloat16), "context", scatter_dimension=0, tiled=True
        ).astype(jnp.float32),
        lax.psum_scatter(
            grad_values.astype(jnp.bfloat16), "context", scatter_dimension=0, tiled=True
        ).astype(jnp.float32),
    )
    grad_query_all = jnp.concatenate(grad_query_parts, axis=0).reshape(row_count, -1, head_size)
    grad_query_lin = rope_query_back(grad_query_all)[0].astype(jnp.bfloat16).reshape(row_count, -1)
    grad_key_lin = rope_key_back(grad_key_own)[0].astype(jnp.bfloat16).reshape(row_count, -1)
    grad_value_low = grad_value_own.astype(jnp.bfloat16).reshape(row_count, -1)
    grad_first_part = jnp.einsum(
        "tc,dc->td", grad_query_lin, query_full, preferred_element_type=jnp.float32
    )
    grad_first_part = grad_first_part + jnp.einsum(
        "tc,dc->td", grad_key_lin, key_full, preferred_element_type=jnp.float32
    )
    grad_first_part = grad_first_part + jnp.einsum(
        "tc,dc->td", grad_value_low, value_full, preferred_element_type=jnp.float32
    )
    grad_first = lax.psum(grad_first_part.astype(jnp.bfloat16), "tensor").astype(jnp.float32)
    grad_input_norm, grad_gain_attn_local = attn_norm_back(grad_first)
    grad_input = (grad_hidden + grad_input_norm).astype(jnp.bfloat16)
    grad_query_local = jnp.einsum(
        "td,tc->dc", first_normalized, grad_query_lin, preferred_element_type=jnp.float32
    )
    grad_key_local = jnp.einsum(
        "td,tc->dc", first_normalized, grad_key_lin, preferred_element_type=jnp.float32
    )
    grad_value_local = jnp.einsum(
        "td,tc->dc", first_normalized, grad_value_low, preferred_element_type=jnp.float32
    )
    reduced = (
        lax.psum_scatter(
            grad_gain_attn_local.astype(jnp.bfloat16),
            ("shard", "context"),
            scatter_dimension=0,
            tiled=True,
        ).astype(jnp.float32),
        lax.psum_scatter(
            grad_query_local.astype(jnp.bfloat16),
            ("shard", "context"),
            scatter_dimension=0,
            tiled=True,
        ).astype(jnp.float32),
        lax.psum_scatter(
            grad_key_local.astype(jnp.bfloat16),
            ("shard", "context"),
            scatter_dimension=0,
            tiled=True,
        ).astype(jnp.float32),
        lax.psum_scatter(
            grad_value_local.astype(jnp.bfloat16),
            ("shard", "context"),
            scatter_dimension=0,
            tiled=True,
        ).astype(jnp.float32),
        lax.psum_scatter(
            grad_out_local.astype(jnp.bfloat16),
            ("shard", "context"),
            scatter_dimension=1,
            tiled=True,
        ).astype(jnp.float32),
        lax.psum_scatter(
            grad_gain_ffn_local.astype(jnp.bfloat16),
            ("shard", "context"),
            scatter_dimension=0,
            tiled=True,
        ).astype(jnp.float32),
    )
    return (
        output,
        grad_input,
        reduced[0],
        reduced[1],
        reduced[2],
        reduced[3],
        reduced[4],
        reduced[5],
        grad_gate_out,
        grad_up_out,
        grad_down_out,
    )


def solution(mesh):
    placed = (
        P(("shard", "context"), None),
        P(("shard", "context")),
        P(("shard", "context"), "tensor"),
        P(("shard", "context"), "tensor"),
        P(("shard", "context"), "tensor"),
        P("tensor", ("shard", "context")),
        P(("shard", "context")),
        P(None, ("shard", "context"), "tensor"),
        P(None, ("shard", "context"), "tensor"),
        P(None, "tensor", ("shard", "context")),
        P("shard"),
        P(("shard", "context"), None),
        P(("shard", "context"), None),
        P(("shard", "context"), None),
    )
    return jax.shard_map(
        on_device,
        mesh=mesh,
        in_specs=placed,
        out_specs=(
            P(("shard", "context"), None),
            P(("shard", "context"), None),
            P(("shard", "context")),
            P(("shard", "context"), "tensor"),
            P(("shard", "context"), "tensor"),
            P(("shard", "context"), "tensor"),
            P("tensor", ("shard", "context")),
            P(("shard", "context")),
            P(None, ("shard", "context"), "tensor"),
            P(None, ("shard", "context"), "tensor"),
            P(None, "tensor", ("shard", "context")),
        ),
        check_vma=False,
    )
```

profile of v0, /device:TPU:0, one launch (start us, length us, event | category | flops | bytes accessed | tf_op | source)
XLA Modules:
  0.0 4325.8 jit_solution(18051430484941807424)
XLA Ops:
  86.2 31.4 all_gather.45
  117.6 33.3 all_gather.43
  268.9 31.2 scatter_custom_fusion.2
  343.0 2161.3 %while.27 = (s32[]{:T(128)}, f32[1024,1536]{1,0:T(8,128)}, f32[5,8,192,128]{3,2,1,0:T(8,128)}, f32[5,8,192,128]{3,2,1,0:T(8,128)}, f32[5,8,128,192]{2,3,1,0:T(8,...) while((s32[]{:T(128)}, f32[1024,1536]{1,0:T(8,128)}, ...), condition=%wide.region_23.24_spmd, body=%wide.region_18.23_spmd.sunk | while | flops 6471884800 | bytes 309822304 | solution.py:274
  413.5 55.3 %all-gather.19.cloned.1.call-done = bf16[8,1536,128]{2,1,0:T(8,128)(2,1)} async-done(((bf16[8,192,128]{2,1,0:T(8,128)(2,1)}), bf16[8,1536,128]{2,1,0:T(8,128)(2,1)}) %all-gather.19.cloned.1.call-update) | async-done | bytes 3145744 | tf_op jit(solution)/shard_map/while/body/eval_jaxpr/all_gather | solution.py:217
  475.3 54.7 %all-gather.23.cloned.1.call-done = bf16[8,128,1536]{1,2,0:T(8,128)(2,1)} async-done(((bf16[8,128,192]{1,2,0:T(8,128)(2,1)}), bf16[8,128,1536]{1,2,0:T(8,128)(2,1)}) %all-gather.23.cloned.1.call-update) | async-done | bytes 3145744 | tf_op jit(solution)/shard_map/while/body/eval_jaxpr/all_gather | solution.py:219
  621.8 75.3 %reduce-scatter.24.cloned.1.call-done = bf16[8,192,128]{2,1,0:T(8,128)(2,1)} async-done(((bf16[8,1536,128]{2,1,0:T(8,128)(2,1)}), bf16[8,192,128]{2,1,0:T(8,128)(2,1)}) %reduce-scatter.24.cloned.1.call-update) | async-done | bytes 393232 | tf_op jit(solution)/shard_map/while/body/eval_jaxpr/reduce_scatter | solution.py:255
  699.0 75.3 %reduce-scatter.26.cloned.1.call-done = bf16[8,128,192]{1,2,0:T(8,128)(2,1)} async-done(((bf16[8,128,1536]{1,2,0:T(8,128)(2,1)}), bf16[8,128,192]{1,2,0:T(8,128)(2,1)}) %reduce-scatter.26.cloned.1.call-update) | async-done | bytes 393232 | tf_op jit(solution)/shard_map/while/body/eval_jaxpr/reduce_scatter | solution.py:263
  845.6 55.5 %all-gather.19.cloned.1.call-done = bf16[8,1536,128]{2,1,0:T(8,128)(2,1)} async-done(((bf16[8,192,128]{2,1,0:T(8,128)(2,1)}), bf16[8,1536,128]{2,1,0:T(8,128)(2,1)}) %all-gather.19.cloned.1.call-update) | async-done | bytes 3145744 | tf_op jit(solution)/shard_map/while/body/eval_jaxpr/all_gather | solution.py:217
  907.5 54.7 %all-gather.23.cloned.1.call-done = bf16[8,128,1536]{1,2,0:T(8,128)(2,1)} async-done(((bf16[8,128,192]{1,2,0:T(8,128)(2,1)}), bf16[8,128,1536]{1,2,0:T(8,128)(2,1)}) %all-gather.23.cloned.1.call-update) | async-done | bytes 3145744 | tf_op jit(solution)/shard_map/while/body/eval_jaxpr/all_gather | solution.py:219
  1054.0 75.2 %reduce-scatter.24.cloned.1.call-done = bf16[8,192,128]{2,1,0:T(8,128)(2,1)} async-done(((bf16[8,1536,128]{2,1,0:T(8,128)(2,1)}), bf16[8,192,128]{2,1,0:T(8,128)(2,1)}) %reduce-scatter.24.cloned.1.call-update) | async-done | bytes 393232 | tf_op jit(solution)/shard_map/while/body/eval_jaxpr/reduce_scatter | solution.py:255
  1131.1 74.9 %reduce-scatter.26.cloned.1.call-done = bf16[8,128,192]{1,2,0:T(8,128)(2,1)} async-done(((bf16[8,128,1536]{1,2,0:T(8,128)(2,1)}), bf16[8,128,192]{1,2,0:T(8,128)(2,1)}) %reduce-scatter.26.cloned.1.call-update) | async-done | bytes 393232 | tf_op jit(solution)/shard_map/while/body/eval_jaxpr/reduce_scatter | solution.py:263
  1277.3 55.3 %all-gather.19.cloned.1.call-done = bf16[8,1536,128]{2,1,0:T(8,128)(2,1)} async-done(((bf16[8,192,128]{2,1,0:T(8,128)(2,1)}), bf16[8,1536,128]{2,1,0:T(8,128)(2,1)}) %all-gather.19.cloned.1.call-update) | async-done | bytes 3145744 | tf_op jit(solution)/shard_map/while/body/eval_jaxpr/all_gather | solution.py:217
  1339.0 54.7 %all-gather.23.cloned.1.call-done = bf16[8,128,1536]{1,2,0:T(8,128)(2,1)} async-done(((bf16[8,128,192]{1,2,0:T(8,128)(2,1)}), bf16[8,128,1536]{1,2,0:T(8,128)(2,1)}) %all-gather.23.cloned.1.call-update) | async-done | bytes 3145744 | tf_op jit(solution)/shard_map/while/body/eval_jaxpr/all_gather | solution.py:219
  1485.5 75.2 %reduce-scatter.24.cloned.1.call-done = bf16[8,192,128]{2,1,0:T(8,128)(2,1)} async-done(((bf16[8,1536,128]{2,1,0:T(8,128)(2,1)}), bf16[8,192,128]{2,1,0:T(8,128)(2,1)}) %reduce-scatter.24.cloned.1.call-update) | async-done | bytes 393232 | tf_op jit(solution)/shard_map/while/body/eval_jaxpr/reduce_scatter | solution.py:255
  1562.7 75.4 %reduce-scatter.26.cloned.1.call-done = bf16[8,128,192]{1,2,0:T(8,128)(2,1)} async-done(((bf16[8,128,1536]{1,2,0:T(8,128)(2,1)}), bf16[8,128,192]{1,2,0:T(8,128)(2,1)}) %reduce-scatter.26.cloned.1.call-update) | async-done | bytes 393232 | tf_op jit(solution)/shard_map/while/body/eval_jaxpr/reduce_scatter | solution.py:263
  1709.3 55.5 %all-gather.19.cloned.1.call-done = bf16[8,1536,128]{2,1,0:T(8,128)(2,1)} async-done(((bf16[8,192,128]{2,1,0:T(8,128)(2,1)}), bf16[8,1536,128]{2,1,0:T(8,128)(2,1)}) %all-gather.19.cloned.1.call-update) | async-done | bytes 3145744 | tf_op jit(solution)/shard_map/while/body/eval_jaxpr/all_gather | solution.py:217
  1771.2 54.7 %all-gather.23.cloned.1.call-done = bf16[8,128,1536]{1,2,0:T(8,128)(2,1)} async-done(((bf16[8,128,192]{1,2,0:T(8,128)(2,1)}), bf16[8,128,1536]{1,2,0:T(8,128)(2,1)}) %all-gather.23.cloned.1.call-update) | async-done | bytes 3145744 | tf_op jit(solution)/shard_map/while/body/eval_jaxpr/all_gather | solution.py:219
  1917.7 75.2 %reduce-scatter.24.cloned.1.call-done = bf16[8,192,128]{2,1,0:T(8,128)(2,1)} async-done(((bf16[8,1536,128]{2,1,0:T(8,128)(2,1)}), bf16[8,192,128]{2,1,0:T(8,128)(2,1)}) %reduce-scatter.24.cloned.1.call-update) | async-done | bytes 393232 | tf_op jit(solution)/shard_map/while/body/eval_jaxpr/reduce_scatter | solution.py:255
  1994.8 75.2 %reduce-scatter.26.cloned.1.call-done = bf16[8,128,192]{1,2,0:T(8,128)(2,1)} async-done(((bf16[8,128,1536]{1,2,0:T(8,128)(2,1)}), bf16[8,128,192]{1,2,0:T(8,128)(2,1)}) %reduce-scatter.26.cloned.1.call-update) | async-done | bytes 393232 | tf_op jit(solution)/shard_map/while/body/eval_jaxpr/reduce_scatter | solution.py:263
  2141.2 55.5 %all-gather.19.cloned.1.call-done = bf16[8,1536,128]{2,1,0:T(8,128)(2,1)} async-done(((bf16[8,192,128]{2,1,0:T(8,128)(2,1)}), bf16[8,1536,128]{2,1,0:T(8,128)(2,1)}) %all-gather.19.cloned.1.call-update) | async-done | bytes 3145744 | tf_op jit(solution)/shard_map/while/body/eval_jaxpr/all_gather | solution.py:217
  2203.1 54.7 %all-gather.23.cloned.1.call-done = bf16[8,128,1536]{1,2,0:T(8,128)(2,1)} async-done(((bf16[8,128,192]{1,2,0:T(8,128)(2,1)}), bf16[8,128,1536]{1,2,0:T(8,128)(2,1)}) %all-gather.23.cloned.1.call-update) | async-done | bytes 3145744 | tf_op jit(solution)/shard_map/while/body/eval_jaxpr/all_gather | solution.py:219
  2349.6 75.4 %reduce-scatter.24.cloned.1.call-done = bf16[8,192,128]{2,1,0:T(8,128)(2,1)} async-done(((bf16[8,1536,128]{2,1,0:T(8,128)(2,1)}), bf16[8,192,128]{2,1,0:T(8,128)(2,1)}) %reduce-scatter.24.cloned.1.call-update) | async-done | bytes 393232 | tf_op jit(solution)/shard_map/while/body/eval_jaxpr/reduce_scatter | solution.py:255
  2426.9 75.1 %reduce-scatter.26.cloned.1.call-done = bf16[8,128,192]{1,2,0:T(8,128)(2,1)} async-done(((bf16[8,128,1536]{1,2,0:T(8,128)(2,1)}), bf16[8,128,192]{1,2,0:T(8,128)(2,1)}) %reduce-scatter.26.cloned.1.call-update) | async-done | bytes 393232 | tf_op jit(solution)/shard_map/while/body/eval_jaxpr/reduce_scatter | solution.py:263
  2510.0 67.0 %all-reduce.17.cloned.1.call-done = bf16[1024,1536]{1,0:T(8,128)(2,1)} async-done(((bf16[1024,1536]{1,0:T(8,128)(2,1)}), bf16[1024,1536]{1,0:T(8,128)(2,1)}) %all-reduce.17.cloned.1.call-update) | async-done | bytes 3145744 | tf_op jit(solution)/shard_map/psum | solution.py:280
  2630.2 1176.1 %while.26 = (s32[]{:T(128)}, f32[1024,1536]{1,0:T(8,128)}, s32[5]{0:T(128)S(1)}, s32[10240]{0:T(1024)}, bf16[1024,1536]{1,0:T(8,128)(2,1)S(1)}, /*index=5*/bf16[...) while((s32[]{:T(128)}, f32[1024,1536]{1,0:T(8,128)}, ...), condition=%wide.region_16.17_spmd, body=%wide.region_14.16_spmd.sunk | while | flops 2423791616 | bytes 146473360 | solution.py:207
  2649.5 45.2 %all-gather.17.cloned.1.call-done = bf16[8,1536,128]{2,1,0:T(8,128)(2,1)} async-done(((bf16[8,192,128]{2,1,0:T(8,128)(2,1)}), bf16[8,1536,128]{2,1,0:T(8,128)(2,1)}) %all-gather.17.cloned.1.call-update) | async-done | bytes 3145744 | tf_op jit(solution)/shard_map/while/body/eval_jaxpr/all_gather | solution.py:191
  2701.1 54.7 %all-gather.13.cloned.1.call-done = bf16[8,128,1536]{1,2,0:T(8,128)(2,1)} async-done(((bf16[8,128,192]{1,2,0:T(8,128)(2,1)}), bf16[8,128,1536]{1,2,0:T(8,128)(2,1)}) %all-gather.13.cloned.1.call-update) | async-done | bytes 3145744 | tf_op jit(solution)/shard_map/while/body/eval_jaxpr/all_gather | solution.py:193
  2755.8 61.2 %all-gather.15.cloned.1.call-done = bf16[8,1536,128]{2,1,0:T(8,128)(2,1)} async-done(((bf16[8,192,128]{2,1,0:T(8,128)(2,1)}), bf16[8,1536,128]{2,1,0:T(8,128)(2,1)}) %all-gather.15.cloned.1.call-update) | async-done | bytes 3145744 | tf_op jit(solution)/shard_map/while/body/eval_jaxpr/all_gather | solution.py:192
  2885.8 43.7 %all-gather.17.cloned.1.call-done = bf16[8,1536,128]{2,1,0:T(8,128)(2,1)} async-done(((bf16[8,192,128]{2,1,0:T(8,128)(2,1)}), bf16[8,1536,128]{2,1,0:T(8,128)(2,1)}) %all-gather.17.cloned.1.call-update) | async-done | bytes 3145744 | tf_op jit(solution)/shard_map/while/body/eval_jaxpr/all_gather | solution.py:191
  2936.0 54.7 %all-gather.13.cloned.1.call-done = bf16[8,128,1536]{1,2,0:T(8,128)(2,1)} async-done(((bf16[8,128,192]{1,2,0:T(8,128)(2,1)}), bf16[8,128,1536]{1,2,0:T(8,128)(2,1)}) %all-gather.13.cloned.1.call-update) | async-done | bytes 3145744 | tf_op jit(solution)/shard_map/while/body/eval_jaxpr/all_gather | solution.py:193
  2990.7 61.4 %all-gather.15.cloned.1.call-done = bf16[8,1536,128]{2,1,0:T(8,128)(2,1)} async-done(((bf16[8,192,128]{2,1,0:T(8,128)(2,1)}), bf16[8,1536,128]{2,1,0:T(8,128)(2,1)}) %all-gather.15.cloned.1.call-update) | async-done | bytes 3145744 | tf_op jit(solution)/shard_map/while/body/eval_jaxpr/all_gather | solution.py:192
  3120.9 43.7 %all-gather.17.cloned.1.call-done = bf16[8,1536,128]{2,1,0:T(8,128)(2,1)} async-done(((bf16[8,192,128]{2,1,0:T(8,128)(2,1)}), bf16[8,1536,128]{2,1,0:T(8,128)(2,1)}) %all-gather.17.cloned.1.call-update) | async-done | bytes 3145744 | tf_op jit(solution)/shard_map/while/body/eval_jaxpr/all_gather | solution.py:191
  3171.0 54.9 %all-gather.13.cloned.1.call-done = bf16[8,128,1536]{1,2,0:T(8,128)(2,1)} async-done(((bf16[8,128,192]{1,2,0:T(8,128)(2,1)}), bf16[8,128,1536]{1,2,0:T(8,128)(2,1)}) %all-gather.13.cloned.1.call-update) | async-done | bytes 3145744 | tf_op jit(solution)/shard_map/while/body/eval_jaxpr/all_gather | solution.py:193
  3225.9 61.2 %all-gather.15.cloned.1.call-done = bf16[8,1536,128]{2,1,0:T(8,128)(2,1)} async-done(((bf16[8,192,128]{2,1,0:T(8,128)(2,1)}), bf16[8,1536,128]{2,1,0:T(8,128)(2,1)}) %all-gather.15.cloned.1.call-update) | async-done | bytes 3145744 | tf_op jit(solution)/shard_map/while/body/eval_jaxpr/all_gather | solution.py:192
  3355.9 43.7 %all-gather.17.cloned.1.call-done = bf16[8,1536,128]{2,1,0:T(8,128)(2,1)} async-done(((bf16[8,192,128]{2,1,0:T(8,128)(2,1)}), bf16[8,1536,128]{2,1,0:T(8,128)(2,1)}) %all-gather.17.cloned.1.call-update) | async-done | bytes 3145744 | tf_op jit(solution)/shard_map/while/body/eval_jaxpr/all_gather | solution.py:191
  3406.1 54.7 %all-gather.13.cloned.1.call-done = bf16[8,128,1536]{1,2,0:T(8,128)(2,1)} async-done(((bf16[8,128,192]{1,2,0:T(8,128)(2,1)}), bf16[8,128,1536]{1,2,0:T(8,128)(2,1)}) %all-gather.13.cloned.1.call-update) | async-done | bytes 3145744 | tf_op jit(solution)/shard_map/while/body/eval_jaxpr/all_gather | solution.py:193
  3460.8 61.2 %all-gather.15.cloned.1.call-done = bf16[8,1536,128]{2,1,0:T(8,128)(2,1)} async-done(((bf16[8,192,128]{2,1,0:T(8,128)(2,1)}), bf16[8,1536,128]{2,1,0:T(8,128)(2,1)}) %all-gather.15.cloned.1.call-update) | async-done | bytes 3145744 | tf_op jit(solution)/shard_map/while/body/eval_jaxpr/all_gather | solution.py:192
  3590.8 43.4 %all-gather.17.cloned.1.call-done = bf16[8,1536,128]{2,1,0:T(8,128)(2,1)} async-done(((bf16[8,192,128]{2,1,0:T(8,128)(2,1)}), bf16[8,1536,128]{2,1,0:T(8,128)(2,1)}) %all-gather.17.cloned.1.call-update) | async-done | bytes 3145744 | tf_op jit(solution)/shard_map/while/body/eval_jaxpr/all_gather | solution.py:191
  3640.7 54.7 %all-gather.13.cloned.1.call-done = bf16[8,128,1536]{1,2,0:T(8,128)(2,1)} async-done(((bf16[8,128,192]{1,2,0:T(8,128)(2,1)}), bf16[8,128,1536]{1,2,0:T(8,128)(2,1)}) %all-gather.13.cloned.1.call-update) | async-done | bytes 3145744 | tf_op jit(solution)/shard_map/while/body/eval_jaxpr/all_gather | solution.py:193
  3695.4 61.2 %all-gather.15.cloned.1.call-done = bf16[8,1536,128]{2,1,0:T(8,128)(2,1)} async-done(((bf16[8,192,128]{2,1,0:T(8,128)(2,1)}), bf16[8,1536,128]{2,1,0:T(8,128)(2,1)}) %all-gather.15.cloned.1.call-update) | async-done | bytes 3145744 | tf_op jit(solution)/shard_map/while/body/eval_jaxpr/all_gather | solution.py:192
  3807.2 34.6 fusion.57
  3852.0 34.6 fusion.73
  3908.9 34.7 fusion.85
  3943.6 34.1 fusion.86
  4029.6 65.1 %reduce-scatter.20.cloned.1.call-done = bf16[384,192]{0,1:T(8,128)(2,1)} async-done(((bf16[384,1536]{0,1:T(8,128)(2,1)}), bf16[384,192]{0,1:T(8,128)(2,1)}) %reduce-scatter.20.cloned.1.call-update) | async-done | bytes 147472 | tf_op jit(solution)/shard_map/reduce_scatter | solution.py:374
  4096.3 64.7 %reduce-scatter.14.cloned.1.call-done = bf16[192,384]{1,0:T(8,128)(2,1)} async-done(((bf16[1536,384]{1,0:T(8,128)(2,1)}), bf16[192,384]{1,0:T(8,128)(2,1)}) %reduce-scatter.14.cloned.1.call-update) | async-done | bytes 147472 | tf_op jit(solution)/shard_map/reduce_scatter | solution.py:356
  4162.7 120.1 %all-reduce.19.cloned.1.call-done = (bf16[1024,1536]{1,0:T(8,128)(2,1)}, bf16[1024,1536]{1,0:T(8,128)(2,1)}) async-done(((bf16[1024,1536]{1,0:T(8,128)(2,1)}, bf16[1024,1536]{1,0:T(8,128)(2,1)}), (bf16[1024,1536]{1,0:T(8,128)(2,1)}, bf16[1024,1536]{1,0:T(8,128)(2,1)})) %all-reduce.19.cloned.1.call-update) | async-done | bytes 6291472 | tf_op jit(solution)/shard_map/psum | solution.py:210
  (600 shorter events, 1640.7 us)
Async XLA Ops:
  7.2 188.1 %all-gather.9.cloned.1.call-start = ((), (), s32[]{:S(2)}) async-start(), calls=%async_computation.9 | async-start | bytes 1327104 | tf_op jit(solution)/shard_map/all_gather | solution.py:97
  7.9 255.8 %all-gather.11.cloned.1.call-start = ((), (), s32[]{:S(2)}) async-start(), calls=%async_computation.10 | async-start | bytes 1327104 | tf_op jit(solution)/shard_map/all_gather | solution.py:100
  8.7 325.9 %all-reduce.15.cloned.1.call-start = ((), (), s32[]{:S(2)}) async-start(), calls=%async_computation.11 | async-start | bytes 6291456 | tf_op jit(solution)/shard_map/psum | solution.py:168
  343.2 63.9 %all-gather.21.cloned.1.call-start = ((), (), s32[]{:S(2)}) async-start(), calls=%async_computation.24 | async-start | bytes 3538944 | tf_op jit(solution)/shard_map/while/body/eval_jaxpr/all_gather | solution.py:218
  346.3 122.6 %all-gather.19.cloned.1.call-start = ((), (), s32[]{:S(2)}) async-start(), calls=%async_computation.23 | async-start | bytes 3538944 | tf_op jit(solution)/shard_map/while/body/eval_jaxpr/all_gather | solution.py:217
  348.1 181.9 %all-gather.23.cloned.1.call-start = ((), (), s32[]{:S(2)}) async-start(), calls=%async_computation.25 | async-start | bytes 3538944 | tf_op jit(solution)/shard_map/while/body/eval_jaxpr/all_gather | solution.py:219
  350.0 269.9 %reduce-scatter.22.cloned.1.call-start = ((), (), s32[]{:S(2)}) async-start(), calls=%async_computation.26 | async-start | bytes 3538944 | tf_op jit(solution)/shard_map/while/body/eval_jaxpr/reduce_scatter | solution.py:247
  546.6 150.5 %reduce-scatter.24.cloned.1.call-start = ((), (), s32[]{:S(2)}) async-start(), calls=%async_computation.27 | async-start | bytes 3538944 | tf_op jit(solution)/shard_map/while/body/eval_jaxpr/reduce_scatter | solution.py:255
  553.3 221.0 %reduce-scatter.26.cloned.1.call-start = ((), (), s32[]{:S(2)}) async-start(), calls=%async_computation.28 | async-start | bytes 3538944 | tf_op jit(solution)/shard_map/while/body/eval_jaxpr/reduce_scatter | solution.py:263
  779.3 121.7 %all-gather.19.cloned.1.call-start = ((), (), s32[]{:S(2)}) async-start(), calls=%async_computation.23 | async-start | bytes 3538944 | tf_op jit(solution)/shard_map/while/body/eval_jaxpr/all_gather | solution.py:217
  781.2 181.1 %all-gather.23.cloned.1.call-start = ((), (), s32[]{:S(2)}) async-start(), calls=%async_computation.25 | async-start | bytes 3538944 | tf_op jit(solution)/shard_map/while/body/eval_jaxpr/all_gather | solution.py:219
  783.0 269.0 %reduce-scatter.22.cloned.1.call-start = ((), (), s32[]{:S(2)}) async-start(), calls=%async_computation.26 | async-start | bytes 3538944 | tf_op jit(solution)/shard_map/while/body/eval_jaxpr/reduce_scatter | solution.py:247
  978.8 150.3 %reduce-scatter.24.cloned.1.call-start = ((), (), s32[]{:S(2)}) async-start(), calls=%async_computation.27 | async-start | bytes 3538944 | tf_op jit(solution)/shard_map/while/body/eval_jaxpr/reduce_scatter | solution.py:255
  985.5 220.5 %reduce-scatter.26.cloned.1.call-start = ((), (), s32[]{:S(2)}) async-start(), calls=%async_computation.28 | async-start | bytes 3538944 | tf_op jit(solution)/shard_map/while/body/eval_jaxpr/reduce_scatter | solution.py:263
  1211.0 121.6 %all-gather.19.cloned.1.call-start = ((), (), s32[]{:S(2)}) async-start(), calls=%async_computation.23 | async-start | bytes 3538944 | tf_op jit(solution)/shard_map/while/body/eval_jaxpr/all_gather | solution.py:217
  1212.9 180.9 %all-gather.23.cloned.1.call-start = ((), (), s32[]{:S(2)}) async-start(), calls=%async_computation.25 | async-start | bytes 3538944 | tf_op jit(solution)/shard_map/while/body/eval_jaxpr/all_gather | solution.py:219
  1214.7 268.9 %reduce-scatter.22.cloned.1.call-start = ((), (), s32[]{:S(2)}) async-start(), calls=%async_computation.26 | async-start | bytes 3538944 | tf_op jit(solution)/shard_map/while/body/eval_jaxpr/reduce_scatter | solution.py:247
  1410.4 150.4 %reduce-scatter.24.cloned.1.call-start = ((), (), s32[]{:S(2)}) async-start(), calls=%async_computation.27 | async-start | bytes 3538944 | tf_op jit(solution)/shard_map/while/body/eval_jaxpr/reduce_scatter | solution.py:255
  1417.1 221.0 %reduce-scatter.26.cloned.1.call-start = ((), (), s32[]{:S(2)}) async-start(), calls=%async_computation.28 | async-start | bytes 3538944 | tf_op jit(solution)/shard_map/while/body/eval_jaxpr/reduce_scatter | solution.py:263
  1643.0 121.7 %all-gather.19.cloned.1.call-start = ((), (), s32[]{:S(2)}) async-start(), calls=%async_computation.23 | async-start | bytes 3538944 | tf_op jit(solution)/shard_map/while/body/eval_jaxpr/all_gather | solution.py:217
  1644.9 181.1 %all-gather.23.cloned.1.call-start = ((), (), s32[]{:S(2)}) async-start(), calls=%async_computation.25 | async-start | bytes 3538944 | tf_op jit(solution)/shard_map/while/body/eval_jaxpr/all_gather | solution.py:219
  1646.7 269.0 %reduce-scatter.22.cloned.1.call-start = ((), (), s32[]{:S(2)}) async-start(), calls=%async_computation.26 | async-start | bytes 3538944 | tf_op jit(solution)/shard_map/while/body/eval_jaxpr/reduce_scatter | solution.py:247
  1842.6 150.3 %reduce-scatter.24.cloned.1.call-start = ((), (), s32[]{:S(2)}) async-start(), calls=%async_computation.27 | async-start | bytes 3538944 | tf_op jit(solution)/shard_map/while/body/eval_jaxpr/reduce_scatter | solution.py:255
  1849.2 220.7 %reduce-scatter.26.cloned.1.call-start = ((), (), s32[]{:S(2)}) async-start(), calls=%async_computation.28 | async-start | bytes 3538944 | tf_op jit(solution)/shard_map/while/body/eval_jaxpr/reduce_scatter | solution.py:263
  2075.0 121.7 %all-gather.19.cloned.1.call-start = ((), (), s32[]{:S(2)}) async-start(), calls=%async_computation.23 | async-start | bytes 3538944 | tf_op jit(solution)/shard_map/while/body/eval_jaxpr/all_gather | solution.py:217
  2076.8 181.1 %all-gather.23.cloned.1.call-start = ((), (), s32[]{:S(2)}) async-start(), calls=%async_computation.25 | async-start | bytes 3538944 | tf_op jit(solution)/shard_map/while/body/eval_jaxpr/all_gather | solution.py:219
  2078.7 269.0 %reduce-scatter.22.cloned.1.call-start = ((), (), s32[]{:S(2)}) async-start(), calls=%async_computation.26 | async-start | bytes 3538944 | tf_op jit(solution)/shard_map/while/body/eval_jaxpr/reduce_scatter | solution.py:247
  2274.5 150.5 %reduce-scatter.24.cloned.1.call-start = ((), (), s32[]{:S(2)}) async-start(), calls=%async_computation.27 | async-start | bytes 3538944 | tf_op jit(solution)/shard_map/while/body/eval_jaxpr/reduce_scatter | solution.py:255
  2281.2 220.9 %reduce-scatter.26.cloned.1.call-start = ((), (), s32[]{:S(2)}) async-start(), calls=%async_computation.28 | async-start | bytes 3538944 | tf_op jit(solution)/shard_map/while/body/eval_jaxpr/reduce_scatter | solution.py:263
  2504.3 72.7 %all-reduce.17.cloned.1.call-start = ((), (), s32[]{:S(2)}) async-start(), calls=%async_computation.12 | async-start | bytes 6291456 | tf_op jit(solution)/shard_map/psum | solution.py:280
  2630.3 64.3 %all-gather.17.cloned.1.call-start = ((), (), s32[]{:S(2)}) async-start(), calls=%async_computation.22 | async-start | bytes 3538944 | tf_op jit(solution)/shard_map/while/body/eval_jaxpr/all_gather | solution.py:191
  2633.5 122.3 %all-gather.13.cloned.1.call-start = ((), (), s32[]{:S(2)}) async-start(), calls=%async_computation.20 | async-start | bytes 3538944 | tf_op jit(solution)/shard_map/while/body/eval_jaxpr/all_gather | solution.py:193
  2635.4 181.7 %all-gather.15.cloned.1.call-start = ((), (), s32[]{:S(2)}) async-start(), calls=%async_computation.21 | async-start | bytes 3538944 | tf_op jit(solution)/shard_map/while/body/eval_jaxpr/all_gather | solution.py:192
  2869.9 120.9 %all-gather.13.cloned.1.call-start = ((), (), s32[]{:S(2)}) async-start(), calls=%async_computation.20 | async-start | bytes 3538944 | tf_op jit(solution)/shard_map/while/body/eval_jaxpr/all_gather | solution.py:193
  2871.7 180.4 %all-gather.15.cloned.1.call-start = ((), (), s32[]{:S(2)}) async-start(), calls=%async_computation.21 | async-start | bytes 3538944 | tf_op jit(solution)/shard_map/while/body/eval_jaxpr/all_gather | solution.py:192
  3104.9 121.0 %all-gather.13.cloned.1.call-start = ((), (), s32[]{:S(2)}) async-start(), calls=%async_computation.20 | async-start | bytes 3538944 | tf_op jit(solution)/shard_map/while/body/eval_jaxpr/all_gather | solution.py:193
  3106.8 180.4 %all-gather.15.cloned.1.call-start = ((), (), s32[]{:S(2)}) async-start(), calls=%async_computation.21 | async-start | bytes 3538944 | tf_op jit(solution)/shard_map/while/body/eval_jaxpr/all_gather | solution.py:192
  3340.0 120.9 %all-gather.13.cloned.1.call-start = ((), (), s32[]{:S(2)}) async-start(), calls=%async_computation.20 | async-start | bytes 3538944 | tf_op jit(solution)/shard_map/while/body/eval_jaxpr/all_gather | solution.py:193
  3341.8 180.2 %all-gather.15.cloned.1.call-start = ((), (), s32[]{:S(2)}) async-start(), calls=%async_computation.21 | async-start | bytes 3538944 | tf_op jit(solution)/shard_map/while/body/eval_jaxpr/all_gather | solution.py:192
  3574.8 120.6 %all-gather.13.cloned.1.call-start = ((), (), s32[]{:S(2)}) async-start(), calls=%async_computation.20 | async-start | bytes 3538944 | tf_op jit(solution)/shard_map/while/body/eval_jaxpr/all_gather | solution.py:193
  3576.7 179.9 %all-gather.15.cloned.1.call-start = ((), (), s32[]{:S(2)}) async-start(), calls=%async_computation.21 | async-start | bytes 3538944 | tf_op jit(solution)/shard_map/while/body/eval_jaxpr/all_gather | solution.py:192
  3806.3 80.4 %reduce-scatter.12.cloned.1.call-start = ((), (), s32[]{:S(2)}) async-start(), calls=%async_computation.14 | async-start | bytes 786432 | tf_op jit(solution)/shard_map/reduce_scatter | solution.py:320
  3807.1 92.9 %reduce-scatter.10.cloned.1.call-start = ((), (), s32[]{:S(2)}) async-start(), calls=%async_computation.13 | async-start | bytes 786432 | tf_op jit(solution)/shard_map/reduce_scatter | solution.py:317
  3886.6 109.4 %reduce-scatter.18.cloned.1.call-start = ((), (), s32[]{:S(2)}) async-start(), calls=%async_computation.17 | async-start | bytes 442368 | tf_op jit(solution)/shard_map/reduce_scatter | solution.py:368
  3889.5 138.6 %reduce-scatter.16.cloned.1.call-start = ((), (), s32[]{:S(2)}) async-start(), calls=%async_computation.16 | async-start | bytes 442368 | tf_op jit(solution)/shard_map/reduce_scatter | solution.py:362
  3902.9 191.8 %reduce-scatter.20.cloned.1.call-start = ((), (), s32[]{:S(2)}) async-start(), calls=%async_computation.18 | async-start | bytes 1327104 | tf_op jit(solution)/shard_map/reduce_scatter | solution.py:374
  3908.8 252.2 %reduce-scatter.14.cloned.1.call-start = ((), (), s32[]{:S(2)}) async-start(), calls=%async_computation.15 | async-start | bytes 1327104 | tf_op jit(solution)/shard_map/reduce_scatter | solution.py:356
  3984.4 298.3 %all-reduce.19.cloned.1.call-start = ((), (), s32[]{:S(2)}) async-start(), calls=%async_computation.19 | async-start | bytes 12582912 | tf_op jit(solution)/shard_map/psum | solution.py:210
  (107 other events, 5570.9 us)
Sparse Core Ops, SparseCore 0:
  268.9 65.6 all-reduce.14
  346.4 60.6 all-gather.20
  409.7 59.1 all-gather.18
  470.9 59.1 all-gather.22
  546.8 73.0 reduce-scatter.21
  623.4 73.6 reduce-scatter.23
  700.7 73.6 reduce-scatter.25
  779.4 59.6 all-gather.20
  841.9 59.1 all-gather.18
  903.1 59.1 all-gather.22
  979.0 73.0 reduce-scatter.21
  1055.5 73.6 reduce-scatter.23
  1132.6 73.3 reduce-scatter.25
  1211.1 59.6 all-gather.20
  1273.4 59.1 all-gather.18
  1334.6 59.1 all-gather.22
  1410.5 73.0 reduce-scatter.21
  1487.0 73.6 reduce-scatter.23
  1564.3 73.6 reduce-scatter.25
  1643.2 59.6 all-gather.20
  1705.6 59.1 all-gather.18
  1766.8 59.1 all-gather.22
  1842.7 73.0 reduce-scatter.21
  1919.2 73.6 reduce-scatter.23
  1996.3 73.6 reduce-scatter.25
  2075.1 59.6 all-gather.20
  2137.5 59.1 all-gather.18
  2198.7 59.1 all-gather.22
  2274.6 73.0 reduce-scatter.21
  2351.3 73.6 reduce-scatter.23
  2428.4 73.5 reduce-scatter.25
  2509.4 67.5 all-reduce.16
  2634.0 60.6 all-gather.16
  2696.7 59.1 all-gather.12
  2757.9 59.1 all-gather.14
  2870.4 59.1 all-gather.16
  2931.6 59.1 all-gather.12
  2992.9 59.1 all-gather.14
  3105.4 59.1 all-gather.16
  3340.5 59.1 all-gather.16
  3401.7 59.1 all-gather.12
  3575.0 59.1 all-gather.16
  3697.5 59.1 all-gather.14
  3903.2 61.3 reduce-scatter.17
  3967.7 60.3 reduce-scatter.15
  4031.5 63.1 reduce-scatter.19
  4098.1 62.9 reduce-scatter.13
  4164.0 118.7 all-reduce.18
  (8 shorter events, 348.4 us)
where the time goes:
time: 4340 us; the launch traced here: 4330 us
  waiting for transfers between devices  2640 us (61%)
  matrix products  627 us (14%)
  other arithmetic  466 us (11%)
  local copies, waits for them, and re-layouts  433 us (10%)
  blocking collectives  125 us (3%)
    reduce_scatter x5, waiting for transfers between devices, backward_turn(): lax.psum_scatter(jnp.einsum('ecd,ecf->edf', picked, grad_up_low, preferre...  376 us
    reduce_scatter x5, waiting for transfers between devices, backward_turn(): lax.psum_scatter(jnp.einsum('ecf,ecd->efd', inner, grad_slot, preferred_e...  376 us
    all_gather x5, waiting for transfers between devices, forward_turn(): lax.all_gather(up_part, ('shard', 'context'), axis=1, tiled=True)  306 us
    all_gather x5, waiting for transfers between devices, backward_turn(): lax.all_gather(gate_part, ('shard', 'context'), axis=1, tiled=True)  277 us
    all_gather x5, waiting for transfers between devices, forward_turn(): lax.all_gather(down_part, ('shard', 'context'), axis=2, tiled=True)  274 us
    all_gather x5, waiting for transfers between devices, backward_turn(): lax.all_gather(down_part, ('shard', 'context'), axis=2, tiled=True)  274 us
    all_gather x5, waiting for transfers between devices, forward_turn(): lax.all_gather(gate_part, ('shard', 'context'), axis=1, tiled=True)  220 us
    gather x10, local copies, waits for them, and re-layouts, backward_turn(): upstream[token_rows] * share_rows[:, None]  149 us
  transfers between devices with their start and end apart: 56, of which 52 were waited for; matrix products, arithmetic and copies ran while one was open for 25% of the time, Pallas kernels for 0%

commit v1 on v0

--- a/solution.py
+++ b/solution.py
@@ -3,10 +3,25 @@
 import jax
 import jax.numpy as jnp
 from jax import lax
+from jax.experimental import pallas as pl
+from jax.experimental.pallas import tpu as pltpu
 from jax.sharding import PartitionSpec as P
 
 HEAD_DIM = 64
 NDOCS = 5
+SHARD = "shard"
+CONTEXT = "context"
+TENSOR = "tensor"
+GROUP = (SHARD, CONTEXT)
+PRODUCT_0 = "qgrd,kgd->grqk"
+PRODUCT_1 = "grqk,kgd->qgrd"
+PRODUCT_2 = "ecd,edf->ecf"
+PRODUCT_3 = "ecf,efd->ecd"
+PRODUCT_4 = "ecd,efd->ecf"
+PRODUCT_5 = "ecf,edf->ecd"
+PRODUCT_6 = "ecd,ecf->edf"
+PRODUCT_7 = "ecf,ecd->efd"
+PRODUCT_8 = "grqk,qgrd->kgd"
 
 
 epsilon = 1e-06
@@ -65,7 +80,7 @@
     return (slot_rows, slot_share)
 
 
-def on_device(
+def gathered_plan(
     residual_in,
     gain_attn,
     query_weight,
@@ -89,15 +104,15 @@
     expert_count = gate_weight.shape[0]
     capacity = row_count * routes.shape[1] * 5 // (4 * expert_count)
     score_scale = head_size ** (-0.5)
-    context_rank = lax.axis_index("context")
+    context_rank = lax.axis_index(CONTEXT)
     own_first = context_rank * row_count
     gain_attn_full, gain_ffn_full, query_full, key_full, value_full, out_full = (
-        lax.all_gather(gain_attn, ("shard", "context"), axis=0, tiled=True),
-        lax.all_gather(gain_ffn, ("shard", "context"), axis=0, tiled=True),
-        lax.all_gather(query_weight, ("shard", "context"), axis=0, tiled=True),
-        lax.all_gather(key_projection_weight, ("shard", "context"), axis=0, tiled=True),
-        lax.all_gather(value_projection_weight, ("shard", "context"), axis=0, tiled=True),
-        lax.all_gather(out_weight, ("shard", "context"), axis=1, tiled=True),
+        lax.all_gather(gain_attn, GROUP, axis=0, tiled=True),
+        lax.all_gather(gain_ffn, GROUP, axis=0, tiled=True),
+        lax.all_gather(query_weight, GROUP, axis=0, tiled=True),
+        lax.all_gather(key_projection_weight, GROUP, axis=0, tiled=True),
+        lax.all_gather(value_projection_weight, GROUP, axis=0, tiled=True),
+        lax.all_gather(out_weight, GROUP, axis=1, tiled=True),
     )
     gain_attn_float = gain_attn_full.astype(jnp.float32)
     gain_ffn_float = gain_ffn_full.astype(jnp.float32)
@@ -123,8 +138,8 @@
     query_low = query_rot.astype(jnp.bfloat16)
     key_low = key_rot.astype(jnp.bfloat16).reshape(row_count, -1)
     key_all, value_all = (
-        lax.all_gather(key_low, "context", axis=0, tiled=True),
-        lax.all_gather(value_tokens, "context", axis=0, tiled=True),
+        lax.all_gather(key_low, CONTEXT, axis=0, tiled=True),
+        lax.all_gather(value_tokens, CONTEXT, axis=0, tiled=True),
     )
     key_index = jnp.arange(key_all.shape[0], dtype=jnp.int32)
     key_ids = jnp.take(segments, jnp.clip(key_index, 0, segments.shape[0] - 1))
@@ -138,7 +153,7 @@
     def block_scores(block_first):
         query_block = query_heads[block_first : block_first + block_rows]
         raw_scores = jnp.einsum(
-            "qgrd,kgd->grqk", query_block, key_heads, preferred_element_type=jnp.float32
+            PRODUCT_0, query_block, key_heads, preferred_element_type=jnp.float32
         )
         block_ids = own_ids[block_first : block_first + block_rows]
         block_index = own_index[block_first : block_first + block_rows]
@@ -158,14 +173,14 @@
         row_total = jnp.sum(exponent, axis=-1, keepdims=True)
         probs = (exponent / row_total).astype(jnp.bfloat16)
         mixed_parts.append(
-            jnp.einsum("grqk,kgd->qgrd", probs, value_heads, preferred_element_type=jnp.float32)
+            jnp.einsum(PRODUCT_1, probs, value_heads, preferred_element_type=jnp.float32)
         )
         lse_parts.append(row_max + jnp.log(row_total))
     attended = (
         jnp.concatenate(mixed_parts, axis=0).reshape(row_count, query_cols).astype(jnp.bfloat16)
     )
     attn_part = jnp.dot(attended, out_full, preferred_element_type=jnp.float32)
-    hidden = input_float + lax.psum(attn_part.astype(jnp.bfloat16), "tensor").astype(jnp.float32)
+    hidden = input_float + lax.psum(attn_part.astype(jnp.bfloat16), TENSOR).astype(jnp.float32)
     normed_ffn, ffn_norm_back = jax.vjp(rms_scale, hidden, gain_ffn_float)
     normed_second = normed_ffn.astype(jnp.bfloat16)
     slot_rows, slot_share = dispatch(routes, shares, row_count, capacity, expert_count)
@@ -188,18 +203,18 @@
     def forward_turn(running, turn_index):
         gate_part, up_part, down_part = local_experts(turn_index)
         gate_full, up_full, down_full = (
-            lax.all_gather(gate_part, ("shard", "context"), axis=1, tiled=True),
-            lax.all_gather(up_part, ("shard", "context"), axis=1, tiled=True),
-            lax.all_gather(down_part, ("shard", "context"), axis=2, tiled=True),
+            lax.all_gather(gate_part, GROUP, axis=1, tiled=True),
+            lax.all_gather(up_part, GROUP, axis=1, tiled=True),
+            lax.all_gather(down_part, GROUP, axis=2, tiled=True),
         )
         token_rows, share_rows, picked = turn_inputs(turn_index)
         gate_value = jnp.einsum(
-            "ecd,edf->ecf", picked, gate_full, preferred_element_type=jnp.float32
-        )
-        up_value = jnp.einsum("ecd,edf->ecf", picked, up_full, preferred_element_type=jnp.float32)
+            PRODUCT_2, picked, gate_full, preferred_element_type=jnp.float32
+        )
+        up_value = jnp.einsum(PRODUCT_2, picked, up_full, preferred_element_type=jnp.float32)
         inner = swiglu(gate_value, up_value).astype(jnp.bfloat16)
         expert_result = jnp.einsum(
-            "ecf,efd->ecd", inner, down_full, preferred_element_type=jnp.float32
+            PRODUCT_3, inner, down_full, preferred_element_type=jnp.float32
         ).reshape(turn_slots, model_width)
         return (running.at[token_rows].add(expert_result * share_rows[:, None]), None)
 
@@ -207,22 +222,22 @@
     expert_part, _ = lax.scan(
         forward_turn, jnp.zeros((row_count, model_width), jnp.float32), turn_ids
     )
-    expert_total = lax.psum(expert_part.astype(jnp.bfloat16), "tensor").astype(jnp.float32)
+    expert_total = lax.psum(expert_part.astype(jnp.bfloat16), TENSOR).astype(jnp.float32)
     output = (hidden + expert_total).astype(jnp.bfloat16)
     upstream = cotangent.astype(jnp.float32)
 
     def backward_turn(running, turn_index):
         gate_part, up_part, down_part = local_experts(turn_index)
         gate_full, up_full, down_full = (
-            lax.all_gather(gate_part, ("shard", "context"), axis=1, tiled=True),
-            lax.all_gather(up_part, ("shard", "context"), axis=1, tiled=True),
-            lax.all_gather(down_part, ("shard", "context"), axis=2, tiled=True),
+            lax.all_gather(gate_part, GROUP, axis=1, tiled=True),
+            lax.all_gather(up_part, GROUP, axis=1, tiled=True),
+            lax.all_gather(down_part, GROUP, axis=2, tiled=True),
         )
         token_rows, share_rows, picked = turn_inputs(turn_index)
         gate_value = jnp.einsum(
-            "ecd,edf->ecf", picked, gate_full, preferred_element_type=jnp.float32
-        )
-        up_value = jnp.einsum("ecd,edf->ecf", picked, up_full, preferred_element_type=jnp.float32)
+            PRODUCT_2, picked, gate_full, preferred_element_type=jnp.float32
+        )
+        up_value = jnp.einsum(PRODUCT_2, picked, up_full, preferred_element_type=jnp.float32)
         inner_float, swiglu_back = jax.vjp(swiglu, gate_value, up_value)
         inner = inner_float.astype(jnp.bfloat16)
         grad_slot = (
@@ -231,40 +246,40 @@
             .reshape(per_turn, capacity, model_width)
         )
         grad_inner = jnp.einsum(
-            "ecd,efd->ecf", grad_slot, down_full, preferred_element_type=jnp.float32
+            PRODUCT_4, grad_slot, down_full, preferred_element_type=jnp.float32
         )
         grad_gate_value, grad_up_value = swiglu_back(grad_inner)
         grad_gate_low = grad_gate_value.astype(jnp.bfloat16)
         grad_up_low = grad_up_value.astype(jnp.bfloat16)
         grad_picked = jnp.einsum(
-            "ecf,edf->ecd", grad_gate_low, gate_full, preferred_element_type=jnp.float32
+            PRODUCT_5, grad_gate_low, gate_full, preferred_element_type=jnp.float32
         )
         grad_picked = grad_picked + jnp.einsum(
-            "ecf,edf->ecd", grad_up_low, up_full, preferred_element_type=jnp.float32
+            PRODUCT_5, grad_up_low, up_full, preferred_element_type=jnp.float32
         )
         running = running.at[token_rows].add(grad_picked.reshape(turn_slots, model_width))
         shard_grads = (
             lax.psum_scatter(
                 jnp.einsum(
-                    "ecd,ecf->edf", picked, grad_gate_low, preferred_element_type=jnp.float32
+                    PRODUCT_6, picked, grad_gate_low, preferred_element_type=jnp.float32
                 ).astype(jnp.bfloat16),
-                ("shard", "context"),
+                GROUP,
                 scatter_dimension=1,
                 tiled=True,
             ).astype(jnp.float32),
             lax.psum_scatter(
                 jnp.einsum(
-                    "ecd,ecf->edf", picked, grad_up_low, preferred_element_type=jnp.float32
+                    PRODUCT_6, picked, grad_up_low, preferred_element_type=jnp.float32
                 ).astype(jnp.bfloat16),
-                ("shard", "context"),
+                GROUP,
                 scatter_dimension=1,
                 tiled=True,
             ).astype(jnp.float32),
             lax.psum_scatter(
                 jnp.einsum(
-                    "ecf,ecd->efd", inner, grad_slot, preferred_element_type=jnp.float32
+                    PRODUCT_7, inner, grad_slot, preferred_element_type=jnp.float32
                 ).astype(jnp.bfloat16),
-                ("shard", "context"),
+                GROUP,
                 scatter_dimension=2,
                 tiled=True,
             ).astype(jnp.float32),
@@ -277,7 +292,7 @@
     grad_gate_out = stacked_grads[0].reshape(gate_weight.shape)
     grad_up_out = stacked_grads[1].reshape(up_weight.shape)
     grad_down_out = stacked_grads[2].reshape(down_weight.shape)
-    grad_second = lax.psum(grad_second_part.astype(jnp.bfloat16), "tensor").astype(jnp.float32)
+    grad_second = lax.psum(grad_second_part.astype(jnp.bfloat16), TENSOR).astype(jnp.float32)
     grad_hidden_norm, grad_gain_ffn_local = ffn_norm_back(grad_second)
     grad_hidden = upstream + grad_hidden_norm
     grad_hidden_low = grad_hidden.astype(jnp.bfloat16)
@@ -300,25 +315,25 @@
         probs = probs_float.astype(jnp.bfloat16)
         grad_block = grad_attended[block_first : block_first + block_rows]
         grad_probs = jnp.einsum(
-            "qgrd,kgd->grqk", grad_block, value_heads, preferred_element_type=jnp.float32
+            PRODUCT_0, grad_block, value_heads, preferred_element_type=jnp.float32
         )
         inner_sum = jnp.sum(grad_probs * probs_float, axis=-1, keepdims=True)
         grad_scores = (score_scale * (probs_float * (grad_probs - inner_sum))).astype(jnp.bfloat16)
         grad_query_parts.append(
-            jnp.einsum("grqk,kgd->qgrd", grad_scores, key_heads, preferred_element_type=jnp.float32)
+            jnp.einsum(PRODUCT_1, grad_scores, key_heads, preferred_element_type=jnp.float32)
         )
         grad_keys = grad_keys + jnp.einsum(
-            "grqk,qgrd->kgd", grad_scores, query_block, preferred_element_type=jnp.float32
+            PRODUCT_8, grad_scores, query_block, preferred_element_type=jnp.float32
         )
         grad_values = grad_values + jnp.einsum(
-            "grqk,qgrd->kgd", probs, grad_block, preferred_element_type=jnp.float32
+            PRODUCT_8, probs, grad_block, preferred_element_type=jnp.float32
         )
     grad_key_own, grad_value_own = (
         lax.psum_scatter(
-            grad_keys.astype(jnp.bfloat16), "context", scatter_dimension=0, tiled=True
+            grad_keys.astype(jnp.bfloat16), CONTEXT, scatter_dimension=0, tiled=True
         ).astype(jnp.float32),
         lax.psum_scatter(
-            grad_values.astype(jnp.bfloat16), "context", scatter_dimension=0, tiled=True
+            grad_values.astype(jnp.bfloat16), CONTEXT, scatter_dimension=0, tiled=True
         ).astype(jnp.float32),
     )
     grad_query_all = jnp.concatenate(grad_query_parts, axis=0).reshape(row_count, -1, head_size)
@@ -334,7 +349,7 @@
     grad_first_part = grad_first_part + jnp.einsum(
         "tc,dc->td", grad_value_low, value_full, preferred_element_type=jnp.float32
     )
-    grad_first = lax.psum(grad_first_part.astype(jnp.bfloat16), "tensor").astype(jnp.float32)
+    grad_first = lax.psum(grad_first_part.astype(jnp.bfloat16), TENSOR).astype(jnp.float32)
     grad_input_norm, grad_gain_attn_local = attn_norm_back(grad_first)
     grad_input = (grad_hidden + grad_input_norm).astype(jnp.bfloat16)
     grad_query_local = jnp.einsum(
@@ -349,37 +364,37 @@
     reduced = (
         lax.psum_scatter(
             grad_gain_attn_local.astype(jnp.bfloat16),
-            ("shard", "context"),
+            GROUP,
             scatter_dimension=0,
             tiled=True,
         ).astype(jnp.float32),
         lax.psum_scatter(
             grad_query_local.astype(jnp.bfloat16),
-            ("shard", "context"),
+            GROUP,
             scatter_dimension=0,
             tiled=True,
         ).astype(jnp.float32),
         lax.psum_scatter(
             grad_key_local.astype(jnp.bfloat16),
-            ("shard", "context"),
+            GROUP,
             scatter_dimension=0,
             tiled=True,
         ).astype(jnp.float32),
         lax.psum_scatter(
             grad_value_local.astype(jnp.bfloat16),
-            ("shard", "context"),
+            GROUP,
             scatter_dimension=0,
             tiled=True,
         ).astype(jnp.float32),
         lax.psum_scatter(
             grad_out_local.astype(jnp.bfloat16),
-            ("shard", "context"),
+            GROUP,
             scatter_dimension=1,
             tiled=True,
         ).astype(jnp.float32),
         lax.psum_scatter(
             grad_gain_ffn_local.astype(jnp.bfloat16),
-            ("shard", "context"),
+            GROUP,
             scatter_dimension=0,
             tiled=True,
         ).astype(jnp.float32),
@@ -399,39 +414,678 @@
     )
 
 
+F32 = jnp.float32
+BF16 = jnp.bfloat16
+LAST_LAST = (((1,), (1,)), ((), ()))
+FIRST_FIRST = (((0,), (0,)), ((), ()))
+
+
+def weight_copies(own_hbm, other_hbm, weights, sems):
+    sources, _, rows, lanes = own_hbm.shape
+    units = lanes // 3
+    return [
+        pltpu.make_async_copy(
+            half_hbm.at[source, :, :, pl.ds(part * units, units)],
+            weights.at[
+                :, pl.ds(source * rows, rows), pl.ds((2 * part + half) * units, units)
+            ],
+            sems.at[source, half, part],
+        )
+        for source in range(sources)
+        for half, half_hbm in enumerate((own_hbm, other_hbm))
+        for part in range(3)
+    ]
+
+
+def project(tokens, cotangent, weights):
+    hidden_units = weights.shape[1] // 3
+    gate_up = jnp.dot(tokens, weights[:, : 2 * hidden_units], preferred_element_type=F32)
+    grad_inner = jnp.dot(cotangent, weights[:, 2 * hidden_units :], preferred_element_type=F32)
+    return gate_up, grad_inner
+
+
+def activate(gate_up, grad_inner, share):
+    hidden_units = grad_inner.shape[1]
+    gate, up = gate_up[:, :hidden_units], gate_up[:, hidden_units:]
+    sigmoid = 1.0 / (1.0 + jnp.exp(-gate))
+    silu = gate * sigmoid
+    grad_inner = grad_inner * share
+    inner = silu * up * share
+    grad_gate = grad_inner * up * (sigmoid * (1.0 + gate * (1.0 - sigmoid)))
+    grad_up = grad_inner * silu
+    return inner.astype(BF16), grad_gate.astype(BF16), grad_up.astype(BF16)
+
+
+def expert_kernel(
+    tokens_ref,
+    cotangent_ref,
+    shares_ref,
+    own_hbm,
+    other_hbm,
+    out_ref,
+    grad_tokens_ref,
+    grad_own_hbm,
+    grad_other_hbm,
+    weights,
+    grads,
+    inner_low,
+    grad_low,
+    stage,
+    load_sems,
+    store_sems,
+    *,
+    steps,
+    chunk,
+):
+    step = pl.program_id(0)
+    expert_count, model_width, all_units = weights.shape
+    hidden_units = all_units // 3
+    units = hidden_units // 2
+
+    @pl.when(step == 0)
+    def _():
+        copies = weight_copies(own_hbm, other_hbm, weights, load_sems)
+        for copy in copies:
+            copy.start()
+        grads[...] = jnp.zeros_like(grads)
+        for copy in copies:
+            copy.wait()
+
+    def run(expert, gate_up, grad_inner):
+        lane = lax.broadcasted_iota(jnp.int32, shares_ref.shape, 1)
+        share = jnp.sum(
+            jnp.where(lane == expert, shares_ref[...], 0.0), axis=1, keepdims=True
+        )
+        inner, grad_gate, grad_up = activate(gate_up, grad_inner, share)
+        inner_low[expert] = inner
+        grad_low[expert, :, :hidden_units] = grad_gate
+        grad_low[expert, :, hidden_units:] = grad_up
+
+    def weight_grads(expert):
+        grads[expert, :, : 2 * hidden_units] += lax.dot_general(
+            tokens_ref[...], grad_low[expert], FIRST_FIRST, preferred_element_type=F32
+        )
+        grads[expert, :, 2 * hidden_units :] += lax.dot_general(
+            cotangent_ref[...], inner_low[expert], FIRST_FIRST, preferred_element_type=F32
+        )
+
+    results = project(tokens_ref[...], cotangent_ref[...], weights[0])
+    for expert in range(expert_count):
+        run(expert, *results)
+        if expert + 1 < expert_count:
+            results = project(tokens_ref[...], cotangent_ref[...], weights[expert + 1])
+        weight_grads(expert)
+
+    @pl.loop(0, model_width // chunk)
+    def _(number):
+        cols = pl.ds(pl.multiple_of(number * chunk, chunk), chunk)
+        total = jnp.zeros((tokens_ref.shape[0], chunk), F32)
+        for expert in range(expert_count):
+            total += lax.dot_general(
+                inner_low[expert],
+                weights[expert, cols, 2 * hidden_units :],
+                LAST_LAST,
+                preferred_element_type=F32,
+            )
+        out_ref[:, cols] = total.astype(BF16)
+        total = jnp.zeros((tokens_ref.shape[0], chunk), F32)
+        for expert in range(expert_count):
+            total += lax.dot_general(
+                grad_low[expert],
+                weights[expert, cols, : 2 * hidden_units],
+                LAST_LAST,
+                preferred_element_type=F32,
+            )
+        grad_tokens_ref[:, cols] = total.astype(BF16)
+
+    @pl.when(step == steps - 1)
+    def _():
+        sources, _, rows, lanes = own_hbm.shape
+
+        @pl.loop(0, expert_count)
+        def _(expert):
+            copies = []
+            for half, half_hbm in enumerate((grad_own_hbm, grad_other_hbm)):
+                for part in range(3):
+                    first = (2 * part + half) * units
+                    stage[half, :, part * units : (part + 1) * units] = grads[
+                        expert, :, first : first + units
+                    ].astype(BF16)
+                for source in range(sources):
+                    copy = pltpu.make_async_copy(
+                        stage.at[half, pl.ds(source * rows, rows), :],
+                        half_hbm.at[source, expert],
+                        store_sems.at[half, source],
+                    )
+                    copy.start()
+                    copies.append(copy)
+            for copy in copies:
+                copy.wait()
+
+
+def experts(tokens, cotangent, shares, own, other, block_rows=512, chunk=512):
+    token_count, model_width = tokens.shape
+    sources, expert_count, rows, lanes = own.shape
+    hidden_units = 2 * lanes // 3
+    steps = token_count // block_rows
+    row_block = pl.BlockSpec((block_rows, model_width), lambda i: (i, 0))
+    in_place = pl.BlockSpec(memory_space=pl.ANY)
+    flops = 2 * token_count * model_width * expert_count * hidden_units * 9
+    return pl.pallas_call(
+        partial(expert_kernel, steps=steps, chunk=chunk),
+        grid=(steps,),
+        in_specs=[
+            row_block,
+            row_block,
+            pl.BlockSpec((block_rows, shares.shape[1]), lambda i: (i, 0)),
+            in_place,
+            in_place,
+        ],
+        out_specs=[row_block, row_block, in_place, in_place],
+        out_shape=[
+            jax.ShapeDtypeStruct(tokens.shape, BF16),
+            jax.ShapeDtypeStruct(tokens.shape, BF16),
+            jax.ShapeDtypeStruct(own.shape, BF16),
+            jax.ShapeDtypeStruct(own.shape, BF16),
+        ],
+        scratch_shapes=[
+            pltpu.VMEM((expert_count, model_width, 3 * hidden_units), BF16),
+            pltpu.VMEM((expert_count, model_width, 3 * hidden_units), F32),
+            pltpu.VMEM((expert_count, block_rows, hidden_units), BF16),
+            pltpu.VMEM((expert_count, block_rows, 2 * hidden_units), BF16),
+            pltpu.VMEM((2, model_width, lanes), BF16),
+            pltpu.SemaphoreType.DMA((sources, 2, 3)),
+            pltpu.SemaphoreType.DMA((2, sources)),
+        ],
+        compiler_params=pltpu.CompilerParams(vmem_limit_bytes=63 * 2**20),
+        cost_estimate=pl.CostEstimate(
+            flops=flops, bytes_accessed=80 * 2**20, transcendentals=0
+        ),
+    )(tokens, cotangent, shares, own, other)
+
+
+def attention_rows(values, kv_head, group_size):
+    first = kv_head * group_size
+    return jnp.concatenate(
+        [values[:, (first + r) * HEAD_DIM : (first + r + 1) * HEAD_DIM] for r in range(group_size)],
+        axis=0,
+    )
+
+
+def quarter_turn(values):
+    half = HEAD_DIM // 2
+    return jnp.concatenate([-values[:, half:], values[:, :half]], axis=1)
+
+
+def window_mask(start, doc_start_ref, first_ref, block_rows, window):
+    key_index = start + lax.broadcasted_iota(jnp.int32, (block_rows, window), 1)
+    query_index = (
+        first_ref[0]
+        + pl.program_id(0) * block_rows
+        + lax.broadcasted_iota(jnp.int32, (block_rows, window), 0)
+    )
+    return (key_index <= query_index) & (key_index >= doc_start_ref[...])
+
+
+def window_start(first_ref, block_rows, window):
+    end = first_ref[0] + (pl.program_id(0) + 1) * block_rows
+    return pl.multiple_of(jnp.maximum(end - window, 0), block_rows)
+
+
+def attention_forward_kernel(
+    first_ref, query_ref, key_value_ref, doc_start_ref, attended_ref, lse_ref, *, group_size, window
+):
+    block_rows = query_ref.shape[0]
+    kv_heads = key_value_ref.shape[1] // (2 * HEAD_DIM)
+    start = window_start(first_ref, block_rows, window)
+    allowed = window_mask(start, doc_start_ref, first_ref, block_rows, window)
+    bias = jnp.where(allowed, 0.0, -1e30)
+    bias = jnp.concatenate([bias] * group_size, axis=0)
+    keys_values = key_value_ref[pl.ds(start, window), :]
+    queries = query_ref[...]
+    parts = []
+    for g in range(kv_heads):
+        keys = keys_values[:, g * HEAD_DIM : (g + 1) * HEAD_DIM]
+        values = keys_values[:, (kv_heads + g) * HEAD_DIM : (kv_heads + g + 1) * HEAD_DIM]
+        scores = lax.dot_general(
+            attention_rows(queries, g, group_size), keys, LAST_LAST, preferred_element_type=F32
+        )
+        scores = scores * HEAD_DIM**-0.5 + bias
+        row_max = jnp.max(scores, axis=1, keepdims=True)
+        exponent = jnp.exp(scores - row_max)
+        total = jnp.sum(exponent, axis=1, keepdims=True)
+        probs = (exponent * (1.0 / total)).astype(BF16)
+        mixed = jnp.dot(probs, values, preferred_element_type=F32).astype(BF16)
+        lse_ref[0, g] = row_max + jnp.log(total)
+        parts += [mixed[r * block_rows : (r + 1) * block_rows] for r in range(group_size)]
+    attended_ref[...] = jnp.concatenate(parts, axis=1)
+
+
+def attention_backward_kernel(
+    first_ref,
+    query_ref,
+    key_value_ref,
+    doc_start_ref,
+    lse_ref,
+    grad_ref,
+    turns_ref,
+    query_turns_ref,
+    grad_query_ref,
+    grad_key_value_ref,
+    grad_keys,
+    grad_values,
+    *,
+    group_size,
+    window,
+    steps,
+):
+    step = pl.program_id(0)
+    block_rows = query_ref.shape[0]
+    kv_heads = key_value_ref.shape[1] // (2 * HEAD_DIM)
+
+    @pl.when(step == 0)
+    def _():
+        grad_keys[...] = jnp.zeros_like(grad_keys)
+        grad_values[...] = jnp.zeros_like(grad_values)
+
+    start = window_start(first_ref, block_rows, window)
+    allowed = window_mask(start, doc_start_ref, first_ref, block_rows, window)
+    bias = jnp.where(allowed, 0.0, -1e30)
+    bias = jnp.concatenate([bias] * group_size, axis=0)
+    rows = pl.ds(start, window)
+    keys_values = key_value_ref[rows, :]
+    queries = query_ref[...]
+    grads = grad_ref[...]
+    query_turns = jnp.concatenate([query_turns_ref[...]] * group_size, axis=0)
+    parts = []
+    for g in range(kv_heads):
+        keys = keys_values[:, g * HEAD_DIM : (g + 1) * HEAD_DIM]
+        values = keys_values[:, (kv_heads + g) * HEAD_DIM : (kv_heads + g + 1) * HEAD_DIM]
+        query_rows = attention_rows(queries, g, group_size)
+        grad_rows = attention_rows(grads, g, group_size)
+        scores = lax.dot_general(query_rows, keys, LAST_LAST, preferred_element_type=F32)
+        probs = jnp.exp(scores * HEAD_DIM**-0.5 + bias - lse_ref[0, g])
+        grad_probs = lax.dot_general(grad_rows, values, LAST_LAST, preferred_element_type=F32)
+        inner = jnp.sum(grad_probs * probs, axis=1, keepdims=True)
+        grad_scores = (HEAD_DIM**-0.5 * (probs * (grad_probs - inner))).astype(BF16)
+        grad_values[g, rows, :] += lax.dot_general(
+            probs.astype(BF16), grad_rows, FIRST_FIRST, preferred_element_type=F32
+        )
+        both_queries = jnp.concatenate([query_rows, quarter_turn(query_rows)], axis=1)
+        grad_keys[g, rows, :] += lax.dot_general(
+            grad_scores, both_queries, FIRST_FIRST, preferred_element_type=F32
+        )
+        both_keys = jnp.concatenate([keys, quarter_turn(keys)], axis=1)
+        turned = jnp.dot(grad_scores, both_keys, preferred_element_type=F32) * query_turns
+        grad_query = (turned[:, :HEAD_DIM] + turned[:, HEAD_DIM:]).astype(BF16)
+        parts += [grad_query[r * block_rows : (r + 1) * block_rows] for r in range(group_size)]
+    grad_query_ref[...] = jnp.concatenate(parts, axis=1)
+
+    @pl.when(step == steps - 1)
+    def _():
+        key_parts, value_parts = [], []
+        for g in range(kv_heads):
+            turned = grad_keys[g] * turns_ref[...]
+            key_parts.append((turned[:, :HEAD_DIM] + turned[:, HEAD_DIM:]).astype(BF16))
+            value_parts.append(grad_values[g].astype(BF16))
+        grad_key_value_ref[...] = jnp.concatenate(key_parts + value_parts, axis=1)
+
+
+def attention_specs(queries, keys_values, block_rows):
+    return dict(
+        smem=pl.BlockSpec(memory_space=pltpu.SMEM),
+        rows=pl.BlockSpec((block_rows, queries.shape[1]), lambda i: (i, 0)),
+        whole=pl.BlockSpec(keys_values.shape, lambda i: (0, 0)),
+        column=pl.BlockSpec((block_rows, 1), lambda i: (i, 0)),
+    )
+
+
+def attention_forward(first, queries, keys_values, doc_start, block_rows=256, reach=1024):
+    row_count, query_cols = queries.shape
+    kv_heads = keys_values.shape[1] // (2 * HEAD_DIM)
+    group_size = query_cols // HEAD_DIM // kv_heads
+    steps = row_count // block_rows
+    window = min(reach + block_rows, keys_values.shape[0])
+    specs = attention_specs(queries, keys_values, block_rows)
+    stacked = group_size * block_rows
+    return pl.pallas_call(
+        partial(attention_forward_kernel, group_size=group_size, window=window),
+        grid=(steps,),
+        in_specs=[specs["smem"], specs["rows"], specs["whole"], specs["column"]],
+        out_specs=[
+            specs["rows"],
+            pl.BlockSpec((1, kv_heads, stacked, 1), lambda i: (i, 0, 0, 0)),
+        ],
+        out_shape=[
+            jax.ShapeDtypeStruct(queries.shape, BF16),
+            jax.ShapeDtypeStruct((steps, kv_heads, stacked, 1), F32),
+        ],
+        compiler_params=pltpu.CompilerParams(vmem_limit_bytes=48 * 2**20),
+        cost_estimate=pl.CostEstimate(
+            flops=4 * row_count * window * query_cols * 8, bytes_accessed=2**22, transcendentals=0
+        ),
+    )(first, queries, keys_values, doc_start)
+
+
+def attention_backward(
+    first, queries, keys_values, doc_start, lse, grads, turns, query_turns, block_rows=256, reach=1024
+):
+    row_count, query_cols = queries.shape
+    kv_heads = keys_values.shape[1] // (2 * HEAD_DIM)
+    group_size = query_cols // HEAD_DIM // kv_heads
+    steps = row_count // block_rows
+    window = min(reach + block_rows, keys_values.shape[0])
+    specs = attention_specs(queries, keys_values, block_rows)
+    stacked = group_size * block_rows
+    return pl.pallas_call(
+        partial(attention_backward_kernel, group_size=group_size, window=window, steps=steps),
+        grid=(steps,),
+        in_specs=[
+            specs["smem"],
+            specs["rows"],
+            specs["whole"],
+            specs["column"],
+            pl.BlockSpec((1, kv_heads, stacked, 1), lambda i: (i, 0, 0, 0)),
+            specs["rows"],
+            pl.BlockSpec(turns.shape, lambda i: (0, 0)),
+            pl.BlockSpec((block_rows, turns.shape[1]), lambda i: (i, 0)),
+        ],
+        out_specs=[specs["rows"], specs["whole"]],
+        out_shape=[
+            jax.ShapeDtypeStruct(queries.shape, BF16),
+            jax.ShapeDtypeStruct(keys_values.shape, BF16),
+        ],
+        scratch_shapes=[
+            pltpu.VMEM((kv_heads, keys_values.shape[0], 2 * HEAD_DIM), F32),
+            pltpu.VMEM((kv_heads, keys_values.shape[0], HEAD_DIM), F32),
+        ],
+        compiler_params=pltpu.CompilerParams(vmem_limit_bytes=48 * 2**20),
+        cost_estimate=pl.CostEstimate(
+            flops=10 * row_count * window * query_cols * 8, bytes_accessed=2**23, transcendentals=0
+        ),
+    )(first, queries, keys_values, doc_start, lse, grads, turns, query_turns)
+
+
+def rotation_tables(positions):
+    half_dim = HEAD_DIM // 2
+    frequencies = 10000.0 ** (-2.0 * jnp.arange(half_dim, dtype=F32) / HEAD_DIM)
+    angles = positions.astype(F32)[:, None] * frequencies[None, :]
+    cosine, sine = jnp.cos(angles), jnp.sin(angles)
+    return jnp.concatenate([cosine, cosine, -sine, -sine], axis=1)
+
+
+def turned_columns(weight):
+    rows, cols = weight.shape
+    halves = weight.reshape(rows, cols // HEAD_DIM, 2, HEAD_DIM // 2)
+    return jnp.stack([-halves[:, :, 1], halves[:, :, 0]], axis=2).reshape(rows, cols)
+
+
+def expert_plan(
+    residual_in,
+    gain_attn,
+    query_weight,
+    key_projection_weight,
+    value_projection_weight,
+    out_weight,
+    gain_ffn,
+    gate_weight,
+    up_weight,
+    down_weight,
+    segments,
+    routes,
+    shares,
+    cotangent,
+    *,
+    groups,
+    tensor_size,
+):
+    row_count, model_width = residual_in.shape
+    query_cols = query_weight.shape[1]
+    kv_cols = key_projection_weight.shape[1]
+    expert_count, slice_rows, unit_count = gate_weight.shape
+    own_experts = expert_count // groups
+    piece_rows = row_count // tensor_size
+    context_rank = lax.axis_index(CONTEXT)
+    tensor_rank = lax.axis_index(TENSOR)
+    group_rank = lax.axis_index(SHARD) * lax.axis_size(CONTEXT) + context_rank
+    own_first = context_rank * row_count
+    piece_first = tensor_rank * piece_rows
+    sibling = [(i, i ^ 1) for i in range(tensor_size)]
+    across = [(i, i ^ 2) for i in range(tensor_size)]
+
+    def own_piece(values):
+        return lax.dynamic_slice_in_dim(values, piece_first, piece_rows)
+
+    def padded_column(gain):
+        return jnp.pad(gain[:, None], ((0, 0), (0, 127)))
+
+    with jax.named_scope("weights"):
+        qkv_full = lax.all_gather(
+            jnp.concatenate(
+                [
+                    query_weight,
+                    key_projection_weight,
+                    value_projection_weight,
+                    padded_column(gain_attn),
+                ],
+                axis=1,
+            ),
+            GROUP,
+            axis=0,
+            tiled=True,
+        )
+        qkv_cols = query_cols + 2 * kv_cols
+        qkv_weight = qkv_full[:, :qkv_cols]
+        gain_attn_float = qkv_full[:, qkv_cols].astype(F32)
+        slices = jnp.concatenate(
+            [gate_weight, up_weight, down_weight.transpose(0, 2, 1)], axis=2
+        )
+        owned = lax.all_to_all(slices, GROUP, 0, 0, tiled=True)
+        out_gathered = lax.all_gather(
+            jnp.concatenate([out_weight.T, padded_column(gain_ffn)], axis=1),
+            GROUP,
+            axis=0,
+            tiled=True,
+        )
+        out_transposed = out_gathered[:, :query_cols]
+        gain_ffn_float = out_gathered[:, query_cols].astype(F32)
+
+    def gather_tokens(piece):
+        own_core = lax.all_gather(piece, GROUP, axis=0, tiled=False)
+        other_core = lax.ppermute(own_core, TENSOR, sibling)
+        return jnp.stack([own_core, other_core], axis=1).reshape(-1, piece.shape[1])
+
+    with jax.named_scope("attention"):
+        positions = doc_positions(segments)
+        turns = rotation_tables(positions)
+        own_turns = lax.dynamic_slice_in_dim(turns, own_first, row_count)
+        own_index = own_first + jnp.arange(row_count, dtype=jnp.int32)
+        doc_start = own_index - lax.dynamic_slice_in_dim(positions, own_first, row_count)
+        input_float = residual_in.astype(F32)
+        first_normalized = rms_scale(input_float, gain_attn_float).astype(BF16)
+        rotated_cols = query_cols + kv_cols
+        projected = jnp.dot(
+            first_normalized,
+            jnp.concatenate([qkv_weight, turned_columns(qkv_weight[:, :rotated_cols])], axis=1),
+            preferred_element_type=F32,
+        )
+        heads = rotated_cols // HEAD_DIM
+        rotated = (
+            projected[:, :rotated_cols] * jnp.tile(own_turns[:, :HEAD_DIM], (1, heads))
+            - projected[:, qkv_cols:] * jnp.tile(own_turns[:, HEAD_DIM:], (1, heads))
+        ).astype(BF16)
+        queries = rotated[:, :query_cols]
+        keys_values = lax.all_gather(
+            jnp.concatenate(
+                [rotated[:, query_cols:], projected[:, rotated_cols:qkv_cols].astype(BF16)], axis=1
+            ),
+            CONTEXT,
+            axis=0,
+            tiled=True,
+        )
+        first = own_first.reshape(1).astype(jnp.int32)
+        attended, lse = attention_forward(first, queries, keys_values, doc_start[:, None])
+
+    with jax.named_scope("routing"):
+        owned, attended = lax.optimization_barrier((owned, attended))
+        others = lax.ppermute(owned, TENSOR, across)
+        cotangent_piece = own_piece(cotangent)
+        cotangent_all = gather_tokens(cotangent_piece)
+        spread = jnp.sum(
+            jnp.where(
+                own_piece(routes)[:, :, None] == jnp.arange(expert_count, dtype=jnp.int32),
+                own_piece(shares)[:, :, None],
+                0.0,
+            ),
+            axis=1,
+        )
+        token_shares = lax.dynamic_slice_in_dim(
+            gather_tokens(spread), group_rank * own_experts, own_experts, axis=1
+        )
+        token_shares = jnp.pad(token_shares, ((0, 0), (0, 8 - own_experts)))
+
+    with jax.named_scope("attention_out"):
+        attn_part = lax.dot_general(
+            attended, out_transposed, LAST_LAST, preferred_element_type=F32
+        )
+        attn_piece = lax.psum_scatter(
+            attn_part.astype(BF16), TENSOR, scatter_dimension=0, tiled=True
+        )
+        hidden = own_piece(residual_in).astype(F32) + attn_piece.astype(F32)
+        normed_ffn, ffn_norm_back = jax.vjp(rms_scale, hidden, gain_ffn_float)
+
+    with jax.named_scope("experts"):
+        tokens_all = gather_tokens(normed_ffn.astype(BF16))
+        shape = (groups, own_experts, slice_rows, 3 * unit_count)
+        out_parts, grad_token_parts, grad_own, grad_other = experts(
+            tokens_all, cotangent_all, token_shares, owned.reshape(shape), others.reshape(shape)
+        )
+
+    def reduce_tokens(parts):
+        parts = parts.reshape(groups, 2, piece_rows, model_width)
+        received = lax.ppermute(parts[:, 1], TENSOR, sibling)
+        both = (parts[:, 0].astype(F32) + received.astype(F32)).astype(BF16)
+        return lax.psum_scatter(
+            both.reshape(groups * piece_rows, model_width),
+            GROUP,
+            scatter_dimension=0,
+            tiled=True,
+        ).astype(F32)
+
+    with jax.named_scope("expert_grads"):
+        grad_second = reduce_tokens(grad_token_parts)
+        received = lax.ppermute(grad_other, TENSOR, across)
+        total = (grad_own.astype(F32) + received.astype(F32)).astype(BF16)
+        returned = lax.all_to_all(
+            total.reshape(expert_count, slice_rows, 3 * unit_count), GROUP, 0, 0, tiled=True
+        )
+        grad_hidden_norm, grad_gain_ffn_local = ffn_norm_back(grad_second)
+        grad_hidden = cotangent_piece.astype(F32) + grad_hidden_norm
+        grad_hidden_low = lax.all_gather(grad_hidden.astype(BF16), TENSOR, axis=0, tiled=True)
+        output_piece = (hidden + reduce_tokens(out_parts)).astype(BF16)
+        output = lax.all_gather(output_piece, TENSOR, axis=0, tiled=True)
+
+    with jax.named_scope("attention_back"):
+        grad_out_local = lax.dot_general(
+            grad_hidden_low, attended, FIRST_FIRST, preferred_element_type=F32
+        )
+        grad_out_transposed = lax.psum_scatter(
+            grad_out_local.astype(BF16), GROUP, scatter_dimension=0, tiled=True
+        )
+        grad_attended = jnp.dot(grad_hidden_low, out_transposed, preferred_element_type=F32)
+        grad_query_lin, grad_key_value = attention_backward(
+            first,
+            queries,
+            keys_values,
+            doc_start[:, None],
+            lse,
+            grad_attended.astype(BF16),
+            turns,
+            own_turns,
+        )
+        grad_key_value = lax.psum_scatter(
+            grad_key_value, CONTEXT, scatter_dimension=0, tiled=True
+        )
+        grad_projected = jnp.concatenate([grad_query_lin, grad_key_value], axis=1)
+        grad_first_part = lax.dot_general(
+            grad_projected, qkv_weight, LAST_LAST, preferred_element_type=F32
+        )
+        grad_first = lax.psum_scatter(
+            grad_first_part.astype(BF16), TENSOR, scatter_dimension=0, tiled=True
+        ).astype(F32)
+        _, attn_norm_back = jax.vjp(
+            rms_scale, own_piece(residual_in).astype(F32), gain_attn_float
+        )
+        grad_input_norm, grad_gain_attn_local = attn_norm_back(grad_first)
+        grad_input = lax.all_gather(
+            (grad_hidden + grad_input_norm).astype(BF16), TENSOR, axis=0, tiled=True
+        )
+        grad_qkv_local = lax.dot_general(
+            first_normalized, grad_projected, FIRST_FIRST, preferred_element_type=F32
+        )
+        grad_qkv = lax.psum_scatter(
+            grad_qkv_local.astype(BF16), GROUP, scatter_dimension=0, tiled=True
+        ).astype(F32)
+        gains = lax.psum(
+            jnp.stack([grad_gain_attn_local, grad_gain_ffn_local]), GROUP + (TENSOR,)
+        )
+        gains = lax.dynamic_slice_in_dim(gains, group_rank * slice_rows, slice_rows, axis=1)
+    units = unit_count
+    return (
+        output,
+        grad_input,
+        gains[0],
+        grad_qkv[:, :query_cols],
+        grad_qkv[:, query_cols:rotated_cols],
+        grad_qkv[:, rotated_cols:],
+        grad_out_transposed.astype(F32).T,
+        gains[1],
+        returned[:, :, :units].astype(F32),
+        returned[:, :, units : 2 * units].astype(F32),
+        returned[:, :, 2 * units :].transpose(0, 2, 1).astype(F32),
+    )
+
+
 def solution(mesh):
     placed = (
-        P(("shard", "context"), None),
-        P(("shard", "context")),
-        P(("shard", "context"), "tensor"),
-        P(("shard", "context"), "tensor"),
-        P(("shard", "context"), "tensor"),
-        P("tensor", ("shard", "context")),
-        P(("shard", "context")),
-        P(None, ("shard", "context"), "tensor"),
-        P(None, ("shard", "context"), "tensor"),
-        P(None, "tensor", ("shard", "context")),
-        P("shard"),
-        P(("shard", "context"), None),
-        P(("shard", "context"), None),
-        P(("shard", "context"), None),
-    )
+        P(GROUP, None),
+        P(GROUP),
+        P(GROUP, TENSOR),
+        P(GROUP, TENSOR),
+        P(GROUP, TENSOR),
+        P(TENSOR, GROUP),
+        P(GROUP),
+        P(None, GROUP, TENSOR),
+        P(None, GROUP, TENSOR),
+        P(None, TENSOR, GROUP),
+        P(SHARD),
+        P(GROUP, None),
+        P(GROUP, None),
+        P(GROUP, None),
+    )
+    sizes = dict(mesh.shape)
+    if sizes[SHARD] == 4 and sizes[CONTEXT] == 2 and sizes[TENSOR] == 4:
+        plan = partial(
+            expert_plan, groups=sizes[SHARD] * sizes[CONTEXT], tensor_size=sizes[TENSOR]
+        )
+    else:
+        plan = gathered_plan
     return jax.shard_map(
-        on_device,
+        plan,
         mesh=mesh,
         in_specs=placed,
         out_specs=(
-            P(("shard", "context"), None),
-            P(("shard", "context"), None),
-            P(("shard", "context")),
-            P(("shard", "context"), "tensor"),
-            P(("shard", "context"), "tensor"),
-            P(("shard", "context"), "tensor"),
-            P("tensor", ("shard", "context")),
-            P(("shard", "context")),
-            P(None, ("shard", "context"), "tensor"),
-            P(None, ("shard", "context"), "tensor"),
-            P(None, "tensor", ("shard", "context")),
+            P(GROUP, None),
+            P(GROUP, None),
+            P(GROUP),
+            P(GROUP, TENSOR),
+            P(GROUP, TENSOR),
+            P(GROUP, TENSOR),
+            P(TENSOR, GROUP),
+            P(GROUP),
+            P(None, GROUP, TENSOR),
+            P(None, GROUP, TENSOR),
+            P(None, TENSOR, GROUP),
         ),
         check_vma=False,
     )

time: 4340 us -> 1530 us (0.35)
  waiting for transfers between devices: 2640 us -> 1020 us
  matrix products: 627 us -> 31 us
  local copies, waits for them, and re-layouts: 433 us -> 49.6 us
  other arithmetic: 466 us -> 89.7 us
  Pallas kernels: 0 us -> 235 us
  blocking collectives: 125 us -> 70.7 us
    all_gather x32 -> x8, waiting for transfers between devices: 1420 us -> 408 us  [the longest x2 197 us: gather_tokens(): own_core = lax.all_gather(piece, GROUP, axis=0, tiled=False)]
    reduce_scatter x21 -> x7, waiting for transfers between devices: 1030 us -> 264 us  [the longest x2 122 us: reduce_tokens(): lax.psum_scatter(both.reshape(groups * piece_rows, model_width), GROUP, s...]
    dot_general x74 -> x6, matrix products: 627 us -> 31 us  [the longest x1 6.2 us: expert_plan(): lax.dot_general(first_normalized, grad_projected, FIRST_FIRST, preferred_...]
    scatter-add x10 -> x0, other arithmetic: 268 us -> none  [the longest x5 134 us: backward_turn(): running.at[token_rows].add(grad_picked.reshape(turn_slots, model_width))]
    gather x21 -> x0, local copies, waits for them, and re-layouts: 262 us -> none  [the longest x10 149 us: backward_turn(): upstream[token_rows] * share_rows[:, None]]
    pallas_call x0 -> x3, Pallas kernels: none -> 235 us  [the longest x1 184 us: experts(): pl.pallas_call(partial(expert_kernel, steps=steps, chunk=chunk), grid=(st...]
    ppermute x0 -> x7, waiting for transfers between devices: none -> 217 us  [the longest x1 133 us: expert_plan(): received = lax.ppermute(grad_other, TENSOR, across)]
    psum x3 -> x0, waiting for transfers between devices: 190 us -> none  [the longest x1 120 us: on_device(): lax.psum(expert_part.astype(jnp.bfloat16), 'tensor').astype(jnp.float32)]
  transfers between devices with their start and end apart: 56 -> 24, of which waited for: 52 -> 18; matrix products, arithmetic and copies ran while one was open for 25% -> 8% of each run, Pallas kernels for 0% -> 1%
where the time goes in v1:
time: 1530 us
  waiting for transfers between devices  1020 us (67%)
  Pallas kernels  235 us (15%)
  other arithmetic  89.7 us (6%)
  blocking collectives  70.7 us (5%)
  local copies, waits for them, and re-layouts  49.6 us (3%)
  matrix products  31 us (2%)
  starting transfers between devices  16.8 us (1%)
    all_gather x2, waiting for transfers between devices, gather_tokens(): own_core = lax.all_gather(piece, GROUP, axis=0, tiled=False)  197 us
    pallas_call x1, Pallas kernels, experts(): pl.pallas_call(partial(expert_kernel, steps=steps, chunk=chunk), grid=(st...  184 us
    ppermute x1, waiting for transfers between devices, expert_plan(): received = lax.ppermute(grad_other, TENSOR, across)  133 us
    all_to_all x1, waiting for transfers between devices, expert_plan(): lax.all_to_all(total.reshape(expert_count, slice_rows, 3 * unit_count), G...  129 us
    all_gather x1, waiting for transfers between devices, expert_plan(): lax.all_gather(jnp.concatenate([query_weight, key_projection_weight, valu...  123 us
    reduce_scatter x2, waiting for transfers between devices, reduce_tokens(): lax.psum_scatter(both.reshape(groups * piece_rows, model_width), GROUP, s...  122 us
    ppermute x1, waiting for transfers between devices, expert_plan(): others = lax.ppermute(owned, TENSOR, across)  72 us
    reduce_scatter x1, waiting for transfers between devices, expert_plan(): lax.psum_scatter(grad_qkv_local.astype(BF16), GROUP, scatter_dimension=0,...  68.7 us
  transfers between devices with their start and end apart: 24, of which 18 were waited for; matrix products, arithmetic and copies ran while one was open for 8% of the time, Pallas kernels for 1%

profile of v1, /device:TPU:0, one launch (start us, length us, event | category | flops | bytes accessed | tf_op | source)
XLA Modules:
  0.0 1526.1 jit_solution(13341711571959807373)
XLA Ops:
  7.2 6.4 pad_maximum_fusion.2
  13.6 7.4 all-to-all-start
  22.3 3.7 multiply_cosine_fusion
  32.1 3.1 copy.107
  35.9 122.8 %all-gather.12.cloned.1.call-done = bf16[1536,768]{1,0:T(8,128)(2,1)} async-done(((bf16[192,768]{1,0:T(8,128)(2,1)}), bf16[1536,768]{1,0:T(8,128)(2,1)}) %all-gather.12.cloned.1.call-update) | async-done | bytes 2359312 | tf_op jit(solution)/shard_map/weights/all_gather | solution.py:863
  158.7 2.7 slice.108
  161.4 2.6 copy.120
  166.7 2.6 copy.104
  171.6 5.9 fusion.5
  180.8 18.0 %all-gather.14.cloned.1.call-done.key_value_ref = bf16[2048,256]{1,0:T(8,128)(2,1)} async-done(((bf16[1024,256]{1,0:T(8,128)(2,1)}), bf16[2048,256]{1,0:T(8,128)(2,1)}) %all-gather.14.cloned.1.call-update) | async-done | bytes 1048592 | tf_op jit(solution)/shard_map/attention/all_gather | solution.py:918
  200.0 18.7 %attention.1 = (bf16[1024,384]{1,0:T(8,128)(2,1)S(1)}, f32[4,2,768,1]{3,2,1,0:T(8,128)}) custom-call(s32[1]{0:T(128)} %bitcast.1.first_ref, bf16[1024,384]{1,0:T(8,128)(2,1)S(1)} %slice.113.query_ref, bf16[2048,256]{1,0:T(8,128)(2,1)S(1)} %copy-done.6, s32[1024,1]{1,0:T(8,128)S(1)} %copy.110.doc_start_ref), custom_call_target="tpu_custom_call" | custom-call | flops 16106127360 | bytes 4194304 | tf_op jit(solution)/shard_map/attention/pallas_call | solution.py:751
  218.7 26.8 %all-gather.16.cloned.1.call-done = bf16[1536,512]{1,0:T(8,128)(2,1)} async-done(((bf16[192,512]{1,0:T(8,128)(2,1)}), bf16[1536,512]{1,0:T(8,128)(2,1)}) %all-gather.16.cloned.1.call-update) | async-done | bytes 1572880 | tf_op jit(solution)/shard_map/weights/all_gather | solution.py:884
  245.5 4.8 convolution_convert_fusion.1
  253.9 33.4 %reduce-scatter.8.cloned.1.call-done = bf16[256,1536]{1,0:T(8,128)(2,1)} async-done(((bf16[1024,1536]{1,0:T(8,128)(2,1)}), bf16[256,1536]{1,0:T(8,128)(2,1)}) %reduce-scatter.8.cloned.1.call-update) | async-done | bytes 786448 | tf_op jit(solution)/shard_map/attention_out/reduce_scatter | solution.py:951
  292.2 96.9 %all-gather.26.cloned.1.call-done = bf16[2048,1536]{1,0:T(8,128)(2,1)} async-done(((bf16[256,1536]{1,0:T(8,128)(2,1)}), bf16[2048,1536]{1,0:T(8,128)(2,1)}) %all-gather.26.cloned.1.call-update) | async-done | bytes 6291472 | tf_op jit(solution)/shard_map/routing/all_gather | solution.py:894
  389.2 100.1 %all-gather.24.cloned.1.call-done = bf16[2048,1536]{1,0:T(8,128)(2,1)} async-done(((bf16[256,1536]{1,0:T(8,128)(2,1)}), bf16[2048,1536]{1,0:T(8,128)(2,1)}) %all-gather.24.cloned.1.call-update) | async-done | bytes 6291472 | tf_op jit(solution)/shard_map/experts/all_gather | solution.py:894
  491.5 30.9 %all-gather.2 = f32[2048,40]{0,1:T(8,128)S(1)} all-gather(f32[256,40]{0,1:T(8,128)S(1)} %select_reduce_fusion), channel_id=4, replica_groups=mesh['shard'=4,'context'=2,'tensor'=4] {'shard','context'}, dimensions={0}, use_global_device_ids=true | all-gather | bytes 368640 | tf_op jit(solution)/shard_map/routing/all_gather | solution.py:894
  526.9 11.6 pad_maximum_fusion.1
  538.5 8.5 pad_maximum_fusion
  547.0 72.0 %collective-permute-done.3 = bf16[40,192,384]{2,1,0:T(8,128)(2,1)} collective-permute-done((bf16[40,192,384]{2,1,0:T(8,128)(2,1)}, bf16[40,192,384]{2,1,0:T(8,128)(2,1)}, u32[]{:S(2)}, u32[]{:S(2)}) %collective-permute-start.3) | collective-permute-done | bytes 5898272 | tf_op jit(solution)/shard_map/routing/ppermute | solution.py:931
  619.1 183.8 %experts.1 = (bf16[4096,1536]{1,0:T(8,128)(2,1)}, bf16[4096,1536]{1,0:T(8,128)(2,1)}, bf16[8,5,192,384]{3,2,1,0:T(8,128)(2,1)}, bf16[8,5,192,384]{3,2,1,0:T(8,128)(2,1)}) custom-call(bf16[4096,1536]{1,0:T(8,128)(2,1)} %bitcast.74, bf16[4096,1536]{1,0:T(8,128)(2,1)} %bitcast.73, f32[4096,8]{1,0:T(8,128)} %pad.13.shares_ref, ...), custom_call_target="tpu_custom_call" | custom-call | flops 144955146240 | bytes 83886080 | tf_op jit(solution)/shard_map/experts/pallas_call | solution.py:574
  802.8 3.5 slice_bitcast_fusion
  806.4 10.1 collective-permute-done.5
  816.5 7.3 fusion
  823.9 116.3 %reduce-scatter.12.cloned.1.call-done = bf16[256,1536]{1,0:T(8,128)(2,1)} async-done(((bf16[2048,1536]{1,0:T(8,128)(2,1)}), bf16[256,1536]{1,0:T(8,128)(2,1)}) %reduce-scatter.12.cloned.1.call-update) | async-done | bytes 786448 | tf_op jit(solution)/shard_map/expert_grads/reduce_scatter | solution.py:968
  940.2 2.4 fusion.15
  942.6 2.7 fusion.36
  946.4 26.7 %all-gather.20.cloned.1.call-done = bf16[1024,1536]{1,0:T(8,128)(2,1)} async-done(((bf16[256,1536]{1,0:T(8,128)(2,1)}), bf16[1024,1536]{1,0:T(8,128)(2,1)}) %all-gather.20.cloned.1.call-update) | async-done | bytes 3145744 | tf_op jit(solution)/shard_map/expert_grads/all_gather | solution.py:984
  973.1 4.1 convolution_convert_fusion.4.grad_ref
  977.2 32.6 %attention_back.1 = (bf16[1024,384]{1,0:T(8,128)(2,1)S(1)}, bf16[2048,256]{1,0:T(8,128)(2,1)}) custom-call(s32[1]{0:T(128)} %bitcast.1.first_ref, bf16[1024,384]{1,0:T(8,128)(2,1)S(1)} %copy-done.3, bf16[2048,256]{1,0:T(8,128)(2,1)S(1)} %copy-done.7, s32[1024,1]{1,0:T(8,128)S(1)} %copy-done.5, f32[4,2,768,1]{3,2,1,0:T(8,128)} %get-tuple-element.26.lse_ref, ...), custom_call_target="tpu_custom_call" | custom-call | flops 40265318400 | bytes 8388608 | tf_op jit(solution)/shard_map/attention_back/pallas_call | solution.py:780
  1009.9 5.8 slice_bitcast_fusion.2
  1016.9 13.4 reduce-scatter.14.cloned.1.call-done
  1032.2 5.3 convolution_convert_fusion
  1037.8 9.5 fusion.1
  1048.9 4.7 convolution_convert_fusion.3
  1053.8 6.2 convolution_convert_fusion.2
  1060.0 133.5 %collective-permute-done.6 = bf16[8,5,192,384]{3,2,1,0:T(8,128)(2,1)} collective-permute-done((bf16[8,5,192,384]{3,2,1,0:T(8,128)(2,1)}, bf16[8,5,192,384]{3,2,1,0:T(8,128)(2,1)}, u32[]{:S(2)}, u32[]{:S(2)}) %collective-permute-start.6) | collective-permute-done | bytes 5898272 | tf_op jit(solution)/shard_map/expert_grads/ppermute | solution.py:977
  1193.5 9.1 add_convert_fusion
  1202.6 5.0 all-to-all-start.1
  1209.5 6.0 reduce-scatter.10.cloned.1.call-done
  1215.5 4.4 fusion.19
  1220.5 129.3 %all-to-all-done.1 = bf16[40,192,384]{2,1,0:T(8,128)(2,1)} async-done(((bf16[40,192,384]{2,1,0:T(8,128)(2,1)}), bf16[40,192,384]{2,1,0:T(8,128)(2,1)}, u32[]{:S(2)}, u32[]{:S(2)}) %all-to-all-start.1) | async-done | bytes 5898272 | tf_op jit(solution)/shard_map/expert_grads/all_to_all | solution.py:979
  1349.8 7.8 convert_bitcast_fusion
  1357.6 25.9 %reduce-scatter.20.cloned.1.call-done = bf16[192,384]{1,0:T(8,128)(2,1)} async-done(((bf16[1536,384]{1,0:T(8,128)(2,1)}), bf16[192,384]{1,0:T(8,128)(2,1)}) %reduce-scatter.20.cloned.1.call-update) | async-done | bytes 147472 | tf_op jit(solution)/shard_map/attention_back/reduce_scatter | solution.py:992
  1385.1 68.7 %reduce-scatter.18.cloned.1.call-done = bf16[192,640]{1,0:T(8,128)(2,1)} async-done(((bf16[1536,640]{1,0:T(8,128)(2,1)}), bf16[192,640]{1,0:T(8,128)(2,1)}) %reduce-scatter.18.cloned.1.call-update) | async-done | bytes 245776 | tf_op jit(solution)/shard_map/attention_back/reduce_scatter | solution.py:1026
  1457.0 39.8 %psum.7 = f32[2,1536]{1,0:T(2,128)S(1)} all-reduce(f32[2,1536]{1,0:T(2,128)S(1)} %pad_maximum_fusion.7), channel_id=1, replica_groups=mesh['shard'=4,'context'=2,'tensor'=4] {'shard','context','tensor'}, use_global_device_ids=true, to_apply=%region_15.16 | all-reduce | flops 3072 | bytes 24576 | tf_op jit(solution)/shard_map/attention_back/psum | solution.py:1029
  1497.4 16.4 %all-gather.22.cloned.1.call-done = bf16[1024,1536]{1,0:T(8,128)(2,1)} async-done(((bf16[256,1536]{1,0:T(8,128)(2,1)}), bf16[1024,1536]{1,0:T(8,128)(2,1)}) %all-gather.22.cloned.1.call-update) | async-done | bytes 3145744 | tf_op jit(solution)/shard_map/attention_back/all_gather | solution.py:1020
  1513.8 3.9 copy.134
  (188 shorter events, 48.7 us)
Async XLA Ops:
  7.2 483.5 %copy-start = (f32[1024,8]{0,1:T(8,128)S(1)}, f32[1024,8]{0,1:T(8,128)}, u32[]{:S(2)}) copy-start(f32[1024,8]{0,1:T(8,128)} %param.26) | copy-start | bytes 98308
  13.6 7.5 copy-start.38
  13.6 7.6 copy-start.26
  13.6 7.6 copy-start.29
  13.6 7.6 copy-start.30
  13.6 8.5 copy-start.31
  13.6 205.1 %all-to-all-start = ((bf16[40,192,384]{2,1,0:T(8,128)(2,1)}), bf16[40,192,384]{2,1,0:T(8,128)(2,1)}, u32[]{:S(2)}, u32[]{:S(2)}) async-start(bf16[40,192,384]{2,1,0:T(8,128)(2,1)} %pad_maximum_fusion.2), calls=%async_computation | async-start | bytes 11796480 | tf_op jit(solution)/shard_map/weights/all_to_all | solution.py:883
  21.1 137.7 %all-gather.12.cloned.1.call-start = ((), (), s32[]{:S(2)}) async-start(), calls=%async_computation.9 | async-start | bytes 2654208 | tf_op jit(solution)/shard_map/weights/all_gather | solution.py:863
  22.0 176.8 %all-gather.14.cloned.1.call-start = ((), (), s32[]{:S(2)}) async-start(), calls=%async_computation.10 | async-start | bytes 1572864 | tf_op jit(solution)/shard_map/attention/all_gather | solution.py:918
  35.9 135.2 %copy-start.36 = (f32[1024]{0:T(1024)}, f32[1024]{0:T(1024)S(1)}, u32[]{:S(2)}) copy-start(f32[1024]{0:T(1024)S(1)} %add_rsqrt_fusion) | copy-start | bytes 12292
  179.2 66.3 %all-gather.16.cloned.1.call-start = ((), (), s32[]{:S(2)}) async-start(), calls=%async_computation.11 | async-start | bytes 1769472 | tf_op jit(solution)/shard_map/weights/all_gather | solution.py:884
  180.4 106.9 %reduce-scatter.8.cloned.1.call-start = ((), (), s32[]{:S(2)}) async-start(), calls=%async_computation.12 | async-start | bytes 3932160 | tf_op jit(solution)/shard_map/attention_out/reduce_scatter | solution.py:951
  180.7 38.0 %copy-start.4 = (s32[1024,1]{1,0:T(8,128)}, s32[1024,1]{1,0:T(8,128)S(1)}, u32[]{:S(2)}) copy-start(s32[1024,1]{1,0:T(8,128)S(1)} %copy.110.doc_start_ref) | copy-start | bytes 12292
  180.8 37.9 %copy-start.2 = (bf16[1024,384]{1,0:T(8,128)(2,1)}, bf16[1024,384]{1,0:T(8,128)(2,1)S(1)}, u32[]{:S(2)}) copy-start(bf16[1024,384]{1,0:T(8,128)(2,1)S(1)} %slice.113.query_ref) | copy-start | bytes 2359300
  218.7 31.6 %copy-start.8 = (bf16[1024,384]{1,0:T(8,128)(2,1)}, bf16[1024,384]{1,0:T(8,128)(2,1)S(1)}, u32[]{:S(2)}) copy-start(bf16[1024,384]{1,0:T(8,128)(2,1)S(1)} %get-tuple-element.22) | copy-start | bytes 2359300
  250.3 36.9 %copy-start.11 = (bf16[1024,1536]{1,0:T(8,128)(2,1)S(1)}, bf16[1024,1536]{1,0:T(8,128)(2,1)}, u32[]{:S(2)}) copy-start(bf16[1024,1536]{1,0:T(8,128)(2,1)} %param.14) | copy-start | bytes 9437188
  250.3 138.8 %all-gather.26.cloned.1.call-start = ((), (), s32[]{:S(2)}) async-start(), calls=%async_computation.23 | async-start | bytes 7077888 | tf_op jit(solution)/shard_map/routing/all_gather | solution.py:894
  252.6 236.6 %all-gather.24.cloned.1.call-start = ((), (), s32[]{:S(2)}) async-start(), calls=%async_computation.22 | async-start | bytes 7077888 | tf_op jit(solution)/shard_map/experts/all_gather | solution.py:894
  253.9 38.3 %copy-start.23 = (f32[1536]{0:T(1024)}, f32[1536]{0:T(1024)S(1)}, u32[]{:S(2)}) copy-start(f32[1536]{0:T(1024)S(1)} %convert_reduce_fusion) | copy-start | bytes 18436
  292.2 648.0 %reduce-scatter.12.cloned.1.call-start = ((), (), s32[]{:S(2)}) async-start(), calls=%async_computation.15 | async-start | bytes 7077888 | tf_op jit(solution)/shard_map/expert_grads/reduce_scatter | solution.py:968
  389.1 137.8 %collective-permute-start.1 = (bf16[8,256,1536]{2,1,0:T(8,128)(2,1)}, bf16[8,256,1536]{2,1,0:T(8,128)(2,1)}, u32[]{:S(2)}, u32[]{:S(2)}) collective-permute-start(bf16[8,256,1536]{2,1,0:T(8,128)(2,1)} %bitcast.84), channel_id=1, source_target_pairs={{0,1},{1,0},{2,3},{3,2},{4,5},{5,4},{6,7},{7,6},{8,9},{9,8},{10,11... | collective-permute-start | bytes 18874376 | tf_op jit(solution)/shard_map/routing/ppermute | solution.py:895
  489.2 49.3 %collective-permute-start = (bf16[8,256,1536]{2,1,0:T(8,128)(2,1)}, bf16[8,256,1536]{2,1,0:T(8,128)(2,1)}, u32[]{:S(2)}, u32[]{:S(2)}) collective-permute-start(bf16[8,256,1536]{2,1,0:T(8,128)(2,1)} %bitcast.86), channel_id=1, source_target_pairs={{0,1},{1,0},{2,3},{3,2},{4,5},{5,4},{6,7},{7,6},{8,9},{9,8},{10,11... | collective-permute-start | bytes 18874376 | tf_op jit(solution)/shard_map/experts/ppermute | solution.py:895
  489.2 129.8 %collective-permute-start.3 = (bf16[40,192,384]{2,1,0:T(8,128)(2,1)}, bf16[40,192,384]{2,1,0:T(8,128)(2,1)}, u32[]{:S(2)}, u32[]{:S(2)}) collective-permute-start(bf16[40,192,384]{2,1,0:T(8,128)(2,1)} %all-to-all-done), channel_id=1, source_target_pairs={{0,2},{1,3},{2,0},{3,1},{4,6},{5,7},{6,4},{7,5},{8,10},{9,11},{10,... | collective-permute-start | bytes 17694728 | tf_op jit(solution)/shard_map/routing/ppermute | solution.py:931
  522.4 1.7 collective-permute-start.2
  526.9 11.6 slice-start.1
  526.9 11.6 slice-start.2
  806.3 10.2 collective-permute-start.5
  823.8 116.4 %copy-start.12 = (bf16[1024,1536]{1,0:T(8,128)(2,1)S(1)}, bf16[1024,1536]{1,0:T(8,128)(2,1)}, u32[]{:S(2)}) copy-start(bf16[1024,1536]{1,0:T(8,128)(2,1)} %param.14) | copy-start | bytes 9437188
  823.8 116.4 %copy-start.24 = (f32[1536]{0:T(1024)S(1)}, f32[1536]{0:T(1024)}, u32[]{:S(2)}) copy-start(f32[1536]{0:T(1024)} %copy-done.23) | copy-start | bytes 18436
  823.8 116.4 %copy-start.33 = (f32[256]{0:T(256)S(1)}, f32[256]{0:T(256)}, u32[]{:S(2)}) copy-start(f32[256]{0:T(256)} %copy-done.32) | copy-start | bytes 3076
  823.8 118.7 %copy-start.35 = (f32[256]{0:T(256)S(1)}, f32[256]{0:T(256)}, u32[]{:S(2)}) copy-start(f32[256]{0:T(256)} %copy-done.34) | copy-start | bytes 3076
  823.8 149.2 %all-gather.20.cloned.1.call-start = ((), (), s32[]{:S(2)}) async-start(), calls=%async_computation.16 | async-start | bytes 3932160 | tf_op jit(solution)/shard_map/expert_grads/all_gather | solution.py:984
  945.3 85.0 %reduce-scatter.14.cloned.1.call-start = ((), (), s32[]{:S(2)}) async-start(), calls=%async_computation.17 | async-start | bytes 1572864 | tf_op jit(solution)/shard_map/attention_back/reduce_scatter | solution.py:1006
  946.4 30.8 %copy-start.3 = (bf16[1024,384]{1,0:T(8,128)(2,1)S(1)}, bf16[1024,384]{1,0:T(8,128)(2,1)}, u32[]{:S(2)}) copy-start(bf16[1024,384]{1,0:T(8,128)(2,1)} %copy-done.2) | copy-start | bytes 2359300
  946.4 30.8 %copy-start.5 = (s32[1024,1]{1,0:T(8,128)S(1)}, s32[1024,1]{1,0:T(8,128)}, u32[]{:S(2)}) copy-start(s32[1024,1]{1,0:T(8,128)} %copy-done.4) | copy-start | bytes 12292
  1009.8 197.8 %reduce-scatter.16.cloned.1.call-start = ((), (), s32[]{:S(2)}) async-start(), calls=%async_computation.18 | async-start | bytes 3932160 | tf_op jit(solution)/shard_map/attention_back/reduce_scatter | solution.py:1013
  1015.7 16.5 %copy-start.19 = (bf16[1536,768]{1,0:T(8,128)(2,1)S(1)}, bf16[1536,768]{1,0:T(8,128)(2,1)}, u32[]{:S(2)}) copy-start(bf16[1536,768]{1,0:T(8,128)(2,1)} %all-gather.12.cloned.1.call-done) | copy-start | bytes 7077892
  1015.7 22.1 %collective-permute-start.4 = (bf16[8,256,1536]{2,1,0:T(8,128)(2,1)}, bf16[8,256,1536]{2,1,0:T(8,128)(2,1)}, u32[]{:S(2)}, u32[]{:S(2)}) collective-permute-start(bf16[8,256,1536]{2,1,0:T(8,128)(2,1)} %slice_bitcast_fusion.2), channel_id=1, source_target_pairs={{0,1},{1,0},{2,3},{3,2},{4,5},{5,4},{6,7},{7,6},{8,9},{9,8},{10,11... | collective-permute-start | bytes 18874376 | tf_op jit(solution)/shard_map/expert_grads/ppermute | solution.py:966
  1037.5 178.0 %reduce-scatter.10.cloned.1.call-start = ((), (), s32[]{:S(2)}) async-start(), calls=%async_computation.13 | async-start | bytes 7077888 | tf_op jit(solution)/shard_map/expert_grads/reduce_scatter | solution.py:968
  1047.3 336.1 %reduce-scatter.20.cloned.1.call-start = ((), (), s32[]{:S(2)}) async-start(), calls=%async_computation.21 | async-start | bytes 1327104 | tf_op jit(solution)/shard_map/attention_back/reduce_scatter | solution.py:992
  1047.4 6.4 copy-start.22
  1047.4 6.4 copy-start.28
  1047.4 6.4 copy-start.37
  1047.4 146.1 %collective-permute-start.6 = (bf16[8,5,192,384]{3,2,1,0:T(8,128)(2,1)}, bf16[8,5,192,384]{3,2,1,0:T(8,128)(2,1)}, u32[]{:S(2)}, u32[]{:S(2)}) collective-permute-start(bf16[8,5,192,384]{3,2,1,0:T(8,128)(2,1)} %get-tuple-element.30), channel_id=1, source_target_pairs={{0,2},{1,3},{2,0},{3,1},{4,6},{5,7},{6,4},{7,5},{8,10},{9,11},{10,... | collective-permute-start | bytes 17694728 | tf_op jit(solution)/shard_map/expert_grads/ppermute | solution.py:977
  1053.7 400.1 %reduce-scatter.18.cloned.1.call-start = ((), (), s32[]{:S(2)}) async-start(), calls=%async_computation.20 | async-start | bytes 2211840 | tf_op jit(solution)/shard_map/attention_back/reduce_scatter | solution.py:1026
  1202.6 147.2 %all-to-all-start.1 = ((bf16[40,192,384]{2,1,0:T(8,128)(2,1)}), bf16[40,192,384]{2,1,0:T(8,128)(2,1)}, u32[]{:S(2)}, u32[]{:S(2)}) async-start(bf16[40,192,384]{2,1,0:T(8,128)(2,1)} %bitcast.72), calls=%async_computation.8 | async-start | bytes 11796480 | tf_op jit(solution)/shard_map/expert_grads/all_to_all | solution.py:979
  1207.6 289.8 %all-gather.18.cloned.1.call-start = ((), (), s32[]{:S(2)}) async-start(), calls=%async_computation.14 | async-start | bytes 3932160 | tf_op jit(solution)/shard_map/expert_grads/all_gather | solution.py:986
  1219.9 293.8 %all-gather.22.cloned.1.call-start = ((), (), s32[]{:S(2)}) async-start(), calls=%async_computation.19 | async-start | bytes 3932160 | tf_op jit(solution)/shard_map/attention_back/all_gather | solution.py:1020
  (19 other events, 57.4 us)
Sparse Core Ops, SparseCore 0:
  24.6 134.0 all-gather.11
  179.3 19.3 all-gather.13
  201.5 43.9 all-gather.15
  250.4 36.7 reduce-scatter.7
  290.1 99.0 all-gather.25
  392.0 97.1 all-gather.23
  824.0 116.1 reduce-scatter.11
  945.4 27.6 all-gather.19
  1010.0 20.3 reduce-scatter.13
  1037.6 54.9 reduce-scatter.15
  1096.6 118.8 reduce-scatter.9
  1219.1 164.2 reduce-scatter.19
  1387.9 65.8 reduce-scatter.17
  1455.2 27.7 all-gather.17
  1485.0 28.7 all-gather.21

commit v2 on v1

--- a/solution.py
+++ b/solution.py
@@ -456,152 +456,546 @@
     return inner.astype(BF16), grad_gate.astype(BF16), grad_up.astype(BF16)
 
 
+MESH_ID = pl.DeviceIdType.MESH
+
+
 def expert_kernel(
-    tokens_ref,
-    cotangent_ref,
+    piece_hbm,
+    cotangent_hbm,
     shares_ref,
     own_hbm,
     other_hbm,
-    out_ref,
-    grad_tokens_ref,
+    out_hbm,
+    grad_piece_hbm,
     grad_own_hbm,
     grad_other_hbm,
+    tokens_hbm,
+    parts_hbm,
+    sibling_hbm,
+    across_hbm,
+    along_hbm,
     weights,
     grads,
+    tokens_buf,
+    cotangent_buf,
     inner_low,
     grad_low,
+    out_buf,
+    grad_buf,
+    terms,
+    sums,
     stage,
     load_sems,
     store_sems,
+    row_sems,
+    part_sems,
+    term_sems,
+    gather_recv,
+    gather_along,
+    gather_across,
+    gather_sibling,
+    sibling_send,
+    sibling_recv,
+    across_send,
+    across_recv,
+    along_send,
+    along_recv,
     *,
-    steps,
+    line,
     chunk,
 ):
-    step = pl.program_id(0)
     expert_count, model_width, all_units = weights.shape
     hidden_units = all_units // 3
     units = hidden_units // 2
-
-    @pl.when(step == 0)
-    def _():
-        copies = weight_copies(own_hbm, other_hbm, weights, load_sems)
-        for copy in copies:
+    steps = 2 * line
+    rows = piece_hbm.shape[0]
+    z, y, t = lax.axis_index(SHARD), lax.axis_index(CONTEXT), lax.axis_index(TENSOR)
+    sibling = (z, y, t + 1 - 2 * (t % 2))
+    partner = (z, 1 - y, t)
+
+    def inside(at):
+        return (at >= 0) & (at < line)
+
+    def block_of(at, column):
+        return at * 2 + column
+
+    def remote(source, target, send, recv, device):
+        return pltpu.make_async_remote_copy(
+            src_ref=source,
+            dst_ref=target,
+            send_sem=send,
+            recv_sem=recv,
+            device_id=device,
+            device_id_type=MESH_ID,
+        )
+
+    def gather_line(at, side):
+        here = block_of(at, y)
+        return remote(
+            tokens_hbm.at[here, 0],
+            tokens_hbm.at[here, 0],
+            gather_along.at[at, (side + 1) // 2],
+            gather_recv.at[here, 0],
+            (z + side, y, t),
+        )
+
+    def gather_pair(at, column):
+        here = block_of(at, column)
+        return remote(
+            tokens_hbm.at[here, 0],
+            tokens_hbm.at[here, 0],
+            gather_across.at[at],
+            gather_recv.at[here, 0],
+            partner,
+        )
+
+    def gather_cores(here):
+        return remote(
+            tokens_hbm.at[here, 0],
+            tokens_hbm.at[here, 1],
+            gather_sibling.at[here],
+            gather_recv.at[here, 1],
+            sibling,
+        )
+
+    def send_cores(here, slot):
+        return remote(
+            grad_buf.at[slot, pl.ds(rows, rows), :],
+            sibling_hbm.at[here],
+            sibling_send.at[here],
+            sibling_recv.at[here],
+            sibling,
+        )
+
+    def send_pair(at, slot):
+        return remote(
+            sums.at[slot], across_hbm.at[at], across_send.at[at], across_recv.at[at], partner
+        )
+
+    def send_line(at, side, distance):
+        last = (distance == 1) & (side == 1)
+        slot = jnp.where(last, line, at)
+        return remote(
+            sums.at[2 + (side + 1) // 2],
+            along_hbm.at[slot],
+            along_send.at[at],
+            along_recv.at[slot],
+            (z + side, y, t),
+        )
+
+    def near(rank):
+        half = z // 2
+        mirrored = z * (1 - half) + (line - 1 - z) * half
+        far = rank // 2
+        place = (1 - far) * (mirrored + rank - 2 * mirrored * rank) + far * rank
+        return place * (1 - half) + (line - 1 - place) * half
+
+    def step_block(step):
+        second = step // line
+        rank = step * (1 - second) + (steps - 1 - step) * second
+        return block_of(near(rank), y * (1 - second) + (1 - y) * second)
+
+    barrier = pltpu.get_barrier_semaphore()
+    for device in (sibling, partner):
+        pl.semaphore_signal(barrier, inc=1, device_id=device, device_id_type=MESH_ID)
+    for side in (-1, 1):
+
+        @pl.when(inside(z + side))
+        def _():
+            pl.semaphore_signal(
+                barrier, inc=1, device_id=(z + side, y, t), device_id_type=MESH_ID
+            )
+
+    below, above = (z + line - 1) // line, (2 * line - 2 - z) // line
+    pl.semaphore_wait(barrier, 2 + below + above)
+
+    own_block = block_of(z, y)
+    own_copy = pltpu.make_async_copy(piece_hbm, tokens_hbm.at[own_block, 0], row_sems.at[0, 0])
+    own_copy.start()
+    own_copy.wait()
+    for side in (-1, 1):
+
+        @pl.when(inside(z + side))
+        def _():
+            gather_line(z, side).start()
+
+    gather_pair(z, y).start()
+    gather_cores(own_block).start()
+    weight_loads = weight_copies(own_hbm, other_hbm, weights, load_sems)
+    for copy in weight_loads:
+        copy.start()
+    grads[...] = jnp.zeros_like(grads)
+
+    def row_copies(step, slot):
+        here = step_block(step)
+        return [
+            pltpu.make_async_copy(
+                tokens_hbm.at[here, 0],
+                tokens_buf.at[slot, pl.ds(0, rows), :],
+                row_sems.at[slot, 0],
+            ),
+            pltpu.make_async_copy(
+                tokens_hbm.at[here, 1],
+                tokens_buf.at[slot, pl.ds(rows, rows), :],
+                row_sems.at[slot, 1],
+            ),
+            pltpu.make_async_copy(
+                cotangent_hbm.at[here], cotangent_buf.at[slot], row_sems.at[slot, 2]
+            ),
+        ]
+
+    def load_rows(step, slot):
+        gather_cores(step_block(step)).wait_recv()
+        for copy in row_copies(step, slot):
             copy.start()
-        grads[...] = jnp.zeros_like(grads)
-        for copy in copies:
+
+    load_rows(0, 0)
+    for copy in weight_loads:
+        copy.wait()
+
+    def part_copies(step, slot):
+        here = step_block(step)
+        return [
+            pltpu.make_async_copy(
+                grad_buf.at[slot, pl.ds(0, rows), :], parts_hbm.at[here], part_sems.at[slot, 0]
+            ),
+            pltpu.make_async_copy(out_buf, out_hbm.at[here], part_sems.at[slot, 1]),
+        ]
+
+    def add_up(sources, slot):
+        copies = [
+            pltpu.make_async_copy(source, terms.at[i], term_sems.at[i])
+            for i, (source, _) in enumerate(sources)
+        ]
+        for copy, (_, there) in zip(copies, sources):
+            if there is None:
+                copy.start()
+            else:
+                pl.when(there)(copy.start)
+        for i, (copy, (_, there)) in enumerate(zip(copies, sources)):
+            if there is None:
+                copy.wait()
+            else:
+                pl.when(there)(copy.wait)
+
+                @pl.when(jnp.logical_not(there))
+                def _():
+                    terms[i] = jnp.zeros_like(terms[i])
+
+        tile = 16
+
+        @pl.loop(0, rows // tile)
+        def _(number):
+            here = pl.ds(pl.multiple_of(number * tile, tile), tile)
+            total = terms[0, here, :].astype(F32)
+            for i in range(1, len(sources)):
+                total += terms[i, here, :].astype(F32)
+            sums[slot, here, :] = total.astype(BF16)
+
+    def tick(number):
+        @pl.when(number < line - 1)
+        def _():
+            distance = number + 1
+            for side in (-1, 1):
+                at = z + side * distance
+
+                @pl.when(inside(at))
+                def _():
+                    gather_line(at, -side).wait_recv()
+
+                    @pl.when(inside(z - side))
+                    def _():
+                        gather_line(at, -side).start()
+
+                    gather_pair(at, y).start()
+                    gather_cores(block_of(at, y)).start()
+
+        def came_across(at):
+            gather_pair(at, 1 - y).wait_recv()
+            gather_cores(block_of(at, 1 - y)).start()
+
+        for distance in range(line):
+
+            @pl.when(number == min(distance + 1, line - 1))
+            def _():
+                if distance == 0:
+                    came_across(z)
+                else:
+                    for side in (-1, 1):
+                        at = z + side * distance
+                        pl.when(inside(at))(partial(came_across, at))
+
+        @pl.when((number > line) & (number <= steps))
+        def _():
+            rank = steps - number
+            at = near(rank)
+            here = block_of(at, 1 - y)
+            slot = number % 2
+
+            @pl.when(number > line + 2)
+            def _():
+                send_pair(near(rank + 2), slot).wait_send()
+
+            send_cores(here, 0).wait_recv()
+            add_up([(parts_hbm.at[here], None), (sibling_hbm.at[here], None)], slot)
+            send_pair(at, slot).start()
+
+        @pl.when((number > line + 1) & (number <= steps))
+        def _():
+            distance = steps + 1 - number
+            for side in (-1, 1):
+                at = z + side * distance
+                here = block_of(at, y)
+                slot = 2 + (side + 1) // 2
+
+                @pl.when(inside(at + side) & (number > line + 2))
+                def _():
+                    send_line(at + side, side, distance + 1).wait_send()
+
+                @pl.when(inside(at))
+                def _():
+                    send_cores(here, 0).wait_recv()
+                    send_pair(at, 0).wait_recv()
+                    farther = inside(z - side)
+
+                    @pl.when(farther)
+                    def _():
+                        send_line(at, side, distance + 1).wait_recv()
+
+                    add_up(
+                        [
+                            (parts_hbm.at[here], None),
+                            (sibling_hbm.at[here], None),
+                            (across_hbm.at[at], None),
+                            (along_hbm.at[at], farther),
+                        ],
+                        slot,
+                    )
+                    send_line(at, side, distance).start()
+
+    @pl.loop(0, steps)
+    def _(step):
+        slot = step % 2
+        for copy in row_copies(step, slot):
             copy.wait()
-
-    def run(expert, gate_up, grad_inner):
-        lane = lax.broadcasted_iota(jnp.int32, shares_ref.shape, 1)
-        share = jnp.sum(
-            jnp.where(lane == expert, shares_ref[...], 0.0), axis=1, keepdims=True
-        )
-        inner, grad_gate, grad_up = activate(gate_up, grad_inner, share)
-        inner_low[expert] = inner
-        grad_low[expert, :, :hidden_units] = grad_gate
-        grad_low[expert, :, hidden_units:] = grad_up
-
-    def weight_grads(expert):
-        grads[expert, :, : 2 * hidden_units] += lax.dot_general(
-            tokens_ref[...], grad_low[expert], FIRST_FIRST, preferred_element_type=F32
-        )
-        grads[expert, :, 2 * hidden_units :] += lax.dot_general(
-            cotangent_ref[...], inner_low[expert], FIRST_FIRST, preferred_element_type=F32
-        )
-
-    results = project(tokens_ref[...], cotangent_ref[...], weights[0])
-    for expert in range(expert_count):
-        run(expert, *results)
-        if expert + 1 < expert_count:
-            results = project(tokens_ref[...], cotangent_ref[...], weights[expert + 1])
-        weight_grads(expert)
-
-    @pl.loop(0, model_width // chunk)
+        here = step_block(step)
+        shares = shares_ref[here]
+        lane = lax.broadcasted_iota(jnp.int32, shares.shape, 1)
+
+        def run(expert, gate_up, grad_inner):
+            share = jnp.sum(jnp.where(lane == expert, shares, 0.0), axis=1, keepdims=True)
+            inner, grad_gate, grad_up = activate(gate_up, grad_inner, share)
+            inner_low[expert] = inner
+            grad_low[expert, :, :hidden_units] = grad_gate
+            grad_low[expert, :, hidden_units:] = grad_up
+
+        def weight_grads(expert):
+            grads[expert, :, : 2 * hidden_units] += lax.dot_general(
+                tokens_buf[slot], grad_low[expert], FIRST_FIRST, preferred_element_type=F32
+            )
+            grads[expert, :, 2 * hidden_units :] += lax.dot_general(
+                cotangent_buf[slot], inner_low[expert], FIRST_FIRST, preferred_element_type=F32
+            )
+
+        results = project(tokens_buf[slot], cotangent_buf[slot], weights[0])
+        for expert in range(expert_count):
+            run(expert, *results)
+            if expert + 1 < expert_count:
+                results = project(tokens_buf[slot], cotangent_buf[slot], weights[expert + 1])
+            weight_grads(expert)
+
+        @pl.when(step >= 1)
+        def _():
+            for copy in part_copies(step - 1, 1 - slot):
+                copy.wait()
+
+        tick(step)
+
+        @pl.when(step >= 2)
+        def _():
+            send_cores(step_block(step - 2), slot).wait_send()
+
+        @pl.loop(0, model_width // chunk)
+        def _(number):
+            @pl.when((number == 1) & (step + 1 < steps))
+            def _():
+                load_rows(step + 1, 1 - slot)
+
+            cols = pl.ds(pl.multiple_of(number * chunk, chunk), chunk)
+            total = jnp.zeros((2 * rows, chunk), F32)
+            for expert in range(expert_count):
+                total += lax.dot_general(
+                    inner_low[expert],
+                    weights[expert, cols, 2 * hidden_units :],
+                    LAST_LAST,
+                    preferred_element_type=F32,
+                )
+            out_buf[:, cols] = total.astype(BF16)
+            total = jnp.zeros((2 * rows, chunk), F32)
+            for expert in range(expert_count):
+                total += lax.dot_general(
+                    grad_low[expert],
+                    weights[expert, cols, : 2 * hidden_units],
+                    LAST_LAST,
+                    preferred_element_type=F32,
+                )
+            grad_buf[slot, :, cols] = total.astype(BF16)
+
+        for copy in part_copies(step, slot):
+            copy.start()
+        send_cores(here, slot).start()
+
+    for copy in part_copies(steps - 1, (steps - 1) % 2):
+        copy.wait()
+    for step in (steps - 2, steps - 1):
+        send_cores(step_block(step), step % 2).wait_send()
+
+    tick(steps)
+
+    sources = own_hbm.shape[0]
+    slice_rows = own_hbm.shape[2]
+
+    def grad_copy(expert, source, half, slot):
+        half_hbm = (grad_own_hbm, grad_other_hbm)[half]
+        return pltpu.make_async_copy(
+            stage.at[slot, half], half_hbm.at[source, expert], store_sems.at[slot, half]
+        )
+
+    @pl.loop(0, expert_count * sources)
     def _(number):
-        cols = pl.ds(pl.multiple_of(number * chunk, chunk), chunk)
-        total = jnp.zeros((tokens_ref.shape[0], chunk), F32)
-        for expert in range(expert_count):
-            total += lax.dot_general(
-                inner_low[expert],
-                weights[expert, cols, 2 * hidden_units :],
-                LAST_LAST,
-                preferred_element_type=F32,
-            )
-        out_ref[:, cols] = total.astype(BF16)
-        total = jnp.zeros((tokens_ref.shape[0], chunk), F32)
-        for expert in range(expert_count):
-            total += lax.dot_general(
-                grad_low[expert],
-                weights[expert, cols, : 2 * hidden_units],
-                LAST_LAST,
-                preferred_element_type=F32,
-            )
-        grad_tokens_ref[:, cols] = total.astype(BF16)
-
-    @pl.when(step == steps - 1)
-    def _():
-        sources, _, rows, lanes = own_hbm.shape
-
-        @pl.loop(0, expert_count)
-        def _(expert):
-            copies = []
-            for half, half_hbm in enumerate((grad_own_hbm, grad_other_hbm)):
-                for part in range(3):
-                    first = (2 * part + half) * units
-                    stage[half, :, part * units : (part + 1) * units] = grads[
-                        expert, :, first : first + units
-                    ].astype(BF16)
-                for source in range(sources):
-                    copy = pltpu.make_async_copy(
-                        stage.at[half, pl.ds(source * rows, rows), :],
-                        half_hbm.at[source, expert],
-                        store_sems.at[half, source],
-                    )
-                    copy.start()
-                    copies.append(copy)
-            for copy in copies:
-                copy.wait()
-
-
-def experts(tokens, cotangent, shares, own, other, block_rows=512, chunk=512):
-    token_count, model_width = tokens.shape
-    sources, expert_count, rows, lanes = own.shape
+        expert, source = number // sources, number % sources
+        slot = number % 2
+
+        @pl.when(number >= 2)
+        def _():
+            for half in range(2):
+                grad_copy(expert, source, half, slot).wait()
+
+        here = pl.ds(pl.multiple_of(source * slice_rows, slice_rows), slice_rows)
+        for half in range(2):
+            for part in range(3):
+                first = (2 * part + half) * units
+                stage[slot, half, :, part * units : (part + 1) * units] = grads[
+                    expert, here, first : first + units
+                ].astype(BF16)
+            grad_copy(expert, source, half, slot).start()
+
+    for slot in range(2):
+        for half in range(2):
+            grad_copy(0, 0, half, slot).wait()
+
+    send_cores(own_block, 0).wait_recv()
+    send_pair(z, 0).wait_recv()
+    for side in (-1, 1):
+
+        @pl.when(inside(z + side))
+        def _():
+            send_line(z, -side, 1).wait_recv()
+
+    send_pair(near(1), (steps - 1) % 2).wait_send()
+    send_pair(near(0), steps % 2).wait_send()
+    add_up(
+        [
+            (parts_hbm.at[own_block], None),
+            (sibling_hbm.at[own_block], None),
+            (across_hbm.at[z], None),
+            (along_hbm.at[z], inside(z + 1)),
+            (along_hbm.at[line], inside(z - 1)),
+        ],
+        0,
+    )
+    final = pltpu.make_async_copy(sums.at[0], grad_piece_hbm, row_sems.at[0, 0])
+    final.start()
+    final.wait()
+
+    for side in (-1, 1):
+
+        @pl.when(inside(z + side))
+        def _():
+            send_line(z + side, side, 1).wait_send()
+            gather_line(z, side).wait_send()
+
+        for distance in range(1, line):
+
+            @pl.when(inside(z - side * distance) & inside(z + side))
+            def _():
+                gather_line(z - side * distance, side).wait_send()
+
+    for at in range(line):
+        gather_pair(at, y).wait_send()
+    for here in range(steps):
+        gather_cores(here).wait_send()
+
+
+def experts(piece, cotangent, shares, own, other, line, chunk=512):
+    rows, model_width = piece.shape
+    sources, expert_count, slice_rows, lanes = own.shape
     hidden_units = 2 * lanes // 3
-    steps = token_count // block_rows
-    row_block = pl.BlockSpec((block_rows, model_width), lambda i: (i, 0))
+    blocks = 2 * line
     in_place = pl.BlockSpec(memory_space=pl.ANY)
-    flops = 2 * token_count * model_width * expert_count * hidden_units * 9
-    return pl.pallas_call(
-        partial(expert_kernel, steps=steps, chunk=chunk),
-        grid=(steps,),
+    flops = 2 * blocks * 2 * rows * model_width * expert_count * hidden_units * 9
+    dma = pltpu.SemaphoreType.DMA
+
+    def low(*shape):
+        return jax.ShapeDtypeStruct(shape, BF16)
+
+    results = pl.pallas_call(
+        partial(expert_kernel, line=line, chunk=chunk),
         in_specs=[
-            row_block,
-            row_block,
-            pl.BlockSpec((block_rows, shares.shape[1]), lambda i: (i, 0)),
+            in_place,
+            in_place,
+            pl.BlockSpec(memory_space=pltpu.VMEM),
             in_place,
             in_place,
         ],
-        out_specs=[row_block, row_block, in_place, in_place],
+        out_specs=[in_place] * 9,
         out_shape=[
-            jax.ShapeDtypeStruct(tokens.shape, BF16),
-            jax.ShapeDtypeStruct(tokens.shape, BF16),
-            jax.ShapeDtypeStruct(own.shape, BF16),
-            jax.ShapeDtypeStruct(own.shape, BF16),
+            low(blocks, 2 * rows, model_width),
+            low(rows, model_width),
+            low(*own.shape),
+            low(*own.shape),
+            low(blocks, 2, rows, model_width),
+            low(blocks, rows, model_width),
+            low(blocks, rows, model_width),
+            low(line, rows, model_width),
+            low(line + 1, rows, model_width),
         ],
         scratch_shapes=[
             pltpu.VMEM((expert_count, model_width, 3 * hidden_units), BF16),
             pltpu.VMEM((expert_count, model_width, 3 * hidden_units), F32),
-            pltpu.VMEM((expert_count, block_rows, hidden_units), BF16),
-            pltpu.VMEM((expert_count, block_rows, 2 * hidden_units), BF16),
-            pltpu.VMEM((2, model_width, lanes), BF16),
-            pltpu.SemaphoreType.DMA((sources, 2, 3)),
-            pltpu.SemaphoreType.DMA((2, sources)),
+            pltpu.VMEM((2, 2 * rows, model_width), BF16),
+            pltpu.VMEM((2, 2 * rows, model_width), BF16),
+            pltpu.VMEM((expert_count, 2 * rows, hidden_units), BF16),
+            pltpu.VMEM((expert_count, 2 * rows, 2 * hidden_units), BF16),
+            pltpu.VMEM((2 * rows, model_width), BF16),
+            pltpu.VMEM((2, 2 * rows, model_width), BF16),
+            pltpu.VMEM((5, rows, model_width), BF16),
+            pltpu.VMEM((4, rows, model_width), BF16),
+            pltpu.VMEM((2, 2, slice_rows, lanes), BF16),
+            dma((sources, 2, 3)),
+            dma((2, 2)),
+            dma((2, 3)),
+            dma((2, 2)),
+            dma((5,)),
+            dma((blocks, 2)),
+            dma((line, 2)),
+            dma((line,)),
+            dma((blocks,)),
+            dma((blocks,)),
+            dma((blocks,)),
+            dma((line,)),
+            dma((line,)),
+            dma((line,)),
+            dma((line + 1,)),
         ],
-        compiler_params=pltpu.CompilerParams(vmem_limit_bytes=63 * 2**20),
+        compiler_params=pltpu.CompilerParams(
+            vmem_limit_bytes=63 * 2**20, collective_id=1, has_side_effects=True
+        ),
         cost_estimate=pl.CostEstimate(
             flops=flops, bytes_accessed=80 * 2**20, transcendentals=0
         ),
-    )(tokens, cotangent, shares, own, other)
+    )(piece, cotangent, shares, own, other)
+    return results[:4]
 
 
 def attention_rows(values, kv_head, group_size):
@@ -955,10 +1349,14 @@
         normed_ffn, ffn_norm_back = jax.vjp(rms_scale, hidden, gain_ffn_float)
 
     with jax.named_scope("experts"):
-        tokens_all = gather_tokens(normed_ffn.astype(BF16))
         shape = (groups, own_experts, slice_rows, 3 * unit_count)
-        out_parts, grad_token_parts, grad_own, grad_other = experts(
-            tokens_all, cotangent_all, token_shares, owned.reshape(shape), others.reshape(shape)
+        out_parts, grad_second, grad_own, grad_other = experts(
+            normed_ffn.astype(BF16),
+            cotangent_all.reshape(groups, 2 * piece_rows, model_width),
+            token_shares.reshape(groups, 2 * piece_rows, 8),
+            owned.reshape(shape),
+            others.reshape(shape),
+            groups // 2,
         )
 
     def reduce_tokens(parts):
@@ -973,13 +1371,12 @@
         ).astype(F32)
 
     with jax.named_scope("expert_grads"):
-        grad_second = reduce_tokens(grad_token_parts)
         received = lax.ppermute(grad_other, TENSOR, across)
         total = (grad_own.astype(F32) + received.astype(F32)).astype(BF16)
         returned = lax.all_to_all(
             total.reshape(expert_count, slice_rows, 3 * unit_count), GROUP, 0, 0, tiled=True
         )
-        grad_hidden_norm, grad_gain_ffn_local = ffn_norm_back(grad_second)
+        grad_hidden_norm, grad_gain_ffn_local = ffn_norm_back(grad_second.astype(F32))
         grad_hidden = cotangent_piece.astype(F32) + grad_hidden_norm
         grad_hidden_low = lax.all_gather(grad_hidden.astype(BF16), TENSOR, axis=0, tiled=True)
         output_piece = (hidden + reduce_tokens(out_parts)).astype(BF16)

time: 1530 us -> 1330 us (0.87)
  waiting for transfers between devices: 1020 us -> 782 us
  Pallas kernels: 235 us -> 288 us
  other arithmetic: 89.7 us -> 73.8 us
    reduce_scatter x1, waiting for transfers between devices: 25.9 us -> 162 us  [expert_plan(): lax.psum_scatter(grad_out_local.astype(BF16), GROUP, scatter_dimension=0,...]
    all_to_all x1, waiting for transfers between devices: 129 us -> 0.01 us  [expert_plan(): lax.all_to_all(total.reshape(expert_count, slice_rows, 3 * unit_count), G...]
    reduce_scatter x2 -> x1, waiting for transfers between devices: 122 us -> 6.17 us  [reduce_tokens(): lax.psum_scatter(both.reshape(groups * piece_rows, model_width), GROUP, s...]
    all_gather x2 -> x1, waiting for transfers between devices: 197 us -> 95.6 us  [gather_tokens(): own_core = lax.all_gather(piece, GROUP, axis=0, tiled=False)]
    all_to_all x1, waiting for transfers between devices: 0.01 us -> 88.2 us  [expert_plan(): owned = lax.all_to_all(slices, GROUP, 0, 0, tiled=True)]
    all_gather x1, waiting for transfers between devices: 123 us -> 40.4 us  [expert_plan(): lax.all_gather(jnp.concatenate([query_weight, key_projection_weight, valu...]
    pallas_call x1, Pallas kernels: 184 us -> 237 us  [experts(): pl.pallas_call(partial(expert_kernel, line=line, chunk=chunk), in_specs=[...]
    all_gather x1, waiting for transfers between devices: 26.8 us -> 1.72 us  [expert_plan(): lax.all_gather(jnp.concatenate([out_weight.T, padded_column(gain_ffn)], a...]
  transfers between devices with their start and end apart: 24 -> 20, of which waited for: 18 -> 15; matrix products, arithmetic and copies ran while one was open for 8% -> 9% of each run, Pallas kernels for 1% -> 1%
where the time goes in v2:
time: 1330 us; the launch traced here: 1320 us
  waiting for transfers between devices  782 us (59%)
  Pallas kernels  288 us (22%)
  other arithmetic  73.8 us (6%)
  blocking collectives  70.8 us (5%)
  local copies, waits for them, and re-layouts  48 us (4%)
  matrix products  30.8 us (2%)
  between operations  14.8 us (1%)
  starting transfers between devices  14.6 us (1%)
    pallas_call x1, Pallas kernels, experts(): pl.pallas_call(partial(expert_kernel, line=line, chunk=chunk), in_specs=[...  237 us
    reduce_scatter x1, waiting for transfers between devices, expert_plan(): lax.psum_scatter(grad_out_local.astype(BF16), GROUP, scatter_dimension=0,...  162 us
    ppermute x1, waiting for transfers between devices, expert_plan(): received = lax.ppermute(grad_other, TENSOR, across)  134 us
    all_gather x1, waiting for transfers between devices, gather_tokens(): own_core = lax.all_gather(piece, GROUP, axis=0, tiled=False)  95.6 us
    all_to_all x1, waiting for transfers between devices, expert_plan(): owned = lax.all_to_all(slices, GROUP, 0, 0, tiled=True)  88.2 us
    ppermute x1, waiting for transfers between devices, expert_plan(): others = lax.ppermute(owned, TENSOR, across)  76.9 us
    reduce_scatter x1, waiting for transfers between devices, expert_plan(): lax.psum_scatter(grad_qkv_local.astype(BF16), GROUP, scatter_dimension=0,...  68.5 us
    all_gather x1, waiting for transfers between devices, expert_plan(): lax.all_gather(jnp.concatenate([query_weight, key_projection_weight, valu...  40.4 us
  transfers between devices with their start and end apart: 20, of which 15 were waited for; matrix products, arithmetic and copies ran while one was open for 9% of the time, Pallas kernels for 1%

profile of v2, /device:TPU:0, one launch (start us, length us, event | category | flops | bytes accessed | tf_op | source)
XLA Modules:
  0.0 1323.1 jit_solution(16194538557684586272)
XLA Ops:
  11.4 3.7 multiply_cosine_fusion
  17.7 1.8 copy.105
  21.2 3.1 copy.103
  25.0 40.4 %all-gather.10.cloned.1.call-done = bf16[1536,768]{1,0:T(8,128)(2,1)} async-done(((bf16[192,768]{1,0:T(8,128)(2,1)}), bf16[1536,768]{1,0:T(8,128)(2,1)}) %all-gather.10.cloned.1.call-update) | async-done | bytes 2359312 | tf_op jit(solution)/shard_map/weights/all_gather | solution.py:1257
  65.4 2.7 slice.100
  68.1 2.6 copy.116
  73.4 2.6 copy.100
  78.3 5.9 fusion.4
  87.4 2.1 constant_dynamic-slice_fusion.4
  89.5 5.7 pad_maximum_fusion.1
  95.2 4.7 all-to-all-start
  100.3 39.1 %all-gather.12.cloned.1.call-done.key_value_ref = bf16[2048,256]{1,0:T(8,128)(2,1)} async-done(((bf16[1024,256]{1,0:T(8,128)(2,1)}), bf16[2048,256]{1,0:T(8,128)(2,1)}) %all-gather.12.cloned.1.call-update) | async-done | bytes 1048592 | tf_op jit(solution)/shard_map/attention/all_gather | solution.py:1312
  140.7 18.7 %attention.1 = (bf16[1024,384]{1,0:T(8,128)(2,1)S(1)}, f32[4,2,768,1]{3,2,1,0:T(8,128)}) custom-call(s32[1]{0:T(128)} %bitcast.1.first_ref, bf16[1024,384]{1,0:T(8,128)(2,1)S(1)} %slice.105.query_ref, bf16[2048,256]{1,0:T(8,128)(2,1)S(1)} %copy-done.6, s32[1024,1]{1,0:T(8,128)S(1)} %copy.106.doc_start_ref), custom_call_target="tpu_custom_call" | custom-call | flops 16106127360 | bytes 4194304 | tf_op jit(solution)/shard_map/attention/pallas_call | solution.py:1145
  159.4 88.2 %all-to-all-done = bf16[40,192,384]{2,1,0:T(8,128)(2,1)} async-done(((bf16[40,192,384]{2,1,0:T(8,128)(2,1)}), bf16[40,192,384]{2,1,0:T(8,128)(2,1)}, u32[]{:S(2)}, u32[]{:S(2)}) %all-to-all-start) | async-done | bytes 5898272 | tf_op jit(solution)/shard_map/weights/all_to_all | solution.py:1277
  247.7 1.7 all-gather.14.cloned.1.call-done
  249.4 4.8 convolution_convert_fusion.1
  254.2 95.6 %all-gather.22.cloned.1.call-done = bf16[2048,1536]{1,0:T(8,128)(2,1)} async-done(((bf16[256,1536]{1,0:T(8,128)(2,1)}), bf16[2048,1536]{1,0:T(8,128)(2,1)}) %all-gather.22.cloned.1.call-update) | async-done | bytes 6291472 | tf_op jit(solution)/shard_map/routing/all_gather | solution.py:1288
  352.0 30.9 %all-gather.1 = f32[2048,40]{0,1:T(8,128)S(1)} all-gather(f32[256,40]{0,1:T(8,128)S(1)} %select_reduce_fusion), channel_id=3, replica_groups=mesh['shard'=4,'context'=2,'tensor'=4] {'shard','context'}, dimensions={0}, use_global_device_ids=true | all-gather | bytes 368640 | tf_op jit(solution)/shard_map/routing/all_gather | solution.py:1288
  385.9 2.0 copy.121
  387.8 3.2 pad.13.clone
  392.3 14.0 %reduce-scatter.7.cloned.1.call-done = bf16[256,1536]{1,0:T(8,128)(2,1)} async-done(((bf16[1024,1536]{1,0:T(8,128)(2,1)}), bf16[256,1536]{1,0:T(8,128)(2,1)}) %reduce-scatter.7.cloned.1.call-update) | async-done | bytes 786448 | tf_op jit(solution)/shard_map/attention_out/reduce_scatter | solution.py:1345
  409.0 10.6 pad_maximum_fusion
  419.6 76.9 %collective-permute-done.2 = bf16[40,192,384]{2,1,0:T(8,128)(2,1)} collective-permute-done((bf16[40,192,384]{2,1,0:T(8,128)(2,1)}, bf16[40,192,384]{2,1,0:T(8,128)(2,1)}, u32[]{:S(2)}, u32[]{:S(2)}) %collective-permute-start.2) | collective-permute-done | bytes 5898272 | tf_op jit(solution)/shard_map/routing/ppermute | solution.py:1325
  496.5 237.1 %experts.1 = (bf16[8,512,1536]{2,1,0:T(8,128)(2,1)}, bf16[256,1536]{1,0:T(8,128)(2,1)}, bf16[8,5,192,384]{3,2,1,0:T(8,128)(2,1)}, bf16[8,5,192,384]{3,2,1,0:T(8,...) custom-call(bf16[256,1536]{1,0:T(8,128)(2,1)} %multiply_convert_fusi, ...), custom_call_target="tpu_custom_call" | custom-call | flops 144955146240 | bytes 83886080 | tf_op jit(solution)/shard_map/experts/pallas_call | solution.py:942
  733.6 2.3 fusion.14
  736.0 3.0 fusion.35
  739.1 31.9 %all-gather.18.cloned.1.call-done = bf16[1024,1536]{1,0:T(8,128)(2,1)} async-done(((bf16[256,1536]{1,0:T(8,128)(2,1)}), bf16[1024,1536]{1,0:T(8,128)(2,1)}) %all-gather.18.cloned.1.call-update) | async-done | bytes 3145744 | tf_op jit(solution)/shard_map/expert_grads/all_gather | solution.py:1381
  771.0 4.1 convolution_convert_fusion.4.grad_ref
  775.1 32.6 %attention_back.1 = (bf16[1024,384]{1,0:T(8,128)(2,1)S(1)}, bf16[2048,256]{1,0:T(8,128)(2,1)}) custom-call(s32[1]{0:T(128)} %bitcast.1.first_ref, bf16[1024,384]{1,0:T(8,128)(2,1)S(1)} %copy-done.3, bf16[2048,256]{1,0:T(8,128)(2,1)S(1)} %copy-done.7, s32[1024,1]{1,0:T(8,128)S(1)} %copy-done.5, f32[4,2,768,1]{3,2,1,0:T(8,128)} %get-tuple-element.26.lse_ref, ...), custom_call_target="tpu_custom_call" | custom-call | flops 40265318400 | bytes 8388608 | tf_op jit(solution)/shard_map/attention_back/pallas_call | solution.py:1174
  808.2 5.8 slice_bitcast_fusion
  815.2 13.0 reduce-scatter.11.cloned.1.call-done
  828.2 1.9 constant_dynamic-update-slice_fusion
  830.1 5.3 convolution_convert_fusion
  835.5 9.5 fusion
  846.6 4.7 convolution_convert_fusion.3
  851.5 6.0 convolution_convert_fusion.2
  857.5 133.6 %collective-permute-done.4 = bf16[8,5,192,384]{3,2,1,0:T(8,128)(2,1)} collective-permute-done((bf16[8,5,192,384]{3,2,1,0:T(8,128)(2,1)}, bf16[8,5,192,384]{3,2,1,0:T(8,128)(2,1)}, u32[]{:S(2)}, u32[]{:S(2)}) %collective-permute-start.4) | collective-permute-done | bytes 5898272 | tf_op jit(solution)/shard_map/expert_grads/ppermute | solution.py:1374
  991.1 9.2 add_convert_fusion
  1000.3 5.0 all-to-all-start.1
  1005.6 1.8 fusion.15
  1007.4 6.2 reduce-scatter.9.cloned.1.call-done
  1013.6 4.4 fusion.18
  1018.8 161.8 %reduce-scatter.17.cloned.1.call-done = bf16[192,384]{1,0:T(8,128)(2,1)} async-done(((bf16[1536,384]{1,0:T(8,128)(2,1)}), bf16[192,384]{1,0:T(8,128)(2,1)}) %reduce-scatter.17.cloned.1.call-update) | async-done | bytes 147472 | tf_op jit(solution)/shard_map/attention_back/reduce_scatter | solution.py:1389
  1182.2 68.5 %reduce-scatter.15.cloned.1.call-done = bf16[192,640]{1,0:T(8,128)(2,1)} async-done(((bf16[1536,640]{1,0:T(8,128)(2,1)}), bf16[192,640]{1,0:T(8,128)(2,1)}) %reduce-scatter.15.cloned.1.call-update) | async-done | bytes 245776 | tf_op jit(solution)/shard_map/attention_back/reduce_scatter | solution.py:1423
  1253.9 39.9 %psum.7 = f32[2,1536]{1,0:T(2,128)S(1)} all-reduce(f32[2,1536]{1,0:T(2,128)S(1)} %pad_maximum_fusion.6), channel_id=1, replica_groups=mesh['shard'=4,'context'=2,'tensor'=4] {'shard','context','tensor'}, use_global_device_ids=true, to_apply=%region_14.15 | all-reduce | flops 3072 | bytes 24576 | tf_op jit(solution)/shard_map/attention_back/psum | solution.py:1426
  1294.5 7.7 convert_bitcast_fusion
  1302.2 8.6 all-gather.20.cloned.1.call-done
  1310.8 3.9 copy.131
  (166 shorter events, 39.6 us)
Async XLA Ops:
  7.2 344.1 %copy-start = (f32[1024,8]{0,1:T(8,128)S(1)}, f32[1024,8]{0,1:T(8,128)}, u32[]{:S(2)}) copy-start(f32[1024,8]{0,1:T(8,128)} %param.26) | copy-start | bytes 98308
  7.2 58.3 %all-gather.10.cloned.1.call-start = ((), (), s32[]{:S(2)}) async-start(), calls=%async_computation.8 | async-start | bytes 2654208 | tf_op jit(solution)/shard_map/weights/all_gather | solution.py:1257
  9.7 129.8 %all-gather.12.cloned.1.call-start = ((), (), s32[]{:S(2)}) async-start(), calls=%async_computation.9 | async-start | bytes 1572864 | tf_op jit(solution)/shard_map/attention/all_gather | solution.py:1312
  21.2 3.1 copy-start.10
  25.0 52.8 %copy-start.34 = (f32[1024]{0:T(1024)}, f32[1024]{0:T(1024)S(1)}, u32[]{:S(2)}) copy-start(f32[1024]{0:T(1024)S(1)} %add_rsqrt_fusion) | copy-start | bytes 12292
  78.3 5.9 copy-start.28
  78.3 5.9 copy-start.15
  78.3 5.9 copy-start.16
  85.1 4.4 copy-start.23
  86.0 163.4 %all-gather.14.cloned.1.call-start = ((), (), s32[]{:S(2)}) async-start(), calls=%async_computation.10 | async-start | bytes 1769472 | tf_op jit(solution)/shard_map/weights/all_gather | solution.py:1278
  87.3 262.4 %all-gather.22.cloned.1.call-start = ((), (), s32[]{:S(2)}) async-start(), calls=%async_computation.20 | async-start | bytes 7077888 | tf_op jit(solution)/shard_map/routing/all_gather | solution.py:1288
  95.2 152.5 %all-to-all-start = ((bf16[40,192,384]{2,1,0:T(8,128)(2,1)}), bf16[40,192,384]{2,1,0:T(8,128)(2,1)}, u32[]{:S(2)}, u32[]{:S(2)}) async-start(bf16[40,192,384]{2,1,0:T(8,128)(2,1)} %pad_maximum_fusion.1), calls=%async_computation | async-start | bytes 11796480 | tf_op jit(solution)/shard_map/weights/all_to_all | solution.py:1277
  99.9 306.3 %reduce-scatter.7.cloned.1.call-start = ((), (), s32[]{:S(2)}) async-start(), calls=%async_computation.11 | async-start | bytes 3932160 | tf_op jit(solution)/shard_map/attention_out/reduce_scatter | solution.py:1345
  100.2 59.2 %copy-start.4 = (s32[1024,1]{1,0:T(8,128)}, s32[1024,1]{1,0:T(8,128)S(1)}, u32[]{:S(2)}) copy-start(s32[1024,1]{1,0:T(8,128)S(1)} %copy.106.doc_start_ref) | copy-start | bytes 12292
  100.3 59.1 %copy-start.2 = (bf16[1024,384]{1,0:T(8,128)(2,1)}, bf16[1024,384]{1,0:T(8,128)(2,1)S(1)}, u32[]{:S(2)}) copy-start(bf16[1024,384]{1,0:T(8,128)(2,1)S(1)} %slice.105.query_ref) | copy-start | bytes 2359300
  159.4 94.7 %copy-start.8 = (bf16[1024,384]{1,0:T(8,128)(2,1)}, bf16[1024,384]{1,0:T(8,128)(2,1)S(1)}, u32[]{:S(2)}) copy-start(bf16[1024,384]{1,0:T(8,128)(2,1)S(1)} %get-tuple-element.22) | copy-start | bytes 2359300
  254.2 516.8 %all-gather.18.cloned.1.call-start = ((), (), s32[]{:S(2)}) async-start(), calls=%async_computation.14 | async-start | bytes 3932160 | tf_op jit(solution)/shard_map/expert_grads/all_gather | solution.py:1381
  349.8 59.2 %collective-permute-start = (bf16[8,256,1536]{2,1,0:T(8,128)(2,1)}, bf16[8,256,1536]{2,1,0:T(8,128)(2,1)}, u32[]{:S(2)}, u32[]{:S(2)}) collective-permute-start(bf16[8,256,1536]{2,1,0:T(8,128)(2,1)} %bitcast.66), channel_id=1, source_target_pairs={{0,1},{1,0},{2,3},{3,2},{4,5},{5,4},{6,7},{7,6},{8,9},{9,8},{10,11... | collective-permute-start | bytes 18874376 | tf_op jit(solution)/shard_map/routing/ppermute | solution.py:1289
  349.8 146.7 %collective-permute-start.2 = (bf16[40,192,384]{2,1,0:T(8,128)(2,1)}, bf16[40,192,384]{2,1,0:T(8,128)(2,1)}, u32[]{:S(2)}, u32[]{:S(2)}) collective-permute-start(bf16[40,192,384]{2,1,0:T(8,128)(2,1)} %all-to-all-done), channel_id=1, source_target_pairs={{0,2},{1,3},{2,0},{3,1},{4,6},{5,7},{6,4},{7,5},{8,10},{9,11},{10,... | collective-permute-start | bytes 17694728 | tf_op jit(solution)/shard_map/routing/ppermute | solution.py:1325
  382.9 1.7 collective-permute-start.1
  387.8 18.4 %copy-start.11 = (bf16[1024,1536]{1,0:T(8,128)(2,1)S(1)}, bf16[1024,1536]{1,0:T(8,128)(2,1)}, u32[]{:S(2)}) copy-start(bf16[1024,1536]{1,0:T(8,128)(2,1)} %param.14) | copy-start | bytes 9437188
  392.2 27.3 %copy-start.25 = (f32[1536]{0:T(1024)}, f32[1536]{0:T(1024)S(1)}, u32[]{:S(2)}) copy-start(f32[1536]{0:T(1024)S(1)} %convert_reduce_fusion) | copy-start | bytes 18436
  407.8 11.8 copy-start.32
  407.8 11.8 copy-start.30
  496.4 237.1 %copy-start.14 = (bf16[256,1536]{1,0:T(8,128)(2,1)S(1)}, bf16[256,1536]{1,0:T(8,128)(2,1)}, u32[]{:S(2)}) copy-start(bf16[256,1536]{1,0:T(8,128)(2,1)} %reduce-scatter.7.cloned.1.call-done) | copy-start | bytes 2359300
  496.4 237.1 %copy-start.26 = (f32[1536]{0:T(1024)S(1)}, f32[1536]{0:T(1024)}, u32[]{:S(2)}) copy-start(f32[1536]{0:T(1024)} %copy-done.25) | copy-start | bytes 18436
  496.5 237.2 %copy-start.31 = (f32[256]{0:T(256)S(1)}, f32[256]{0:T(256)}, u32[]{:S(2)}) copy-start(f32[256]{0:T(256)} %copy-done.30) | copy-start | bytes 3076
  736.0 3.0 copy-start.21
  739.0 89.3 %reduce-scatter.11.cloned.1.call-start = ((), (), s32[]{:S(2)}) async-start(), calls=%async_computation.15 | async-start | bytes 1572864 | tf_op jit(solution)/shard_map/attention_back/reduce_scatter | solution.py:1403
  739.1 36.0 %copy-start.3 = (bf16[1024,384]{1,0:T(8,128)(2,1)S(1)}, bf16[1024,384]{1,0:T(8,128)(2,1)}, u32[]{:S(2)}) copy-start(bf16[1024,384]{1,0:T(8,128)(2,1)} %copy-done.2) | copy-start | bytes 2359300
  739.1 36.0 %copy-start.5 = (s32[1024,1]{1,0:T(8,128)S(1)}, s32[1024,1]{1,0:T(8,128)}, u32[]{:S(2)}) copy-start(s32[1024,1]{1,0:T(8,128)} %copy-done.4) | copy-start | bytes 12292
  771.0 4.1 copy-start.7
  807.7 197.8 %reduce-scatter.13.cloned.1.call-start = ((), (), s32[]{:S(2)}) async-start(), calls=%async_computation.16 | async-start | bytes 3932160 | tf_op jit(solution)/shard_map/attention_back/reduce_scatter | solution.py:1410
  814.0 16.1 %copy-start.19 = (bf16[1536,768]{1,0:T(8,128)(2,1)S(1)}, bf16[1536,768]{1,0:T(8,128)(2,1)}, u32[]{:S(2)}) copy-start(bf16[1536,768]{1,0:T(8,128)(2,1)} %all-gather.10.cloned.1.call-done) | copy-start | bytes 7077892
  814.0 21.5 %collective-permute-start.3 = (bf16[8,256,1536]{2,1,0:T(8,128)(2,1)}, bf16[8,256,1536]{2,1,0:T(8,128)(2,1)}, u32[]{:S(2)}, u32[]{:S(2)}) collective-permute-start(bf16[8,256,1536]{2,1,0:T(8,128)(2,1)} %slice_bitcast_fusion), channel_id=1, source_target_pairs={{0,1},{1,0},{2,3},{3,2},{4,5},{5,4},{6,7},{7,6},{8,9},{9,8},{10,11... | collective-permute-start | bytes 18874376 | tf_op jit(solution)/shard_map/expert_grads/ppermute | solution.py:1364
  835.4 178.2 %reduce-scatter.9.cloned.1.call-start = ((), (), s32[]{:S(2)}) async-start(), calls=%async_computation.12 | async-start | bytes 7077888 | tf_op jit(solution)/shard_map/expert_grads/reduce_scatter | solution.py:1366
  845.0 335.6 %reduce-scatter.17.cloned.1.call-start = ((), (), s32[]{:S(2)}) async-start(), calls=%async_computation.19 | async-start | bytes 1327104 | tf_op jit(solution)/shard_map/attention_back/reduce_scatter | solution.py:1389
  845.1 6.4 copy-start.24
  845.1 6.4 copy-start.29
  845.1 6.4 copy-start.35
  845.1 146.0 %collective-permute-start.4 = (bf16[8,5,192,384]{3,2,1,0:T(8,128)(2,1)}, bf16[8,5,192,384]{3,2,1,0:T(8,128)(2,1)}, u32[]{:S(2)}, u32[]{:S(2)}) collective-permute-start(bf16[8,5,192,384]{3,2,1,0:T(8,128)(2,1)} %get-tuple-element.30), channel_id=1, source_target_pairs={{0,2},{1,3},{2,0},{3,1},{4,6},{5,7},{6,4},{7,5},{8,10},{9,11},{10,... | collective-permute-start | bytes 17694728 | tf_op jit(solution)/shard_map/expert_grads/ppermute | solution.py:1374
  851.4 399.4 %reduce-scatter.15.cloned.1.call-start = ((), (), s32[]{:S(2)}) async-start(), calls=%async_computation.18 | async-start | bytes 2211840 | tf_op jit(solution)/shard_map/attention_back/reduce_scatter | solution.py:1423
  1000.3 5.3 copy-start.12
  1000.3 294.2 %all-to-all-start.1 = ((bf16[40,192,384]{2,1,0:T(8,128)(2,1)}), bf16[40,192,384]{2,1,0:T(8,128)(2,1)}, u32[]{:S(2)}, u32[]{:S(2)}) async-start(bf16[40,192,384]{2,1,0:T(8,128)(2,1)} %bitcast.58), calls=%async_computation.7 | async-start | bytes 11796480 | tf_op jit(solution)/shard_map/expert_grads/all_to_all | solution.py:1376
  1005.3 296.9 %all-gather.16.cloned.1.call-start = ((), (), s32[]{:S(2)}) async-start(), calls=%async_computation.13 | async-start | bytes 3932160 | tf_op jit(solution)/shard_map/expert_grads/all_gather | solution.py:1383
  1018.0 292.8 %all-gather.20.cloned.1.call-start = ((), (), s32[]{:S(2)}) async-start(), calls=%async_computation.17 | async-start | bytes 3932160 | tf_op jit(solution)/shard_map/attention_back/all_gather | solution.py:1417
  1310.8 3.9 copy-start.22
  1310.8 5.6 copy-start.1
  (10 other events, 17.1 us)
Sparse Core Ops, SparseCore 0:
  10.8 54.6 all-gather.9
  86.1 53.3 all-gather.11
  142.3 107.0 all-gather.13
  252.0 97.7 all-gather.21
  352.7 53.4 reduce-scatter.6
  739.1 31.8 all-gather.17
  807.9 20.3 reduce-scatter.10
  835.5 54.9 reduce-scatter.12
  894.5 119.0 reduce-scatter.8
  1017.8 162.7 reduce-scatter.16
  1185.1 65.6 reduce-scatter.14
  1252.1 27.8 all-gather.15
  1282.2 28.6 all-gather.19

commit v3 on v1

--- a/solution.py
+++ b/solution.py
@@ -456,152 +456,644 @@
     return inner.astype(BF16), grad_gate.astype(BF16), grad_up.astype(BF16)
 
 
-def expert_kernel(
-    tokens_ref,
-    cotangent_ref,
-    shares_ref,
-    own_hbm,
-    other_hbm,
-    out_ref,
-    grad_tokens_ref,
-    grad_own_hbm,
-    grad_other_hbm,
-    weights,
-    grads,
-    inner_low,
-    grad_low,
-    stage,
-    load_sems,
-    store_sems,
-    *,
-    steps,
-    chunk,
-):
-    step = pl.program_id(0)
+MESH_ID = pl.DeviceIdType.MESH
+
+
+class Place:
+    def __init__(self, line):
+        self.line = line
+        self.z, self.y = lax.axis_index(SHARD), lax.axis_index(CONTEXT)
+        self.t = lax.axis_index(TENSOR)
+        self.sibling = (self.z, self.y, self.t + 1 - 2 * (self.t % 2))
+        self.partner = (self.z, 1 - self.y, self.t)
+        self.across = (self.z, self.y, (self.t + 2) % 4)
+
+    def beside(self, side):
+        return (self.z + side, self.y, self.t)
+
+    def inside(self, at):
+        return (at >= 0) & (at < self.line)
+
+    def near(self, rank):
+        z, line = self.z, self.line
+        half = z // 2
+        mirrored = z * (1 - half) + (line - 1 - z) * half
+        far = rank // 2
+        place = (1 - far) * (mirrored + rank - 2 * mirrored * rank) + far * rank
+        return place * (1 - half) + (line - 1 - place) * half
+
+    def block(self, order, step):
+        rank, across = order[0]
+        for number, (later_rank, later_across) in enumerate(order[1:], 1):
+            rank = jnp.where(step == number, later_rank, rank)
+            across = jnp.where(step == number, later_across, across)
+        column = self.y + across - 2 * self.y * across
+        return self.near(rank) * 2 + column
+
+    def meet(self):
+        z, line = self.z, self.line
+        barrier = pltpu.get_barrier_semaphore()
+        for device in (self.sibling, self.partner, self.across):
+            pl.semaphore_signal(barrier, inc=1, device_id=device, device_id_type=MESH_ID)
+        for side in (-1, 1):
+
+            @pl.when(self.inside(z + side))
+            def _():
+                pl.semaphore_signal(
+                    barrier, inc=1, device_id=self.beside(side), device_id_type=MESH_ID
+                )
+
+        below, above = (z + line - 1) // line, (2 * line - 2 - z) // line
+        pl.semaphore_wait(barrier, 3 + below + above)
+
+
+def remote(source, target, send, recv, device):
+    return pltpu.make_async_remote_copy(
+        src_ref=source,
+        dst_ref=target,
+        send_sem=send,
+        recv_sem=recv,
+        device_id=device,
+        device_id_type=MESH_ID,
+    )
+
+
+class Gather:
+    order = ((0, 0), (1, 0), (0, 1), (2, 0), (1, 1), (3, 0), (2, 1), (3, 1))
+    rounds = (0, 2, 4)
+    crossings = (1, 3, 5, 6)
+
+    def __init__(self, place, tokens, sems):
+        self.place, self.tokens = place, tokens
+        self.recv, self.along, self.across, self.cores = sems
+
+    def line_copy(self, at, side):
+        here, tokens = at * 2 + self.place.y, self.tokens
+        return remote(
+            tokens.at[here, 0],
+            tokens.at[here, 0],
+            self.along.at[at, (side + 1) // 2],
+            self.recv.at[here, 0],
+            self.place.beside(side),
+        )
+
+    def pair_copy(self, at, column):
+        here, tokens = at * 2 + column, self.tokens
+        return remote(
+            tokens.at[here, 0],
+            tokens.at[here, 0],
+            self.across.at[at],
+            self.recv.at[here, 0],
+            self.place.partner,
+        )
+
+    def core_copy(self, here):
+        tokens = self.tokens
+        return remote(
+            tokens.at[here, 0],
+            tokens.at[here, 1],
+            self.cores.at[here],
+            self.recv.at[here, 1],
+            self.place.sibling,
+        )
+
+    def start(self):
+        place = self.place
+        for side in (-1, 1):
+            pl.when(place.inside(place.z + side))(lambda: self.line_copy(place.z, side).start())
+        self.pair_copy(place.z, place.y).start()
+        self.core_copy(place.z * 2 + place.y).start()
+
+    def came_along(self, at, side):
+        place = self.place
+        self.line_copy(at, -side).wait_recv()
+        pl.when(place.inside(place.z - side))(lambda: self.line_copy(at, -side).start())
+        self.pair_copy(at, place.y).start()
+        self.core_copy(at * 2 + place.y).start()
+
+    def came_across(self, at):
+        column = 1 - self.place.y
+        self.pair_copy(at, column).wait_recv()
+        self.core_copy(at * 2 + column).start()
+
+    def tick(self, number):
+        place = self.place
+        for distance, when in enumerate(self.rounds, 1):
+
+            @pl.when(number == when)
+            def _():
+                for side in (-1, 1):
+                    at = place.z + side * distance
+                    pl.when(place.inside(at))(partial(self.came_along, at, side))
+
+        for distance, when in enumerate(self.crossings):
+
+            @pl.when(number == when)
+            def _():
+                for side in (-1, 1) if distance else (1,):
+                    at = place.z + side * distance
+                    pl.when(place.inside(at))(partial(self.came_across, at))
+
+    def finish(self):
+        place = self.place
+        for side in (-1, 1):
+            for distance in range(place.line):
+                at = place.z - side * distance
+
+                @pl.when(place.inside(at) & place.inside(place.z + side))
+                def _():
+                    self.line_copy(at, side).wait_send()
+
+        for at in range(place.line):
+            self.pair_copy(at, place.y).wait_send()
+        for here in range(2 * place.line):
+            self.core_copy(here).wait_send()
+
+
+class Reduce:
+    order = ((3, 1), (3, 0), (2, 1), (2, 0), (1, 1), (1, 0), (0, 1), (0, 0))
+
+    def __init__(self, place, arrays, terms, sums, sems):
+        self.place, self.terms, self.sums = place, terms, sums
+        self.parts, self.from_core, self.from_pair, self.from_line = arrays
+        (
+            self.term_sems,
+            self.core_send,
+            self.core_recv,
+            self.pair_send,
+            self.pair_recv,
+            self.line_send,
+            self.line_recv,
+        ) = sems
+
+    def core_copy(self, here, source):
+        return remote(
+            source,
+            self.from_core.at[here],
+            self.core_send.at[here],
+            self.core_recv.at[here],
+            self.place.sibling,
+        )
+
+    def core_arrived(self, here):
+        self.core_copy(here, self.from_core.at[here]).wait_recv()
+
+    def pair_copy(self, at, slot):
+        return remote(
+            self.sums.at[slot],
+            self.from_pair.at[at],
+            self.pair_send.at[at],
+            self.pair_recv.at[at],
+            self.place.partner,
+        )
+
+    def line_copy(self, at, side, distance):
+        slot = self.place.line if distance == 1 and side == 1 else at
+        return remote(
+            self.sums.at[2 + (side + 1) // 2],
+            self.from_line.at[slot],
+            self.line_send.at[at],
+            self.line_recv.at[slot],
+            self.place.beside(side),
+        )
+
+    def add_up(self, sources, slot):
+        terms = self.terms
+        copies = [
+            pltpu.make_async_copy(source, terms.at[i], self.term_sems.at[i])
+            for i, (source, _) in enumerate(sources)
+        ]
+        for copy, (_, there) in zip(copies, sources):
+            if there is None:
+                copy.start()
+            else:
+                pl.when(there)(copy.start)
+        for i, (copy, (_, there)) in enumerate(zip(copies, sources)):
+            if there is None:
+                copy.wait()
+            else:
+                pl.when(there)(copy.wait)
+
+                @pl.when(jnp.logical_not(there))
+                def _():
+                    terms[i] = jnp.zeros_like(terms[i])
+
+        tile = 16
+
+        @pl.loop(0, terms.shape[1] // tile)
+        def _(number):
+            here = pl.ds(pl.multiple_of(number * tile, tile), tile)
+            total = terms[0, here, :].astype(F32)
+            for i in range(1, len(sources)):
+                total += terms[i, here, :].astype(F32)
+            self.sums[slot, here, :] = total.astype(BF16)
+
+    def cross(self, rank):
+        place = self.place
+        at = place.near(rank)
+        here = at * 2 + 1 - place.y
+        slot = rank % 2
+        if rank + 2 < place.line:
+            self.pair_copy(place.near(rank + 2), slot).wait_send()
+        self.core_arrived(here)
+        self.add_up([(self.parts.at[here], None), (self.from_core.at[here], None)], slot)
+        self.pair_copy(at, slot).start()
+
+    def advance(self, distance):
+        place = self.place
+        for side in (-1, 1):
+            at = place.z + side * distance
+            here = at * 2 + place.y
+            farther = place.inside(place.z - side)
+            if distance + 1 < place.line:
+
+                @pl.when(place.inside(at + side))
+                def _():
+                    self.line_copy(at + side, side, distance + 1).wait_send()
+
+            @pl.when(place.inside(at))
+            def _():
+                self.core_arrived(here)
+                self.pair_copy(at, 0).wait_recv()
+                sources = [
+                    (self.parts.at[here], None),
+                    (self.from_core.at[here], None),
+                    (self.from_pair.at[at], None),
+                ]
+                if distance + 1 < place.line:
+
+                    @pl.when(farther)
+                    def _():
+                        self.line_copy(at, side, distance + 1).wait_recv()
+
+                    sources.append((self.from_line.at[at], farther))
+                self.add_up(sources, 2 + (side + 1) // 2)
+                self.line_copy(at, side, distance).start()
+
+    def tick(self, number):
+        line = self.place.line
+        for rank in range(line):
+
+            @pl.when(number == 2 * (line - rank) - 1)
+            def _():
+                self.cross(rank)
+                if rank + 1 < line:
+                    self.advance(rank + 1)
+
+    def finish(self, result, sem):
+        place = self.place
+        z, line = place.z, place.line
+        here = z * 2 + place.y
+        self.core_arrived(here)
+        self.pair_copy(z, 0).wait_recv()
+        for side in (-1, 1):
+            pl.when(place.inside(z + side))(lambda: self.line_copy(z, -side, 1).wait_recv())
+        for rank in (1, 0):
+            self.pair_copy(place.near(rank), rank % 2).wait_send()
+        self.add_up(
+            [
+                (self.parts.at[here], None),
+                (self.from_core.at[here], None),
+                (self.from_pair.at[z], None),
+                (self.from_line.at[z], place.inside(z + 1)),
+                (self.from_line.at[line], place.inside(z - 1)),
+            ],
+            0,
+        )
+        copy = pltpu.make_async_copy(self.sums.at[0], result, sem)
+        copy.start()
+        copy.wait()
+        for side in (-1, 1):
+
+            @pl.when(place.inside(z + side))
+            def _():
+                self.line_copy(z + side, side, 1).wait_send()
+
+
+def expert_kernel(*refs, line, chunk, gathers):
+    refs = list(refs)
+
+    def take(count):
+        taken = refs[:count]
+        del refs[:count]
+        return taken[0] if count == 1 else taken
+
+    tokens_in, cotangent_own, cotangent_other, shares_ref, own_hbm, other_hbm = take(6)
+    exchanged = take(1)
+    if not gathers:
+        out_before, grad_before = take(2)
+        out_hbm, grad_piece, grad_own, grad_other, out_core, received = take(6)
+        arrays = take(4)
+        tokens_hbm = tokens_in
+    else:
+        out_hbm, grad_hbm, grad_own, grad_other, tokens_hbm, received = take(6)
+    weights, grads, tokens_buf, cotangent_buf, inner_low, grad_low = take(6)
+    out_buf, grad_buf, stage, load_sems, store_sems, row_sems, part_sems, exchange_sems = take(8)
+
     expert_count, model_width, all_units = weights.shape
     hidden_units = all_units // 3
     units = hidden_units // 2
-
-    @pl.when(step == 0)
-    def _():
-        copies = weight_copies(own_hbm, other_hbm, weights, load_sems)
-        for copy in copies:
+    steps = 2 * line
+    rows = tokens_hbm.shape[2]
+    place = Place(line)
+    first_rows, second_rows = pl.ds(0, rows), pl.ds(rows, rows)
+    if gathers:
+        mover = Gather(place, tokens_hbm, take(4))
+    else:
+        before_buf, terms, sums = take(3)
+        core_out_send, core_out_recv = take(2)
+        mover = Reduce(place, arrays, terms, sums, take(7))
+    order = mover.order
+
+    place.meet()
+    exchange = remote(
+        exchanged, received, exchange_sems.at[0], exchange_sems.at[1], place.across
+    )
+    exchange.start()
+    if gathers:
+        own_block = place.z * 2 + place.y
+        own_copy = pltpu.make_async_copy(tokens_in, tokens_hbm.at[own_block, 0], row_sems.at[0, 0])
+        own_copy.start()
+        own_copy.wait()
+        mover.start()
+    weight_loads = weight_copies(own_hbm, other_hbm, weights, load_sems)
+    for copy in weight_loads:
+        copy.start()
+    grads[...] = jnp.zeros_like(grads)
+
+    def row_copies(step, slot):
+        here = place.block(order, step)
+        lanes = pl.ds(0, model_width)
+        pairs = [
+            (tokens_hbm.at[here, 0], tokens_buf.at[slot, first_rows, :]),
+            (tokens_hbm.at[here, 1], tokens_buf.at[slot, second_rows, :]),
+            (cotangent_own.at[here, :, lanes], cotangent_buf.at[slot, first_rows, :]),
+            (cotangent_other.at[here, :, lanes], cotangent_buf.at[slot, second_rows, :]),
+        ]
+        if not gathers:
+            pairs.append((out_before.at[here], before_buf.at[slot, 0]))
+            pairs.append((grad_before.at[here], before_buf.at[slot, 1]))
+        return [
+            pltpu.make_async_copy(source, target, row_sems.at[slot, i])
+            for i, (source, target) in enumerate(pairs)
+        ]
+
+    def load_rows(step, slot):
+        if gathers:
+            mover.core_copy(place.block(order, step)).wait_recv()
+        for copy in row_copies(step, slot):
             copy.start()
-        grads[...] = jnp.zeros_like(grads)
-        for copy in copies:
+
+    load_rows(0, 0)
+    for copy in weight_loads:
+        copy.wait()
+
+    def out_core_copy(step):
+        here = place.block(order, step)
+        return remote(
+            out_buf.at[second_rows],
+            out_core.at[here],
+            core_out_send.at[here],
+            core_out_recv.at[here],
+            place.sibling,
+        )
+
+    def grad_core_copy(step, slot):
+        return mover.core_copy(place.block(order, step), grad_buf.at[slot, second_rows, :])
+
+    def part_copies(step, slot):
+        here = place.block(order, step)
+        if gathers:
+            pairs = [(out_buf, out_hbm.at[here]), (grad_buf.at[slot], grad_hbm.at[here])]
+        else:
+            pairs = [
+                (out_buf.at[first_rows], out_hbm.at[here]),
+                (grad_buf.at[slot, first_rows, :], arrays[0].at[here]),
+            ]
+        return [
+            pltpu.make_async_copy(source, target, part_sems.at[i])
+            for i, (source, target) in enumerate(pairs)
+        ]
+
+    @pl.loop(0, steps)
+    def _(step):
+        slot = step % 2
+        for copy in row_copies(step, slot):
             copy.wait()
-
-    def run(expert, gate_up, grad_inner):
-        lane = lax.broadcasted_iota(jnp.int32, shares_ref.shape, 1)
-        share = jnp.sum(
-            jnp.where(lane == expert, shares_ref[...], 0.0), axis=1, keepdims=True
-        )
-        inner, grad_gate, grad_up = activate(gate_up, grad_inner, share)
-        inner_low[expert] = inner
-        grad_low[expert, :, :hidden_units] = grad_gate
-        grad_low[expert, :, hidden_units:] = grad_up
-
-    def weight_grads(expert):
-        grads[expert, :, : 2 * hidden_units] += lax.dot_general(
-            tokens_ref[...], grad_low[expert], FIRST_FIRST, preferred_element_type=F32
-        )
-        grads[expert, :, 2 * hidden_units :] += lax.dot_general(
-            cotangent_ref[...], inner_low[expert], FIRST_FIRST, preferred_element_type=F32
-        )
-
-    results = project(tokens_ref[...], cotangent_ref[...], weights[0])
-    for expert in range(expert_count):
-        run(expert, *results)
-        if expert + 1 < expert_count:
-            results = project(tokens_ref[...], cotangent_ref[...], weights[expert + 1])
-        weight_grads(expert)
-
-    @pl.loop(0, model_width // chunk)
+        shares = shares_ref[place.block(order, step)]
+        lane = lax.broadcasted_iota(jnp.int32, shares.shape, 1)
+
+        def run(expert, gate_up, grad_inner):
+            share = jnp.sum(jnp.where(lane == expert, shares, 0.0), axis=1, keepdims=True)
+            inner, grad_gate, grad_up = activate(gate_up, grad_inner, share)
+            inner_low[expert] = inner
+            grad_low[expert, :, :hidden_units] = grad_gate
+            grad_low[expert, :, hidden_units:] = grad_up
+
+        def weight_grads(expert):
+            grads[expert, :, : 2 * hidden_units] += lax.dot_general(
+                tokens_buf[slot], grad_low[expert], FIRST_FIRST, preferred_element_type=F32
+            )
+            grads[expert, :, 2 * hidden_units :] += lax.dot_general(
+                cotangent_buf[slot], inner_low[expert], FIRST_FIRST, preferred_element_type=F32
+            )
+
+        results = project(tokens_buf[slot], cotangent_buf[slot], weights[0])
+        for expert in range(expert_count):
+            run(expert, *results)
+            if expert + 1 < expert_count:
+                results = project(tokens_buf[slot], cotangent_buf[slot], weights[expert + 1])
+            weight_grads(expert)
+
+        @pl.when(step >= 1)
+        def _():
+            for copy in part_copies(step - 1, 1 - slot):
+                copy.wait()
+            if not gathers:
+                out_core_copy(step - 1).wait_send()
+
+        mover.tick(step)
+
+        if not gathers:
+
+            @pl.when(step >= 2)
+            def _():
+                grad_core_copy(step - 2, slot).wait_send()
+
+        @pl.loop(0, model_width // chunk)
+        def _(number):
+            @pl.when((number == 1) & (step + 1 < steps))
+            def _():
+                load_rows(step + 1, 1 - slot)
+
+            cols = pl.ds(pl.multiple_of(number * chunk, chunk), chunk)
+
+            def total_of(kind, lows, lanes):
+                if gathers:
+                    total = jnp.zeros((2 * rows, chunk), F32)
+                else:
+                    total = before_buf[slot, kind, :, cols].astype(F32)
+                for expert in range(expert_count):
+                    total += lax.dot_general(
+                        lows[expert],
+                        weights[expert, cols, lanes],
+                        LAST_LAST,
+                        preferred_element_type=F32,
+                    )
+                return total.astype(BF16)
+
+            out_buf[:, cols] = total_of(0, inner_low, pl.ds(2 * hidden_units, hidden_units))
+            grad_buf[slot, :, cols] = total_of(1, grad_low, pl.ds(0, 2 * hidden_units))
+
+        for copy in part_copies(step, slot):
+            copy.start()
+        if not gathers:
+            out_core_copy(step).start()
+            grad_core_copy(step, slot).start()
+
+    last = (steps - 1) % 2
+    for copy in part_copies(steps - 1, last):
+        copy.wait()
+    if not gathers:
+        out_core_copy(steps - 1).wait_send()
+        grad_core_copy(steps - 2, 1 - last).wait_send()
+        grad_core_copy(steps - 1, last).wait_send()
+
+    sources, _, slice_rows, _ = own_hbm.shape
+
+    def grad_copy(expert, source, half, slot):
+        return pltpu.make_async_copy(
+            stage.at[slot, half],
+            (grad_own, grad_other)[half].at[source, expert],
+            store_sems.at[slot, half],
+        )
+
+    @pl.loop(0, expert_count * sources)
     def _(number):
-        cols = pl.ds(pl.multiple_of(number * chunk, chunk), chunk)
-        total = jnp.zeros((tokens_ref.shape[0], chunk), F32)
-        for expert in range(expert_count):
-            total += lax.dot_general(
-                inner_low[expert],
-                weights[expert, cols, 2 * hidden_units :],
-                LAST_LAST,
-                preferred_element_type=F32,
-            )
-        out_ref[:, cols] = total.astype(BF16)
-        total = jnp.zeros((tokens_ref.shape[0], chunk), F32)
-        for expert in range(expert_count):
-            total += lax.dot_general(
-                grad_low[expert],
-                weights[expert, cols, : 2 * hidden_units],
-                LAST_LAST,
-                preferred_element_type=F32,
-            )
-        grad_tokens_ref[:, cols] = total.astype(BF16)
-
-    @pl.when(step == steps - 1)
-    def _():
-        sources, _, rows, lanes = own_hbm.shape
-
-        @pl.loop(0, expert_count)
-        def _(expert):
-            copies = []
-            for half, half_hbm in enumerate((grad_own_hbm, grad_other_hbm)):
-                for part in range(3):
-                    first = (2 * part + half) * units
-                    stage[half, :, part * units : (part + 1) * units] = grads[
-                        expert, :, first : first + units
-                    ].astype(BF16)
-                for source in range(sources):
-                    copy = pltpu.make_async_copy(
-                        stage.at[half, pl.ds(source * rows, rows), :],
-                        half_hbm.at[source, expert],
-                        store_sems.at[half, source],
-                    )
-                    copy.start()
-                    copies.append(copy)
-            for copy in copies:
-                copy.wait()
-
-
-def experts(tokens, cotangent, shares, own, other, block_rows=512, chunk=512):
-    token_count, model_width = tokens.shape
-    sources, expert_count, rows, lanes = own.shape
+        expert, source = number // sources, number % sources
+        slot = number % 2
+
+        @pl.when(number >= 2)
+        def _():
+            for half in range(2):
+                grad_copy(expert, source, half, slot).wait()
+
+        here = pl.ds(pl.multiple_of(source * slice_rows, slice_rows), slice_rows)
+        for half in range(2):
+            for part in range(3):
+                first = (2 * part + half) * units
+                stage[slot, half, :, part * units : (part + 1) * units] = grads[
+                    expert, here, first : first + units
+                ].astype(BF16)
+            grad_copy(expert, source, half, slot).start()
+
+    for slot in range(2):
+        for half in range(2):
+            grad_copy(0, 0, half, slot).wait()
+
+    exchange.wait()
+    if gathers:
+        mover.finish()
+    else:
+        for step in range(steps):
+            out_core_copy(step).wait_recv()
+        mover.finish(grad_piece, row_sems.at[0, 0])
+
+
+def expert_call(operands, own, shares, line, rows, model_width, gathers, collective_id, chunk=512):
+    sources, expert_count, slice_rows, lanes = own.shape
     hidden_units = 2 * lanes // 3
-    steps = token_count // block_rows
-    row_block = pl.BlockSpec((block_rows, model_width), lambda i: (i, 0))
+    blocks = 2 * line
     in_place = pl.BlockSpec(memory_space=pl.ANY)
-    flops = 2 * token_count * model_width * expert_count * hidden_units * 9
-    return pl.pallas_call(
-        partial(expert_kernel, steps=steps, chunk=chunk),
-        grid=(steps,),
-        in_specs=[
-            row_block,
-            row_block,
-            pl.BlockSpec((block_rows, shares.shape[1]), lambda i: (i, 0)),
-            in_place,
-            in_place,
-        ],
-        out_specs=[row_block, row_block, in_place, in_place],
-        out_shape=[
-            jax.ShapeDtypeStruct(tokens.shape, BF16),
-            jax.ShapeDtypeStruct(tokens.shape, BF16),
-            jax.ShapeDtypeStruct(own.shape, BF16),
-            jax.ShapeDtypeStruct(own.shape, BF16),
-        ],
+    dma = pltpu.SemaphoreType.DMA
+    flops = 2 * blocks * 2 * rows * model_width * expert_count * hidden_units * 9
+
+    def low(*shape):
+        return jax.ShapeDtypeStruct(shape, BF16)
+
+    if gathers:
+        out_shape = [
+            low(blocks, 2 * rows, model_width),
+            low(blocks, 2 * rows, model_width),
+            low(*own.shape),
+            low(*own.shape),
+            low(blocks, 2, rows, model_width),
+            low(*operands[6].shape),
+        ]
+        own_scratch = [dma((blocks, 2)), dma((line, 2)), dma((line,)), dma((blocks,))]
+    else:
+        out_shape = [
+            low(blocks, rows, model_width),
+            low(rows, model_width),
+            low(*own.shape),
+            low(*own.shape),
+            low(blocks, rows, model_width),
+            low(*operands[6].shape),
+            low(blocks, rows, model_width),
+            low(blocks, rows, model_width),
+            low(line, rows, model_width),
+            low(line + 1, rows, model_width),
+        ]
+        own_scratch = [
+            pltpu.VMEM((2, 2, 2 * rows, model_width), BF16),
+            pltpu.VMEM((5, rows, model_width), BF16),
+            pltpu.VMEM((4, rows, model_width), BF16),
+            dma((blocks,)),
+            dma((blocks,)),
+            dma((5,)),
+            dma((blocks,)),
+            dma((blocks,)),
+            dma((line,)),
+            dma((line,)),
+            dma((line,)),
+            dma((line + 1,)),
+        ]
+    in_specs = [in_place] * len(operands)
+    in_specs[3] = pl.BlockSpec(memory_space=pltpu.VMEM)
+    results = pl.pallas_call(
+        partial(expert_kernel, line=line, chunk=chunk, gathers=gathers),
+        in_specs=in_specs,
+        out_specs=[in_place] * len(out_shape),
+        out_shape=out_shape,
         scratch_shapes=[
             pltpu.VMEM((expert_count, model_width, 3 * hidden_units), BF16),
             pltpu.VMEM((expert_count, model_width, 3 * hidden_units), F32),
-            pltpu.VMEM((expert_count, block_rows, hidden_units), BF16),
-            pltpu.VMEM((expert_count, block_rows, 2 * hidden_units), BF16),
-            pltpu.VMEM((2, model_width, lanes), BF16),
-            pltpu.SemaphoreType.DMA((sources, 2, 3)),
-            pltpu.SemaphoreType.DMA((2, sources)),
-        ],
-        compiler_params=pltpu.CompilerParams(vmem_limit_bytes=63 * 2**20),
+            pltpu.VMEM((2, 2 * rows, model_width), BF16),
+            pltpu.VMEM((2, 2 * rows, model_width), BF16),
+            pltpu.VMEM((expert_count, 2 * rows, hidden_units), BF16),
+            pltpu.VMEM((expert_count, 2 * rows, 2 * hidden_units), BF16),
+            pltpu.VMEM((2 * rows, model_width), BF16),
+            pltpu.VMEM((2, 2 * rows, model_width), BF16),
+            pltpu.VMEM((2, 2, slice_rows, lanes), BF16),
+            dma((sources, 2, 3)),
+            dma((2, 2)),
+            dma((2, 6)),
+            dma((2,)),
+            dma((2,)),
+        ]
+        + own_scratch,
+        compiler_params=pltpu.CompilerParams(
+            vmem_limit_bytes=60 * 2**20, collective_id=collective_id, has_side_effects=True
+        ),
         cost_estimate=pl.CostEstimate(
             flops=flops, bytes_accessed=80 * 2**20, transcendentals=0
         ),
-    )(tokens, cotangent, shares, own, other)
+    )(*operands)
+    return results[:6]
+
+
+def experts_gathering(piece, cotangents, shares, own, other, exchanged, line):
+    rows, model_width = piece.shape
+    operands = (piece, *cotangents, shares, own, other, exchanged)
+    return expert_call(operands, own, shares, line, rows, model_width, True, 1)
+
+
+def experts_reducing(
+    tokens, cotangents, shares, own, other, exchanged, out_parts, grad_parts, line
+):
+    _, _, rows, model_width = tokens.shape
+    operands = (tokens, *cotangents, shares, own, other, exchanged, out_parts, grad_parts)
+    return expert_call(operands, own, shares, line, rows, model_width, False, 2)
 
 
 def attention_rows(values, kv_head, group_size):
@@ -845,19 +1337,46 @@
     expert_count, slice_rows, unit_count = gate_weight.shape
     own_experts = expert_count // groups
     piece_rows = row_count // tensor_size
+    first_count = own_experts * 2 // 5
     context_rank = lax.axis_index(CONTEXT)
     tensor_rank = lax.axis_index(TENSOR)
     group_rank = lax.axis_index(SHARD) * lax.axis_size(CONTEXT) + context_rank
+    chip_half, core = tensor_rank // 2, tensor_rank % 2
     own_first = context_rank * row_count
     piece_first = tensor_rank * piece_rows
     sibling = [(i, i ^ 1) for i in range(tensor_size)]
     across = [(i, i ^ 2) for i in range(tensor_size)]
+    pair = [(0, 1), (1, 0)]
 
     def own_piece(values):
         return lax.dynamic_slice_in_dim(values, piece_first, piece_rows)
 
-    def padded_column(gain):
-        return jnp.pad(gain[:, None], ((0, 0), (0, 127)))
+    def pick(values, axis, index):
+        return lax.dynamic_index_in_dim(values, index, axis, keepdims=False)
+
+    def sum_over_tensor(parts):
+        parts = parts.astype(BF16).reshape(2, 2, piece_rows, -1)
+        received = lax.ppermute(pick(parts, 1, 1 - core), TENSOR, sibling)
+        half = pick(parts, 1, core).astype(F32) + received.astype(F32)
+        received = lax.ppermute(pick(half, 0, 1 - chip_half).astype(BF16), TENSOR, across)
+        return pick(half, 0, chip_half) + received.astype(F32)
+
+    def gather_over_tensor(piece):
+        other = lax.ppermute(piece, TENSOR, across)
+        chips = jnp.where(
+            chip_half == 0, jnp.concatenate([piece, other]), jnp.concatenate([other, piece])
+        ).reshape(2, 1, piece_rows, -1)
+        others = lax.ppermute(chips, TENSOR, sibling)
+        both = jnp.where(
+            core == 0,
+            jnp.concatenate([chips, others], axis=1),
+            jnp.concatenate([others, chips], axis=1),
+        )
+        return both.reshape(row_count, -1)
+
+    def padded_columns(*gains):
+        columns = jnp.stack(gains, axis=1)
+        return jnp.pad(columns, ((0, 0), (0, 128 - len(gains))))
 
     with jax.named_scope("weights"):
         qkv_full = lax.all_gather(
@@ -866,7 +1385,8 @@
                     query_weight,
                     key_projection_weight,
                     value_projection_weight,
-                    padded_column(gain_attn),
+                    out_weight.T,
+                    padded_columns(gain_attn, gain_ffn),
                 ],
                 axis=1,
             ),
@@ -876,24 +1396,45 @@
         )
         qkv_cols = query_cols + 2 * kv_cols
         qkv_weight = qkv_full[:, :qkv_cols]
-        gain_attn_float = qkv_full[:, qkv_cols].astype(F32)
-        slices = jnp.concatenate(
-            [gate_weight, up_weight, down_weight.transpose(0, 2, 1)], axis=2
-        )
-        owned = lax.all_to_all(slices, GROUP, 0, 0, tiled=True)
-        out_gathered = lax.all_gather(
-            jnp.concatenate([out_weight.T, padded_column(gain_ffn)], axis=1),
-            GROUP,
-            axis=0,
-            tiled=True,
-        )
-        out_transposed = out_gathered[:, :query_cols]
-        gain_ffn_float = out_gathered[:, query_cols].astype(F32)
-
-    def gather_tokens(piece):
-        own_core = lax.all_gather(piece, GROUP, axis=0, tiled=False)
-        other_core = lax.ppermute(own_core, TENSOR, sibling)
-        return jnp.stack([own_core, other_core], axis=1).reshape(-1, piece.shape[1])
+        out_transposed = qkv_full[:, qkv_cols : qkv_cols + query_cols]
+        gain_attn_float = qkv_full[:, qkv_cols + query_cols].astype(F32)
+        gain_ffn_float = qkv_full[:, qkv_cols + query_cols + 1].astype(F32)
+        lanes = 3 * unit_count
+
+
+        def expert_slices(first, count):
+            slices = jnp.concatenate(
+                [
+                    weight.reshape((groups, own_experts) + weight.shape[1:])[:, first : first + count]
+                    for weight in (gate_weight, up_weight, down_weight.transpose(0, 2, 1))
+                ],
+                axis=3,
+            ).reshape(groups * count, slice_rows, lanes)
+            owned = lax.all_to_all(slices, GROUP, 0, 0, tiled=True)
+            return owned.reshape(groups, count, slice_rows, lanes)
+
+        owned_first = expert_slices(0, first_count)
+        owned_second = expert_slices(first_count, own_experts - first_count)
+
+    with jax.named_scope("cotangents"):
+        cotangent_piece = own_piece(cotangent)
+        spread = jnp.sum(
+            jnp.where(
+                own_piece(routes)[:, :, None] == jnp.arange(expert_count, dtype=jnp.int32),
+                own_piece(shares)[:, :, None],
+                0.0,
+            ),
+            axis=1,
+        )
+        spread_high = spread.astype(BF16)
+        spread_low = (spread - spread_high.astype(F32)).astype(BF16)
+        spread_both = jnp.pad(
+            jnp.concatenate([spread_high, spread_low], axis=1),
+            ((0, 0), (0, 128 - 2 * expert_count)),
+        )
+        cotangent_own = lax.all_gather(
+            jnp.concatenate([cotangent_piece, spread_both], axis=1), GROUP, axis=0, tiled=False
+        )
 
     with jax.named_scope("attention"):
         positions = doc_positions(segments)
@@ -915,75 +1456,98 @@
             - projected[:, qkv_cols:] * jnp.tile(own_turns[:, HEAD_DIM:], (1, heads))
         ).astype(BF16)
         queries = rotated[:, :query_cols]
-        keys_values = lax.all_gather(
-            jnp.concatenate(
-                [rotated[:, query_cols:], projected[:, rotated_cols:qkv_cols].astype(BF16)], axis=1
-            ),
-            CONTEXT,
-            axis=0,
-            tiled=True,
-        )
+        own_keys_values = jnp.concatenate(
+            [rotated[:, query_cols:], projected[:, rotated_cols:qkv_cols].astype(BF16)], axis=1
+        )
+        owned_first, own_keys_values = lax.optimization_barrier((owned_first, own_keys_values))
+        other_keys_values = lax.ppermute(own_keys_values, CONTEXT, pair)
+        keys_values = jnp.where(
+            context_rank == 0,
+            jnp.concatenate([own_keys_values, other_keys_values]),
+            jnp.concatenate([other_keys_values, own_keys_values]),
+        )
+        others_first = lax.ppermute(owned_first, TENSOR, across)
         first = own_first.reshape(1).astype(jnp.int32)
         attended, lse = attention_forward(first, queries, keys_values, doc_start[:, None])
-
-    with jax.named_scope("routing"):
-        owned, attended = lax.optimization_barrier((owned, attended))
-        others = lax.ppermute(owned, TENSOR, across)
-        cotangent_piece = own_piece(cotangent)
-        cotangent_all = gather_tokens(cotangent_piece)
-        spread = jnp.sum(
-            jnp.where(
-                own_piece(routes)[:, :, None] == jnp.arange(expert_count, dtype=jnp.int32),
-                own_piece(shares)[:, :, None],
-                0.0,
-            ),
-            axis=1,
-        )
-        token_shares = lax.dynamic_slice_in_dim(
-            gather_tokens(spread), group_rank * own_experts, own_experts, axis=1
-        )
-        token_shares = jnp.pad(token_shares, ((0, 0), (0, 8 - own_experts)))
-
-    with jax.named_scope("attention_out"):
         attn_part = lax.dot_general(
             attended, out_transposed, LAST_LAST, preferred_element_type=F32
         )
-        attn_piece = lax.psum_scatter(
-            attn_part.astype(BF16), TENSOR, scatter_dimension=0, tiled=True
-        )
-        hidden = own_piece(residual_in).astype(F32) + attn_piece.astype(F32)
+        attn_piece = sum_over_tensor(attn_part)
+        others_first, owned_second, attn_piece = lax.optimization_barrier(
+            (others_first, owned_second, attn_piece)
+        )
+        hidden = own_piece(residual_in).astype(F32) + attn_piece
         normed_ffn, ffn_norm_back = jax.vjp(rms_scale, hidden, gain_ffn_float)
 
+    with jax.named_scope("exchange"):
+        cotangent_own, normed_ffn = lax.optimization_barrier((cotangent_own, normed_ffn))
+        cotangent_other = lax.ppermute(cotangent_own, TENSOR, sibling)
+        spread_all = jnp.concatenate(
+            [cotangent_own[:, :, model_width:], cotangent_other[:, :, model_width:]], axis=1
+        )
+
+        def shares_of(first, count):
+            start = group_rank * own_experts + first
+            high = lax.dynamic_slice_in_dim(spread_all, start, count, axis=2)
+            low = lax.dynamic_slice_in_dim(spread_all, start + expert_count, count, axis=2)
+            total = high.astype(F32) + low.astype(F32)
+            return jnp.pad(total, ((0, 0), (0, 0), (0, 8 - count)))
+
+        shares_first = shares_of(0, first_count)
+        shares_second = shares_of(first_count, own_experts - first_count)
+
     with jax.named_scope("experts"):
-        tokens_all = gather_tokens(normed_ffn.astype(BF16))
-        shape = (groups, own_experts, slice_rows, 3 * unit_count)
-        out_parts, grad_token_parts, grad_own, grad_other = experts(
-            tokens_all, cotangent_all, token_shares, owned.reshape(shape), others.reshape(shape)
-        )
-
-    def reduce_tokens(parts):
-        parts = parts.reshape(groups, 2, piece_rows, model_width)
-        received = lax.ppermute(parts[:, 1], TENSOR, sibling)
-        both = (parts[:, 0].astype(F32) + received.astype(F32)).astype(BF16)
-        return lax.psum_scatter(
-            both.reshape(groups * piece_rows, model_width),
+        line = groups // 2
+        cotangents = (cotangent_own, cotangent_other)
+        out_parts, grad_parts, grad_own_first, grad_other_first, tokens, others_second = (
+            experts_gathering(
+                normed_ffn.astype(BF16),
+                cotangents,
+                shares_first,
+                owned_first,
+                others_first,
+                owned_second,
+                line,
+            )
+        )
+        out_own, grad_second, grad_own_second, grad_other_second, out_other, received_first = (
+            experts_reducing(
+                tokens,
+                cotangents,
+                shares_second,
+                owned_second,
+                others_second,
+                grad_other_first,
+                out_parts,
+                grad_parts,
+                line,
+            )
+        )
+
+    with jax.named_scope("expert_grads"):
+
+        def added(own, received):
+            return (own.astype(F32) + received.astype(F32)).astype(BF16)
+
+        def returned(total):
+            flat = total.reshape((total.shape[0] * total.shape[1],) + total.shape[2:])
+            return lax.all_to_all(flat, GROUP, 0, 0, tiled=True).reshape(total.shape)
+
+        total_first = added(grad_own_first, received_first)
+        received_second = lax.ppermute(grad_other_second, TENSOR, across)
+        total_first, grad_second = lax.optimization_barrier((total_first, grad_second))
+        returned_first = returned(total_first)
+        grad_hidden_norm, grad_gain_ffn_local = ffn_norm_back(grad_second.astype(F32))
+        grad_hidden = cotangent_piece.astype(F32) + grad_hidden_norm
+        grad_hidden_low = gather_over_tensor(grad_hidden.astype(BF16))
+        out_sum = (out_own.astype(F32) + out_other.astype(F32)).astype(BF16)
+        out_piece = lax.psum_scatter(
+            out_sum.reshape(groups * piece_rows, model_width),
             GROUP,
             scatter_dimension=0,
             tiled=True,
-        ).astype(F32)
-
-    with jax.named_scope("expert_grads"):
-        grad_second = reduce_tokens(grad_token_parts)
-        received = lax.ppermute(grad_other, TENSOR, across)
-        total = (grad_own.astype(F32) + received.astype(F32)).astype(BF16)
-        returned = lax.all_to_all(
-            total.reshape(expert_count, slice_rows, 3 * unit_count), GROUP, 0, 0, tiled=True
-        )
-        grad_hidden_norm, grad_gain_ffn_local = ffn_norm_back(grad_second)
-        grad_hidden = cotangent_piece.astype(F32) + grad_hidden_norm
-        grad_hidden_low = lax.all_gather(grad_hidden.astype(BF16), TENSOR, axis=0, tiled=True)
-        output_piece = (hidden + reduce_tokens(out_parts)).astype(BF16)
-        output = lax.all_gather(output_piece, TENSOR, axis=0, tiled=True)
+        )
+        output = gather_over_tensor((hidden + out_piece.astype(F32)).astype(BF16))
 
     with jax.named_scope("attention_back"):
         grad_out_local = lax.dot_general(
@@ -1003,46 +1567,66 @@
             turns,
             own_turns,
         )
-        grad_key_value = lax.psum_scatter(
-            grad_key_value, CONTEXT, scatter_dimension=0, tiled=True
-        )
+        received_second, grad_key_value = lax.optimization_barrier(
+            (received_second, grad_key_value)
+        )
+        total_second = added(grad_own_second, received_second)
+        grad_key_value = grad_key_value.reshape(2, row_count, -1)
+        received = lax.ppermute(pick(grad_key_value, 0, 1 - context_rank), CONTEXT, pair)
+        grad_key_value = (
+            pick(grad_key_value, 0, context_rank).astype(F32) + received.astype(F32)
+        ).astype(BF16)
         grad_projected = jnp.concatenate([grad_query_lin, grad_key_value], axis=1)
         grad_first_part = lax.dot_general(
             grad_projected, qkv_weight, LAST_LAST, preferred_element_type=F32
         )
-        grad_first = lax.psum_scatter(
-            grad_first_part.astype(BF16), TENSOR, scatter_dimension=0, tiled=True
-        ).astype(F32)
+        returned_first, total_second, grad_first_part = lax.optimization_barrier(
+            (returned_first, total_second, grad_first_part)
+        )
+        returned_second = returned(total_second)
+        grad_first = sum_over_tensor(grad_first_part)
+        out_piece, grad_first = lax.optimization_barrier((out_piece, grad_first))
         _, attn_norm_back = jax.vjp(
             rms_scale, own_piece(residual_in).astype(F32), gain_attn_float
         )
         grad_input_norm, grad_gain_attn_local = attn_norm_back(grad_first)
-        grad_input = lax.all_gather(
-            (grad_hidden + grad_input_norm).astype(BF16), TENSOR, axis=0, tiled=True
-        )
+        grad_input = gather_over_tensor((grad_hidden + grad_input_norm).astype(BF16))
         grad_qkv_local = lax.dot_general(
             first_normalized, grad_projected, FIRST_FIRST, preferred_element_type=F32
         )
         grad_qkv = lax.psum_scatter(
-            grad_qkv_local.astype(BF16), GROUP, scatter_dimension=0, tiled=True
+            jnp.concatenate(
+                [grad_qkv_local, padded_columns(grad_gain_attn_local, grad_gain_ffn_local)], axis=1
+            ).astype(BF16),
+            GROUP,
+            scatter_dimension=0,
+            tiled=True,
         ).astype(F32)
-        gains = lax.psum(
-            jnp.stack([grad_gain_attn_local, grad_gain_ffn_local]), GROUP + (TENSOR,)
-        )
-        gains = lax.dynamic_slice_in_dim(gains, group_rank * slice_rows, slice_rows, axis=1)
+        gains = grad_qkv[:, qkv_cols : qkv_cols + 2]
+        gains = gains + lax.ppermute(gains, TENSOR, sibling)
+        gains = gains + lax.ppermute(gains, TENSOR, across)
+
+    def whole(first, last, turned):
+        parts = [
+            part[..., first:last].transpose(0, 1, 3, 2) if turned else part[..., first:last]
+            for part in (returned_first, returned_second)
+        ]
+        joined = jnp.concatenate(parts, axis=1).astype(F32)
+        return joined.reshape((expert_count,) + joined.shape[2:])
+
     units = unit_count
     return (
         output,
         grad_input,
-        gains[0],
+        gains[:, 0],
         grad_qkv[:, :query_cols],
         grad_qkv[:, query_cols:rotated_cols],
-        grad_qkv[:, rotated_cols:],
+        grad_qkv[:, rotated_cols:qkv_cols],
         grad_out_transposed.astype(F32).T,
-        gains[1],
-        returned[:, :, :units].astype(F32),
-        returned[:, :, units : 2 * units].astype(F32),
-        returned[:, :, 2 * units :].transpose(0, 2, 1).astype(F32),
+        gains[:, 1],
+        whole(0, units, False),
+        whole(units, 2 * units, False),
+        whole(2 * units, 3 * units, True),
     )
 
 

time: 1530 us -> 958 us (0.63)
  waiting for transfers between devices: 1020 us -> 415 us
  Pallas kernels: 235 us -> 319 us
  blocking collectives: 70.7 us -> 0 us
  starting transfers between devices: 16.8 us -> 35.9 us
    all_gather x7 -> x1, waiting for transfers between devices: 285 us -> 4.59 us  [expert_plan(): lax.all_gather(jnp.concatenate([cotangent_piece, spread_both], axis=1), G...]
    reduce_scatter x6 -> x1, waiting for transfers between devices: 238 us -> 4.08 us  [expert_plan(): lax.psum_scatter(out_sum.reshape(groups * piece_rows, model_width), GROUP...]
    all_to_all x2 -> x4, waiting for transfers between devices: 129 us -> 29.2 us  [the longest x2 29.2 us: expert_slices(): owned = lax.all_to_all(slices, GROUP, 0, 0, tiled=True)]
    pallas_call x1 -> x2, Pallas kernels: 184 us -> 268 us  [expert_call(): pl.pallas_call(partial(expert_kernel, line=line, chunk=chunk, gathers=gat...]
    reduce_scatter x1, waiting for transfers between devices: 25.9 us -> 88.9 us  [expert_plan(): lax.psum_scatter(grad_out_local.astype(BF16), GROUP, scatter_dimension=0,...]
    ppermute x7 -> x17, waiting for transfers between devices: 217 us -> 167 us  [the longest x2 76.9 us: sum_over_tensor(): lax.ppermute(pick(half, 0, 1 - chip_half).astype(BF16), TENSOR, across)]
    all_gather x1, waiting for transfers between devices: 123 us -> 79.9 us  [expert_plan(): lax.all_gather(jnp.concatenate([query_weight, key_projection_weight, valu...]
    unnamed x15 -> x6, waiting for transfers between devices: 0.76 us -> 41.2 us
  transfers between devices with their start and end apart: 24 -> 26, of which waited for: 18 -> 15; matrix products, arithmetic and copies ran while one was open for 8% -> 14% of each run, Pallas kernels for 1% -> 5%
where the time goes in v3:
time: 958 us; the launch traced here: 951 us
  waiting for transfers between devices  415 us (43%)
  Pallas kernels  319 us (33%)
  other arithmetic  80.2 us (8%)
  local copies, waits for them, and re-layouts  61.7 us (6%)
  starting transfers between devices  35.9 us (4%)
  matrix products  24.6 us (3%)
  between operations  15.2 us (2%)
    pallas_call x2, Pallas kernels, expert_call(): pl.pallas_call(partial(expert_kernel, line=line, chunk=chunk, gathers=gat...  268 us
    reduce_scatter x1, waiting for transfers between devices, expert_plan(): lax.psum_scatter(grad_out_local.astype(BF16), GROUP, scatter_dimension=0,...  88.9 us
    all_gather x1, waiting for transfers between devices, expert_plan(): lax.all_gather(jnp.concatenate([query_weight, key_projection_weight, valu...  79.9 us
    ppermute x2, waiting for transfers between devices, sum_over_tensor(): lax.ppermute(pick(half, 0, 1 - chip_half).astype(BF16), TENSOR, across)  76.9 us
    unnamed x6, waiting for transfers between devices  41.2 us
    ppermute x1, waiting for transfers between devices, expert_plan(): received_second = lax.ppermute(grad_other_second, TENSOR, across)  33.4 us
    pallas_call x1, Pallas kernels, attention_backward(): pl.pallas_call(partial(attention_backward_kernel, group_size=group_size,...  31.6 us
    ppermute x3, waiting for transfers between devices, gather_over_tensor(): other = lax.ppermute(piece, TENSOR, across)  29.9 us
  transfers between devices with their start and end apart: 26, of which 15 were waited for; matrix products, arithmetic and copies ran while one was open for 14% of the time, Pallas kernels for 5%

profile of v3, /device:TPU:0, one launch (start us, length us, event | category | flops | bytes accessed | tf_op | source)
XLA Modules:
  0.0 951.2 jit_solution(3479339778557109067)
XLA Ops:
  18.5 7.3 all-to-all-start
  29.4 3.7 multiply_cosine_fusion
  35.7 2.3 copy.113
  39.8 3.0 copy.115
  43.5 79.9 %all-gather.4.cloned.1.call-done = bf16[1536,1152]{1,0:T(8,128)(2,1)} async-done(((bf16[192,1152]{1,0:T(8,128)(2,1)}), bf16[1536,1152]{1,0:T(8,128)(2,1)}) %all-gather.4.cloned.1.call-update) | async-done | bytes 3538960 | tf_op jit(solution)/shard_map/weights/all_gather | solution.py:1382
  123.5 2.7 slice.143
  126.1 2.6 copy.137
  131.5 2.6 copy.110
  137.6 4.3 fusion.3
  148.0 4.5 all-to-all-start.1
  153.0 4.9 collective-permute-done.1
  158.1 18.9 %attention.1 = (bf16[1024,384]{1,0:T(8,128)(2,1)S(1)}, f32[4,2,768,1]{3,2,1,0:T(8,128)}) custom-call(s32[1]{0:T(128)} %bitcast.14.first_ref, bf16[1024,384]{1,0:T(8,128)(2,1)S(1)} %slice.153.query_ref, bf16[2048,256]{1,0:T(8,128)(2,1)S(1)} %maximum_select_fusion.6.key_value_ref, s32[1024,1]{1,0:T(8,128)S(1)} %copy.116.doc_start_ref), custom_call_target="tpu_custom_call" | custom-call | flops 16106127360 | bytes 4194304 | tf_op jit(solution)/shard_map/attention/pallas_call | solution.py:1243
  177.1 3.4 convolution_convert_fusion
  185.8 2.3 convert_add_fusion.1
  190.7 62.4 %collective-permute-done.3 = bf16[256,1536]{1,0:T(8,128)(2,1)} collective-permute-done((bf16[256,1536]{1,0:T(8,128)(2,1)}, bf16[256,1536]{1,0:T(8,128)(2,1)}, u32[]{:S(2)}, u32[]{:S(2)}) %collective-permute-start.3) | collective-permute-done | bytes 786464 | tf_op jit(solution)/shard_map/attention/ppermute | solution.py:1361
  253.1 2.5 bitcast_add_fusion.1
  255.6 29.2 %all-to-all-done.1 = bf16[24,192,384]{2,1,0:T(8,128)(2,1)} async-done(((bf16[24,192,384]{2,1,0:T(8,128)(2,1)}), bf16[24,192,384]{2,1,0:T(8,128)(2,1)}, u32[]{:S(2)}, u32[]{:S(2)}) %all-to-all-start.1) | async-done | bytes 3538976 | tf_op jit(solution)/shard_map/weights/all_to_all | solution.py:1413
  284.8 2.6 multiply_reduce_fusion
  289.6 4.6 all-gather.6.cloned.1.call-done
  295.4 10.1 %collective-permute-done.4.refs_2_ = bf16[8,256,1664]{2,1,0:T(8,128)(2,1)} collective-permute-done((bf16[8,256,1664]{2,1,0:T(8,128)(2,1)}, bf16[8,256,1664]{2,1,0:T(8,128)(2,1)}, u32[]{:S(2)}, u32[]{:S(2)}) %collective-permute-start.4) | collective-permute-done | bytes 6815776 | tf_op jit(solution)/shard_map/exchange/ppermute | solution.py:1484
  310.7 129.0 %experts.2 = (bf16[8,512,1536]{2,1,0:T(8,128)(2,1)}, bf16[8,512,1536]{2,1,0:T(8,128)(2,1)}, bf16[8,2,192,384]{3,2,1,0:T(8,128)(2,1)}, bf16[8,2,192,384]{3,2,1,0:...) custom-call(bf16[256,1536]{1,0:T(8,128)(2,1)} %multiply_multiply_fusion.refs_0_, ...), custom_call_target="tpu_custom_call" | custom-call | flops 57982058496 | bytes 83886080 | tf_op jit(solution)/shard_map/experts/pallas_call | solution.py:1053
  439.7 139.2 %experts.3 = (bf16[8,256,1536]{2,1,0:T(8,128)(2,1)}, bf16[256,1536]{1,0:T(8,128)(2,1)}, bf16[8,3,192,384]{3,2,1,0:T(8,128)(2,1)}, bf16[8,3,192,384]{3,2,1,0:T(8,...) custom-call(bf16[8,2,256,1536]{3,2,1,0:T(8,128)(2,1)} %get-tuple-ele, ...), custom_call_target="tpu_custom_call" | custom-call | flops 86973087744 | bytes 83886080 | tf_op jit(solution)/shard_map/experts/pallas_call | solution.py:1053
  579.0 9.2 add_convert_fusion
  589.9 3.9 add_convert_fusion.2
  597.5 18.5 %collective-permute-done.8 = bf16[256,1536]{1,0:T(8,128)(2,1)} collective-permute-done((bf16[256,1536]{1,0:T(8,128)(2,1)S(1)}, bf16[256,1536]{1,0:T(8,128)(2,1)}, u32[]{:S(2)}, u32[]{:S(2)}) %collective-permute-start.8) | collective-permute-done | bytes 786464 | tf_op jit(solution)/shard_map/expert_grads/ppermute | solution.py:1365
  619.4 6.1 all-to-all-start.2
  625.5 2.4 maximum_select_fusion.1
  628.0 4.1 convolution_convert_fusion.3.grad_ref
  632.1 31.6 %attention_back.1 = (bf16[1024,384]{1,0:T(8,128)(2,1)S(1)}, bf16[2048,256]{1,0:T(8,128)(2,1)S(1)}) custom-call(s32[1]{0:T(128)} %bitcast.14.first_ref, bf16[1024,384]{1,0:T(8,128)(2,1)S(1)} %copy-done.5, bf16[2048,256]{1,0:T(8,128)(2,1)S(1)} %copy-done.3, s32[1024,1]{1,0:T(8,128)S(1)} %copy-done.7, f32[4,2,768,1]{3,2,1,0:T(8,128)} %get-tuple-element.64.lse_ref, ...), custom_call_target="tpu_custom_call" | custom-call | flops 40265318400 | bytes 8388608 | tf_op jit(solution)/shard_map/attention_back/pallas_call | solution.py:1272
  663.8 33.4 %collective-permute-done.7 = bf16[8,3,192,384]{3,2,1,0:T(8,128)(2,1)} collective-permute-done((bf16[8,3,192,384]{3,2,1,0:T(8,128)(2,1)}, bf16[8,3,192,384]{3,2,1,0:T(8,128)(2,1)}, u32[]{:S(2)}, u32[]{:S(2)}) %collective-permute-start.7) | collective-permute-done | bytes 3538976 | tf_op jit(solution)/shard_map/expert_grads/ppermute | solution.py:1537
  697.3 6.2 add_convert_fusion.1
  703.5 9.8 %collective-permute-done.10 = bf16[1024,256]{1,0:T(8,128)(2,1)S(1)} collective-permute-done((bf16[1024,256]{1,0:T(8,128)(2,1)S(1)}, bf16[1024,256]{1,0:T(8,128)(2,1)S(1)}, u32[]{:S(2)}, u32[]{:S(2)}) %collective-permute-start.10) | collective-permute-done | bytes 524320 | tf_op jit(solution)/shard_map/attention_back/ppermute | solution.py:1575
  714.2 4.2 fusion.30
  718.5 2.7 dynamic-slice_bitcast_fusion
  721.1 4.6 all-to-all-start.3
  725.8 4.8 convolution_convert_fusion.2
  734.6 3.8 convolution_convert_fusion.1
  738.4 14.5 %collective-permute-done.12 = bf16[256,1536]{1,0:T(8,128)(2,1)S(1)} collective-permute-done((bf16[256,1536]{1,0:T(8,128)(2,1)S(1)}, bf16[256,1536]{1,0:T(8,128)(2,1)S(1)}, u32[]{:S(2)}, u32[]{:S(2)}) %collective-permute-start.12) | collective-permute-done | bytes 786464 | tf_op jit(solution)/shard_map/attention_back/ppermute | solution.py:1361
  753.0 4.1 reduce-scatter.6.cloned.1.call-done
  760.5 4.5 copy.135
  766.4 3.8 fusion.15
  774.0 88.9 %reduce-scatter.8.cloned.1.call-done = bf16[192,384]{1,0:T(8,128)(2,1)} async-done(((bf16[1536,384]{1,0:T(8,128)(2,1)}), bf16[192,384]{1,0:T(8,128)(2,1)}) %reduce-scatter.8.cloned.1.call-update) | async-done | bytes 147472 | tf_op jit(solution)/shard_map/attention_back/reduce_scatter | solution.py:1556
  871.0 11.4 %collective-permute-done.5 = bf16[256,1536]{1,0:T(8,128)(2,1)} collective-permute-done((bf16[256,1536]{1,0:T(8,128)(2,1)S(1)}, bf16[256,1536]{1,0:T(8,128)(2,1)}, u32[]{:S(2)}, u32[]{:S(2)}) %collective-permute-start.5) | collective-permute-done | bytes 786464 | tf_op jit(solution)/shard_map/expert_grads/ppermute | solution.py:1365
  884.4 2.5 bitcast_convert_fusion
  887.0 2.5 bitcast_convert_fusion.1
  889.5 2.5 bitcast_convert_fusion.2
  893.9 41.1 %reduce-scatter.10.cloned.1.call-done = bf16[192,768]{1,0:T(8,128)(2,1)} async-done(((bf16[1536,768]{1,0:T(8,128)(2,1)}), bf16[192,768]{1,0:T(8,128)(2,1)}) %reduce-scatter.10.cloned.1.call-update) | async-done | bytes 294928
  936.3 3.6 maximum_select_fusion
  (222 shorter events, 89.1 us)
Async XLA Ops:
  7.2 18.6 %copy-start = (f32[1024,8]{0,1:T(8,128)S(1)}, f32[1024,8]{0,1:T(8,128)}, u32[]{:S(2)}) copy-start(f32[1024,8]{0,1:T(8,128)} %param.26) | copy-start | bytes 98308
  7.2 116.3 %all-gather.4.cloned.1.call-start = ((), (), s32[]{:S(2)}) async-start(), calls=%async_computation.7 | async-start | bytes 3981312 | tf_op jit(solution)/shard_map/weights/all_gather | solution.py:1382
  18.5 124.4 %all-to-all-start = ((bf16[16,192,384]{2,1,0:T(8,128)(2,1)}), bf16[16,192,384]{2,1,0:T(8,128)(2,1)}, u32[]{:S(2)}, u32[]{:S(2)}) async-start(bf16[16,192,384]{2,1,0:T(8,128)(2,1)} %bitcast.4), calls=%async_computation | async-start | bytes 4718592 | tf_op jit(solution)/shard_map/weights/all_to_all | solution.py:1413
  25.7 268.5 %all-gather.6.cloned.1.call-start = ((), (), s32[]{:S(2)}) async-start(), calls=%async_computation.10 | async-start | bytes 7667712 | tf_op jit(solution)/shard_map/cotangents/all_gather | solution.py:1435
  43.5 94.0 %copy-start.41 = (f32[1024]{0:T(1024)}, f32[1024]{0:T(1024)S(1)}, u32[]{:S(2)}) copy-start(f32[1024]{0:T(1024)S(1)} %add_rsqrt_fusion) | copy-start | bytes 12292
  137.5 4.4 copy-start.33
  137.5 149.9 %copy-start.31 = (f32[1536]{0:T(1024)}, f32[1536]{0:T(1024)S(1)}, u32[]{:S(2)}) copy-start(f32[1536]{0:T(1024)S(1)} %get-tuple-element.130) | copy-start | bytes 18436
  137.6 4.4 copy-start.15
  137.6 4.4 copy-start.16
  142.9 15.0 %collective-permute-start.1 = (bf16[1024,256]{1,0:T(8,128)(2,1)S(1)}, bf16[1024,256]{1,0:T(8,128)(2,1)S(1)}, u32[]{:S(2)}, u32[]{:S(2)}) collective-permute-start(bf16[1024,256]{1,0:T(8,128)(2,1)S(1)} %pad_maximum_fusion.12), channel_id=1, source_target_pairs={{0,4},{4,0},{1,5},{5,1},{2,6},{6,2},{3,7},{7,3},{8,12},{12,8},{9,1... | collective-permute-start | bytes 1572872 | tf_op jit(solution)/shard_map/attention/ppermute | solution.py:1463
  148.0 136.8 %all-to-all-start.1 = ((bf16[24,192,384]{2,1,0:T(8,128)(2,1)}), bf16[24,192,384]{2,1,0:T(8,128)(2,1)}, u32[]{:S(2)}, u32[]{:S(2)}) async-start(bf16[24,192,384]{2,1,0:T(8,128)(2,1)} %bitcast.12), calls=%async_computation.1 | async-start | bytes 7077888 | tf_op jit(solution)/shard_map/weights/all_to_all | solution.py:1413
  152.5 604.6 %reduce-scatter.6.cloned.1.call-start = ((), (), s32[]{:S(2)}) async-start(), calls=%async_computation.8 | async-start | bytes 7077888 | tf_op jit(solution)/shard_map/expert_grads/reduce_scatter | solution.py:1544
  152.8 24.2 %copy-start.6 = (s32[1024,1]{1,0:T(8,128)}, s32[1024,1]{1,0:T(8,128)S(1)}, u32[]{:S(2)}) copy-start(s32[1024,1]{1,0:T(8,128)S(1)} %copy.116.doc_start_ref) | copy-start | bytes 12292
  153.0 24.1 %copy-start.4 = (bf16[1024,384]{1,0:T(8,128)(2,1)}, bf16[1024,384]{1,0:T(8,128)(2,1)S(1)}, u32[]{:S(2)}) copy-start(bf16[1024,384]{1,0:T(8,128)(2,1)S(1)} %slice.153.query_ref) | copy-start | bytes 2359300
  158.1 18.9 %copy-start.2 = (bf16[2048,256]{1,0:T(8,128)(2,1)}, bf16[2048,256]{1,0:T(8,128)(2,1)S(1)}, u32[]{:S(2)}) copy-start(bf16[2048,256]{1,0:T(8,128)(2,1)S(1)} %maximum_select_fusion.6.key_value_ref) | copy-start | bytes 3145732
  182.2 3.6 collective-permute-start.2
  182.3 102.5 %collective-permute-start = (bf16[8,2,192,384]{3,2,1,0:T(8,128)(2,1)}, bf16[8,2,192,384]{3,2,1,0:T(8,128)(2,1)}, u32[]{:S(2)}, u32[]{:S(2)}) collective-permute-start(bf16[8,2,192,384]{3,2,1,0:T(8,128)(2,1)} %bitcast.5.refs_4_), channel_id=1, source_target_pairs={{0,2},{1,3},{2,0},{3,1},{4,6},{5,7},{6,4},{7,5},{8,10},{9,11},{10,... | collective-permute-start | bytes 7077896 | tf_op jit(solution)/shard_map/attention/ppermute | solution.py:1469
  189.2 64.0 %collective-permute-start.3 = (bf16[256,1536]{1,0:T(8,128)(2,1)}, bf16[256,1536]{1,0:T(8,128)(2,1)}, u32[]{:S(2)}, u32[]{:S(2)}) collective-permute-start(bf16[256,1536]{1,0:T(8,128)(2,1)} %fusion.31), channel_id=1, source_target_pairs={{0,2},{1,3},{2,0},{3,1},{4,6},{5,7},{6,4},{7,5},{8,10},{9,11},{10,... | collective-permute-start | bytes 2359304 | tf_op jit(solution)/shard_map/attention/ppermute | solution.py:1361
  287.4 19.1 %copy-start.39 = (f32[256]{0:T(256)}, f32[256]{0:T(256)S(1)}, u32[]{:S(2)}) copy-start(f32[256]{0:T(256)S(1)} %get-tuple-element.134) | copy-start | bytes 3076
  287.4 19.1 %copy-start.36 = (f32[256]{0:T(256)}, f32[256]{0:T(256)S(1)}, u32[]{:S(2)}) copy-start(f32[256]{0:T(256)S(1)} %fusion.39) | copy-start | bytes 3076
  294.2 11.3 %collective-permute-start.4 = (bf16[8,256,1664]{2,1,0:T(8,128)(2,1)}, bf16[8,256,1664]{2,1,0:T(8,128)(2,1)}, u32[]{:S(2)}, u32[]{:S(2)}) collective-permute-start(bf16[8,256,1664]{2,1,0:T(8,128)(2,1)} %bitcast.122), channel_id=1, source_target_pairs={{0,1},{1,0},{2,3},{3,2},{4,5},{5,4},{6,7},{7,6},{8,9},{9,8},{10,11... | collective-permute-start | bytes 20447240 | tf_op jit(solution)/shard_map/exchange/ppermute | solution.py:1484
  589.9 3.9 copy-start.32
  589.9 3.9 copy-start.37
  596.1 21.8 %copy-start.19 = (f32[2048,128]{1,0:T(8,128)S(1)}, f32[2048,128]{1,0:T(8,128)}, u32[]{:S(2)}) copy-start(f32[2048,128]{1,0:T(8,128)} %copy-done.18) | copy-start | bytes 3145732
  596.1 19.9 %collective-permute-start.8 = (bf16[256,1536]{1,0:T(8,128)(2,1)S(1)}, bf16[256,1536]{1,0:T(8,128)(2,1)}, u32[]{:S(2)}, u32[]{:S(2)}) collective-permute-start(bf16[256,1536]{1,0:T(8,128)(2,1)S(1)} %fusion.45), channel_id=1, source_target_pairs={{0,2},{1,3},{2,0},{3,1},{4,6},{5,7},{6,4},{7,5},{8,10},{9,11},{10,... | collective-permute-start | bytes 2359304 | tf_op jit(solution)/shard_map/expert_grads/ppermute | solution.py:1365
  617.8 7.7 collective-permute-start.9
  617.9 79.3 %collective-permute-start.7 = (bf16[8,3,192,384]{3,2,1,0:T(8,128)(2,1)}, bf16[8,3,192,384]{3,2,1,0:T(8,128)(2,1)}, u32[]{:S(2)}, u32[]{:S(2)}) collective-permute-start(bf16[8,3,192,384]{3,2,1,0:T(8,128)(2,1)} %get-tuple-element.63), channel_id=1, source_target_pairs={{0,2},{1,3},{2,0},{3,1},{4,6},{5,7},{6,4},{7,5},{8,10},{9,11},{10,... | collective-permute-start | bytes 10616840 | tf_op jit(solution)/shard_map/expert_grads/ppermute | solution.py:1537
  619.4 99.1 %all-to-all-start.2 = ((bf16[16,192,384]{2,1,0:T(8,128)(2,1)}), bf16[16,192,384]{2,1,0:T(8,128)(2,1)}, u32[]{:S(2)}, u32[]{:S(2)}) async-start(bf16[16,192,384]{2,1,0:T(8,128)(2,1)} %bitcast.97), calls=%async_computation.3 | async-start | bytes 4718592 | tf_op jit(solution)/shard_map/expert_grads/all_to_all | solution.py:1534
  627.9 4.2 copy-start.21
  627.9 4.2 copy-start.3
  627.9 4.2 copy-start.5
  628.0 4.2 copy-start.7
  697.3 16.0 %collective-permute-start.10 = (bf16[1024,256]{1,0:T(8,128)(2,1)S(1)}, bf16[1024,256]{1,0:T(8,128)(2,1)S(1)}, u32[]{:S(2)}, u32[]{:S(2)}) collective-permute-start(bf16[1024,256]{1,0:T(8,128)(2,1)S(1)} %dynamic-slice_bitcast_fusion.2), channel_id=1, source_target_pairs={{0,4},{4,0},{1,5},{5,1},{2,6},{6,2},{3,7},{7,3},{8,12},{12,8},{9,1... | collective-permute-start | bytes 1572872 | tf_op jit(solution)/shard_map/attention_back/ppermute | solution.py:1575
  697.3 16.9 %copy-start.20 = (bf16[1536,1152]{1,0:T(8,128)(2,1)S(1)}, bf16[1536,1152]{1,0:T(8,128)(2,1)}, u32[]{:S(2)}) copy-start(bf16[1536,1152]{1,0:T(8,128)(2,1)} %all-gather.4.cloned.1.call-done) | copy-start | bytes 10616836
  721.1 9.6 %collective-permute-start.11 = (bf16[2,256,1536]{2,1,0:T(8,128)(2,1)}, bf16[2,256,1536]{2,1,0:T(8,128)(2,1)S(1)}, u32[]{:S(2)}, u32[]{:S(2)}) collective-permute-start(bf16[2,256,1536]{2,1,0:T(8,128)(2,1)} %dynamic-slice_bitcast_fusion), channel_id=1, source_target_pairs={{0,1},{1,0},{2,3},{3,2},{4,5},{5,4},{6,7},{7,6},{8,9},{9,8},{10,11... | collective-permute-start | bytes 4718600 | tf_op jit(solution)/shard_map/attention_back/ppermute | solution.py:1359
  721.1 4.7 copy-start.9
  721.1 144.9 %all-to-all-start.3 = ((bf16[24,192,384]{2,1,0:T(8,128)(2,1)}), bf16[24,192,384]{2,1,0:T(8,128)(2,1)}, u32[]{:S(2)}, u32[]{:S(2)}) async-start(bf16[24,192,384]{2,1,0:T(8,128)(2,1)} %bitcast.96), calls=%async_computation.5 | async-start | bytes 7077888 | tf_op jit(solution)/shard_map/attention_back/all_to_all | solution.py:1534
  725.8 137.1 %reduce-scatter.8.cloned.1.call-start = ((), (), s32[]{:S(2)}) async-start(), calls=%async_computation.9 | async-start | bytes 1327104 | tf_op jit(solution)/shard_map/attention_back/reduce_scatter | solution.py:1556
  730.7 204.4 %reduce-scatter.10.cloned.1.call-start = ((), (), s32[]{:S(2)}) async-start(), calls=%async_computation.11 | async-start | bytes 2654208
  732.9 20.0 %collective-permute-start.12 = (bf16[256,1536]{1,0:T(8,128)(2,1)S(1)}, bf16[256,1536]{1,0:T(8,128)(2,1)S(1)}, u32[]{:S(2)}, u32[]{:S(2)}) collective-permute-start(bf16[256,1536]{1,0:T(8,128)(2,1)S(1)} %fusion.32), channel_id=1, source_target_pairs={{0,2},{1,3},{2,0},{3,1},{4,6},{5,7},{6,4},{7,5},{8,10},{9,11},{10,... | collective-permute-start | bytes 2359304 | tf_op jit(solution)/shard_map/attention_back/ppermute | solution.py:1361
  770.2 94.3 %copy-start.23 = (bf16[256,1536]{1,0:T(8,128)(2,1)S(1)}, bf16[256,1536]{1,0:T(8,128)(2,1)}, u32[]{:S(2)}) copy-start(bf16[256,1536]{1,0:T(8,128)(2,1)} %get-tuple-element.144) | copy-start | bytes 2359300
  770.2 98.0 %collective-permute-start.13 = (bf16[256,1536]{1,0:T(8,128)(2,1)}, bf16[256,1536]{1,0:T(8,128)(2,1)}, u32[]{:S(2)}, u32[]{:S(2)}) collective-permute-start(bf16[256,1536]{1,0:T(8,128)(2,1)} %get-tuple-element.143), channel_id=1, source_target_pairs={{0,2},{1,3},{2,0},{3,1},{4,6},{5,7},{6,4},{7,5},{8,10},{9,11},{10,... | collective-permute-start | bytes 2359304 | tf_op jit(solution)/shard_map/attention_back/ppermute | solution.py:1365
  864.6 17.8 %collective-permute-start.5 = (bf16[256,1536]{1,0:T(8,128)(2,1)S(1)}, bf16[256,1536]{1,0:T(8,128)(2,1)}, u32[]{:S(2)}, u32[]{:S(2)}) collective-permute-start(bf16[256,1536]{1,0:T(8,128)(2,1)S(1)} %copy-done.23), channel_id=1, source_target_pairs={{0,2},{1,3},{2,0},{3,1},{4,6},{5,7},{6,4},{7,5},{8,10},{9,11},{10,... | collective-permute-start | bytes 2359304 | tf_op jit(solution)/shard_map/expert_grads/ppermute | solution.py:1365
  870.6 21.4 %collective-permute-start.14 = (bf16[2,1,256,1536]{3,2,1,0:T(8,128)(2,1)S(1)}, bf16[2,1,256,1536]{3,2,1,0:T(8,128)(2,1)S(1)}, u32[]{:S(2)}, u32[]{:S(2)}) collective-permute-start(bf16[2,1,256,1536]{3,2,1,0:T(8,128)(2,1)S(1)} %bitcast.104), channel_id=1, source_target_pairs={{0,1},{1,0},{2,3},{3,2},{4,5},{5,4},{6,7},{7,6},{8,9},{9,8},{10,11... | collective-permute-start | bytes 4718600 | tf_op jit(solution)/shard_map/attention_back/ppermute | solution.py:1369
  884.2 52.1 %collective-permute-start.6 = (bf16[2,1,256,1536]{3,2,1,0:T(8,128)(2,1)S(1)}, bf16[2,1,256,1536]{3,2,1,0:T(8,128)(2,1)}, u32[]{:S(2)}, u32[]{:S(2)}) collective-permute-start(bf16[2,1,256,1536]{3,2,1,0:T(8,128)(2,1)S(1)} %bitcast.102), channel_id=1, source_target_pairs={{0,1},{1,0},{2,3},{3,2},{4,5},{5,4},{6,7},{7,6},{8,9},{9,8},{10,11... | collective-permute-start | bytes 4718600 | tf_op jit(solution)/shard_map/expert_grads/ppermute | solution.py:1369
  936.2 3.8 collective-permute-start.15
  936.2 8.2 copy-start.1
  940.0 3.9 collective-permute-start.16
  (21 other events, 53.3 us)
Sparse Core Ops, SparseCore 0:
  13.2 110.2 all-gather.3
  125.7 168.5 all-gather.5
  588.3 168.7 reduce-scatter.5
  760.4 102.5 reduce-scatter.7
  866.8 68.1 reduce-scatter.9

commit v4 on v3

--- a/solution.py
+++ b/solution.py
@@ -613,18 +613,12 @@
 class Reduce:
     order = ((3, 1), (3, 0), (2, 1), (2, 0), (1, 1), (1, 0), (0, 1), (0, 0))
 
-    def __init__(self, place, arrays, terms, sums, sems):
-        self.place, self.terms, self.sums = place, terms, sums
+    def __init__(self, place, arrays, terms, term_sems, sums, base, sems):
+        self.place, self.terms, self.term_sems = place, terms, term_sems
+        self.sums, self.base = sums, base
         self.parts, self.from_core, self.from_pair, self.from_line = arrays
-        (
-            self.term_sems,
-            self.core_send,
-            self.core_recv,
-            self.pair_send,
-            self.pair_recv,
-            self.line_send,
-            self.line_recv,
-        ) = sems
+        self.core_send, self.core_recv, self.pair_send, self.pair_recv = sems[:4]
+        self.line_send, self.line_recv = sems[4:]
 
     def core_copy(self, here, source):
         return remote(
@@ -640,7 +634,7 @@
 
     def pair_copy(self, at, slot):
         return remote(
-            self.sums.at[slot],
+            self.sums.at[self.base + slot],
             self.from_pair.at[at],
             self.pair_send.at[at],
             self.pair_recv.at[at],
@@ -650,7 +644,7 @@
     def line_copy(self, at, side, distance):
         slot = self.place.line if distance == 1 and side == 1 else at
         return remote(
-            self.sums.at[2 + (side + 1) // 2],
+            self.sums.at[self.base + 2 + (side + 1) // 2],
             self.from_line.at[slot],
             self.line_send.at[at],
             self.line_recv.at[slot],
@@ -686,7 +680,7 @@
             total = terms[0, here, :].astype(F32)
             for i in range(1, len(sources)):
                 total += terms[i, here, :].astype(F32)
-            self.sums[slot, here, :] = total.astype(BF16)
+            self.sums[self.base + slot, here, :] = total.astype(BF16)
 
     def cross(self, rank):
         place = self.place
@@ -730,15 +724,13 @@
                 self.add_up(sources, 2 + (side + 1) // 2)
                 self.line_copy(at, side, distance).start()
 
-    def tick(self, number):
+    def tick(self, number, late):
         line = self.place.line
         for rank in range(line):
-
-            @pl.when(number == 2 * (line - rank) - 1)
-            def _():
-                self.cross(rank)
-                if rank + 1 < line:
-                    self.advance(rank + 1)
+            when = 2 * (line - rank) - 1
+            pl.when(number == when)(partial(self.cross, rank))
+            if rank + 1 < line:
+                pl.when(number == when + late)(partial(self.advance, rank + 1))
 
     def finish(self, result, sem):
         place = self.place
@@ -760,7 +752,7 @@
             ],
             0,
         )
-        copy = pltpu.make_async_copy(self.sums.at[0], result, sem)
+        copy = pltpu.make_async_copy(self.sums.at[self.base], result, sem)
         copy.start()
         copy.wait()
         for side in (-1, 1):
@@ -781,14 +773,14 @@
     tokens_in, cotangent_own, cotangent_other, shares_ref, own_hbm, other_hbm = take(6)
     exchanged = take(1)
     if not gathers:
-        out_before, grad_before = take(2)
-        out_hbm, grad_piece, grad_own, grad_other, out_core, received = take(6)
-        arrays = take(4)
+        before = take(1)
+        grad_piece, out_piece, grad_own, grad_other, received = take(5)
+        grad_arrays, out_arrays = take(4), take(4)
         tokens_hbm = tokens_in
     else:
-        out_hbm, grad_hbm, grad_own, grad_other, tokens_hbm, received = take(6)
+        parts_hbm, grad_own, grad_other, tokens_hbm, received = take(5)
     weights, grads, tokens_buf, cotangent_buf, inner_low, grad_low = take(6)
-    out_buf, grad_buf, stage, load_sems, store_sems, row_sems, part_sems, exchange_sems = take(8)
+    both_buf, stage, load_sems, store_sems, row_sems, part_sems, exchange_sems = take(7)
 
     expert_count, model_width, all_units = weights.shape
     hidden_units = all_units // 3
@@ -800,10 +792,12 @@
     if gathers:
         mover = Gather(place, tokens_hbm, take(4))
     else:
-        before_buf, terms, sums = take(3)
-        core_out_send, core_out_recv = take(2)
-        mover = Reduce(place, arrays, terms, sums, take(7))
-    order = mover.order
+        before_buf, terms, sums, term_sems = take(4)
+        movers = [
+            Reduce(place, arrays, terms, term_sems, sums, 4 * number, take(6))
+            for number, arrays in enumerate((grad_arrays, out_arrays))
+        ]
+    order = mover.order if gathers else Reduce.order
 
     place.meet()
     exchange = remote(
@@ -831,8 +825,7 @@
             (cotangent_other.at[here, :, lanes], cotangent_buf.at[slot, second_rows, :]),
         ]
         if not gathers:
-            pairs.append((out_before.at[here], before_buf.at[slot, 0]))
-            pairs.append((grad_before.at[here], before_buf.at[slot, 1]))
+            pairs.append((before.at[here], before_buf.at[slot]))
         return [
             pltpu.make_async_copy(source, target, row_sems.at[slot, i])
             for i, (source, target) in enumerate(pairs)
@@ -848,30 +841,26 @@
     for copy in weight_loads:
         copy.wait()
 
-    def out_core_copy(step):
+    halves = [pl.ds(number * model_width, model_width) for number in range(2)]
+
+    def core_copies(step, slot):
         here = place.block(order, step)
-        return remote(
-            out_buf.at[second_rows],
-            out_core.at[here],
-            core_out_send.at[here],
-            core_out_recv.at[here],
-            place.sibling,
-        )
-
-    def grad_core_copy(step, slot):
-        return mover.core_copy(place.block(order, step), grad_buf.at[slot, second_rows, :])
+        return [
+            mover.core_copy(here, both_buf.at[slot, second_rows, lanes])
+            for mover, lanes in zip(movers, halves)
+        ]
 
     def part_copies(step, slot):
         here = place.block(order, step)
         if gathers:
-            pairs = [(out_buf, out_hbm.at[here]), (grad_buf.at[slot], grad_hbm.at[here])]
+            pairs = [(both_buf.at[slot], parts_hbm.at[here])]
         else:
             pairs = [
-                (out_buf.at[first_rows], out_hbm.at[here]),
-                (grad_buf.at[slot, first_rows, :], arrays[0].at[here]),
+                (both_buf.at[slot, first_rows, lanes], mover.parts.at[here])
+                for mover, lanes in zip(movers, halves)
             ]
         return [
-            pltpu.make_async_copy(source, target, part_sems.at[i])
+            pltpu.make_async_copy(source, target, part_sems.at[slot, i])
             for i, (source, target) in enumerate(pairs)
         ]
 
@@ -909,16 +898,17 @@
         def _():
             for copy in part_copies(step - 1, 1 - slot):
                 copy.wait()
-            if not gathers:
-                out_core_copy(step - 1).wait_send()
-
-        mover.tick(step)
-
-        if not gathers:
+
+        if gathers:
+            mover.tick(step)
+        else:
+            for late, reducer in enumerate(movers):
+                reducer.tick(step, late)
 
             @pl.when(step >= 2)
             def _():
-                grad_core_copy(step - 2, slot).wait_send()
+                for copy in core_copies(step - 2, slot):
+                    copy.wait_send()
 
         @pl.loop(0, model_width // chunk)
         def _(number):
@@ -928,11 +918,11 @@
 
             cols = pl.ds(pl.multiple_of(number * chunk, chunk), chunk)
 
-            def total_of(kind, lows, lanes):
+            def total_of(lows, lanes, target):
                 if gathers:
                     total = jnp.zeros((2 * rows, chunk), F32)
                 else:
-                    total = before_buf[slot, kind, :, cols].astype(F32)
+                    total = before_buf[slot, :, target].astype(F32)
                 for expert in range(expert_count):
                     total += lax.dot_general(
                         lows[expert],
@@ -940,24 +930,25 @@
                         LAST_LAST,
                         preferred_element_type=F32,
                     )
-                return total.astype(BF16)
-
-            out_buf[:, cols] = total_of(0, inner_low, pl.ds(2 * hidden_units, hidden_units))
-            grad_buf[slot, :, cols] = total_of(1, grad_low, pl.ds(0, 2 * hidden_units))
-
+                both_buf[slot, :, target] = total.astype(BF16)
+
+            beyond = pl.ds(pl.multiple_of(model_width + number * chunk, chunk), chunk)
+            total_of(grad_low, pl.ds(0, 2 * hidden_units), cols)
+            total_of(inner_low, pl.ds(2 * hidden_units, hidden_units), beyond)
+
+        if not gathers:
+            for copy in core_copies(step, slot):
+                copy.start()
         for copy in part_copies(step, slot):
             copy.start()
-        if not gathers:
-            out_core_copy(step).start()
-            grad_core_copy(step, slot).start()
 
     last = (steps - 1) % 2
     for copy in part_copies(steps - 1, last):
         copy.wait()
     if not gathers:
-        out_core_copy(steps - 1).wait_send()
-        grad_core_copy(steps - 2, 1 - last).wait_send()
-        grad_core_copy(steps - 1, last).wait_send()
+        for copy in core_copies(steps - 2, 1 - last) + core_copies(steps - 1, last):
+            copy.wait_send()
+        movers[1].advance(1)
 
     sources, _, slice_rows, _ = own_hbm.shape
 
@@ -995,9 +986,8 @@
     if gathers:
         mover.finish()
     else:
-        for step in range(steps):
-            out_core_copy(step).wait_recv()
-        mover.finish(grad_piece, row_sems.at[0, 0])
+        for number, result in enumerate((grad_piece, out_piece)):
+            movers[number].finish(result, row_sems.at[0, number])
 
 
 def expert_call(operands, own, shares, line, rows, model_width, gathers, collective_id, chunk=512):
@@ -1013,8 +1003,7 @@
 
     if gathers:
         out_shape = [
-            low(blocks, 2 * rows, model_width),
-            low(blocks, 2 * rows, model_width),
+            low(blocks, 2 * rows, 2 * model_width),
             low(*own.shape),
             low(*own.shape),
             low(blocks, 2, rows, model_width),
@@ -1023,24 +1012,25 @@
         own_scratch = [dma((blocks, 2)), dma((line, 2)), dma((line,)), dma((blocks,))]
     else:
         out_shape = [
-            low(blocks, rows, model_width),
+            low(rows, model_width),
             low(rows, model_width),
             low(*own.shape),
             low(*own.shape),
-            low(blocks, rows, model_width),
             low(*operands[6].shape),
+        ]
+        out_shape += 2 * [
             low(blocks, rows, model_width),
             low(blocks, rows, model_width),
             low(line, rows, model_width),
             low(line + 1, rows, model_width),
         ]
         own_scratch = [
-            pltpu.VMEM((2, 2, 2 * rows, model_width), BF16),
+            pltpu.VMEM((2, 2 * rows, 2 * model_width), BF16),
             pltpu.VMEM((5, rows, model_width), BF16),
-            pltpu.VMEM((4, rows, model_width), BF16),
-            dma((blocks,)),
-            dma((blocks,)),
+            pltpu.VMEM((8, rows, model_width), BF16),
             dma((5,)),
+        ]
+        own_scratch += 2 * [
             dma((blocks,)),
             dma((blocks,)),
             dma((line,)),
@@ -1062,13 +1052,12 @@
             pltpu.VMEM((2, 2 * rows, model_width), BF16),
             pltpu.VMEM((expert_count, 2 * rows, hidden_units), BF16),
             pltpu.VMEM((expert_count, 2 * rows, 2 * hidden_units), BF16),
-            pltpu.VMEM((2 * rows, model_width), BF16),
-            pltpu.VMEM((2, 2 * rows, model_width), BF16),
+            pltpu.VMEM((2, 2 * rows, 2 * model_width), BF16),
             pltpu.VMEM((2, 2, slice_rows, lanes), BF16),
             dma((sources, 2, 3)),
             dma((2, 2)),
-            dma((2, 6)),
-            dma((2,)),
+            dma((2, 5)),
+            dma((2, 2)),
             dma((2,)),
         ]
         + own_scratch,
@@ -1079,7 +1068,7 @@
             flops=flops, bytes_accessed=80 * 2**20, transcendentals=0
         ),
     )(*operands)
-    return results[:6]
+    return results[:5]
 
 
 def experts_gathering(piece, cotangents, shares, own, other, exchanged, line):
@@ -1089,10 +1078,10 @@
 
 
 def experts_reducing(
-    tokens, cotangents, shares, own, other, exchanged, out_parts, grad_parts, line
+    tokens, cotangents, shares, own, other, exchanged, parts, line
 ):
     _, _, rows, model_width = tokens.shape
-    operands = (tokens, *cotangents, shares, own, other, exchanged, out_parts, grad_parts)
+    operands = (tokens, *cotangents, shares, own, other, exchanged, parts)
     return expert_call(operands, own, shares, line, rows, model_width, False, 2)
 
 
@@ -1499,7 +1488,7 @@
     with jax.named_scope("experts"):
         line = groups // 2
         cotangents = (cotangent_own, cotangent_other)
-        out_parts, grad_parts, grad_own_first, grad_other_first, tokens, others_second = (
+        parts, grad_own_first, grad_other_first, tokens, others_second = (
             experts_gathering(
                 normed_ffn.astype(BF16),
                 cotangents,
@@ -1510,7 +1499,7 @@
                 line,
             )
         )
-        out_own, grad_second, grad_own_second, grad_other_second, out_other, received_first = (
+        grad_second, out_piece, grad_own_second, grad_other_second, received_first = (
             experts_reducing(
                 tokens,
                 cotangents,
@@ -1518,8 +1507,7 @@
                 owned_second,
                 others_second,
                 grad_other_first,
-                out_parts,
-                grad_parts,
+                parts,
                 line,
             )
         )
@@ -1540,13 +1528,6 @@
         grad_hidden_norm, grad_gain_ffn_local = ffn_norm_back(grad_second.astype(F32))
         grad_hidden = cotangent_piece.astype(F32) + grad_hidden_norm
         grad_hidden_low = gather_over_tensor(grad_hidden.astype(BF16))
-        out_sum = (out_own.astype(F32) + out_other.astype(F32)).astype(BF16)
-        out_piece = lax.psum_scatter(
-            out_sum.reshape(groups * piece_rows, model_width),
-            GROUP,
-            scatter_dimension=0,
-            tiled=True,
-        )
         output = gather_over_tensor((hidden + out_piece.astype(F32)).astype(BF16))
 
     with jax.named_scope("attention_back"):
@@ -1567,9 +1548,6 @@
             turns,
             own_turns,
         )
-        received_second, grad_key_value = lax.optimization_barrier(
-            (received_second, grad_key_value)
-        )
         total_second = added(grad_own_second, received_second)
         grad_key_value = grad_key_value.reshape(2, row_count, -1)
         received = lax.ppermute(pick(grad_key_value, 0, 1 - context_rank), CONTEXT, pair)
@@ -1580,31 +1558,34 @@
         grad_first_part = lax.dot_general(
             grad_projected, qkv_weight, LAST_LAST, preferred_element_type=F32
         )
-        returned_first, total_second, grad_first_part = lax.optimization_barrier(
-            (returned_first, total_second, grad_first_part)
+        grad_qkv_local = lax.dot_general(
+            first_normalized, grad_projected, FIRST_FIRST, preferred_element_type=F32
+        ).astype(BF16)
+        returned_first, total_second, grad_out_transposed, grad_first_part, grad_qkv_local = (
+            lax.optimization_barrier(
+                (returned_first, total_second, grad_out_transposed, grad_first_part, grad_qkv_local)
+            )
         )
         returned_second = returned(total_second)
         grad_first = sum_over_tensor(grad_first_part)
-        out_piece, grad_first = lax.optimization_barrier((out_piece, grad_first))
         _, attn_norm_back = jax.vjp(
             rms_scale, own_piece(residual_in).astype(F32), gain_attn_float
         )
         grad_input_norm, grad_gain_attn_local = attn_norm_back(grad_first)
         grad_input = gather_over_tensor((grad_hidden + grad_input_norm).astype(BF16))
-        grad_qkv_local = lax.dot_general(
-            first_normalized, grad_projected, FIRST_FIRST, preferred_element_type=F32
-        )
         grad_qkv = lax.psum_scatter(
-            jnp.concatenate(
-                [grad_qkv_local, padded_columns(grad_gain_attn_local, grad_gain_ffn_local)], axis=1
-            ).astype(BF16),
-            GROUP,
-            scatter_dimension=0,
-            tiled=True,
+            grad_qkv_local, GROUP, scatter_dimension=0, tiled=True
         ).astype(F32)
-        gains = grad_qkv[:, qkv_cols : qkv_cols + 2]
-        gains = gains + lax.ppermute(gains, TENSOR, sibling)
-        gains = gains + lax.ppermute(gains, TENSOR, across)
+        gains = jnp.stack([grad_gain_attn_local, grad_gain_ffn_local])
+        for axis, step, size in (
+            (TENSOR, 1, tensor_size),
+            (TENSOR, 2, tensor_size),
+            (CONTEXT, 1, 2),
+            (SHARD, 1, groups // 2),
+            (SHARD, 2, groups // 2),
+        ):
+            gains = gains + lax.ppermute(gains, axis, [(i, i ^ step) for i in range(size)])
+        gains = lax.dynamic_slice_in_dim(gains, group_rank * slice_rows, slice_rows, axis=1)
 
     def whole(first, last, turned):
         parts = [
@@ -1618,12 +1599,12 @@
     return (
         output,
         grad_input,
-        gains[:, 0],
+        gains[0],
         grad_qkv[:, :query_cols],
         grad_qkv[:, query_cols:rotated_cols],
         grad_qkv[:, rotated_cols:qkv_cols],
         grad_out_transposed.astype(F32).T,
-        gains[:, 1],
+        gains[1],
         whole(0, units, False),
         whole(units, 2 * units, False),
         whole(2 * units, 3 * units, True),

time: 958 us -> 909 us (0.949)
  waiting for transfers between devices: 415 us -> 338 us
  Pallas kernels: 319 us -> 352 us
  other arithmetic: 80.2 us -> 69.1 us
    reduce_scatter x1, waiting for transfers between devices: 88.9 us -> 16.7 us  [expert_plan(): lax.psum_scatter(grad_out_local.astype(BF16), GROUP, scatter_dimension=0,...]
    unnamed x6 -> x4, waiting for transfers between devices: 41.2 us -> 0.07 us
    pallas_call x2, Pallas kernels: 268 us -> 302 us  [expert_call(): pl.pallas_call(partial(expert_kernel, line=line, chunk=chunk, gathers=gat...]
    ppermute x1, waiting for transfers between devices: 33.4 us -> 0.01 us  [expert_plan(): received_second = lax.ppermute(grad_other_second, TENSOR, across)]
    ppermute x2 -> x5, waiting for transfers between devices: 0.01 us -> 21.8 us  [expert_plan(): lax.ppermute(gains, axis, [(i, i ^ step) for i in range(size)])]
    reduce_scatter x1, waiting for transfers between devices: 4.08 us -> 23.4 us  [expert_plan(): lax.psum_scatter(grad_qkv_local, GROUP, scatter_dimension=0, tiled=True)]
    ppermute x3, waiting for transfers between devices: 29.9 us -> 47 us  [gather_over_tensor(): other = lax.ppermute(piece, TENSOR, across)]
    unnamed x97 -> x94, local copies, waits for them, and re-layouts: 22.9 us -> 14.3 us
  transfers between devices with their start and end apart: 26 -> 28, of which waited for: 15 -> 17; matrix products, arithmetic and copies ran while one was open for 14% -> 12% of each run, Pallas kernels for 5% -> 6%
where the time goes in v4:
time: 909 us; the launch traced here: 901 us
  Pallas kernels  352 us (39%)
  waiting for transfers between devices  338 us (37%)
  other arithmetic  69.1 us (8%)
  local copies, waits for them, and re-layouts  58.9 us (6%)
  starting transfers between devices  43.5 us (5%)
  matrix products  24.9 us (3%)
  between operations  15.2 us (2%)
    pallas_call x2, Pallas kernels, expert_call(): pl.pallas_call(partial(expert_kernel, line=line, chunk=chunk, gathers=gat...  302 us
    ppermute x2, waiting for transfers between devices, sum_over_tensor(): lax.ppermute(pick(half, 0, 1 - chip_half).astype(BF16), TENSOR, across)  81 us
    all_gather x1, waiting for transfers between devices, expert_plan(): lax.all_gather(jnp.concatenate([query_weight, key_projection_weight, valu...  80.3 us
    ppermute x3, waiting for transfers between devices, gather_over_tensor(): other = lax.ppermute(piece, TENSOR, across)  47 us
    pallas_call x1, Pallas kernels, attention_backward(): pl.pallas_call(partial(attention_backward_kernel, group_size=group_size,...  31.6 us
    all_to_all x2, waiting for transfers between devices, expert_slices(): owned = lax.all_to_all(slices, GROUP, 0, 0, tiled=True)  29.9 us
    reduce_scatter x1, waiting for transfers between devices, expert_plan(): lax.psum_scatter(grad_qkv_local, GROUP, scatter_dimension=0, tiled=True)  23.4 us
    ppermute x5, waiting for transfers between devices, expert_plan(): lax.ppermute(gains, axis, [(i, i ^ step) for i in range(size)])  21.8 us
  transfers between devices with their start and end apart: 28, of which 17 were waited for; matrix products, arithmetic and copies ran while one was open for 12% of the time, Pallas kernels for 6%

profile of v4, /device:TPU:0, one launch (start us, length us, event | category | flops | bytes accessed | tf_op | source)
XLA Modules:
  0.0 901.3 jit_solution(3082879005022256763)
XLA Ops:
  18.5 7.3 all-to-all-start
  29.4 3.7 multiply_cosine_fusion
  39.4 3.0 copy.103
  43.2 80.3 %all-gather.4.cloned.1.call-done = bf16[1536,1152]{1,0:T(8,128)(2,1)} async-done(((bf16[192,1152]{1,0:T(8,128)(2,1)}), bf16[1536,1152]{1,0:T(8,128)(2,1)}) %all-gather.4.cloned.1.call-update) | async-done | bytes 3538960 | tf_op jit(solution)/shard_map/weights/all_gather | solution.py:1371
  123.5 2.7 slice.139
  126.1 2.6 copy.120
  131.5 2.6 copy.98
  137.6 4.3 fusion.3
  148.0 4.7 all-to-all-start.1
  153.1 4.3 collective-permute-done.1
  157.7 18.7 %attention.1 = (bf16[1024,384]{1,0:T(8,128)(2,1)S(1)}, f32[4,2,768,1]{3,2,1,0:T(8,128)}) custom-call(s32[1]{0:T(128)} %bitcast.14.first_ref, bf16[1024,384]{1,0:T(8,128)(2,1)S(1)} %slice.149.query_ref, bf16[2048,256]{1,0:T(8,128)(2,1)S(1)} %maximum_select_fusion.6.key_value_ref, s32[1024,1]{1,0:T(8,128)S(1)} %copy.104.doc_start_ref), custom_call_target="tpu_custom_call" | custom-call | flops 16106127360 | bytes 4194304 | tf_op jit(solution)/shard_map/attention/pallas_call | solution.py:1232
  176.4 3.4 convolution_convert_fusion
  190.1 62.3 %collective-permute-done.3 = bf16[256,1536]{1,0:T(8,128)(2,1)} collective-permute-done((bf16[256,1536]{1,0:T(8,128)(2,1)}, bf16[256,1536]{1,0:T(8,128)(2,1)}, u32[]{:S(2)}, u32[]{:S(2)}) %collective-permute-start.3) | collective-permute-done | bytes 786464 | tf_op jit(solution)/shard_map/attention/ppermute | solution.py:1350
  252.5 2.5 bitcast_add_fusion.1
  255.0 29.9 %all-to-all-done.1 = bf16[24,192,384]{2,1,0:T(8,128)(2,1)} async-done(((bf16[24,192,384]{2,1,0:T(8,128)(2,1)}), bf16[24,192,384]{2,1,0:T(8,128)(2,1)}, u32[]{:S(2)}, u32[]{:S(2)}) %all-to-all-start.1) | async-done | bytes 3538976 | tf_op jit(solution)/shard_map/weights/all_to_all | solution.py:1402
  284.8 2.6 multiply_reduce_fusion
  289.6 4.6 all-gather.6.cloned.1.call-done
  295.4 10.1 %collective-permute-done.4.refs_2_ = bf16[8,256,1664]{2,1,0:T(8,128)(2,1)} collective-permute-done((bf16[8,256,1664]{2,1,0:T(8,128)(2,1)}, bf16[8,256,1664]{2,1,0:T(8,128)(2,1)}, u32[]{:S(2)}, u32[]{:S(2)}) %collective-permute-start.4) | collective-permute-done | bytes 6815776 | tf_op jit(solution)/shard_map/exchange/ppermute | solution.py:1473
  310.8 128.2 %experts.2 = (bf16[8,512,3072]{2,1,0:T(8,128)(2,1)}, bf16[8,2,192,384]{3,2,1,0:T(8,128)(2,1)}, bf16[8,2,192,384]{3,2,1,0:T(8,128)(2,1)}, bf16[8,2,256,1536]{3,2,1,0:T(8,128)(2,1)}, bf16[8,3,192,384]{3,2,1,0:T(8,128)(2,1)}) custom-call(bf16[256,1536]{1,0:T(8,128)(2,1)} %multiply_multiply_fusion.refs_0_, bf16[8,256,1664]{2,1,0:T(8,128)(2,1)} %bitcast.125, ...), custom_call_target="tpu_custom_call" | custom-call | flops 57982058496 | bytes 83886080 | tf_op jit(solution)/shard_map/experts/pallas_call | solution.py:1043
  438.9 173.5 %experts.3 = (bf16[256,1536]{1,0:T(8,128)(2,1)}, bf16[256,1536]{1,0:T(8,128)(2,1)}, bf16[8,3,192,384]{3,2,1,0:T(8,128)(2,1)}, bf16[8,3,192,384]{3,2,1,0:T(8,128)...) custom-call(bf16[8,2,256,1536]{3,2,1,0:T(8,128)(2,1)} %get-tuple-ele, ...), custom_call_target="tpu_custom_call" | custom-call | flops 86973087744 | bytes 83886080 | tf_op jit(solution)/shard_map/experts/pallas_call | solution.py:1043
  612.5 3.9 add_convert_fusion.1
  619.3 16.4 %collective-permute-done.8 = bf16[256,1536]{1,0:T(8,128)(2,1)} collective-permute-done((bf16[256,1536]{1,0:T(8,128)(2,1)S(1)}, bf16[256,1536]{1,0:T(8,128)(2,1)}, u32[]{:S(2)}, u32[]{:S(2)}) %collective-permute-start.8) | collective-permute-done | bytes 786464 | tf_op jit(solution)/shard_map/expert_grads/ppermute | solution.py:1354
  635.8 2.9 maximum_select_fusion.4
  639.1 9.8 %all-to-all-start.2 = ((bf16[16,192,384]{2,1,0:T(8,128)(2,1)}), bf16[16,192,384]{2,1,0:T(8,128)(2,1)}, u32[]{:S(2)}, u32[]{:S(2)}) async-start(bf16[16,192,384]{2,1,0:T(8,128)(2,1)} %bitcast.27), calls=%async_computation.2 | async-start | bytes 4718592 | tf_op jit(solution)/shard_map/expert_grads/all_to_all | solution.py:1522
  649.0 3.6 maximum_select_fusion.1
  654.3 2.9 convolution_convert_fusion.2
  657.2 4.1 convolution_convert_fusion.3.grad_ref
  661.4 31.6 %attention_back.1 = (bf16[1024,384]{1,0:T(8,128)(2,1)S(1)}, bf16[2048,256]{1,0:T(8,128)(2,1)S(1)}) custom-call(s32[1]{0:T(128)} %bitcast.14.first_ref, bf16[1024,384]{1,0:T(8,128)(2,1)S(1)} %copy-done.5, bf16[2048,256]{1,0:T(8,128)(2,1)S(1)} %copy-done.3, s32[1024,1]{1,0:T(8,128)S(1)} %copy-done.7, f32[4,2,768,1]{3,2,1,0:T(8,128)} %get-tuple-element.59.lse_ref, ...), custom_call_target="tpu_custom_call" | custom-call | flops 40265318400 | bytes 8388608 | tf_op jit(solution)/shard_map/attention_back/pallas_call | solution.py:1261
  695.8 16.7 %collective-permute-done.10 = bf16[1024,256]{1,0:T(8,128)(2,1)S(1)} collective-permute-done((bf16[1024,256]{1,0:T(8,128)(2,1)}, bf16[1024,256]{1,0:T(8,128)(2,1)S(1)}, u32[]{:S(2)}, u32[]{:S(2)}) %collective-permute-start.10) | collective-permute-done | bytes 524320 | tf_op jit(solution)/shard_map/attention_back/ppermute | solution.py:1553
  712.7 6.0 fusion.30
  718.7 4.2 convolution_convert_fusion.1
  722.9 6.0 add_convert_fusion
  728.9 16.7 %reduce-scatter.3.cloned.1.call-done = bf16[192,384]{1,0:T(8,128)(2,1)} async-done(((bf16[1536,384]{1,0:T(8,128)(2,1)}), bf16[192,384]{1,0:T(8,128)(2,1)}) %reduce-scatter.3.cloned.1.call-update) | async-done | bytes 147472 | tf_op jit(solution)/shard_map/attention_back/reduce_scatter | solution.py:1537
  745.6 2.7 dynamic-slice_bitcast_fusion
  748.3 4.5 all-to-all-start.3
  758.9 18.6 %collective-permute-done.12 = bf16[256,1536]{1,0:T(8,128)(2,1)S(1)} collective-permute-done((bf16[256,1536]{1,0:T(8,128)(2,1)}, bf16[256,1536]{1,0:T(8,128)(2,1)S(1)}, u32[]{:S(2)}, u32[]{:S(2)}) %collective-permute-start.12) | collective-permute-done | bytes 786464 | tf_op jit(solution)/shard_map/attention_back/ppermute | solution.py:1350
  779.8 2.7 fusion.15
  787.5 15.5 %collective-permute-done.13 = bf16[256,1536]{1,0:T(8,128)(2,1)S(1)} collective-permute-done((bf16[256,1536]{1,0:T(8,128)(2,1)S(1)}, bf16[256,1536]{1,0:T(8,128)(2,1)S(1)}, u32[]{:S(2)}, u32[]{:S(2)}) %collective-permute-start.13) | collective-permute-done | bytes 786464 | tf_op jit(solution)/shard_map/attention_back/ppermute | solution.py:1354
  803.7 15.1 %collective-permute-done.5 = bf16[256,1536]{1,0:T(8,128)(2,1)S(1)} collective-permute-done((bf16[256,1536]{1,0:T(8,128)(2,1)S(1)}, bf16[256,1536]{1,0:T(8,128)(2,1)S(1)}, u32[]{:S(2)}, u32[]{:S(2)}) %collective-permute-start.5) | collective-permute-done | bytes 786464 | tf_op jit(solution)/shard_map/expert_grads/ppermute | solution.py:1354
  820.9 2.5 collective-permute-done.17
  824.7 3.1 slice_bitcast_fusion.1
  831.0 18.2 %collective-permute-done.19 = f32[2,1536]{1,0:T(2,128)S(1)} collective-permute-done((f32[2,1536]{1,0:T(2,128)S(1)}, f32[2,1536]{1,0:T(2,128)S(1)}, u32[]{:S(2)}, u32[]{:S(2)}) %collective-permute-start.19) | collective-permute-done | bytes 12320 | tf_op jit(solution)/shard_map/attention_back/ppermute | solution.py:1587
  849.8 23.4 %reduce-scatter.5.cloned.1.call-done = bf16[192,640]{1,0:T(8,128)(2,1)} async-done(((bf16[1536,640]{1,0:T(8,128)(2,1)}), bf16[192,640]{1,0:T(8,128)(2,1)}) %reduce-scatter.5.cloned.1.call-update) | async-done | bytes 245776 | tf_op jit(solution)/shard_map/attention_back/reduce_scatter | solution.py:1576
  876.4 3.8 maximum_select_fusion.2
  880.2 3.7 maximum_select_fusion
  886.4 2.5 bitcast_convert_fusion
  889.3 2.5 bitcast_convert_fusion.1
  891.8 2.5 bitcast_convert_fusion.2
  (220 shorter events, 88.6 us)
Async XLA Ops:
  7.2 18.6 %copy-start = (f32[1024,8]{0,1:T(8,128)S(1)}, f32[1024,8]{0,1:T(8,128)}, u32[]{:S(2)}) copy-start(f32[1024,8]{0,1:T(8,128)} %param.26) | copy-start | bytes 98308
  7.2 116.3 %all-gather.4.cloned.1.call-start = ((), (), s32[]{:S(2)}) async-start(), calls=%async_computation.6 | async-start | bytes 3981312 | tf_op jit(solution)/shard_map/weights/all_gather | solution.py:1371
  18.5 124.4 %all-to-all-start = ((bf16[16,192,384]{2,1,0:T(8,128)(2,1)}), bf16[16,192,384]{2,1,0:T(8,128)(2,1)}, u32[]{:S(2)}, u32[]{:S(2)}) async-start(bf16[16,192,384]{2,1,0:T(8,128)(2,1)} %bitcast.4), calls=%async_computation | async-start | bytes 4718592 | tf_op jit(solution)/shard_map/weights/all_to_all | solution.py:1402
  25.7 268.5 %all-gather.6.cloned.1.call-start = ((), (), s32[]{:S(2)}) async-start(), calls=%async_computation.9 | async-start | bytes 7667712 | tf_op jit(solution)/shard_map/cotangents/all_gather | solution.py:1424
  43.2 94.4 %copy-start.42 = (f32[1024]{0:T(1024)}, f32[1024]{0:T(1024)S(1)}, u32[]{:S(2)}) copy-start(f32[1024]{0:T(1024)S(1)} %add_rsqrt_fusion) | copy-start | bytes 12292
  137.5 4.4 copy-start.34
  137.5 149.9 %copy-start.31 = (f32[1536]{0:T(1024)}, f32[1536]{0:T(1024)S(1)}, u32[]{:S(2)}) copy-start(f32[1536]{0:T(1024)S(1)} %get-tuple-element.69) | copy-start | bytes 18436
  137.5 4.4 copy-start.17
  137.6 4.4 copy-start.18
  142.9 14.5 %collective-permute-start.1 = (bf16[1024,256]{1,0:T(8,128)(2,1)S(1)}, bf16[1024,256]{1,0:T(8,128)(2,1)S(1)}, u32[]{:S(2)}, u32[]{:S(2)}) collective-permute-start(bf16[1024,256]{1,0:T(8,128)(2,1)S(1)} %pad_maximum_fusion.11), channel_id=1, source_target_pairs={{0,4},{4,0},{1,5},{5,1},{2,6},{6,2},{3,7},{7,3},{8,12},{12,8},{9,1... | collective-permute-start | bytes 1572872 | tf_op jit(solution)/shard_map/attention/ppermute | solution.py:1452
  148.0 136.9 %all-to-all-start.1 = ((bf16[24,192,384]{2,1,0:T(8,128)(2,1)}), bf16[24,192,384]{2,1,0:T(8,128)(2,1)}, u32[]{:S(2)}, u32[]{:S(2)}) async-start(bf16[24,192,384]{2,1,0:T(8,128)(2,1)} %bitcast.99), calls=%async_computation.1 | async-start | bytes 7077888 | tf_op jit(solution)/shard_map/weights/all_to_all | solution.py:1402
  153.0 23.4 %copy-start.6 = (s32[1024,1]{1,0:T(8,128)}, s32[1024,1]{1,0:T(8,128)S(1)}, u32[]{:S(2)}) copy-start(s32[1024,1]{1,0:T(8,128)S(1)} %copy.104.doc_start_ref) | copy-start | bytes 12292
  153.1 23.3 %copy-start.4 = (bf16[1024,384]{1,0:T(8,128)(2,1)}, bf16[1024,384]{1,0:T(8,128)(2,1)S(1)}, u32[]{:S(2)}) copy-start(bf16[1024,384]{1,0:T(8,128)(2,1)S(1)} %slice.149.query_ref) | copy-start | bytes 2359300
  157.7 18.7 %copy-start.2 = (bf16[2048,256]{1,0:T(8,128)(2,1)}, bf16[2048,256]{1,0:T(8,128)(2,1)S(1)}, u32[]{:S(2)}) copy-start(bf16[2048,256]{1,0:T(8,128)(2,1)S(1)} %maximum_select_fusion.6.key_value_ref) | copy-start | bytes 3145732
  181.6 3.6 collective-permute-start.2
  181.7 103.2 %collective-permute-start = (bf16[8,2,192,384]{3,2,1,0:T(8,128)(2,1)}, bf16[8,2,192,384]{3,2,1,0:T(8,128)(2,1)}, u32[]{:S(2)}, u32[]{:S(2)}) collective-permute-start(bf16[8,2,192,384]{3,2,1,0:T(8,128)(2,1)} %bitcast.5.refs_4_), channel_id=1, source_target_pairs={{0,2},{1,3},{2,0},{3,1},{4,6},{5,7},{6,4},{7,5},{8,10},{9,11},{10,... | collective-permute-start | bytes 7077896 | tf_op jit(solution)/shard_map/attention/ppermute | solution.py:1458
  188.5 64.0 %collective-permute-start.3 = (bf16[256,1536]{1,0:T(8,128)(2,1)}, bf16[256,1536]{1,0:T(8,128)(2,1)}, u32[]{:S(2)}, u32[]{:S(2)}) collective-permute-start(bf16[256,1536]{1,0:T(8,128)(2,1)} %fusion.31), channel_id=1, source_target_pairs={{0,2},{1,3},{2,0},{3,1},{4,6},{5,7},{6,4},{7,5},{8,10},{9,11},{10,... | collective-permute-start | bytes 2359304 | tf_op jit(solution)/shard_map/attention/ppermute | solution.py:1350
  287.4 19.2 %copy-start.40 = (f32[256]{0:T(256)}, f32[256]{0:T(256)S(1)}, u32[]{:S(2)}) copy-start(f32[256]{0:T(256)S(1)} %get-tuple-element.73) | copy-start | bytes 3076
  287.4 19.2 %copy-start.37 = (f32[256]{0:T(256)}, f32[256]{0:T(256)S(1)}, u32[]{:S(2)}) copy-start(f32[256]{0:T(256)S(1)} %fusion.37) | copy-start | bytes 3076
  294.2 11.3 %collective-permute-start.4 = (bf16[8,256,1664]{2,1,0:T(8,128)(2,1)}, bf16[8,256,1664]{2,1,0:T(8,128)(2,1)}, u32[]{:S(2)}, u32[]{:S(2)}) collective-permute-start(bf16[8,256,1664]{2,1,0:T(8,128)(2,1)} %bitcast.123), channel_id=1, source_target_pairs={{0,1},{1,0},{2,3},{3,2},{4,5},{5,4},{6,7},{7,6},{8,9},{9,8},{10,11... | collective-permute-start | bytes 20447240 | tf_op jit(solution)/shard_map/exchange/ppermute | solution.py:1473
  438.9 173.5 %copy-start.27 = (bf16[8,2,192,384]{3,2,1,0:T(8,128)(2,1)S(1)}, bf16[8,2,192,384]{3,2,1,0:T(8,128)(2,1)}, u32[]{:S(2)}) copy-start(bf16[8,2,192,384]{3,2,1,0:T(8,128)(2,1)} %get-tuple-element.52) | copy-start | bytes 7077892
  618.7 20.0 %copy-start.21 = (f32[2048,128]{1,0:T(8,128)S(1)}, f32[2048,128]{1,0:T(8,128)}, u32[]{:S(2)}) copy-start(f32[2048,128]{1,0:T(8,128)} %copy-done.20) | copy-start | bytes 3145732
  618.7 17.0 %collective-permute-start.8 = (bf16[256,1536]{1,0:T(8,128)(2,1)S(1)}, bf16[256,1536]{1,0:T(8,128)(2,1)}, u32[]{:S(2)}, u32[]{:S(2)}) collective-permute-start(bf16[256,1536]{1,0:T(8,128)(2,1)S(1)} %fusion.44), channel_id=1, source_target_pairs={{0,2},{1,3},{2,0},{3,1},{4,6},{5,7},{6,4},{7,5},{8,10},{9,11},{10,... | collective-permute-start | bytes 2359304 | tf_op jit(solution)/shard_map/expert_grads/ppermute | solution.py:1354
  638.7 10.3 %collective-permute-start.9 = (bf16[2,1,256,1536]{3,2,1,0:T(8,128)(2,1)}, bf16[2,1,256,1536]{3,2,1,0:T(8,128)(2,1)}, u32[]{:S(2)}, u32[]{:S(2)}) collective-permute-start(bf16[2,1,256,1536]{3,2,1,0:T(8,128)(2,1)} %bitcast.30), channel_id=1, source_target_pairs={{0,1},{1,0},{2,3},{3,2},{4,5},{5,4},{6,7},{7,6},{8,9},{9,8},{10,11... | collective-permute-start | bytes 4718600 | tf_op jit(solution)/shard_map/expert_grads/ppermute | solution.py:1358
  638.7 84.2 %collective-permute-start.7 = (bf16[8,3,192,384]{3,2,1,0:T(8,128)(2,1)}, bf16[8,3,192,384]{3,2,1,0:T(8,128)(2,1)}, u32[]{:S(2)}, u32[]{:S(2)}) collective-permute-start(bf16[8,3,192,384]{3,2,1,0:T(8,128)(2,1)} %get-tuple-element.58), channel_id=1, source_target_pairs={{0,2},{1,3},{2,0},{3,1},{4,6},{5,7},{6,4},{7,5},{8,10},{9,11},{10,... | collective-permute-start | bytes 10616840 | tf_op jit(solution)/shard_map/expert_grads/ppermute | solution.py:1525
  639.1 89.9 %all-to-all-start.2 = ((bf16[16,192,384]{2,1,0:T(8,128)(2,1)}), bf16[16,192,384]{2,1,0:T(8,128)(2,1)}, u32[]{:S(2)}, u32[]{:S(2)}) async-start(bf16[16,192,384]{2,1,0:T(8,128)(2,1)} %bitcast.27), calls=%async_computation.2 | async-start | bytes 4718592 | tf_op jit(solution)/shard_map/expert_grads/all_to_all | solution.py:1522
  648.9 5.4 copy-start.9
  648.9 96.7 %reduce-scatter.3.cloned.1.call-start = ((), (), s32[]{:S(2)}) async-start(), calls=%async_computation.7 | async-start | bytes 1327104 | tf_op jit(solution)/shard_map/attention_back/reduce_scatter | solution.py:1537
  693.9 18.7 %collective-permute-start.10 = (bf16[1024,256]{1,0:T(8,128)(2,1)}, bf16[1024,256]{1,0:T(8,128)(2,1)S(1)}, u32[]{:S(2)}, u32[]{:S(2)}) collective-permute-start(bf16[1024,256]{1,0:T(8,128)(2,1)} %dynamic-slice_bitcast_fusion.2), channel_id=1, source_target_pairs={{0,4},{4,0},{1,5},{5,1},{2,6},{6,2},{3,7},{7,3},{8,12},{12,8},{9,1... | collective-permute-start | bytes 1572872 | tf_op jit(solution)/shard_map/attention_back/ppermute | solution.py:1553
  712.7 6.0 copy-start.16
  712.7 6.0 copy-start.35
  712.7 6.0 copy-start.43
  748.3 4.5 collective-permute-start.11
  748.3 135.6 %all-to-all-start.3 = ((bf16[24,192,384]{2,1,0:T(8,128)(2,1)}), bf16[24,192,384]{2,1,0:T(8,128)(2,1)}, u32[]{:S(2)}, u32[]{:S(2)}) async-start(bf16[24,192,384]{2,1,0:T(8,128)(2,1)} %bitcast.100), calls=%async_computation.5 | async-start | bytes 7077888 | tf_op jit(solution)/shard_map/attention_back/all_to_all | solution.py:1522
  752.8 120.4 %reduce-scatter.5.cloned.1.call-start = ((), (), s32[]{:S(2)}) async-start(), calls=%async_computation.8 | async-start | bytes 2211840 | tf_op jit(solution)/shard_map/attention_back/reduce_scatter | solution.py:1576
  757.3 22.4 %copy-start.12 = (f32[256,1536]{1,0:T(8,128)S(1)}, f32[256,1536]{1,0:T(8,128)}, u32[]{:S(2)}) copy-start(f32[256,1536]{1,0:T(8,128)} %copy-done.10) | copy-start | bytes 4718596
  757.3 20.2 %collective-permute-start.12 = (bf16[256,1536]{1,0:T(8,128)(2,1)}, bf16[256,1536]{1,0:T(8,128)(2,1)S(1)}, u32[]{:S(2)}, u32[]{:S(2)}) collective-permute-start(bf16[256,1536]{1,0:T(8,128)(2,1)} %fusion.32), channel_id=1, source_target_pairs={{0,2},{1,3},{2,0},{3,1},{4,6},{5,7},{6,4},{7,5},{8,10},{9,11},{10,... | collective-permute-start | bytes 2359304 | tf_op jit(solution)/shard_map/attention_back/ppermute | solution.py:1350
  758.9 20.9 %copy-start.14 = (f32[2,256,1536]{2,1,0:T(8,128)S(1)}, f32[2,256,1536]{2,1,0:T(8,128)}, u32[]{:S(2)}) copy-start(f32[2,256,1536]{2,1,0:T(8,128)} %copy-done.13) | copy-start | bytes 9437188
  782.5 20.5 %collective-permute-start.13 = (bf16[256,1536]{1,0:T(8,128)(2,1)S(1)}, bf16[256,1536]{1,0:T(8,128)(2,1)S(1)}, u32[]{:S(2)}, u32[]{:S(2)}) collective-permute-start(bf16[256,1536]{1,0:T(8,128)(2,1)S(1)} %get-tuple-element.82), channel_id=1, source_target_pairs={{0,2},{1,3},{2,0},{3,1},{4,6},{5,7},{6,4},{7,5},{8,10},{9,11},{10,... | collective-permute-start | bytes 2359304 | tf_op jit(solution)/shard_map/attention_back/ppermute | solution.py:1354
  784.1 34.7 %collective-permute-start.5 = (bf16[256,1536]{1,0:T(8,128)(2,1)S(1)}, bf16[256,1536]{1,0:T(8,128)(2,1)S(1)}, u32[]{:S(2)}, u32[]{:S(2)}) collective-permute-start(bf16[256,1536]{1,0:T(8,128)(2,1)S(1)} %get-tuple-element.83), channel_id=1, source_target_pairs={{0,2},{1,3},{2,0},{3,1},{4,6},{5,7},{6,4},{7,5},{8,10},{9,11},{10,... | collective-permute-start | bytes 2359304 | tf_op jit(solution)/shard_map/expert_grads/ppermute | solution.py:1354
  784.7 1.2 collective-permute-start.15
  785.9 33.6 %collective-permute-start.16 = (f32[2,1536]{1,0:T(2,128)S(1)}, f32[2,1536]{1,0:T(2,128)S(1)}, u32[]{:S(2)}, u32[]{:S(2)}) collective-permute-start(f32[2,1536]{1,0:T(2,128)S(1)} %fusion.43), channel_id=1, source_target_pairs={{0,2},{1,3},{2,0},{3,1},{4,6},{5,7},{6,4},{7,5},{8,10},{9,11},{10,... | collective-permute-start | bytes 36872 | tf_op jit(solution)/shard_map/attention_back/ppermute | solution.py:1587
  803.6 72.7 %collective-permute-start.14 = (bf16[2,1,256,1536]{3,2,1,0:T(8,128)(2,1)S(1)}, bf16[2,1,256,1536]{3,2,1,0:T(8,128)(2,1)}, u32[]{:S(2)}, u32[]{:S(2)}) collective-permute-start(bf16[2,1,256,1536]{3,2,1,0:T(8,128)(2,1)S(1)} %bitcast.105), channel_id=1, source_target_pairs={{0,1},{1,0},{2,3},{3,2},{4,5},{5,4},{6,7},{7,6},{8,9},{9,8},{10,11... | collective-permute-start | bytes 4718600 | tf_op jit(solution)/shard_map/attention_back/ppermute | solution.py:1358
  819.5 60.7 %collective-permute-start.6 = (bf16[2,1,256,1536]{3,2,1,0:T(8,128)(2,1)S(1)}, bf16[2,1,256,1536]{3,2,1,0:T(8,128)(2,1)}, u32[]{:S(2)}, u32[]{:S(2)}) collective-permute-start(bf16[2,1,256,1536]{3,2,1,0:T(8,128)(2,1)S(1)} %bitcast.107), channel_id=1, source_target_pairs={{0,1},{1,0},{2,3},{3,2},{4,5},{5,4},{6,7},{7,6},{8,9},{9,8},{10,11... | collective-permute-start | bytes 4718600 | tf_op jit(solution)/shard_map/expert_grads/ppermute | solution.py:1358
  819.6 3.8 collective-permute-start.17
  823.4 6.9 copy-start.33
  823.4 4.4 collective-permute-start.18
  827.8 21.4 %collective-permute-start.19 = (f32[2,1536]{1,0:T(2,128)S(1)}, f32[2,1536]{1,0:T(2,128)S(1)}, u32[]{:S(2)}, u32[]{:S(2)}) collective-permute-start(f32[2,1536]{1,0:T(2,128)S(1)} %add.221), channel_id=1, source_target_pairs={{0,16},{8,24},{16,0},{24,8},{1,17},{9,25},{17,1},{25,9},{2,18},{10... | collective-permute-start | bytes 36872 | tf_op jit(solution)/shard_map/attention_back/ppermute | solution.py:1587
  (24 other events, 64.3 us)
Sparse Core Ops, SparseCore 0:
  13.2 110.2 all-gather.3
  125.7 168.5 all-gather.5
  657.3 88.3 reduce-scatter.2
  759.0 114.1 reduce-scatter.4

commit v5 on v4

--- a/solution.py
+++ b/solution.py
@@ -770,15 +770,17 @@
         del refs[:count]
         return taken[0] if count == 1 else taken
 
-    tokens_in, cotangent_own, cotangent_other, shares_ref, own_hbm, other_hbm = take(6)
-    exchanged = take(1)
+    tokens_in, cotangent_own = take(2)
+    if not gathers:
+        cotangent_other = take(1)
+    shares_ref, own_hbm, other_hbm, exchanged = take(4)
     if not gathers:
         before = take(1)
         grad_piece, out_piece, grad_own, grad_other, received = take(5)
         grad_arrays, out_arrays = take(4), take(4)
         tokens_hbm = tokens_in
     else:
-        parts_hbm, grad_own, grad_other, tokens_hbm, received = take(5)
+        parts_hbm, grad_own, grad_other, tokens_hbm, received, cotangent_other = take(6)
     weights, grads, tokens_buf, cotangent_buf, inner_low, grad_low = take(6)
     both_buf, stage, load_sems, store_sems, row_sems, part_sems, exchange_sems = take(7)
 
@@ -791,6 +793,7 @@
     first_rows, second_rows = pl.ds(0, rows), pl.ds(rows, rows)
     if gathers:
         mover = Gather(place, tokens_hbm, take(4))
+        cotangent_send, cotangent_recv = take(2)
     else:
         before_buf, terms, sums, term_sems = take(4)
         movers = [
@@ -799,6 +802,16 @@
         ]
     order = mover.order if gathers else Reduce.order
 
+    def cotangent_copy(step):
+        here = place.block(order, step)
+        return remote(
+            cotangent_own.at[here],
+            cotangent_other.at[here],
+            cotangent_send.at[here],
+            cotangent_recv.at[here],
+            place.sibling,
+        )
+
     place.meet()
     exchange = remote(
         exchanged, received, exchange_sems.at[0], exchange_sems.at[1], place.across
@@ -810,6 +823,8 @@
         own_copy.start()
         own_copy.wait()
         mover.start()
+        for step in range(steps):
+            cotangent_copy(step).start()
     weight_loads = weight_copies(own_hbm, other_hbm, weights, load_sems)
     for copy in weight_loads:
         copy.start()
@@ -834,6 +849,7 @@
     def load_rows(step, slot):
         if gathers:
             mover.core_copy(place.block(order, step)).wait_recv()
+            cotangent_copy(step).wait_recv()
         for copy in row_copies(step, slot):
             copy.start()
 
@@ -985,6 +1001,8 @@
     exchange.wait()
     if gathers:
         mover.finish()
+        for step in range(steps):
+            cotangent_copy(step).wait_send()
     else:
         for number, result in enumerate((grad_piece, out_piece)):
             movers[number].finish(result, row_sems.at[0, number])
@@ -1007,9 +1025,11 @@
             low(*own.shape),
             low(*own.shape),
             low(blocks, 2, rows, model_width),
-            low(*operands[6].shape),
+            low(*operands[5].shape),
+            low(*operands[1].shape),
         ]
         own_scratch = [dma((blocks, 2)), dma((line, 2)), dma((line,)), dma((blocks,))]
+        own_scratch += [dma((blocks,)), dma((blocks,))]
     else:
         out_shape = [
             low(rows, model_width),
@@ -1039,7 +1059,7 @@
             dma((line + 1,)),
         ]
     in_specs = [in_place] * len(operands)
-    in_specs[3] = pl.BlockSpec(memory_space=pltpu.VMEM)
+    in_specs[2 if gathers else 3] = pl.BlockSpec(memory_space=pltpu.VMEM)
     results = pl.pallas_call(
         partial(expert_kernel, line=line, chunk=chunk, gathers=gathers),
         in_specs=in_specs,
@@ -1068,12 +1088,12 @@
             flops=flops, bytes_accessed=80 * 2**20, transcendentals=0
         ),
     )(*operands)
-    return results[:5]
-
-
-def experts_gathering(piece, cotangents, shares, own, other, exchanged, line):
+    return results[: 6 if gathers else 5]
+
+
+def experts_gathering(piece, cotangent, shares, own, other, exchanged, line):
     rows, model_width = piece.shape
-    operands = (piece, *cotangents, shares, own, other, exchanged)
+    operands = (piece, cotangent, shares, own, other, exchanged)
     return expert_call(operands, own, shares, line, rows, model_width, True, 1)
 
 
@@ -1368,6 +1388,26 @@
         return jnp.pad(columns, ((0, 0), (0, 128 - len(gains))))
 
     with jax.named_scope("weights"):
+        lanes = 3 * unit_count
+
+        def slices(first, count):
+            return jnp.concatenate(
+                [
+                    weight.reshape((groups, own_experts) + weight.shape[1:])[:, first : first + count]
+                    for weight in (gate_weight, up_weight, down_weight.transpose(0, 2, 1))
+                ],
+                axis=3,
+            ).reshape(groups * count, slice_rows, lanes)
+
+        def to_groups(values):
+            owned = lax.all_to_all(values, GROUP, 0, 0, tiled=True)
+            return owned.reshape(groups, -1, slice_rows, lanes)
+
+        slices_first, slices_second = lax.optimization_barrier(
+            (slices(0, first_count), slices(first_count, own_experts - first_count))
+        )
+        owned_first, owned_second = to_groups(slices_first), to_groups(slices_second)
+
         qkv_full = lax.all_gather(
             jnp.concatenate(
                 [
@@ -1384,26 +1424,13 @@
             tiled=True,
         )
         qkv_cols = query_cols + 2 * kv_cols
+        owned_first, qkv_full = lax.optimization_barrier((owned_first, qkv_full))
+        others_first = lax.ppermute(owned_first, TENSOR, across)
         qkv_weight = qkv_full[:, :qkv_cols]
         out_transposed = qkv_full[:, qkv_cols : qkv_cols + query_cols]
         gain_attn_float = qkv_full[:, qkv_cols + query_cols].astype(F32)
         gain_ffn_float = qkv_full[:, qkv_cols + query_cols + 1].astype(F32)
-        lanes = 3 * unit_count
-
-
-        def expert_slices(first, count):
-            slices = jnp.concatenate(
-                [
-                    weight.reshape((groups, own_experts) + weight.shape[1:])[:, first : first + count]
-                    for weight in (gate_weight, up_weight, down_weight.transpose(0, 2, 1))
-                ],
-                axis=3,
-            ).reshape(groups * count, slice_rows, lanes)
-            owned = lax.all_to_all(slices, GROUP, 0, 0, tiled=True)
-            return owned.reshape(groups, count, slice_rows, lanes)
-
-        owned_first = expert_slices(0, first_count)
-        owned_second = expert_slices(first_count, own_experts - first_count)
+
 
     with jax.named_scope("cotangents"):
         cotangent_piece = own_piece(cotangent)
@@ -1448,14 +1475,12 @@
         own_keys_values = jnp.concatenate(
             [rotated[:, query_cols:], projected[:, rotated_cols:qkv_cols].astype(BF16)], axis=1
         )
-        owned_first, own_keys_values = lax.optimization_barrier((owned_first, own_keys_values))
         other_keys_values = lax.ppermute(own_keys_values, CONTEXT, pair)
         keys_values = jnp.where(
             context_rank == 0,
             jnp.concatenate([own_keys_values, other_keys_values]),
             jnp.concatenate([other_keys_values, own_keys_values]),
         )
-        others_first = lax.ppermute(owned_first, TENSOR, across)
         first = own_first.reshape(1).astype(jnp.int32)
         attended, lse = attention_forward(first, queries, keys_values, doc_start[:, None])
         attn_part = lax.dot_general(
@@ -1470,9 +1495,9 @@
 
     with jax.named_scope("exchange"):
         cotangent_own, normed_ffn = lax.optimization_barrier((cotangent_own, normed_ffn))
-        cotangent_other = lax.ppermute(cotangent_own, TENSOR, sibling)
+        spread_own = cotangent_own[:, :, model_width:]
         spread_all = jnp.concatenate(
-            [cotangent_own[:, :, model_width:], cotangent_other[:, :, model_width:]], axis=1
+            [spread_own, lax.ppermute(spread_own, TENSOR, sibling)], axis=1
         )
 
         def shares_of(first, count):
@@ -1487,11 +1512,10 @@
 
     with jax.named_scope("experts"):
         line = groups // 2
-        cotangents = (cotangent_own, cotangent_other)
-        parts, grad_own_first, grad_other_first, tokens, others_second = (
+        parts, grad_own_first, grad_other_first, tokens, others_second, cotangent_other = (
             experts_gathering(
                 normed_ffn.astype(BF16),
-                cotangents,
+                cotangent_own,
                 shares_first,
                 owned_first,
                 others_first,
@@ -1502,7 +1526,7 @@
         grad_second, out_piece, grad_own_second, grad_other_second, received_first = (
             experts_reducing(
                 tokens,
-                cotangents,
+                (cotangent_own, cotangent_other),
                 shares_second,
                 owned_second,
                 others_second,
@@ -1538,6 +1562,7 @@
             grad_out_local.astype(BF16), GROUP, scatter_dimension=0, tiled=True
         )
         grad_attended = jnp.dot(grad_hidden_low, out_transposed, preferred_element_type=F32)
+        returned_first, grad_attended = lax.optimization_barrier((returned_first, grad_attended))
         grad_query_lin, grad_key_value = attention_backward(
             first,
             queries,
@@ -1561,9 +1586,9 @@
         grad_qkv_local = lax.dot_general(
             first_normalized, grad_projected, FIRST_FIRST, preferred_element_type=F32
         ).astype(BF16)
-        returned_first, total_second, grad_out_transposed, grad_first_part, grad_qkv_local = (
+        total_second, grad_out_transposed, grad_first_part, grad_qkv_local = (
             lax.optimization_barrier(
-                (returned_first, total_second, grad_out_transposed, grad_first_part, grad_qkv_local)
+                (total_second, grad_out_transposed, grad_first_part, grad_qkv_local)
             )
         )
         returned_second = returned(total_second)
@@ -1573,9 +1598,7 @@
         )
         grad_input_norm, grad_gain_attn_local = attn_norm_back(grad_first)
         grad_input = gather_over_tensor((grad_hidden + grad_input_norm).astype(BF16))
-        grad_qkv = lax.psum_scatter(
-            grad_qkv_local, GROUP, scatter_dimension=0, tiled=True
-        ).astype(F32)
+        grad_qkv = lax.psum_scatter(grad_qkv_local, GROUP, scatter_dimension=0, tiled=True)
         gains = jnp.stack([grad_gain_attn_local, grad_gain_ffn_local])
         for axis, step, size in (
             (TENSOR, 1, tensor_size),
@@ -1586,6 +1609,11 @@
         ):
             gains = gains + lax.ppermute(gains, axis, [(i, i ^ step) for i in range(size)])
         gains = lax.dynamic_slice_in_dim(gains, group_rank * slice_rows, slice_rows, axis=1)
+
+    returned_second, grad_qkv, gains, grad_input, output = lax.optimization_barrier(
+        (returned_second, grad_qkv, gains, grad_input, output)
+    )
+    grad_qkv = grad_qkv.astype(F32)
 
     def whole(first, last, turned):
         parts = [

time: 909 us -> 886 us (0.975)
  waiting for transfers between devices: 338 us -> 318 us
    all_gather x1, waiting for transfers between devices: 80.3 us -> 2.76 us  [expert_plan(): lax.all_gather(jnp.concatenate([query_weight, key_projection_weight, valu...]
    all_to_all x2, waiting for transfers between devices: 29.9 us -> 102 us  [to_groups(): owned = lax.all_to_all(values, GROUP, 0, 0, tiled=True)]
    all_to_all x2, waiting for transfers between devices: 0.01 us -> 19.9 us  [returned(): return lax.all_to_all(flat, GROUP, 0, 0, tiled=True).reshape(total.shape)]
    reduce_scatter x1, waiting for transfers between devices: 16.7 us -> 0.01 us  [expert_plan(): lax.psum_scatter(grad_out_local.astype(BF16), GROUP, scatter_dimension=0,...]
    ppermute x1, waiting for transfers between devices: 16.7 us -> 0.01 us  [expert_plan(): lax.ppermute(pick(grad_key_value, 0, 1 - context_rank), CONTEXT, pair)]
  transfers between devices with their start and end apart: 28 -> 28, of which waited for: 17 -> 19; matrix products, arithmetic and copies ran while one was open for 12% -> 12% of each run, Pallas kernels for 6% -> 6%
where the time goes in v5:
time: 886 us; the launch traced here: 878 us
  Pallas kernels  351 us (40%)
  waiting for transfers between devices  318 us (36%)
  other arithmetic  68.9 us (8%)
  local copies, waits for them, and re-layouts  55.4 us (6%)
  starting transfers between devices  45.8 us (5%)
  matrix products  23.7 us (3%)
  between operations  15.3 us (2%)
    pallas_call x2, Pallas kernels, expert_call(): pl.pallas_call(partial(expert_kernel, line=line, chunk=chunk, gathers=gat...  300 us
    all_to_all x2, waiting for transfers between devices, to_groups(): owned = lax.all_to_all(values, GROUP, 0, 0, tiled=True)  102 us
    ppermute x2, waiting for transfers between devices, sum_over_tensor(): lax.ppermute(pick(half, 0, 1 - chip_half).astype(BF16), TENSOR, across)  81 us
    ppermute x3, waiting for transfers between devices, gather_over_tensor(): other = lax.ppermute(piece, TENSOR, across)  42.1 us
    pallas_call x1, Pallas kernels, attention_backward(): pl.pallas_call(partial(attention_backward_kernel, group_size=group_size,...  31.9 us
    ppermute x5, waiting for transfers between devices, expert_plan(): lax.ppermute(gains, axis, [(i, i ^ step) for i in range(size)])  23.7 us
    all_to_all x2, waiting for transfers between devices, returned(): return lax.all_to_all(flat, GROUP, 0, 0, tiled=True).reshape(total.shape)  19.9 us
    reduce_scatter x1, waiting for transfers between devices, expert_plan(): lax.psum_scatter(grad_qkv_local, GROUP, scatter_dimension=0, tiled=True)  19.8 us
  transfers between devices with their start and end apart: 28, of which 19 were waited for; matrix products, arithmetic and copies ran while one was open for 12% of the time, Pallas kernels for 6%

profile of v5, /device:TPU:0, one launch (start us, length us, event | category | flops | bytes accessed | tf_op | source)
XLA Modules:
  0.0 878.2 jit_solution(18021678574091150265)
XLA Ops:
  21.1 7.3 all-to-all-start
  32.1 3.7 multiply_cosine_fusion
  42.2 3.0 copy.106
  45.9 73.1 %all-to-all-done = bf16[16,192,384]{2,1,0:T(8,128)(2,1)} async-done(((bf16[16,192,384]{2,1,0:T(8,128)(2,1)}), bf16[16,192,384]{2,1,0:T(8,128)(2,1)}, u32[]{:S(2)}, u32[]{:S(2)}) %all-to-all-start) | async-done | bytes 2359328 | tf_op jit(solution)/shard_map/weights/all_to_all | solution.py:1403
  119.0 2.8 all-gather.4.cloned.1.call-done
  121.8 5.7 copy.100
  130.4 2.7 copy.101
  134.8 6.8 fusion.3
  144.0 4.8 all-to-all-start.1
  149.1 9.5 %collective-permute-done.1 = bf16[1024,256]{1,0:T(8,128)(2,1)S(1)} collective-permute-done((bf16[1024,256]{1,0:T(8,128)(2,1)S(1)}, bf16[1024,256]{1,0:T(8,128)(2,1)S(1)}, u32[]{:S(2)}, u32[]{:S(2)}) %collective-permute-start.1) | collective-permute-done | bytes 524320 | tf_op jit(solution)/shard_map/attention/ppermute | solution.py:1478
  159.0 18.7 %attention.1 = (bf16[1024,384]{1,0:T(8,128)(2,1)S(1)}, f32[4,2,768,1]{3,2,1,0:T(8,128)}) custom-call(s32[1]{0:T(128)} %bitcast.11.first_ref, bf16[1024,384]{1,0:T(8,128)(2,1)S(1)} %slice.141.query_ref, bf16[2048,256]{1,0:T(8,128)(2,1)S(1)} %maximum_select_fusion.6.key_value_ref, s32[1024,1]{1,0:T(8,128)S(1)} %copy.107.doc_start_ref), custom_call_target="tpu_custom_call" | custom-call | flops 16106127360 | bytes 4194304 | tf_op jit(solution)/shard_map/attention/pallas_call | solution.py:1252
  189.7 62.5 %collective-permute-done.3 = bf16[256,1536]{1,0:T(8,128)(2,1)} collective-permute-done((bf16[256,1536]{1,0:T(8,128)(2,1)}, bf16[256,1536]{1,0:T(8,128)(2,1)}, u32[]{:S(2)}, u32[]{:S(2)}) %collective-permute-start.3) | collective-permute-done | bytes 786464 | tf_op jit(solution)/shard_map/attention/ppermute | solution.py:1370
  252.2 2.5 bitcast_add_fusion.1
  254.7 29.1 %all-to-all-done.1 = bf16[24,192,384]{2,1,0:T(8,128)(2,1)} async-done(((bf16[24,192,384]{2,1,0:T(8,128)(2,1)}), bf16[24,192,384]{2,1,0:T(8,128)(2,1)}, u32[]{:S(2)}, u32[]{:S(2)}) %all-to-all-start.1) | async-done | bytes 3538976 | tf_op jit(solution)/shard_map/weights/all_to_all | solution.py:1403
  283.8 2.6 multiply_reduce_fusion
  288.6 4.7 all-gather.6.cloned.1.call-done
  300.5 127.2 %experts.2 = (bf16[8,512,3072]{2,1,0:T(8,128)(2,1)}, bf16[8,2,192,384]{3,2,1,0:T(8,128)(2,1)}, bf16[8,2,192,384]{3,2,1,0:T(8,128)(2,1)}, bf16[8,2,256,1536]{3,2,...) custom-call(bf16[256,1536]{1,0:T(8,128)(2,1)} %multiply_multiply_fusion.refs_0_, ...), custom_call_target="tpu_custom_call" | custom-call | flops 57982058496 | bytes 83886080 | tf_op jit(solution)/shard_map/experts/pallas_call | solution.py:1063
  427.8 172.9 %experts.3 = (bf16[256,1536]{1,0:T(8,128)(2,1)}, bf16[256,1536]{1,0:T(8,128)(2,1)}, bf16[8,3,192,384]{3,2,1,0:T(8,128)(2,1)}, bf16[8,3,192,384]{3,2,1,0:T(8,128)...) custom-call(bf16[8,2,256,1536]{3,2,1,0:T(8,128)(2,1)} %get-tuple-ele, ...), custom_call_target="tpu_custom_call" | custom-call | flops 86973087744 | bytes 83886080 | tf_op jit(solution)/shard_map/experts/pallas_call | solution.py:1063
  600.7 4.6 add_convert_fusion.1
  606.0 6.2 all-to-all-start.2
  612.5 2.9 add_convert_fusion.2
  616.9 18.0 %collective-permute-done.6 = bf16[256,1536]{1,0:T(8,128)(2,1)} collective-permute-done((bf16[256,1536]{1,0:T(8,128)(2,1)S(1)}, bf16[256,1536]{1,0:T(8,128)(2,1)}, u32[]{:S(2)}, u32[]{:S(2)}) %collective-permute-start.6) | collective-permute-done | bytes 786464 | tf_op jit(solution)/shard_map/expert_grads/ppermute | solution.py:1374
  640.3 2.4 maximum_select_fusion
  644.4 2.9 convolution_convert_fusion.2
  647.3 5.0 fusion.26.grad_ref
  652.3 19.9 %all-to-all-done.2 = bf16[16,192,384]{2,1,0:T(8,128)(2,1)} async-done(((bf16[16,192,384]{2,1,0:T(8,128)(2,1)}), bf16[16,192,384]{2,1,0:T(8,128)(2,1)}, u32[]{:S(2)}, u32[]{:S(2)}) %all-to-all-start.2) | async-done | bytes 2359328 | tf_op jit(solution)/shard_map/expert_grads/all_to_all | solution.py:1546
  674.4 31.9 %attention_back.1 = (bf16[1024,384]{1,0:T(8,128)(2,1)S(1)}, bf16[2048,256]{1,0:T(8,128)(2,1)S(1)}) custom-call(s32[1]{0:T(128)} %bitcast.11.first_ref, bf16[1024,384]{1,0:T(8,128)(2,1)S(1)} %copy-done.5, bf16[2048,256]{1,0:T(8,128)(2,1)S(1)} %copy-done.3, s32[1024,1]{1,0:T(8,128)S(1)} %copy-done.7, f32[4,2,768,1]{3,2,1,0:T(8,128)} %get-tuple-element.69.lse_ref, ...), custom_call_target="tpu_custom_call" | custom-call | flops 40265318400 | bytes 8388608 | tf_op jit(solution)/shard_map/attention_back/pallas_call | solution.py:1281
  707.2 2.6 collective-permute-start.8
  709.8 7.1 collective-permute-done.5
  716.9 6.2 add_convert_fusion
  723.2 2.9 fusion.31
  726.2 4.3 convolution_convert_fusion.1
  731.7 5.7 all-to-all-start.3
  742.6 18.4 %collective-permute-done.10 = bf16[256,1536]{1,0:T(8,128)(2,1)S(1)} collective-permute-done((bf16[256,1536]{1,0:T(8,128)(2,1)}, bf16[256,1536]{1,0:T(8,128)(2,1)S(1)}, u32[]{:S(2)}, u32[]{:S(2)}) %collective-permute-start.10) | collective-permute-done | bytes 786464 | tf_op jit(solution)/shard_map/attention_back/ppermute | solution.py:1370
  766.8 11.2 %collective-permute-done.18 = bf16[256,1536]{1,0:T(8,128)(2,1)} collective-permute-done((bf16[256,1536]{1,0:T(8,128)(2,1)}, bf16[256,1536]{1,0:T(8,128)(2,1)}, u32[]{:S(2)}, u32[]{:S(2)}) %collective-permute-start.18) | collective-permute-done | bytes 786464 | tf_op jit(solution)/shard_map/expert_grads/ppermute | solution.py:1374
  778.0 2.5 maximum_select_fusion.5
  781.1 12.9 %collective-permute-done.16 = bf16[256,1536]{1,0:T(8,128)(2,1)S(1)} collective-permute-done((bf16[256,1536]{1,0:T(8,128)(2,1)S(1)}, bf16[256,1536]{1,0:T(8,128)(2,1)S(1)}, u32[]{:S(2)}, u32[]{:S(2)}) %collective-permute-start.16) | collective-permute-done | bytes 786464 | tf_op jit(solution)/shard_map/attention_back/ppermute | solution.py:1374
  795.9 2.6 collective-permute-done.12
  800.3 3.8 maximum_select_fusion.2
  805.6 2.7 slice_bitcast_fusion.1
  808.3 2.5 collective-permute-done.14
  810.8 3.4 collective-permute-start.15
  815.0 18.6 %collective-permute-done.15 = f32[2,1536]{1,0:T(2,128)S(1)} collective-permute-done((f32[2,1536]{1,0:T(2,128)S(1)}, f32[2,1536]{1,0:T(2,128)S(1)}, u32[]{:S(2)}, u32[]{:S(2)}) %collective-permute-start.15) | collective-permute-done | bytes 12320 | tf_op jit(solution)/shard_map/attention_back/ppermute | solution.py:1610
  833.6 3.8 maximum_select_fusion.1
  837.4 19.8 %reduce-scatter.5.cloned.1.call-done = bf16[192,640]{1,0:T(8,128)(2,1)} async-done(((bf16[1536,640]{1,0:T(8,128)(2,1)}), bf16[192,640]{1,0:T(8,128)(2,1)}) %reduce-scatter.5.cloned.1.call-update) | async-done | bytes 245776 | tf_op jit(solution)/shard_map/attention_back/reduce_scatter | solution.py:1601
  862.7 2.5 bitcast_convert_fusion
  865.6 2.5 bitcast_convert_fusion.1
  868.1 2.5 bitcast_convert_fusion.2
  (231 shorter events, 91.2 us)
Async XLA Ops:
  7.2 21.3 %copy-start = (f32[1024,8]{0,1:T(8,128)S(1)}, f32[1024,8]{0,1:T(8,128)}, u32[]{:S(2)}) copy-start(f32[1024,8]{0,1:T(8,128)} %param.26) | copy-start | bytes 98308
  7.2 114.6 %all-gather.4.cloned.1.call-start = ((), (), s32[]{:S(2)}) async-start(), calls=%async_computation.6 | async-start | bytes 3981312 | tf_op jit(solution)/shard_map/weights/all_gather | solution.py:1411
  21.1 97.9 %all-to-all-start = ((bf16[16,192,384]{2,1,0:T(8,128)(2,1)}), bf16[16,192,384]{2,1,0:T(8,128)(2,1)}, u32[]{:S(2)}, u32[]{:S(2)}) async-start(bf16[16,192,384]{2,1,0:T(8,128)(2,1)} %bitcast.5), calls=%async_computation | async-start | bytes 4718592 | tf_op jit(solution)/shard_map/weights/all_to_all | solution.py:1403
  28.4 264.9 %all-gather.6.cloned.1.call-start = ((), (), s32[]{:S(2)}) async-start(), calls=%async_computation.9 | async-start | bytes 7667712 | tf_op jit(solution)/shard_map/cotangents/all_gather | solution.py:1451
  45.9 88.8 %copy-start.47 = (f32[1024]{0:T(1024)}, f32[1024]{0:T(1024)S(1)}, u32[]{:S(2)}) copy-start(f32[1024]{0:T(1024)S(1)} %add_rsqrt_fusion) | copy-start | bytes 12292
  134.7 6.9 copy-start.39
  134.7 151.7 %copy-start.36 = (f32[1536]{0:T(1024)}, f32[1536]{0:T(1024)S(1)}, u32[]{:S(2)}) copy-start(f32[1536]{0:T(1024)S(1)} %get-tuple-element.87) | copy-start | bytes 18436
  134.7 6.9 copy-start.23
  134.7 6.9 copy-start.24
  142.5 16.1 %collective-permute-start.1 = (bf16[1024,256]{1,0:T(8,128)(2,1)S(1)}, bf16[1024,256]{1,0:T(8,128)(2,1)S(1)}, u32[]{:S(2)}, u32[]{:S(2)}) collective-permute-start(bf16[1024,256]{1,0:T(8,128)(2,1)S(1)} %pad_maximum_fusion.11), channel_id=1, source_target_pairs={{0,4},{4,0},{1,5},{5,1},{2,6},{6,2},{3,7},{7,3},{8,12},{12,8},{9,1... | collective-permute-start | bytes 1572872 | tf_op jit(solution)/shard_map/attention/ppermute | solution.py:1478
  144.0 139.9 %all-to-all-start.1 = ((bf16[24,192,384]{2,1,0:T(8,128)(2,1)}), bf16[24,192,384]{2,1,0:T(8,128)(2,1)}, u32[]{:S(2)}, u32[]{:S(2)}) async-start(bf16[24,192,384]{2,1,0:T(8,128)(2,1)} %bitcast.99), calls=%async_computation.1 | async-start | bytes 7077888 | tf_op jit(solution)/shard_map/weights/all_to_all | solution.py:1403
  149.0 28.7 %copy-start.6 = (s32[1024,1]{1,0:T(8,128)}, s32[1024,1]{1,0:T(8,128)S(1)}, u32[]{:S(2)}) copy-start(s32[1024,1]{1,0:T(8,128)S(1)} %copy.107.doc_start_ref) | copy-start | bytes 12292
  149.1 28.6 %copy-start.4 = (bf16[1024,384]{1,0:T(8,128)(2,1)}, bf16[1024,384]{1,0:T(8,128)(2,1)S(1)}, u32[]{:S(2)}) copy-start(bf16[1024,384]{1,0:T(8,128)(2,1)S(1)} %slice.141.query_ref) | copy-start | bytes 2359300
  158.9 18.7 %copy-start.2 = (bf16[2048,256]{1,0:T(8,128)(2,1)}, bf16[2048,256]{1,0:T(8,128)(2,1)S(1)}, u32[]{:S(2)}) copy-start(bf16[2048,256]{1,0:T(8,128)(2,1)S(1)} %maximum_select_fusion.6.key_value_ref) | copy-start | bytes 3145732
  159.0 18.8 %copy-start.19 = (bf16[1536,1152]{1,0:T(8,128)(2,1)S(1)}, bf16[1536,1152]{1,0:T(8,128)(2,1)}, u32[]{:S(2)}) copy-start(bf16[1536,1152]{1,0:T(8,128)(2,1)} %all-gather.4.cloned.1.call-done) | copy-start | bytes 10616836
  181.3 3.6 collective-permute-start.2
  181.4 102.4 %collective-permute-start = (bf16[8,2,192,384]{3,2,1,0:T(8,128)(2,1)}, bf16[8,2,192,384]{3,2,1,0:T(8,128)(2,1)}, u32[]{:S(2)}, u32[]{:S(2)}) collective-permute-start(bf16[8,2,192,384]{3,2,1,0:T(8,128)(2,1)} %bitcast.8.refs_3_), channel_id=1, source_target_pairs={{0,2},{1,3},{2,0},{3,1},{4,6},{5,7},{6,4},{7,5},{8,10},{9,11},{10,... | collective-permute-start | bytes 7077896 | tf_op jit(solution)/shard_map/weights/ppermute | solution.py:1428
  188.3 64.0 %collective-permute-start.3 = (bf16[256,1536]{1,0:T(8,128)(2,1)}, bf16[256,1536]{1,0:T(8,128)(2,1)}, u32[]{:S(2)}, u32[]{:S(2)}) collective-permute-start(bf16[256,1536]{1,0:T(8,128)(2,1)} %fusion.32), channel_id=1, source_target_pairs={{0,2},{1,3},{2,0},{3,1},{4,6},{5,7},{6,4},{7,5},{8,10},{9,11},{10,... | collective-permute-start | bytes 2359304 | tf_op jit(solution)/shard_map/attention/ppermute | solution.py:1370
  286.4 10.6 %copy-start.45 = (f32[256]{0:T(256)}, f32[256]{0:T(256)S(1)}, u32[]{:S(2)}) copy-start(f32[256]{0:T(256)S(1)} %get-tuple-element.91) | copy-start | bytes 3076
  286.4 10.6 %copy-start.42 = (f32[256]{0:T(256)}, f32[256]{0:T(256)S(1)}, u32[]{:S(2)}) copy-start(f32[256]{0:T(256)S(1)} %fusion.38) | copy-start | bytes 3076
  294.4 2.0 collective-permute-start.4
  606.0 66.2 %all-to-all-start.2 = ((bf16[16,192,384]{2,1,0:T(8,128)(2,1)}), bf16[16,192,384]{2,1,0:T(8,128)(2,1)}, u32[]{:S(2)}, u32[]{:S(2)}) async-start(bf16[16,192,384]{2,1,0:T(8,128)(2,1)} %bitcast.101), calls=%async_computation.3 | async-start | bytes 4718592 | tf_op jit(solution)/shard_map/expert_grads/all_to_all | solution.py:1546
  612.2 118.2 %reduce-scatter.3.cloned.1.call-start = ((), (), s32[]{:S(2)}) async-start(), calls=%async_computation.7 | async-start | bytes 1327104 | tf_op jit(solution)/shard_map/attention_back/reduce_scatter | solution.py:1561
  615.4 21.4 %copy-start.28 = (f32[2048,128]{1,0:T(8,128)S(1)}, f32[2048,128]{1,0:T(8,128)}, u32[]{:S(2)}) copy-start(f32[2048,128]{1,0:T(8,128)} %copy-done.27) | copy-start | bytes 3145732
  615.4 19.5 %collective-permute-start.6 = (bf16[256,1536]{1,0:T(8,128)(2,1)S(1)}, bf16[256,1536]{1,0:T(8,128)(2,1)}, u32[]{:S(2)}, u32[]{:S(2)}) collective-permute-start(bf16[256,1536]{1,0:T(8,128)(2,1)S(1)} %get-tuple-element.101), channel_id=1, source_target_pairs={{0,2},{1,3},{2,0},{3,1},{4,6},{5,7},{6,4},{7,5},{8,10},{9,11},{10,... | collective-permute-start | bytes 2359304 | tf_op jit(solution)/shard_map/expert_grads/ppermute | solution.py:1374
  636.7 3.6 collective-permute-start.7
  637.6 79.2 %collective-permute-start.5 = (bf16[8,3,192,384]{3,2,1,0:T(8,128)(2,1)}, bf16[8,3,192,384]{3,2,1,0:T(8,128)(2,1)}, u32[]{:S(2)}, u32[]{:S(2)}) collective-permute-start(bf16[8,3,192,384]{3,2,1,0:T(8,128)(2,1)} %get-tuple-element.64), channel_id=1, source_target_pairs={{0,2},{1,3},{2,0},{3,1},{4,6},{5,7},{6,4},{7,5},{8,10},{9,11},{10,... | collective-permute-start | bytes 10616840 | tf_op jit(solution)/shard_map/expert_grads/ppermute | solution.py:1549
  647.2 25.0 %copy-start.3 = (bf16[2048,256]{1,0:T(8,128)(2,1)S(1)}, bf16[2048,256]{1,0:T(8,128)(2,1)}, u32[]{:S(2)}) copy-start(bf16[2048,256]{1,0:T(8,128)(2,1)} %copy-done.2) | copy-start | bytes 3145732
  647.2 25.0 %copy-start.5 = (bf16[1024,384]{1,0:T(8,128)(2,1)S(1)}, bf16[1024,384]{1,0:T(8,128)(2,1)}, u32[]{:S(2)}) copy-start(bf16[1024,384]{1,0:T(8,128)(2,1)} %copy-done.4) | copy-start | bytes 2359300
  647.2 25.0 %copy-start.7 = (s32[1024,1]{1,0:T(8,128)S(1)}, s32[1024,1]{1,0:T(8,128)}, u32[]{:S(2)}) copy-start(s32[1024,1]{1,0:T(8,128)} %copy-done.6) | copy-start | bytes 12292
  707.2 15.8 %collective-permute-start.8 = (bf16[1024,256]{1,0:T(8,128)(2,1)S(1)}, bf16[1024,256]{1,0:T(8,128)(2,1)S(1)}, u32[]{:S(2)}, u32[]{:S(2)}) collective-permute-start(bf16[1024,256]{1,0:T(8,128)(2,1)S(1)} %dynamic-slice_bitcast_fusion.2), channel_id=1, source_target_pairs={{0,4},{4,0},{1,5},{5,1},{2,6},{6,2},{3,7},{7,3},{8,12},{12,8},{9,1... | collective-permute-start | bytes 1572872 | tf_op jit(solution)/shard_map/attention_back/ppermute | solution.py:1578
  731.7 5.7 collective-permute-start.9
  731.7 125.5 %all-to-all-start.3 = ((bf16[24,192,384]{2,1,0:T(8,128)(2,1)}), bf16[24,192,384]{2,1,0:T(8,128)(2,1)}, u32[]{:S(2)}, u32[]{:S(2)}) async-start(bf16[24,192,384]{2,1,0:T(8,128)(2,1)} %bitcast.100), calls=%async_computation.4 | async-start | bytes 7077888 | tf_op jit(solution)/shard_map/attention_back/all_to_all | solution.py:1546
  737.4 119.8 %reduce-scatter.5.cloned.1.call-start = ((), (), s32[]{:S(2)}) async-start(), calls=%async_computation.8 | async-start | bytes 2211840 | tf_op jit(solution)/shard_map/attention_back/reduce_scatter | solution.py:1601
  737.4 25.8 %copy-start.26 = (bf16[256,1536]{1,0:T(8,128)(2,1)S(1)}, bf16[256,1536]{1,0:T(8,128)(2,1)}, u32[]{:S(2)}) copy-start(bf16[256,1536]{1,0:T(8,128)(2,1)} %get-tuple-element.68) | copy-start | bytes 2359300
  740.4 20.6 %collective-permute-start.10 = (bf16[256,1536]{1,0:T(8,128)(2,1)}, bf16[256,1536]{1,0:T(8,128)(2,1)S(1)}, u32[]{:S(2)}, u32[]{:S(2)}) collective-permute-start(bf16[256,1536]{1,0:T(8,128)(2,1)} %fusion.33), channel_id=1, source_target_pairs={{0,2},{1,3},{2,0},{3,1},{4,6},{5,7},{6,4},{7,5},{8,10},{9,11},{10,... | collective-permute-start | bytes 2359304 | tf_op jit(solution)/shard_map/attention_back/ppermute | solution.py:1370
  741.5 21.7 %copy-start.16 = (f32[256,1536]{1,0:T(8,128)S(1)}, f32[256,1536]{1,0:T(8,128)}, u32[]{:S(2)}) copy-start(f32[256,1536]{1,0:T(8,128)} %copy-done.14) | copy-start | bytes 4718596
  741.5 36.4 %collective-permute-start.18 = (bf16[256,1536]{1,0:T(8,128)(2,1)}, bf16[256,1536]{1,0:T(8,128)(2,1)}, u32[]{:S(2)}, u32[]{:S(2)}) collective-permute-start(bf16[256,1536]{1,0:T(8,128)(2,1)} %get-tuple-element.100), channel_id=1, source_target_pairs={{0,2},{1,3},{2,0},{3,1},{4,6},{5,7},{6,4},{7,5},{8,10},{9,11},{10,... | collective-permute-start | bytes 2359304 | tf_op jit(solution)/shard_map/expert_grads/ppermute | solution.py:1374
  742.6 20.7 %copy-start.18 = (f32[2,256,1536]{2,1,0:T(8,128)S(1)}, f32[2,256,1536]{2,1,0:T(8,128)}, u32[]{:S(2)}) copy-start(f32[2,256,1536]{2,1,0:T(8,128)} %copy-done.17) | copy-start | bytes 9437188
  765.6 28.4 %collective-permute-start.16 = (bf16[256,1536]{1,0:T(8,128)(2,1)S(1)}, bf16[256,1536]{1,0:T(8,128)(2,1)S(1)}, u32[]{:S(2)}, u32[]{:S(2)}) collective-permute-start(bf16[256,1536]{1,0:T(8,128)(2,1)S(1)} %fusion.15), channel_id=1, source_target_pairs={{0,2},{1,3},{2,0},{3,1},{4,6},{5,7},{6,4},{7,5},{8,10},{9,11},{10,... | collective-permute-start | bytes 2359304 | tf_op jit(solution)/shard_map/attention_back/ppermute | solution.py:1374
  780.4 19.9 %collective-permute-start.19 = (bf16[2,1,256,1536]{3,2,1,0:T(8,128)(2,1)S(1)}, bf16[2,1,256,1536]{3,2,1,0:T(8,128)(2,1)}, u32[]{:S(2)}, u32[]{:S(2)}) collective-permute-start(bf16[2,1,256,1536]{3,2,1,0:T(8,128)(2,1)S(1)} %bitcast.108), channel_id=1, source_target_pairs={{0,1},{1,0},{2,3},{3,2},{4,5},{5,4},{6,7},{7,6},{8,9},{9,8},{10,11... | collective-permute-start | bytes 4718600 | tf_op jit(solution)/shard_map/expert_grads/ppermute | solution.py:1378
  780.6 14.2 %collective-permute-start.11 = (f32[2,1536]{1,0:T(2,128)S(1)}, f32[2,1536]{1,0:T(2,128)S(1)}, u32[]{:S(2)}, u32[]{:S(2)}) collective-permute-start(f32[2,1536]{1,0:T(2,128)S(1)} %pad_maximum_fusion.12), channel_id=1, source_target_pairs={{0,1},{1,0},{2,3},{3,2},{4,5},{5,4},{6,7},{7,6},{8,9},{9,8},{10,11... | collective-permute-start | bytes 36872 | tf_op jit(solution)/shard_map/attention_back/ppermute | solution.py:1610
  794.6 39.0 %collective-permute-start.17 = (bf16[2,1,256,1536]{3,2,1,0:T(8,128)(2,1)S(1)}, bf16[2,1,256,1536]{3,2,1,0:T(8,128)(2,1)}, u32[]{:S(2)}, u32[]{:S(2)}) collective-permute-start(bf16[2,1,256,1536]{3,2,1,0:T(8,128)(2,1)S(1)} %bitcast.106), channel_id=1, source_target_pairs={{0,1},{1,0},{2,3},{3,2},{4,5},{5,4},{6,7},{7,6},{8,9},{9,8},{10,11... | collective-permute-start | bytes 4718600 | tf_op jit(solution)/shard_map/attention_back/ppermute | solution.py:1378
  794.7 3.8 collective-permute-start.12
  798.5 5.5 collective-permute-start.13
  804.1 10.2 %copy-start.38 = (bf16[192,384]{1,0:T(8,128)(2,1)S(1)}, bf16[192,384]{1,0:T(8,128)(2,1)}, u32[]{:S(2)}) copy-start(bf16[192,384]{1,0:T(8,128)(2,1)} %reduce-scatter.3.cloned.1.call-done) | copy-start | bytes 442372
  804.1 6.7 collective-permute-start.14
  810.8 22.7 %collective-permute-start.15 = (f32[2,1536]{1,0:T(2,128)S(1)}, f32[2,1536]{1,0:T(2,128)S(1)}, u32[]{:S(2)}, u32[]{:S(2)}) collective-permute-start(f32[2,1536]{1,0:T(2,128)S(1)} %add.219), channel_id=1, source_target_pairs={{0,16},{8,24},{16,0},{24,8},{1,17},{9,25},{17,1},{25,9},{2,18},{10... | collective-permute-start | bytes 36872 | tf_op jit(solution)/shard_map/attention_back/ppermute | solution.py:1610
  (31 other events, 90.8 us)
Sparse Core Ops, SparseCore 0:
  13.2 108.5 all-gather.3
  124.0 169.2 all-gather.5
  647.4 66.4 reduce-scatter.2
  742.7 114.4 reduce-scatter.4

commit v6 on v5

--- a/solution.py
+++ b/solution.py
@@ -1408,6 +1408,21 @@
         )
         owned_first, owned_second = to_groups(slices_first), to_groups(slices_second)
 
+        spread_lanes = slice_rows * 128 // piece_rows
+        spread = jnp.sum(
+            jnp.where(
+                own_piece(routes)[:, :, None] == jnp.arange(expert_count, dtype=jnp.int32),
+                own_piece(shares)[:, :, None],
+                0.0,
+            ),
+            axis=1,
+        )
+        spread_high = spread.astype(BF16)
+        spread_low = (spread - spread_high.astype(F32)).astype(BF16)
+        spread_both = jnp.pad(
+            jnp.concatenate([spread_high, spread_low], axis=1),
+            ((0, 0), (0, spread_lanes - 2 * expert_count)),
+        )
         qkv_full = lax.all_gather(
             jnp.concatenate(
                 [
@@ -1416,6 +1431,7 @@
                     value_projection_weight,
                     out_weight.T,
                     padded_columns(gain_attn, gain_ffn),
+                    spread_both.reshape(slice_rows, 128),
                 ],
                 axis=1,
             ),
@@ -1434,23 +1450,7 @@
 
     with jax.named_scope("cotangents"):
         cotangent_piece = own_piece(cotangent)
-        spread = jnp.sum(
-            jnp.where(
-                own_piece(routes)[:, :, None] == jnp.arange(expert_count, dtype=jnp.int32),
-                own_piece(shares)[:, :, None],
-                0.0,
-            ),
-            axis=1,
-        )
-        spread_high = spread.astype(BF16)
-        spread_low = (spread - spread_high.astype(F32)).astype(BF16)
-        spread_both = jnp.pad(
-            jnp.concatenate([spread_high, spread_low], axis=1),
-            ((0, 0), (0, 128 - 2 * expert_count)),
-        )
-        cotangent_own = lax.all_gather(
-            jnp.concatenate([cotangent_piece, spread_both], axis=1), GROUP, axis=0, tiled=False
-        )
+        cotangent_own = lax.all_gather(cotangent_piece, GROUP, axis=0, tiled=False)
 
     with jax.named_scope("attention"):
         positions = doc_positions(segments)
@@ -1495,7 +1495,8 @@
 
     with jax.named_scope("exchange"):
         cotangent_own, normed_ffn = lax.optimization_barrier((cotangent_own, normed_ffn))
-        spread_own = cotangent_own[:, :, model_width:]
+        spread_own = qkv_full[:, qkv_cols + query_cols + 128 :]
+        spread_own = spread_own.reshape(groups, piece_rows, spread_lanes)
         spread_all = jnp.concatenate(
             [spread_own, lax.ppermute(spread_own, TENSOR, sibling)], axis=1
         )

time: 886 us -> 891 us (level)
  Pallas kernels: 351 us -> 360 us
    pallas_call x2, Pallas kernels: 300 us -> 310 us  [expert_call(): pl.pallas_call(partial(expert_kernel, line=line, chunk=chunk, gathers=gat...]
  transfers between devices with their start and end apart: 28 -> 28, of which waited for: 19 -> 18; matrix products, arithmetic and copies ran while one was open for 12% -> 12% of each run, Pallas kernels for 6% -> 6%
where the time goes in v6:
time: 891 us; the launch traced here: 883 us
  Pallas kernels  360 us (40%)
  waiting for transfers between devices  312 us (35%)
  other arithmetic  68.8 us (8%)
  local copies, waits for them, and re-layouts  57.9 us (6%)
  starting transfers between devices  44.8 us (5%)
  matrix products  23.7 us (3%)
  between operations  15.1 us (2%)
    pallas_call x2, Pallas kernels, expert_call(): pl.pallas_call(partial(expert_kernel, line=line, chunk=chunk, gathers=gat...  310 us
    all_to_all x2, waiting for transfers between devices, to_groups(): owned = lax.all_to_all(values, GROUP, 0, 0, tiled=True)  104 us
    ppermute x2, waiting for transfers between devices, sum_over_tensor(): lax.ppermute(pick(half, 0, 1 - chip_half).astype(BF16), TENSOR, across)  74.4 us
    ppermute x3, waiting for transfers between devices, gather_over_tensor(): other = lax.ppermute(piece, TENSOR, across)  42.3 us
    pallas_call x1, Pallas kernels, attention_backward(): pl.pallas_call(partial(attention_backward_kernel, group_size=group_size,...  31.8 us
    ppermute x5, waiting for transfers between devices, expert_plan(): lax.ppermute(gains, axis, [(i, i ^ step) for i in range(size)])  23.5 us
    reduce_scatter x1, waiting for transfers between devices, expert_plan(): lax.psum_scatter(grad_qkv_local, GROUP, scatter_dimension=0, tiled=True)  20.2 us
    all_to_all x2, waiting for transfers between devices, returned(): return lax.all_to_all(flat, GROUP, 0, 0, tiled=True).reshape(total.shape)  19.4 us
  transfers between devices with their start and end apart: 28, of which 18 were waited for; matrix products, arithmetic and copies ran while one was open for 12% of the time, Pallas kernels for 6%

profile of v6, /device:TPU:0, one launch (start us, length us, event | category | flops | bytes accessed | tf_op | source)
XLA Modules:
  0.0 882.6 jit_solution(7124454822556688920)
XLA Ops:
  21.0 7.3 all-to-all-start
  30.7 3.7 multiply_cosine_fusion
  40.5 3.0 copy.105
  44.2 80.1 %all-to-all-done = bf16[16,192,384]{2,1,0:T(8,128)(2,1)} async-done(((bf16[16,192,384]{2,1,0:T(8,128)(2,1)}), bf16[16,192,384]{2,1,0:T(8,128)(2,1)}, u32[]{:S(2)}, u32[]{:S(2)}) %all-to-all-start) | async-done | bytes 2359328 | tf_op jit(solution)/shard_map/weights/all_to_all | solution.py:1403
  124.4 6.1 all-gather.4.cloned.1.call-done
  130.5 6.3 copy.99
  139.7 2.7 copy.100
  144.1 6.8 fusion.3
  152.0 4.8 all-to-all-start.1
  157.1 10.7 %collective-permute-done.1 = bf16[1024,256]{1,0:T(8,128)(2,1)S(1)} collective-permute-done((bf16[1024,256]{1,0:T(8,128)(2,1)S(1)}, bf16[1024,256]{1,0:T(8,128)(2,1)S(1)}, u32[]{:S(2)}, u32[]{:S(2)}) %collective-permute-start.1) | collective-permute-done | bytes 524320 | tf_op jit(solution)/shard_map/attention/ppermute | solution.py:1478
  168.2 18.7 %attention.1 = (bf16[1024,384]{1,0:T(8,128)(2,1)S(1)}, f32[4,2,768,1]{3,2,1,0:T(8,128)}) custom-call(s32[1]{0:T(128)} %bitcast.11.first_ref, bf16[1024,384]{1,0:T(8,128)(2,1)S(1)} %slice.141.query_ref, bf16[2048,256]{1,0:T(8,128)(2,1)S(1)} %maximum_select_fusion.6.key_value_ref, s32[1024,1]{1,0:T(8,128)S(1)} %copy.106.doc_start_ref), custom_call_target="tpu_custom_call" | custom-call | flops 16106127360 | bytes 4194304 | tf_op jit(solution)/shard_map/attention/pallas_call | solution.py:1252
  194.2 3.0 convert_add_fusion.1
  205.3 56.2 %collective-permute-done.3 = bf16[256,1536]{1,0:T(8,128)(2,1)} collective-permute-done((bf16[256,1536]{1,0:T(8,128)(2,1)}, bf16[256,1536]{1,0:T(8,128)(2,1)}, u32[]{:S(2)}, u32[]{:S(2)}) %collective-permute-start.3) | collective-permute-done | bytes 786464 | tf_op jit(solution)/shard_map/attention/ppermute | solution.py:1370
  261.5 2.5 bitcast_add_fusion.1
  263.9 23.6 %all-to-all-done.1 = bf16[24,192,384]{2,1,0:T(8,128)(2,1)} async-done(((bf16[24,192,384]{2,1,0:T(8,128)(2,1)}), bf16[24,192,384]{2,1,0:T(8,128)(2,1)}, u32[]{:S(2)}, u32[]{:S(2)}) %all-to-all-start.1) | async-done | bytes 3538976 | tf_op jit(solution)/shard_map/weights/all_to_all | solution.py:1403
  287.5 2.6 multiply_reduce_fusion
  292.3 2.4 all-gather.6.cloned.1.call-done
  294.7 128.6 %experts.2 = (bf16[8,512,3072]{2,1,0:T(8,128)(2,1)}, bf16[8,2,192,384]{3,2,1,0:T(8,128)(2,1)}, bf16[8,2,192,384]{3,2,1,0:T(8,128)(2,1)}, bf16[8,2,256,1536]{3,2,...) custom-call(bf16[256,1536]{1,0:T(8,128)(2,1)} %multiply_multiply_fusion.refs_0_, ...), custom_call_target="tpu_custom_call" | custom-call | flops 57982058496 | bytes 83886080 | tf_op jit(solution)/shard_map/experts/pallas_call | solution.py:1063
  423.4 181.1 %experts.3 = (bf16[256,1536]{1,0:T(8,128)(2,1)}, bf16[256,1536]{1,0:T(8,128)(2,1)}, bf16[8,3,192,384]{3,2,1,0:T(8,128)(2,1)}, bf16[8,3,192,384]{3,2,1,0:T(8,128)...) custom-call(bf16[8,2,256,1536]{3,2,1,0:T(8,128)(2,1)} %get-tuple-ele, ...), custom_call_target="tpu_custom_call" | custom-call | flops 86973087744 | bytes 83886080 | tf_op jit(solution)/shard_map/experts/pallas_call | solution.py:1063
  604.5 4.6 add_convert_fusion.1
  609.8 6.4 all-to-all-start.2
  616.2 2.9 add_convert_fusion.2
  620.6 18.5 %collective-permute-done.6 = bf16[256,1536]{1,0:T(8,128)(2,1)} collective-permute-done((bf16[256,1536]{1,0:T(8,128)(2,1)S(1)}, bf16[256,1536]{1,0:T(8,128)(2,1)}, u32[]{:S(2)}, u32[]{:S(2)}) %collective-permute-start.6) | collective-permute-done | bytes 786464 | tf_op jit(solution)/shard_map/expert_grads/ppermute | solution.py:1374
  644.6 2.8 maximum_select_fusion
  649.1 2.8 convolution_convert_fusion.2
  652.0 5.0 fusion.22.grad_ref
  657.0 19.4 %all-to-all-done.2 = bf16[16,192,384]{2,1,0:T(8,128)(2,1)} async-done(((bf16[16,192,384]{2,1,0:T(8,128)(2,1)}), bf16[16,192,384]{2,1,0:T(8,128)(2,1)}, u32[]{:S(2)}, u32[]{:S(2)}) %all-to-all-start.2) | async-done | bytes 2359328 | tf_op jit(solution)/shard_map/expert_grads/all_to_all | solution.py:1547
  678.7 31.8 %attention_back.1 = (bf16[1024,384]{1,0:T(8,128)(2,1)S(1)}, bf16[2048,256]{1,0:T(8,128)(2,1)S(1)}) custom-call(s32[1]{0:T(128)} %bitcast.11.first_ref, bf16[1024,384]{1,0:T(8,128)(2,1)S(1)} %copy-done.5, bf16[2048,256]{1,0:T(8,128)(2,1)S(1)} %copy-done.3, s32[1024,1]{1,0:T(8,128)S(1)} %copy-done.7, f32[4,2,768,1]{3,2,1,0:T(8,128)} %get-tuple-element.69.lse_ref, ...), custom_call_target="tpu_custom_call" | custom-call | flops 40265318400 | bytes 8388608 | tf_op jit(solution)/shard_map/attention_back/pallas_call | solution.py:1281
  711.4 2.4 collective-permute-start.8
  713.8 7.4 collective-permute-done.5
  721.2 6.2 add_convert_fusion
  727.5 2.9 fusion.27
  730.5 4.3 convolution_convert_fusion.1
  736.0 5.7 all-to-all-start.3
  747.1 18.2 %collective-permute-done.10 = bf16[256,1536]{1,0:T(8,128)(2,1)S(1)} collective-permute-done((bf16[256,1536]{1,0:T(8,128)(2,1)}, bf16[256,1536]{1,0:T(8,128)(2,1)S(1)}, u32[]{:S(2)}, u32[]{:S(2)}) %collective-permute-start.10) | collective-permute-done | bytes 786464 | tf_op jit(solution)/shard_map/attention_back/ppermute | solution.py:1370
  771.5 10.8 %collective-permute-done.18 = bf16[256,1536]{1,0:T(8,128)(2,1)} collective-permute-done((bf16[256,1536]{1,0:T(8,128)(2,1)}, bf16[256,1536]{1,0:T(8,128)(2,1)}, u32[]{:S(2)}, u32[]{:S(2)}) %collective-permute-start.18) | collective-permute-done | bytes 786464 | tf_op jit(solution)/shard_map/expert_grads/ppermute | solution.py:1374
  782.2 2.3 maximum_select_fusion.5
  785.2 13.0 %collective-permute-done.16 = bf16[256,1536]{1,0:T(8,128)(2,1)S(1)} collective-permute-done((bf16[256,1536]{1,0:T(8,128)(2,1)S(1)}, bf16[256,1536]{1,0:T(8,128)(2,1)S(1)}, u32[]{:S(2)}, u32[]{:S(2)}) %collective-permute-start.16) | collective-permute-done | bytes 786464 | tf_op jit(solution)/shard_map/attention_back/ppermute | solution.py:1374
  804.6 3.7 maximum_select_fusion.2
  809.8 2.7 slice_bitcast_fusion.1
  812.5 2.7 collective-permute-done.14
  815.2 3.3 collective-permute-start.15
  819.2 18.6 %collective-permute-done.15 = f32[2,1536]{1,0:T(2,128)S(1)} collective-permute-done((f32[2,1536]{1,0:T(2,128)S(1)}, f32[2,1536]{1,0:T(2,128)S(1)}, u32[]{:S(2)}, u32[]{:S(2)}) %collective-permute-start.15) | collective-permute-done | bytes 12320 | tf_op jit(solution)/shard_map/attention_back/ppermute | solution.py:1611
  837.9 3.8 maximum_select_fusion.1
  841.7 20.2 %reduce-scatter.5.cloned.1.call-done = bf16[192,640]{1,0:T(8,128)(2,1)} async-done(((bf16[1536,640]{1,0:T(8,128)(2,1)}), bf16[192,640]{1,0:T(8,128)(2,1)}) %reduce-scatter.5.cloned.1.call-update) | async-done | bytes 245776 | tf_op jit(solution)/shard_map/attention_back/reduce_scatter | solution.py:1602
  867.4 2.5 bitcast_convert_fusion
  870.3 2.5 bitcast_convert_fusion.1
  872.8 2.5 bitcast_convert_fusion.2
  (237 shorter events, 87.6 us)
Async XLA Ops:
  7.2 7.7 copy-start.33
  7.2 123.3 %all-gather.4.cloned.1.call-start = ((), (), s32[]{:S(2)}) async-start(), calls=%async_computation.6 | async-start | bytes 4423680 | tf_op jit(solution)/shard_map/weights/all_gather | solution.py:1426
  21.0 103.4 %all-to-all-start = ((bf16[16,192,384]{2,1,0:T(8,128)(2,1)}), bf16[16,192,384]{2,1,0:T(8,128)(2,1)}, u32[]{:S(2)}, u32[]{:S(2)}) async-start(bf16[16,192,384]{2,1,0:T(8,128)(2,1)} %bitcast.5), calls=%async_computation | async-start | bytes 4718592 | tf_op jit(solution)/shard_map/weights/all_to_all | solution.py:1403
  28.3 266.5 %all-gather.6.cloned.1.call-start = ((), (), s32[]{:S(2)}) async-start(), calls=%async_computation.9 | async-start | bytes 7077888 | tf_op jit(solution)/shard_map/cotangents/all_gather | solution.py:1453
  44.2 99.8 %copy-start.48 = (f32[1024]{0:T(1024)}, f32[1024]{0:T(1024)S(1)}, u32[]{:S(2)}) copy-start(f32[1024]{0:T(1024)S(1)} %add_rsqrt_fusion) | copy-start | bytes 12292
  144.1 146.1 %copy-start.37 = (f32[1536]{0:T(1024)}, f32[1536]{0:T(1024)S(1)}, u32[]{:S(2)}) copy-start(f32[1536]{0:T(1024)S(1)} %get-tuple-element.87) | copy-start | bytes 18436
  144.1 6.9 copy-start.23
  144.1 6.9 copy-start.24
  151.9 15.9 %collective-permute-start.1 = (bf16[1024,256]{1,0:T(8,128)(2,1)S(1)}, bf16[1024,256]{1,0:T(8,128)(2,1)S(1)}, u32[]{:S(2)}, u32[]{:S(2)}) collective-permute-start(bf16[1024,256]{1,0:T(8,128)(2,1)S(1)} %pad_maximum_fusion.10), channel_id=1, source_target_pairs={{0,4},{4,0},{1,5},{5,1},{2,6},{6,2},{3,7},{7,3},{8,12},{12,8},{9,1... | collective-permute-start | bytes 1572872 | tf_op jit(solution)/shard_map/attention/ppermute | solution.py:1478
  152.0 135.6 %all-to-all-start.1 = ((bf16[24,192,384]{2,1,0:T(8,128)(2,1)}), bf16[24,192,384]{2,1,0:T(8,128)(2,1)}, u32[]{:S(2)}, u32[]{:S(2)}) async-start(bf16[24,192,384]{2,1,0:T(8,128)(2,1)} %bitcast.99), calls=%async_computation.1 | async-start | bytes 7077888 | tf_op jit(solution)/shard_map/weights/all_to_all | solution.py:1403
  157.0 29.9 %copy-start.6 = (s32[1024,1]{1,0:T(8,128)}, s32[1024,1]{1,0:T(8,128)S(1)}, u32[]{:S(2)}) copy-start(s32[1024,1]{1,0:T(8,128)S(1)} %copy.106.doc_start_ref) | copy-start | bytes 12292
  157.1 29.8 %copy-start.4 = (bf16[1024,384]{1,0:T(8,128)(2,1)}, bf16[1024,384]{1,0:T(8,128)(2,1)S(1)}, u32[]{:S(2)}) copy-start(bf16[1024,384]{1,0:T(8,128)(2,1)S(1)} %slice.141.query_ref) | copy-start | bytes 2359300
  168.2 18.8 %copy-start.2 = (bf16[2048,256]{1,0:T(8,128)(2,1)}, bf16[2048,256]{1,0:T(8,128)(2,1)S(1)}, u32[]{:S(2)}) copy-start(bf16[2048,256]{1,0:T(8,128)(2,1)S(1)} %maximum_select_fusion.6.key_value_ref) | copy-start | bytes 3145732
  168.2 18.8 %copy-start.19 = (bf16[1536,1280]{1,0:T(8,128)(2,1)S(1)}, bf16[1536,1280]{1,0:T(8,128)(2,1)}, u32[]{:S(2)}) copy-start(bf16[1536,1280]{1,0:T(8,128)(2,1)} %all-gather.4.cloned.1.call-done) | copy-start | bytes 11796484
  190.6 3.6 collective-permute-start.2
  190.6 96.9 %collective-permute-start = (bf16[8,2,192,384]{3,2,1,0:T(8,128)(2,1)}, bf16[8,2,192,384]{3,2,1,0:T(8,128)(2,1)}, u32[]{:S(2)}, u32[]{:S(2)}) collective-permute-start(bf16[8,2,192,384]{3,2,1,0:T(8,128)(2,1)} %bitcast.8.refs_3_), channel_id=1, source_target_pairs={{0,2},{1,3},{2,0},{3,1},{4,6},{5,7},{6,4},{7,5},{8,10},{9,11},{10,... | collective-permute-start | bytes 7077896 | tf_op jit(solution)/shard_map/weights/ppermute | solution.py:1444
  193.0 6.9 collective-permute-start.4
  198.2 63.3 %collective-permute-start.3 = (bf16[256,1536]{1,0:T(8,128)(2,1)}, bf16[256,1536]{1,0:T(8,128)(2,1)}, u32[]{:S(2)}, u32[]{:S(2)}) collective-permute-start(bf16[256,1536]{1,0:T(8,128)(2,1)} %fusion.28), channel_id=1, source_target_pairs={{0,2},{1,3},{2,0},{3,1},{4,6},{5,7},{6,4},{7,5},{8,10},{9,11},{10,... | collective-permute-start | bytes 2359304 | tf_op jit(solution)/shard_map/attention/ppermute | solution.py:1370
  290.1 133.3 %copy-start.46 = (f32[256]{0:T(256)}, f32[256]{0:T(256)S(1)}, u32[]{:S(2)}) copy-start(f32[256]{0:T(256)S(1)} %get-tuple-element.91) | copy-start | bytes 3076
  290.1 133.3 %copy-start.43 = (f32[256]{0:T(256)}, f32[256]{0:T(256)S(1)}, u32[]{:S(2)}) copy-start(f32[256]{0:T(256)S(1)} %fusion.31) | copy-start | bytes 3076
  609.8 66.6 %all-to-all-start.2 = ((bf16[16,192,384]{2,1,0:T(8,128)(2,1)}), bf16[16,192,384]{2,1,0:T(8,128)(2,1)}, u32[]{:S(2)}, u32[]{:S(2)}) async-start(bf16[16,192,384]{2,1,0:T(8,128)(2,1)} %bitcast.101), calls=%async_computation.3 | async-start | bytes 4718592 | tf_op jit(solution)/shard_map/expert_grads/all_to_all | solution.py:1547
  616.2 118.5 %reduce-scatter.3.cloned.1.call-start = ((), (), s32[]{:S(2)}) async-start(), calls=%async_computation.7 | async-start | bytes 1327104 | tf_op jit(solution)/shard_map/attention_back/reduce_scatter | solution.py:1562
  619.1 22.0 %copy-start.28 = (f32[2048,128]{1,0:T(8,128)S(1)}, f32[2048,128]{1,0:T(8,128)}, u32[]{:S(2)}) copy-start(f32[2048,128]{1,0:T(8,128)} %copy-done.27) | copy-start | bytes 3145732
  619.1 20.0 %collective-permute-start.6 = (bf16[256,1536]{1,0:T(8,128)(2,1)S(1)}, bf16[256,1536]{1,0:T(8,128)(2,1)}, u32[]{:S(2)}, u32[]{:S(2)}) collective-permute-start(bf16[256,1536]{1,0:T(8,128)(2,1)S(1)} %get-tuple-element.103), channel_id=1, source_target_pairs={{0,2},{1,3},{2,0},{3,1},{4,6},{5,7},{6,4},{7,5},{8,10},{9,11},{10,... | collective-permute-start | bytes 2359304 | tf_op jit(solution)/shard_map/expert_grads/ppermute | solution.py:1374
  641.0 3.6 collective-permute-start.7
  641.9 7.2 copy-start.10
  641.9 79.2 %collective-permute-start.5 = (bf16[8,3,192,384]{3,2,1,0:T(8,128)(2,1)}, bf16[8,3,192,384]{3,2,1,0:T(8,128)(2,1)}, u32[]{:S(2)}, u32[]{:S(2)}) collective-permute-start(bf16[8,3,192,384]{3,2,1,0:T(8,128)(2,1)} %get-tuple-element.64), channel_id=1, source_target_pairs={{0,2},{1,3},{2,0},{3,1},{4,6},{5,7},{6,4},{7,5},{8,10},{9,11},{10,... | collective-permute-start | bytes 10616840 | tf_op jit(solution)/shard_map/expert_grads/ppermute | solution.py:1550
  652.0 24.5 %copy-start.3 = (bf16[2048,256]{1,0:T(8,128)(2,1)S(1)}, bf16[2048,256]{1,0:T(8,128)(2,1)}, u32[]{:S(2)}) copy-start(bf16[2048,256]{1,0:T(8,128)(2,1)} %copy-done.2) | copy-start | bytes 3145732
  652.0 24.5 %copy-start.5 = (bf16[1024,384]{1,0:T(8,128)(2,1)S(1)}, bf16[1024,384]{1,0:T(8,128)(2,1)}, u32[]{:S(2)}) copy-start(bf16[1024,384]{1,0:T(8,128)(2,1)} %copy-done.4) | copy-start | bytes 2359300
  652.0 24.5 %copy-start.7 = (s32[1024,1]{1,0:T(8,128)S(1)}, s32[1024,1]{1,0:T(8,128)}, u32[]{:S(2)}) copy-start(s32[1024,1]{1,0:T(8,128)} %copy-done.6) | copy-start | bytes 12292
  711.4 15.9 %collective-permute-start.8 = (bf16[1024,256]{1,0:T(8,128)(2,1)S(1)}, bf16[1024,256]{1,0:T(8,128)(2,1)S(1)}, u32[]{:S(2)}, u32[]{:S(2)}) collective-permute-start(bf16[1024,256]{1,0:T(8,128)(2,1)S(1)} %dynamic-slice_bitcast_fusion.2), channel_id=1, source_target_pairs={{0,4},{4,0},{1,5},{5,1},{2,6},{6,2},{3,7},{7,3},{8,12},{12,8},{9,1... | collective-permute-start | bytes 1572872 | tf_op jit(solution)/shard_map/attention_back/ppermute | solution.py:1579
  736.0 5.7 collective-permute-start.9
  736.0 125.9 %all-to-all-start.3 = ((bf16[24,192,384]{2,1,0:T(8,128)(2,1)}), bf16[24,192,384]{2,1,0:T(8,128)(2,1)}, u32[]{:S(2)}, u32[]{:S(2)}) async-start(bf16[24,192,384]{2,1,0:T(8,128)(2,1)} %bitcast.100), calls=%async_computation.4 | async-start | bytes 7077888 | tf_op jit(solution)/shard_map/attention_back/all_to_all | solution.py:1547
  741.6 120.2 %reduce-scatter.5.cloned.1.call-start = ((), (), s32[]{:S(2)}) async-start(), calls=%async_computation.8 | async-start | bytes 2211840 | tf_op jit(solution)/shard_map/attention_back/reduce_scatter | solution.py:1602
  741.7 25.8 %copy-start.26 = (bf16[256,1536]{1,0:T(8,128)(2,1)S(1)}, bf16[256,1536]{1,0:T(8,128)(2,1)}, u32[]{:S(2)}) copy-start(bf16[256,1536]{1,0:T(8,128)(2,1)} %get-tuple-element.68) | copy-start | bytes 2359300
  744.7 20.6 %collective-permute-start.10 = (bf16[256,1536]{1,0:T(8,128)(2,1)}, bf16[256,1536]{1,0:T(8,128)(2,1)S(1)}, u32[]{:S(2)}, u32[]{:S(2)}) collective-permute-start(bf16[256,1536]{1,0:T(8,128)(2,1)} %fusion.29), channel_id=1, source_target_pairs={{0,2},{1,3},{2,0},{3,1},{4,6},{5,7},{6,4},{7,5},{8,10},{9,11},{10,... | collective-permute-start | bytes 2359304 | tf_op jit(solution)/shard_map/attention_back/ppermute | solution.py:1370
  746.2 21.3 %copy-start.16 = (f32[256,1536]{1,0:T(8,128)S(1)}, f32[256,1536]{1,0:T(8,128)}, u32[]{:S(2)}) copy-start(f32[256,1536]{1,0:T(8,128)} %copy-done.14) | copy-start | bytes 4718596
  746.2 36.0 %collective-permute-start.18 = (bf16[256,1536]{1,0:T(8,128)(2,1)}, bf16[256,1536]{1,0:T(8,128)(2,1)}, u32[]{:S(2)}, u32[]{:S(2)}) collective-permute-start(bf16[256,1536]{1,0:T(8,128)(2,1)} %get-tuple-element.102), channel_id=1, source_target_pairs={{0,2},{1,3},{2,0},{3,1},{4,6},{5,7},{6,4},{7,5},{8,10},{9,11},{10,... | collective-permute-start | bytes 2359304 | tf_op jit(solution)/shard_map/expert_grads/ppermute | solution.py:1374
  747.1 20.4 %copy-start.18 = (f32[2,256,1536]{2,1,0:T(8,128)S(1)}, f32[2,256,1536]{2,1,0:T(8,128)}, u32[]{:S(2)}) copy-start(f32[2,256,1536]{2,1,0:T(8,128)} %copy-done.17) | copy-start | bytes 9437188
  769.9 28.4 %collective-permute-start.16 = (bf16[256,1536]{1,0:T(8,128)(2,1)S(1)}, bf16[256,1536]{1,0:T(8,128)(2,1)S(1)}, u32[]{:S(2)}, u32[]{:S(2)}) collective-permute-start(bf16[256,1536]{1,0:T(8,128)(2,1)S(1)} %fusion.15), channel_id=1, source_target_pairs={{0,2},{1,3},{2,0},{3,1},{4,6},{5,7},{6,4},{7,5},{8,10},{9,11},{10,... | collective-permute-start | bytes 2359304 | tf_op jit(solution)/shard_map/attention_back/ppermute | solution.py:1374
  784.6 20.0 %collective-permute-start.19 = (bf16[2,1,256,1536]{3,2,1,0:T(8,128)(2,1)S(1)}, bf16[2,1,256,1536]{3,2,1,0:T(8,128)(2,1)}, u32[]{:S(2)}, u32[]{:S(2)}) collective-permute-start(bf16[2,1,256,1536]{3,2,1,0:T(8,128)(2,1)S(1)} %bitcast.108), channel_id=1, source_target_pairs={{0,1},{1,0},{2,3},{3,2},{4,5},{5,4},{6,7},{7,6},{8,9},{9,8},{10,11... | collective-permute-start | bytes 4718600 | tf_op jit(solution)/shard_map/expert_grads/ppermute | solution.py:1378
  784.7 14.3 %collective-permute-start.11 = (f32[2,1536]{1,0:T(2,128)S(1)}, f32[2,1536]{1,0:T(2,128)S(1)}, u32[]{:S(2)}, u32[]{:S(2)}) collective-permute-start(f32[2,1536]{1,0:T(2,128)S(1)} %pad_maximum_fusion.12), channel_id=1, source_target_pairs={{0,1},{1,0},{2,3},{3,2},{4,5},{5,4},{6,7},{7,6},{8,9},{9,8},{10,11... | collective-permute-start | bytes 36872 | tf_op jit(solution)/shard_map/attention_back/ppermute | solution.py:1611
  798.9 39.0 %collective-permute-start.17 = (bf16[2,1,256,1536]{3,2,1,0:T(8,128)(2,1)S(1)}, bf16[2,1,256,1536]{3,2,1,0:T(8,128)(2,1)}, u32[]{:S(2)}, u32[]{:S(2)}) collective-permute-start(bf16[2,1,256,1536]{3,2,1,0:T(8,128)(2,1)S(1)} %bitcast.106), channel_id=1, source_target_pairs={{0,1},{1,0},{2,3},{3,2},{4,5},{5,4},{6,7},{7,6},{8,9},{9,8},{10,11... | collective-permute-start | bytes 4718600 | tf_op jit(solution)/shard_map/attention_back/ppermute | solution.py:1378
  799.0 3.8 collective-permute-start.12
  802.8 5.5 collective-permute-start.13
  808.3 10.2 %copy-start.39 = (bf16[192,384]{1,0:T(8,128)(2,1)S(1)}, bf16[192,384]{1,0:T(8,128)(2,1)}, u32[]{:S(2)}) copy-start(bf16[192,384]{1,0:T(8,128)(2,1)} %reduce-scatter.3.cloned.1.call-done) | copy-start | bytes 442372
  808.3 6.9 collective-permute-start.14
  815.2 22.6 %collective-permute-start.15 = (f32[2,1536]{1,0:T(2,128)S(1)}, f32[2,1536]{1,0:T(2,128)S(1)}, u32[]{:S(2)}, u32[]{:S(2)}) collective-permute-start(f32[2,1536]{1,0:T(2,128)S(1)} %add.219), channel_id=1, source_target_pairs={{0,16},{8,24},{16,0},{24,8},{1,17},{9,25},{17,1},{25,9},{2,18},{10... | collective-permute-start | bytes 36872 | tf_op jit(solution)/shard_map/attention_back/ppermute | solution.py:1611
  (33 other events, 94.4 us)
Sparse Core Ops, SparseCore 0:
  15.0 115.4 all-gather.3
  132.7 162.0 all-gather.5
  652.1 66.8 reduce-scatter.2
  747.2 114.5 reduce-scatter.4

commit v7 on v5

--- a/solution.py
+++ b/solution.py
@@ -527,42 +527,44 @@
         self.place, self.tokens = place, tokens
         self.recv, self.along, self.across, self.cores = sems
 
-    def line_copy(self, at, side):
+    def line_copy(self, at, side, source=None):
         here, tokens = at * 2 + self.place.y, self.tokens
         return remote(
-            tokens.at[here, 0],
+            tokens.at[here, 0] if source is None else source,
             tokens.at[here, 0],
             self.along.at[at, (side + 1) // 2],
             self.recv.at[here, 0],
             self.place.beside(side),
         )
 
-    def pair_copy(self, at, column):
+    def pair_copy(self, at, column, source=None):
         here, tokens = at * 2 + column, self.tokens
         return remote(
-            tokens.at[here, 0],
+            tokens.at[here, 0] if source is None else source,
             tokens.at[here, 0],
             self.across.at[at],
             self.recv.at[here, 0],
             self.place.partner,
         )
 
-    def core_copy(self, here):
+    def core_copy(self, here, source=None):
         tokens = self.tokens
         return remote(
-            tokens.at[here, 0],
+            tokens.at[here, 0] if source is None else source,
             tokens.at[here, 1],
             self.cores.at[here],
             self.recv.at[here, 1],
             self.place.sibling,
         )
 
-    def start(self):
+    def start(self, piece):
         place = self.place
         for side in (-1, 1):
-            pl.when(place.inside(place.z + side))(lambda: self.line_copy(place.z, side).start())
-        self.pair_copy(place.z, place.y).start()
-        self.core_copy(place.z * 2 + place.y).start()
+            pl.when(place.inside(place.z + side))(
+                lambda: self.line_copy(place.z, side, piece).start()
+            )
+        self.pair_copy(place.z, place.y, piece).start()
+        self.core_copy(place.z * 2 + place.y, piece).start()
 
     def came_along(self, at, side):
         place = self.place
@@ -820,9 +822,8 @@
     if gathers:
         own_block = place.z * 2 + place.y
         own_copy = pltpu.make_async_copy(tokens_in, tokens_hbm.at[own_block, 0], row_sems.at[0, 0])
+        mover.start(tokens_in)
         own_copy.start()
-        own_copy.wait()
-        mover.start()
         for step in range(steps):
             cotangent_copy(step).start()
     weight_loads = weight_copies(own_hbm, other_hbm, weights, load_sems)
@@ -853,6 +854,8 @@
         for copy in row_copies(step, slot):
             copy.start()
 
+    if gathers:
+        own_copy.wait()
     load_rows(0, 0)
     for copy in weight_loads:
         copy.wait()

time: 886 us -> 875 us (0.988)
  Pallas kernels: 351 us -> 338 us
    pallas_call x2, Pallas kernels: 300 us -> 288 us  [expert_call(): pl.pallas_call(partial(expert_kernel, line=line, chunk=chunk, gathers=gat...]
where the time goes in v7:
time: 875 us; the launch traced here: 867 us
  Pallas kernels  338 us (39%)
  waiting for transfers between devices  319 us (36%)
  other arithmetic  68.9 us (8%)
  local copies, waits for them, and re-layouts  55.4 us (6%)
  starting transfers between devices  47.2 us (5%)
  matrix products  23.7 us (3%)
  between operations  15.3 us (2%)
    pallas_call x2, Pallas kernels, expert_call(): pl.pallas_call(partial(expert_kernel, line=line, chunk=chunk, gathers=gat...  288 us
    all_to_all x2, waiting for transfers between devices, to_groups(): owned = lax.all_to_all(values, GROUP, 0, 0, tiled=True)  102 us
    ppermute x2, waiting for transfers between devices, sum_over_tensor(): lax.ppermute(pick(half, 0, 1 - chip_half).astype(BF16), TENSOR, across)  81 us
    ppermute x3, waiting for transfers between devices, gather_over_tensor(): other = lax.ppermute(piece, TENSOR, across)  42.1 us
    pallas_call x1, Pallas kernels, attention_backward(): pl.pallas_call(partial(attention_backward_kernel, group_size=group_size,...  31.9 us
    ppermute x5, waiting for transfers between devices, expert_plan(): lax.ppermute(gains, axis, [(i, i ^ step) for i in range(size)])  23.7 us
    reduce_scatter x1, waiting for transfers between devices, expert_plan(): lax.psum_scatter(grad_qkv_local, GROUP, scatter_dimension=0, tiled=True)  20 us
    all_to_all x2, waiting for transfers between devices, returned(): return lax.all_to_all(flat, GROUP, 0, 0, tiled=True).reshape(total.shape)  19.9 us
  transfers between devices with their start and end apart: 28, of which 19 were waited for; matrix products, arithmetic and copies ran while one was open for 12% of the time, Pallas kernels for 6%

profile of v7, /device:TPU:0, one launch (start us, length us, event | category | flops | bytes accessed | tf_op | source)
XLA Modules:
  0.0 867.5 jit_solution(4192316266498860629)
XLA Ops:
  21.1 7.3 all-to-all-start
  32.1 3.7 multiply_cosine_fusion
  42.2 3.0 copy.106
  45.9 73.1 %all-to-all-done = bf16[16,192,384]{2,1,0:T(8,128)(2,1)} async-done(((bf16[16,192,384]{2,1,0:T(8,128)(2,1)}), bf16[16,192,384]{2,1,0:T(8,128)(2,1)}, u32[]{:S(2)}, u32[]{:S(2)}) %all-to-all-start) | async-done | bytes 2359328 | tf_op jit(solution)/shard_map/weights/all_to_all | solution.py:1406
  119.0 2.8 all-gather.4.cloned.1.call-done
  121.8 5.7 copy.100
  130.4 2.7 copy.101
  134.8 6.8 fusion.3
  144.0 4.8 all-to-all-start.1
  149.1 9.5 %collective-permute-done.1 = bf16[1024,256]{1,0:T(8,128)(2,1)S(1)} collective-permute-done((bf16[1024,256]{1,0:T(8,128)(2,1)S(1)}, bf16[1024,256]{1,0:T(8,128)(2,1)S(1)}, u32[]{:S(2)}, u32[]{:S(2)}) %collective-permute-start.1) | collective-permute-done | bytes 524320 | tf_op jit(solution)/shard_map/attention/ppermute | solution.py:1481
  159.0 18.7 %attention.1 = (bf16[1024,384]{1,0:T(8,128)(2,1)S(1)}, f32[4,2,768,1]{3,2,1,0:T(8,128)}) custom-call(s32[1]{0:T(128)} %bitcast.11.first_ref, bf16[1024,384]{1,0:T(8,128)(2,1)S(1)} %slice.141.query_ref, bf16[2048,256]{1,0:T(8,128)(2,1)S(1)} %maximum_select_fusion.6.key_value_ref, s32[1024,1]{1,0:T(8,128)S(1)} %copy.107.doc_start_ref), custom_call_target="tpu_custom_call" | custom-call | flops 16106127360 | bytes 4194304 | tf_op jit(solution)/shard_map/attention/pallas_call | solution.py:1255
  189.7 62.5 %collective-permute-done.3 = bf16[256,1536]{1,0:T(8,128)(2,1)} collective-permute-done((bf16[256,1536]{1,0:T(8,128)(2,1)}, bf16[256,1536]{1,0:T(8,128)(2,1)}, u32[]{:S(2)}, u32[]{:S(2)}) %collective-permute-start.3) | collective-permute-done | bytes 786464 | tf_op jit(solution)/shard_map/attention/ppermute | solution.py:1373
  252.2 2.5 bitcast_add_fusion.1
  254.7 29.1 %all-to-all-done.1 = bf16[24,192,384]{2,1,0:T(8,128)(2,1)} async-done(((bf16[24,192,384]{2,1,0:T(8,128)(2,1)}), bf16[24,192,384]{2,1,0:T(8,128)(2,1)}, u32[]{:S(2)}, u32[]{:S(2)}) %all-to-all-start.1) | async-done | bytes 3538976 | tf_op jit(solution)/shard_map/weights/all_to_all | solution.py:1406
  283.8 2.6 multiply_reduce_fusion
  288.6 4.7 all-gather.6.cloned.1.call-done
  300.5 116.8 %experts.2 = (bf16[8,512,3072]{2,1,0:T(8,128)(2,1)}, bf16[8,2,192,384]{3,2,1,0:T(8,128)(2,1)}, bf16[8,2,192,384]{3,2,1,0:T(8,128)(2,1)}, bf16[8,2,256,1536]{3,2,...) custom-call(bf16[256,1536]{1,0:T(8,128)(2,1)} %multiply_multiply_fusion.refs_0_, ...), custom_call_target="tpu_custom_call" | custom-call | flops 57982058496 | bytes 83886080 | tf_op jit(solution)/shard_map/experts/pallas_call | solution.py:1066
  417.4 171.0 %experts.3 = (bf16[256,1536]{1,0:T(8,128)(2,1)}, bf16[256,1536]{1,0:T(8,128)(2,1)}, bf16[8,3,192,384]{3,2,1,0:T(8,128)(2,1)}, bf16[8,3,192,384]{3,2,1,0:T(8,128)...) custom-call(bf16[8,2,256,1536]{3,2,1,0:T(8,128)(2,1)} %get-tuple-ele, ...), custom_call_target="tpu_custom_call" | custom-call | flops 86973087744 | bytes 83886080 | tf_op jit(solution)/shard_map/experts/pallas_call | solution.py:1066
  588.4 4.6 add_convert_fusion.1
  593.7 7.6 all-to-all-start.2
  601.6 2.9 add_convert_fusion.2
  605.9 18.0 %collective-permute-done.6 = bf16[256,1536]{1,0:T(8,128)(2,1)} collective-permute-done((bf16[256,1536]{1,0:T(8,128)(2,1)S(1)}, bf16[256,1536]{1,0:T(8,128)(2,1)}, u32[]{:S(2)}, u32[]{:S(2)}) %collective-permute-start.6) | collective-permute-done | bytes 786464 | tf_op jit(solution)/shard_map/expert_grads/ppermute | solution.py:1377
  629.4 2.4 maximum_select_fusion
  633.4 2.9 convolution_convert_fusion.2
  636.3 5.0 fusion.26.grad_ref
  641.4 19.9 %all-to-all-done.2 = bf16[16,192,384]{2,1,0:T(8,128)(2,1)} async-done(((bf16[16,192,384]{2,1,0:T(8,128)(2,1)}), bf16[16,192,384]{2,1,0:T(8,128)(2,1)}, u32[]{:S(2)}, u32[]{:S(2)}) %all-to-all-start.2) | async-done | bytes 2359328 | tf_op jit(solution)/shard_map/expert_grads/all_to_all | solution.py:1549
  663.5 31.9 %attention_back.1 = (bf16[1024,384]{1,0:T(8,128)(2,1)S(1)}, bf16[2048,256]{1,0:T(8,128)(2,1)S(1)}) custom-call(s32[1]{0:T(128)} %bitcast.11.first_ref, bf16[1024,384]{1,0:T(8,128)(2,1)S(1)} %copy-done.5, bf16[2048,256]{1,0:T(8,128)(2,1)S(1)} %copy-done.3, s32[1024,1]{1,0:T(8,128)S(1)} %copy-done.7, f32[4,2,768,1]{3,2,1,0:T(8,128)} %get-tuple-element.69.lse_ref, ...), custom_call_target="tpu_custom_call" | custom-call | flops 40265318400 | bytes 8388608 | tf_op jit(solution)/shard_map/attention_back/pallas_call | solution.py:1284
  696.3 2.6 collective-permute-start.8
  698.9 7.1 collective-permute-done.5
  706.0 6.2 add_convert_fusion
  712.3 2.9 fusion.31
  715.3 4.3 convolution_convert_fusion.1
  720.8 5.7 all-to-all-start.3
  731.6 18.4 %collective-permute-done.10 = bf16[256,1536]{1,0:T(8,128)(2,1)S(1)} collective-permute-done((bf16[256,1536]{1,0:T(8,128)(2,1)}, bf16[256,1536]{1,0:T(8,128)(2,1)S(1)}, u32[]{:S(2)}, u32[]{:S(2)}) %collective-permute-start.10) | collective-permute-done | bytes 786464 | tf_op jit(solution)/shard_map/attention_back/ppermute | solution.py:1373
  755.8 11.2 %collective-permute-done.18 = bf16[256,1536]{1,0:T(8,128)(2,1)} collective-permute-done((bf16[256,1536]{1,0:T(8,128)(2,1)}, bf16[256,1536]{1,0:T(8,128)(2,1)}, u32[]{:S(2)}, u32[]{:S(2)}) %collective-permute-start.18) | collective-permute-done | bytes 786464 | tf_op jit(solution)/shard_map/expert_grads/ppermute | solution.py:1377
  767.0 2.5 maximum_select_fusion.5
  770.2 12.9 %collective-permute-done.16 = bf16[256,1536]{1,0:T(8,128)(2,1)S(1)} collective-permute-done((bf16[256,1536]{1,0:T(8,128)(2,1)S(1)}, bf16[256,1536]{1,0:T(8,128)(2,1)S(1)}, u32[]{:S(2)}, u32[]{:S(2)}) %collective-permute-start.16) | collective-permute-done | bytes 786464 | tf_op jit(solution)/shard_map/attention_back/ppermute | solution.py:1377
  785.0 2.6 collective-permute-done.12
  789.4 3.8 maximum_select_fusion.2
  794.7 2.7 slice_bitcast_fusion.1
  797.4 2.5 collective-permute-done.14
  799.9 3.4 collective-permute-start.15
  804.0 18.6 %collective-permute-done.15 = f32[2,1536]{1,0:T(2,128)S(1)} collective-permute-done((f32[2,1536]{1,0:T(2,128)S(1)}, f32[2,1536]{1,0:T(2,128)S(1)}, u32[]{:S(2)}, u32[]{:S(2)}) %collective-permute-start.15) | collective-permute-done | bytes 12320 | tf_op jit(solution)/shard_map/attention_back/ppermute | solution.py:1613
  822.7 3.8 maximum_select_fusion.1
  826.4 20.0 %reduce-scatter.5.cloned.1.call-done = bf16[192,640]{1,0:T(8,128)(2,1)} async-done(((bf16[1536,640]{1,0:T(8,128)(2,1)}), bf16[192,640]{1,0:T(8,128)(2,1)}) %reduce-scatter.5.cloned.1.call-update) | async-done | bytes 245776 | tf_op jit(solution)/shard_map/attention_back/reduce_scatter | solution.py:1604
  852.1 2.5 bitcast_convert_fusion
  854.9 2.5 bitcast_convert_fusion.1
  857.4 2.5 bitcast_convert_fusion.2
  (231 shorter events, 91.1 us)
Async XLA Ops:
  7.2 21.3 %copy-start = (f32[1024,8]{0,1:T(8,128)S(1)}, f32[1024,8]{0,1:T(8,128)}, u32[]{:S(2)}) copy-start(f32[1024,8]{0,1:T(8,128)} %param.26) | copy-start | bytes 98308
  7.2 114.6 %all-gather.4.cloned.1.call-start = ((), (), s32[]{:S(2)}) async-start(), calls=%async_computation.6 | async-start | bytes 3981312 | tf_op jit(solution)/shard_map/weights/all_gather | solution.py:1414
  21.1 97.9 %all-to-all-start = ((bf16[16,192,384]{2,1,0:T(8,128)(2,1)}), bf16[16,192,384]{2,1,0:T(8,128)(2,1)}, u32[]{:S(2)}, u32[]{:S(2)}) async-start(bf16[16,192,384]{2,1,0:T(8,128)(2,1)} %bitcast.5), calls=%async_computation | async-start | bytes 4718592 | tf_op jit(solution)/shard_map/weights/all_to_all | solution.py:1406
  28.4 264.9 %all-gather.6.cloned.1.call-start = ((), (), s32[]{:S(2)}) async-start(), calls=%async_computation.9 | async-start | bytes 7667712 | tf_op jit(solution)/shard_map/cotangents/all_gather | solution.py:1454
  45.9 88.8 %copy-start.47 = (f32[1024]{0:T(1024)}, f32[1024]{0:T(1024)S(1)}, u32[]{:S(2)}) copy-start(f32[1024]{0:T(1024)S(1)} %add_rsqrt_fusion) | copy-start | bytes 12292
  134.7 6.9 copy-start.39
  134.7 151.7 %copy-start.36 = (f32[1536]{0:T(1024)}, f32[1536]{0:T(1024)S(1)}, u32[]{:S(2)}) copy-start(f32[1536]{0:T(1024)S(1)} %get-tuple-element.87) | copy-start | bytes 18436
  134.7 6.9 copy-start.23
  134.7 6.9 copy-start.24
  142.5 16.1 %collective-permute-start.1 = (bf16[1024,256]{1,0:T(8,128)(2,1)S(1)}, bf16[1024,256]{1,0:T(8,128)(2,1)S(1)}, u32[]{:S(2)}, u32[]{:S(2)}) collective-permute-start(bf16[1024,256]{1,0:T(8,128)(2,1)S(1)} %pad_maximum_fusion.11), channel_id=1, source_target_pairs={{0,4},{4,0},{1,5},{5,1},{2,6},{6,2},{3,7},{7,3},{8,12},{12,8},{9,1... | collective-permute-start | bytes 1572872 | tf_op jit(solution)/shard_map/attention/ppermute | solution.py:1481
  144.0 139.9 %all-to-all-start.1 = ((bf16[24,192,384]{2,1,0:T(8,128)(2,1)}), bf16[24,192,384]{2,1,0:T(8,128)(2,1)}, u32[]{:S(2)}, u32[]{:S(2)}) async-start(bf16[24,192,384]{2,1,0:T(8,128)(2,1)} %bitcast.99), calls=%async_computation.1 | async-start | bytes 7077888 | tf_op jit(solution)/shard_map/weights/all_to_all | solution.py:1406
  149.0 28.7 %copy-start.6 = (s32[1024,1]{1,0:T(8,128)}, s32[1024,1]{1,0:T(8,128)S(1)}, u32[]{:S(2)}) copy-start(s32[1024,1]{1,0:T(8,128)S(1)} %copy.107.doc_start_ref) | copy-start | bytes 12292
  149.1 28.6 %copy-start.4 = (bf16[1024,384]{1,0:T(8,128)(2,1)}, bf16[1024,384]{1,0:T(8,128)(2,1)S(1)}, u32[]{:S(2)}) copy-start(bf16[1024,384]{1,0:T(8,128)(2,1)S(1)} %slice.141.query_ref) | copy-start | bytes 2359300
  158.9 18.7 %copy-start.2 = (bf16[2048,256]{1,0:T(8,128)(2,1)}, bf16[2048,256]{1,0:T(8,128)(2,1)S(1)}, u32[]{:S(2)}) copy-start(bf16[2048,256]{1,0:T(8,128)(2,1)S(1)} %maximum_select_fusion.6.key_value_ref) | copy-start | bytes 3145732
  159.0 18.8 %copy-start.19 = (bf16[1536,1152]{1,0:T(8,128)(2,1)S(1)}, bf16[1536,1152]{1,0:T(8,128)(2,1)}, u32[]{:S(2)}) copy-start(bf16[1536,1152]{1,0:T(8,128)(2,1)} %all-gather.4.cloned.1.call-done) | copy-start | bytes 10616836
  181.3 3.6 collective-permute-start.2
  181.4 102.4 %collective-permute-start = (bf16[8,2,192,384]{3,2,1,0:T(8,128)(2,1)}, bf16[8,2,192,384]{3,2,1,0:T(8,128)(2,1)}, u32[]{:S(2)}, u32[]{:S(2)}) collective-permute-start(bf16[8,2,192,384]{3,2,1,0:T(8,128)(2,1)} %bitcast.8.refs_3_), channel_id=1, source_target_pairs={{0,2},{1,3},{2,0},{3,1},{4,6},{5,7},{6,4},{7,5},{8,10},{9,11},{10,... | collective-permute-start | bytes 7077896 | tf_op jit(solution)/shard_map/weights/ppermute | solution.py:1431
  188.3 64.0 %collective-permute-start.3 = (bf16[256,1536]{1,0:T(8,128)(2,1)}, bf16[256,1536]{1,0:T(8,128)(2,1)}, u32[]{:S(2)}, u32[]{:S(2)}) collective-permute-start(bf16[256,1536]{1,0:T(8,128)(2,1)} %fusion.32), channel_id=1, source_target_pairs={{0,2},{1,3},{2,0},{3,1},{4,6},{5,7},{6,4},{7,5},{8,10},{9,11},{10,... | collective-permute-start | bytes 2359304 | tf_op jit(solution)/shard_map/attention/ppermute | solution.py:1373
  286.4 10.6 %copy-start.45 = (f32[256]{0:T(256)}, f32[256]{0:T(256)S(1)}, u32[]{:S(2)}) copy-start(f32[256]{0:T(256)S(1)} %get-tuple-element.91) | copy-start | bytes 3076
  286.4 10.6 %copy-start.42 = (f32[256]{0:T(256)}, f32[256]{0:T(256)S(1)}, u32[]{:S(2)}) copy-start(f32[256]{0:T(256)S(1)} %fusion.38) | copy-start | bytes 3076
  294.4 2.0 collective-permute-start.4
  593.7 67.6 %all-to-all-start.2 = ((bf16[16,192,384]{2,1,0:T(8,128)(2,1)}), bf16[16,192,384]{2,1,0:T(8,128)(2,1)}, u32[]{:S(2)}, u32[]{:S(2)}) async-start(bf16[16,192,384]{2,1,0:T(8,128)(2,1)} %bitcast.101), calls=%async_computation.3 | async-start | bytes 4718592 | tf_op jit(solution)/shard_map/expert_grads/all_to_all | solution.py:1549
  601.3 118.2 %reduce-scatter.3.cloned.1.call-start = ((), (), s32[]{:S(2)}) async-start(), calls=%async_computation.7 | async-start | bytes 1327104 | tf_op jit(solution)/shard_map/attention_back/reduce_scatter | solution.py:1564
  604.5 21.4 %copy-start.28 = (f32[2048,128]{1,0:T(8,128)S(1)}, f32[2048,128]{1,0:T(8,128)}, u32[]{:S(2)}) copy-start(f32[2048,128]{1,0:T(8,128)} %copy-done.27) | copy-start | bytes 3145732
  604.5 19.5 %collective-permute-start.6 = (bf16[256,1536]{1,0:T(8,128)(2,1)S(1)}, bf16[256,1536]{1,0:T(8,128)(2,1)}, u32[]{:S(2)}, u32[]{:S(2)}) collective-permute-start(bf16[256,1536]{1,0:T(8,128)(2,1)S(1)} %get-tuple-element.101), channel_id=1, source_target_pairs={{0,2},{1,3},{2,0},{3,1},{4,6},{5,7},{6,4},{7,5},{8,10},{9,11},{10,... | collective-permute-start | bytes 2359304 | tf_op jit(solution)/shard_map/expert_grads/ppermute | solution.py:1377
  625.8 3.6 collective-permute-start.7
  626.7 79.2 %collective-permute-start.5 = (bf16[8,3,192,384]{3,2,1,0:T(8,128)(2,1)}, bf16[8,3,192,384]{3,2,1,0:T(8,128)(2,1)}, u32[]{:S(2)}, u32[]{:S(2)}) collective-permute-start(bf16[8,3,192,384]{3,2,1,0:T(8,128)(2,1)} %get-tuple-element.64), channel_id=1, source_target_pairs={{0,2},{1,3},{2,0},{3,1},{4,6},{5,7},{6,4},{7,5},{8,10},{9,11},{10,... | collective-permute-start | bytes 10616840 | tf_op jit(solution)/shard_map/expert_grads/ppermute | solution.py:1552
  636.3 25.0 %copy-start.3 = (bf16[2048,256]{1,0:T(8,128)(2,1)S(1)}, bf16[2048,256]{1,0:T(8,128)(2,1)}, u32[]{:S(2)}) copy-start(bf16[2048,256]{1,0:T(8,128)(2,1)} %copy-done.2) | copy-start | bytes 3145732
  636.3 25.0 %copy-start.5 = (bf16[1024,384]{1,0:T(8,128)(2,1)S(1)}, bf16[1024,384]{1,0:T(8,128)(2,1)}, u32[]{:S(2)}) copy-start(bf16[1024,384]{1,0:T(8,128)(2,1)} %copy-done.4) | copy-start | bytes 2359300
  636.3 25.0 %copy-start.7 = (s32[1024,1]{1,0:T(8,128)S(1)}, s32[1024,1]{1,0:T(8,128)}, u32[]{:S(2)}) copy-start(s32[1024,1]{1,0:T(8,128)} %copy-done.6) | copy-start | bytes 12292
  696.3 15.8 %collective-permute-start.8 = (bf16[1024,256]{1,0:T(8,128)(2,1)S(1)}, bf16[1024,256]{1,0:T(8,128)(2,1)S(1)}, u32[]{:S(2)}, u32[]{:S(2)}) collective-permute-start(bf16[1024,256]{1,0:T(8,128)(2,1)S(1)} %dynamic-slice_bitcast_fusion.2), channel_id=1, source_target_pairs={{0,4},{4,0},{1,5},{5,1},{2,6},{6,2},{3,7},{7,3},{8,12},{12,8},{9,1... | collective-permute-start | bytes 1572872 | tf_op jit(solution)/shard_map/attention_back/ppermute | solution.py:1581
  720.8 5.7 collective-permute-start.9
  720.8 125.7 %all-to-all-start.3 = ((bf16[24,192,384]{2,1,0:T(8,128)(2,1)}), bf16[24,192,384]{2,1,0:T(8,128)(2,1)}, u32[]{:S(2)}, u32[]{:S(2)}) async-start(bf16[24,192,384]{2,1,0:T(8,128)(2,1)} %bitcast.100), calls=%async_computation.4 | async-start | bytes 7077888 | tf_op jit(solution)/shard_map/attention_back/all_to_all | solution.py:1549
  726.4 120.0 %reduce-scatter.5.cloned.1.call-start = ((), (), s32[]{:S(2)}) async-start(), calls=%async_computation.8 | async-start | bytes 2211840 | tf_op jit(solution)/shard_map/attention_back/reduce_scatter | solution.py:1604
  726.5 25.8 %copy-start.26 = (bf16[256,1536]{1,0:T(8,128)(2,1)S(1)}, bf16[256,1536]{1,0:T(8,128)(2,1)}, u32[]{:S(2)}) copy-start(bf16[256,1536]{1,0:T(8,128)(2,1)} %get-tuple-element.68) | copy-start | bytes 2359300
  729.5 20.6 %collective-permute-start.10 = (bf16[256,1536]{1,0:T(8,128)(2,1)}, bf16[256,1536]{1,0:T(8,128)(2,1)S(1)}, u32[]{:S(2)}, u32[]{:S(2)}) collective-permute-start(bf16[256,1536]{1,0:T(8,128)(2,1)} %fusion.33), channel_id=1, source_target_pairs={{0,2},{1,3},{2,0},{3,1},{4,6},{5,7},{6,4},{7,5},{8,10},{9,11},{10,... | collective-permute-start | bytes 2359304 | tf_op jit(solution)/shard_map/attention_back/ppermute | solution.py:1373
  730.6 21.7 %copy-start.16 = (f32[256,1536]{1,0:T(8,128)S(1)}, f32[256,1536]{1,0:T(8,128)}, u32[]{:S(2)}) copy-start(f32[256,1536]{1,0:T(8,128)} %copy-done.14) | copy-start | bytes 4718596
  730.6 36.4 %collective-permute-start.18 = (bf16[256,1536]{1,0:T(8,128)(2,1)}, bf16[256,1536]{1,0:T(8,128)(2,1)}, u32[]{:S(2)}, u32[]{:S(2)}) collective-permute-start(bf16[256,1536]{1,0:T(8,128)(2,1)} %get-tuple-element.100), channel_id=1, source_target_pairs={{0,2},{1,3},{2,0},{3,1},{4,6},{5,7},{6,4},{7,5},{8,10},{9,11},{10,... | collective-permute-start | bytes 2359304 | tf_op jit(solution)/shard_map/expert_grads/ppermute | solution.py:1377
  731.6 20.7 %copy-start.18 = (f32[2,256,1536]{2,1,0:T(8,128)S(1)}, f32[2,256,1536]{2,1,0:T(8,128)}, u32[]{:S(2)}) copy-start(f32[2,256,1536]{2,1,0:T(8,128)} %copy-done.17) | copy-start | bytes 9437188
  754.7 28.4 %collective-permute-start.16 = (bf16[256,1536]{1,0:T(8,128)(2,1)S(1)}, bf16[256,1536]{1,0:T(8,128)(2,1)S(1)}, u32[]{:S(2)}, u32[]{:S(2)}) collective-permute-start(bf16[256,1536]{1,0:T(8,128)(2,1)S(1)} %fusion.15), channel_id=1, source_target_pairs={{0,2},{1,3},{2,0},{3,1},{4,6},{5,7},{6,4},{7,5},{8,10},{9,11},{10,... | collective-permute-start | bytes 2359304 | tf_op jit(solution)/shard_map/attention_back/ppermute | solution.py:1377
  769.5 19.9 %collective-permute-start.19 = (bf16[2,1,256,1536]{3,2,1,0:T(8,128)(2,1)S(1)}, bf16[2,1,256,1536]{3,2,1,0:T(8,128)(2,1)}, u32[]{:S(2)}, u32[]{:S(2)}) collective-permute-start(bf16[2,1,256,1536]{3,2,1,0:T(8,128)(2,1)S(1)} %bitcast.108), channel_id=1, source_target_pairs={{0,1},{1,0},{2,3},{3,2},{4,5},{5,4},{6,7},{7,6},{8,9},{9,8},{10,11... | collective-permute-start | bytes 4718600 | tf_op jit(solution)/shard_map/expert_grads/ppermute | solution.py:1381
  769.6 14.2 %collective-permute-start.11 = (f32[2,1536]{1,0:T(2,128)S(1)}, f32[2,1536]{1,0:T(2,128)S(1)}, u32[]{:S(2)}, u32[]{:S(2)}) collective-permute-start(f32[2,1536]{1,0:T(2,128)S(1)} %pad_maximum_fusion.12), channel_id=1, source_target_pairs={{0,1},{1,0},{2,3},{3,2},{4,5},{5,4},{6,7},{7,6},{8,9},{9,8},{10,11... | collective-permute-start | bytes 36872 | tf_op jit(solution)/shard_map/attention_back/ppermute | solution.py:1613
  783.7 39.0 %collective-permute-start.17 = (bf16[2,1,256,1536]{3,2,1,0:T(8,128)(2,1)S(1)}, bf16[2,1,256,1536]{3,2,1,0:T(8,128)(2,1)}, u32[]{:S(2)}, u32[]{:S(2)}) collective-permute-start(bf16[2,1,256,1536]{3,2,1,0:T(8,128)(2,1)S(1)} %bitcast.106), channel_id=1, source_target_pairs={{0,1},{1,0},{2,3},{3,2},{4,5},{5,4},{6,7},{7,6},{8,9},{9,8},{10,11... | collective-permute-start | bytes 4718600 | tf_op jit(solution)/shard_map/attention_back/ppermute | solution.py:1381
  783.8 3.8 collective-permute-start.12
  787.6 5.5 collective-permute-start.13
  793.1 10.2 %copy-start.38 = (bf16[192,384]{1,0:T(8,128)(2,1)S(1)}, bf16[192,384]{1,0:T(8,128)(2,1)}, u32[]{:S(2)}) copy-start(bf16[192,384]{1,0:T(8,128)(2,1)} %reduce-scatter.3.cloned.1.call-done) | copy-start | bytes 442372
  793.2 6.7 collective-permute-start.14
  799.9 22.7 %collective-permute-start.15 = (f32[2,1536]{1,0:T(2,128)S(1)}, f32[2,1536]{1,0:T(2,128)S(1)}, u32[]{:S(2)}, u32[]{:S(2)}) collective-permute-start(f32[2,1536]{1,0:T(2,128)S(1)} %add.219), channel_id=1, source_target_pairs={{0,16},{8,24},{16,0},{24,8},{1,17},{9,25},{17,1},{25,9},{2,18},{10... | collective-permute-start | bytes 36872 | tf_op jit(solution)/shard_map/attention_back/ppermute | solution.py:1613
  (31 other events, 90.7 us)
Sparse Core Ops, SparseCore 0:
  13.2 108.5 all-gather.3
  124.0 169.2 all-gather.5
  636.4 66.4 reduce-scatter.2
  731.8 114.6 reduce-scatter.4
